TPU v7x, 32 devices: a whole 2x2x4 slice. The times are simulated.
32 devices in a mesh: req: 4 (over y, core), tp: 8 (over z, x).
Axes of the slice: x: 2, y: 2, z: 4, core: 2. Of those that a mesh axis runs over, the one named last changes fastest.
Arguments:
- queries: bfloat16 [512, 1536], P(('req', 'tp')), may hold values from -8 to 8
- new_kv: bfloat16 [512, 1024], P(('req', 'tp')), may hold values from -6 to 6
- residual: bfloat16 [512, 1536], P(('req', 'tp')), may hold values from -6 to 6
- placement: int32 [8], P('req'), may hold values from 0 to 7, as said below
- lengths: int32 [8], P('req'), may hold values from 2 to 1024
- page_table: int32 [8, 1, 8], P('req', None, 'tp'), may hold values from 0 to 1, as said below
- cache_keys: bfloat16 [64, 128, 512], P(('req', 'tp')), may hold values from -6 to 6
- cache_values: bfloat16 [64, 128, 512], P(('req', 'tp')), may hold values from -6 to 6
- parents: int32 [8, 64], P('req'), may hold values from 0 to 62, as said below
- accept_leaf: int32 [8], P('req'), may hold values from 0 to 63
- out_weight: bfloat16 [1536, 1536], replicated, may hold values from -0.15625 to 0.15625
- norm_gain: float32 [1536], replicated, may hold values from 0.1 to 1.9
- router_weight: bfloat16 [1536, 40], replicated, may hold values from -0.15625 to 0.15625
- expert_ids: int32 [512, 8], P('req'), may hold values from 0 to 39, all different within a row
- gate_up: bfloat16 [160, 1536, 256], P('tp'), may hold values from -0.15625 to 0.15625
- down_weight: bfloat16 [160, 128, 1536], P('tp'), may hold values from -0.25 to 0.25
Outputs:
- attn_out: bfloat16 [512, 1536], P(('req', 'tp'))
- layer_out: bfloat16 [512, 1536], P(('req', 'tp'))
- accepted_kv: bfloat16 [512, 1024], P(('req', 'tp'))
Inputs may be any that keep to these rules, and one draw needn't show every extreme that they name: `placement`: slot s of each group of 2 slots holds a request whose index is s modulo 2; every request is held once. `page_table`: within each group of 2 slots and each last index, the 2 entries are distinct. parents[s, n] < n for n > 0; parents[s, 0] = 0.
All inputs are finite; a program needn't handle non-finite values.
Results may differ from a plain program's by a relative error of at most 0.01.
Values may be sent and summed in bfloat16 or wider, within the bound.
No kernel may reach another device: no remote copies, remote signals or barrier semaphores. Data moves between devices by JAX's collectives and lax.ppermute only.
A program may use at most 128 MiB of HBM per device.

v0:
```python
import math

import jax
import jax.numpy as jnp
from jax import lax
from jax.sharding import PartitionSpec as P

HEADS = 24
KV_HEADS = 8
HEAD = 64
FF_E = 512
UNIT = 128
DRAFT = 64


neg_big = -1e30
norm_eps = 1e-06


def joined_2(part, axis, combine):
    gathered = jax.tree.map(lambda a: lax.all_gather(a, axis), part)

    def take(source):
        return jax.tree.map(lambda a: lax.dynamic_index_in_dim(a, source, 0, False), gathered)

    return lax.fori_loop(
        1, lax.axis_size(axis), lambda source, state: combine(state, take(source)), take(0)
    )


def ancestry(parents):
    node_count = parents.shape[-1]
    node_ids = jnp.arange(node_count, dtype=jnp.int32)
    linked = (parents[:, :, None] == node_ids[None, None, :]) & (node_ids[None, :, None] > 0)
    reached = jnp.maximum(linked.astype(jnp.float32), jnp.eye(node_count, dtype=jnp.float32)[None])
    for _ in range(node_count.bit_length()):
        reached = jnp.minimum(
            jnp.einsum("rnm,rmk->rnk", reached, reached, precision=lax.Precision.HIGHEST), 1.0
        )
    return reached


def combine_stats(left_stats, right_stats):
    left_max, left_sum, left_out = left_stats
    right_max, right_sum, right_out = right_stats
    top_score = jnp.maximum(left_max, right_max)
    left_scale = jnp.exp(left_max - top_score)
    right_scale = jnp.exp(right_max - top_score)
    row_count, head_count = left_max.shape
    out_sum = (
        left_out.reshape(row_count, head_count, -1) * left_scale[..., None]
        + right_out.reshape(row_count, head_count, -1) * right_scale[..., None]
    )
    return (
        top_score,
        left_sum * left_scale + right_sum * right_scale,
        out_sum.reshape(row_count, -1),
    )


def finish_rows(stat_sum, stat_out):
    row_count, head_count = stat_sum.shape
    return (
        (stat_out.reshape(row_count, head_count, -1) / stat_sum[..., None])
        .reshape(row_count, -1)
        .astype(jnp.bfloat16)
    )


def project_rows(attn_rows, res_rows, out_weight):
    return res_rows.astype(jnp.float32) + jnp.dot(
        attn_rows, out_weight, preferred_element_type=jnp.float32
    )


def rms_normed(hidden, norm_gain):
    scale_rows = lax.rsqrt(jnp.mean(hidden * hidden, axis=-1, keepdims=True) + norm_eps)
    return (hidden * scale_rows * norm_gain).astype(jnp.bfloat16)


def unit_shares(normed_all, router_weight, expert_ids, tp_rank, units_dev):
    logits = jnp.dot(normed_all, router_weight, preferred_element_type=jnp.float32)
    expert_range = jnp.arange(router_weight.shape[1], dtype=jnp.int32)
    onehot = (expert_ids[:, :, None] == expert_range[None, None, :]).astype(jnp.float32)
    chosen = jnp.sum(logits[:, None, :] * onehot, axis=-1)
    expo_chosen = jnp.exp(chosen)
    expert_probs = expo_chosen / jnp.sum(expo_chosen, axis=-1, keepdims=True)
    routing = jnp.sum(expert_probs[:, :, None] * onehot, axis=1)
    unit_ids = tp_rank * units_dev + jnp.arange(units_dev, dtype=jnp.int32)
    expert_of_unit = unit_ids // (FF_E // UNIT)
    pick = (expert_range[:, None] == expert_of_unit[None, :]).astype(jnp.float32)
    return jnp.dot(routing, pick, precision=lax.Precision.HIGHEST)


def per_device(
    queries,
    new_kv,
    residual,
    placement,
    lengths,
    page_table,
    cache_keys,
    cache_values,
    parents,
    accept_leaf,
    out_weight,
    norm_gain,
    router_weight,
    expert_ids,
    gate_up,
    down_weight,
):
    tok_dev = queries.shape[0]
    tp_count = lax.axis_size("tp")
    tp_rank = lax.axis_index("tp")
    group_rows = tok_dev * tp_count
    slot_count = placement.shape[0]
    kv_width = cache_keys.shape[2]
    page_len = cache_keys.shape[1]
    group_size = HEADS // KV_HEADS
    score_scale = 1.0 / math.sqrt(HEAD)
    row_start = tp_rank * tok_dev
    pulled_q, pulled_kv, pulled_res = (
        lax.all_gather(queries, "req", axis=0, tiled=True),
        lax.all_gather(new_kv, "req", axis=0, tiled=True),
        lax.all_gather(residual, "req", axis=0, tiled=True),
    )
    row_offsets = jnp.arange(tok_dev, dtype=jnp.int32)
    row_pos = row_start + row_offsets
    row_slot = row_pos // DRAFT
    slot_match = row_slot[:, None] == jnp.arange(slot_count, dtype=jnp.int32)[None, :]
    source_group = jnp.sum(jnp.where(slot_match, placement[None, :] // slot_count, 0), axis=1)
    source_rows = source_group * tok_dev + row_offsets
    own_q = jnp.take(pulled_q, source_rows, axis=0)
    own_kv = jnp.take(pulled_kv, source_rows, axis=0)
    own_res = jnp.take(pulled_res, source_rows, axis=0)
    all_q, all_kv = (
        lax.all_gather(own_q, "tp", axis=0, tiled=True),
        lax.all_gather(own_kv, "tp", axis=0, tiled=True),
    )
    local_pages = page_table.shape[1]
    page_ids = page_table[:, :, 0].reshape(-1)
    keys_local = jnp.take(cache_keys, page_ids, axis=0).reshape(
        slot_count, local_pages, page_len, KV_HEADS, HEAD
    )
    values_local = jnp.take(cache_values, page_ids, axis=0).reshape(
        slot_count, local_pages, page_len, KV_HEADS, HEAD
    )
    query_blocks = all_q.reshape(slot_count, DRAFT, KV_HEADS, group_size, HEAD)
    scores = (
        jnp.einsum(
            "sqgrd,sltgd->sqgrlt", query_blocks, keys_local, preferred_element_type=jnp.float32
        )
        * score_scale
    )
    positions = (
        jnp.arange(local_pages, dtype=jnp.int32)[:, None] * tp_count + tp_rank
    ) * page_len + jnp.arange(page_len, dtype=jnp.int32)[None, :]
    is_valid = (positions[None] < lengths[:, None, None])[:, None, None, None]
    scores = jnp.where(is_valid, scores, neg_big)
    block_max = jnp.max(scores, axis=-1)
    weights = jnp.where(is_valid, jnp.exp(scores - block_max[..., None]), 0.0).astype(jnp.bfloat16)
    block_sum = jnp.sum(weights.astype(jnp.float32), axis=-1)
    block_out = jnp.einsum(
        "sqgrlt,sltgd->sqgrld", weights, values_local, preferred_element_type=jnp.float32
    )
    page_top = jnp.max(block_max, axis=-1)
    page_scale = jnp.exp(block_max - page_top[..., None])
    stat_max = page_top.reshape(group_rows, HEADS)
    stat_sum = jnp.sum(block_sum * page_scale, axis=-1).reshape(group_rows, HEADS)
    stat_out = jnp.sum(block_out * page_scale[..., None], axis=-2).reshape(group_rows, HEADS * HEAD)
    reached = ancestry(parents)
    reach_rows = jnp.take(reached.reshape(slot_count * DRAFT, DRAFT), row_pos, axis=0)
    key_slot = jnp.arange(group_rows, dtype=jnp.int32) // DRAFT
    same_slot = key_slot[None, :] == row_slot[:, None]
    allowed = same_slot & (jnp.tile(reach_rows, (1, slot_count)) > 0.5)
    tree_keys = all_kv[:, :kv_width].reshape(group_rows, KV_HEADS, HEAD)
    tree_values = all_kv[:, kv_width:].reshape(group_rows, KV_HEADS, HEAD)
    own_blocks = own_q.reshape(tok_dev, KV_HEADS, group_size, HEAD)
    tree_scores = (
        jnp.einsum("igrd,kgd->igrk", own_blocks, tree_keys, preferred_element_type=jnp.float32)
        * score_scale
    )
    tree_mask = allowed[:, None, None, :]
    tree_scores = jnp.where(tree_mask, tree_scores, neg_big)
    tree_max = jnp.max(tree_scores, axis=-1)
    tree_weights = jnp.where(tree_mask, jnp.exp(tree_scores - tree_max[..., None]), 0.0).astype(
        jnp.bfloat16
    )
    tree_sum = jnp.sum(tree_weights.astype(jnp.float32), axis=-1)
    tree_out = jnp.einsum(
        "igrk,kgd->igrd", tree_weights, tree_values, preferred_element_type=jnp.float32
    )
    own_stats = (
        lax.dynamic_slice_in_dim(stat_max, row_start, tok_dev, 0),
        lax.dynamic_slice_in_dim(stat_sum, row_start, tok_dev, 0),
        lax.dynamic_slice_in_dim(stat_out, row_start, tok_dev, 0),
    )
    tree_stats = (
        tree_max.reshape(tok_dev, HEADS),
        tree_sum.reshape(tok_dev, HEADS),
        tree_out.reshape(tok_dev, HEADS * HEAD),
    )
    joined = combine_stats(own_stats, tree_stats)
    stat_max = lax.dynamic_update_slice_in_dim(stat_max, joined[0], row_start, 0)
    stat_sum = lax.dynamic_update_slice_in_dim(stat_sum, joined[1], row_start, 0)
    stat_out = lax.dynamic_update_slice_in_dim(stat_out, joined[2], row_start, 0)
    normed_all = None
    merged = joined_2((stat_max, stat_sum, stat_out), "tp", combine_stats)
    attn_own = finish_rows(
        lax.dynamic_slice_in_dim(merged[1], row_start, tok_dev, 0),
        lax.dynamic_slice_in_dim(merged[2], row_start, tok_dev, 0),
    )
    hidden_own = project_rows(attn_own, own_res, out_weight)
    normed_own = rms_normed(hidden_own, norm_gain)
    units_dev = gate_up.shape[0]
    unit_width = gate_up.shape[2] // 2
    normed_all = lax.all_gather(normed_own, "tp", axis=0, tiled=True)
    shares = unit_shares(normed_all, router_weight, expert_ids, tp_rank, units_dev)
    gate_both = jnp.einsum("td,udh->tuh", normed_all, gate_up, preferred_element_type=jnp.float32)
    activated = (
        jax.nn.silu(gate_both[..., :unit_width]) * gate_both[..., unit_width:] * shares[:, :, None]
    ).astype(jnp.bfloat16)
    moe_own = lax.psum_scatter(
        jnp.einsum("tuh,uhd->td", activated, down_weight, preferred_element_type=jnp.float32),
        "tp",
        scatter_dimension=0,
        tiled=True,
    )
    layer_out = (hidden_own + moe_own).astype(jnp.bfloat16)
    node_ids = jnp.arange(DRAFT, dtype=jnp.int32)
    leaf_pick = (accept_leaf[:, None] == node_ids[None, :]).astype(jnp.float32)
    path_weight = jnp.einsum("sn,snk->sk", leaf_pick, reached, precision=lax.Precision.HIGHEST)
    path_flags = (path_weight > 0.5).astype(jnp.int32)
    path_rank = jnp.cumsum(path_flags, axis=1) - 1
    chosen_node = (path_flags[:, None, :] > 0) & (path_rank[:, None, :] == node_ids[None, :, None])
    own_choice = jnp.take(chosen_node.reshape(slot_count * DRAFT, DRAFT), row_pos, axis=0)
    spread = same_slot & jnp.tile(own_choice, (1, slot_count))
    accepted = jnp.dot(
        spread.astype(jnp.bfloat16), all_kv, preferred_element_type=jnp.float32
    ).astype(jnp.bfloat16)
    return (attn_own, layer_out, accepted)


def solution(mesh):
    in_specs = (
        P(("req", "tp"), None),
        P(("req", "tp"), None),
        P(("req", "tp"), None),
        P("req"),
        P("req"),
        P("req", None, "tp"),
        P(("req", "tp"), None, None),
        P(("req", "tp"), None, None),
        P("req", None),
        P("req"),
        P(),
        P(),
        P(),
        P("req", None),
        P("tp", None, None),
        P("tp", None, None),
    )
    out_specs = (P(("req", "tp"), None), P(("req", "tp"), None), P(("req", "tp"), None))
    return jax.shard_map(
        per_device, mesh=mesh, in_specs=in_specs, out_specs=out_specs, check_vma=False
    )
```

profile of v0, /device:TPU:0, one launch (start us, length us, event | category | flops | bytes accessed | tf_op | source)
XLA Modules:
  0.0 341.5 jit_solution(1608662630412190746)
XLA Ops:
  10.4 7.1 %all_gather.40 = bf16[64,1536]{1,0:T(8,128)(2,1)S(1)} all-gather(bf16[16,1536]{1,0:T(8,128)(2,1)} %param.22), channel_id=1, replica_groups=mesh['req'=4,'tp'=8] {'req'}, dimensions={0}, use_global_device_ids=true | all-gather | bytes 245760 | tf_op jit(solution)/shard_map/all_gather | solution.py:124
  18.9 31.7 %all_gather.41 = bf16[128,1536]{1,0:T(8,128)(2,1)S(1)} all-gather(bf16[16,1536]{1,0:T(8,128)(2,1)S(1)} %broadcast_select_fusion.2), channel_id=1, replica_groups=mesh['req'=4,'tp'=8] {'tp'}, dimensions={0}, use_global_device_ids=true | all-gather | bytes 442368 | tf_op jit(solution)/shard_map/all_gather | solution.py:138
  56.0 1.2 copy.117
  64.5 5.4 %all_gather.43 = bf16[64,1024]{1,0:T(8,128)(2,1)S(1)} all-gather(bf16[16,1024]{1,0:T(8,128)(2,1)S(1)} %copy-done.8), channel_id=1, replica_groups=mesh['req'=4,'tp'=8] {'req'}, dimensions={0}, use_global_device_ids=true | all-gather | bytes 163840 | tf_op jit(solution)/shard_map/all_gather | solution.py:125
  70.6 30.7 %all_gather.44 = bf16[128,1024]{1,0:T(8,128)(2,1)S(1)} all-gather(bf16[16,1024]{1,0:T(8,128)(2,1)S(1)} %broadcast_select_fusion.3), channel_id=1, replica_groups=mesh['req'=4,'tp'=8] {'tp'}, dimensions={0}, use_global_device_ids=true | all-gather | bytes 294912 | tf_op jit(solution)/shard_map/all_gather | solution.py:139
  104.1 3.4 dynamic_update_slice.14
  108.9 5.6 %all_gather.52 = bf16[64,1536]{1,0:T(8,128)(2,1)S(1)} all-gather(bf16[16,1536]{1,0:T(8,128)(2,1)S(1)} %copy-done.7), channel_id=1, replica_groups=mesh['req'=4,'tp'=8] {'req'}, dimensions={0}, use_global_device_ids=true | all-gather | bytes 245760 | tf_op jit(solution)/shard_map/all_gather | solution.py:126
  115.7 32.1 %all_gather.48 = f32[8,128,24]{1,2,0:T(8,128)S(1)} all-gather(f32[1,128,24]{1,2,0:T(8,128)S(1)} %dynamic_update_slice.13), channel_id=1, replica_groups=mesh['req'=4,'tp'=8] {'tp'}, dimensions={0}, use_global_device_ids=true | all-gather | bytes 110592 | tf_op jit(solution)/shard_map/all_gather | solution.py:21
  147.8 31.7 %all_gather.46 = f32[8,128,24]{1,2,0:T(8,128)S(1)} all-gather(f32[1,128,24]{1,2,0:T(8,128)S(1)} %dynamic_update_slice.12), channel_id=1, replica_groups=mesh['req'=4,'tp'=8] {'tp'}, dimensions={0}, use_global_device_ids=true | all-gather | bytes 110592 | tf_op jit(solution)/shard_map/all_gather | solution.py:21
  179.5 32.2 %all-gather.2.cloned.1.call-done = f32[8,128,1536]{2,1,0:T(8,128)} async-done(((f32[1,128,1536]{2,1,0:T(8,128)}), f32[8,128,1536]{2,1,0:T(8,128)}) %all-gather.2.cloned.1.call-update) | async-done | bytes 6291472 | tf_op jit(solution)/shard_map/all_gather | solution.py:21
  213.2 12.8 %while.19 = (s32[]{:T(128)}, f32[128,24]{0,1:T(8,128)S(1)}, f32[128,24]{0,1:T(8,128)S(1)}, f32[128,1536]{0,1:T(8,128)S(1)}, f32[8,128,24]{1,2,0:T(8,128)S(1)}, /...) while((s32[]{:T(128)}, f32[128,24]{0,1:T(8,128)S(1)}, ...), condition=%wide.region_6.9_spmd, body=%wide.region_5.8_spmd.sunk | while | flops 608261 | bytes 5628047 | solution.py:26
  213.3 1.2 constant_dynamic-slice_fusion.3
  215.1 1.2 constant_dynamic-slice_fusion.3
  217.0 1.2 constant_dynamic-slice_fusion.3
  218.8 1.2 constant_dynamic-slice_fusion.3
  220.6 1.2 constant_dynamic-slice_fusion.3
  222.5 1.2 constant_dynamic-slice_fusion.3
  224.3 1.2 constant_dynamic-slice_fusion.3
  226.8 3.2 multiply_reduce_fusion
  230.2 31.1 %all_gather.53 = bf16[128,1536]{1,0:T(8,128)(2,1)S(1)} all-gather(bf16[16,1536]{1,0:T(8,128)(2,1)S(1)} %multiply_convert_fusion), channel_id=1, replica_groups=mesh['req'=4,'tp'=8] {'tp'}, dimensions={0}, use_global_device_ids=true | all-gather | bytes 442368 | tf_op jit(solution)/shard_map/all_gather | solution.py:218
  261.6 7.8 %fusion.16 = f32[128,20,256]{2,0,1:T(8,128)S(1)} fusion(bf16[20,1536,256]{2,1,0:T(8,128)(2,1)} %param.36, bf16[128,1536]{1,0:T(8,128)(2,1)S(1)} %all_gather.53), kind=kOutput, calls=%fused_computation.50 | convolution fusion | flops 2013265920 | bytes 18743296 | tf_op jit(solution)/shard_map/td,udh->tuh/dot_general | solution.py:220
  269.7 2.4 convolution_bitcast_fusion
  273.0 60.1 %reduce-scatter.2.cloned.1.call-done = f32[16,1536]{1,0:T(8,128)} async-done(((f32[128,1536]{1,0:T(8,128)}), f32[16,1536]{1,0:T(8,128)}) %reduce-scatter.2.cloned.1.call-update) | async-done | bytes 98320 | tf_op jit(solution)/shard_map/reduce_scatter | solution.py:224
  333.2 1.5 add_convert_fusion
  (155 shorter events, 30.8 us)
Async XLA Ops:
  7.2 43.5 %copy-start = (bf16[2,128,512]{2,1,0:T(8,128)(2,1)S(1)}, bf16[2,128,512]{2,1,0:T(8,128)(2,1)}, u32[]{:S(2)}) copy-start(bf16[2,128,512]{2,1,0:T(8,128)(2,1)} %param.29) | copy-start | bytes 786436
  7.2 44.0 %copy-start.4 = (bf16[2,128,512]{2,1,0:T(8,128)(2,1)S(1)}, bf16[2,128,512]{2,1,0:T(8,128)(2,1)}, u32[]{:S(2)}) copy-start(bf16[2,128,512]{2,1,0:T(8,128)(2,1)} %param.28) | copy-start | bytes 786436
  7.2 204.6 %all-gather.2.cloned.1.call-start = ((), (), s32[]{:S(2)}) async-start(), calls=%async_computation.1 | async-start | bytes 7077888 | tf_op jit(solution)/shard_map/all_gather | solution.py:21
  51.8 1.2 copy-start.12
  58.1 1.7 copy-start.9
  58.1 6.4 %copy-start.8 = (bf16[16,1024]{1,0:T(8,128)(2,1)S(1)}, bf16[16,1024]{1,0:T(8,128)(2,1)}, u32[]{:S(2)}) copy-start(bf16[16,1024]{1,0:T(8,128)(2,1)} %param.23) | copy-start | bytes 98308
  61.0 41.4 %copy-start.3 = (bf16[16,8,3,64]{3,2,1,0:T(4,128)(2,1)S(1)}, bf16[16,8,3,64]{3,2,1,0:T(4,128)(2,1)}, u32[]{:S(2)}) copy-start(bf16[16,8,3,64]{3,2,1,0:T(4,128)(2,1)} %reshape.454) | copy-start | bytes 147460
  101.3 0.7 copy-start.1
  107.5 1.4 copy-start.7
  108.7 224.5 %reduce-scatter.2.cloned.1.call-start = ((), (), s32[]{:S(2)}) async-start(), calls=%async_computation.2 | async-start | bytes 884736 | tf_op jit(solution)/shard_map/reduce_scatter | solution.py:224
  226.8 3.3 copy-start.5
  226.8 3.3 copy-start.11
  226.8 34.5 %copy-start.6 = (bf16[1536,40]{0,1:T(8,128)(2,1)S(1)}, bf16[1536,40]{0,1:T(8,128)(2,1)}, u32[]{:S(2)}) copy-start(bf16[1536,40]{0,1:T(8,128)(2,1)} %param.34) | copy-start | bytes 368644
  226.8 34.7 %copy-start.10 = (s32[128,8]{0,1:T(8,128)S(1)}, s32[128,8]{0,1:T(8,128)}, u32[]{:S(2)}) copy-start(s32[128,8]{0,1:T(8,128)} %param.35) | copy-start | bytes 12292
  230.2 39.5 %slice-start = ((s8[7864320]{0:T(1024)(128)(4,1)}), s8[4194304]{0:T(1024)(128)(4,1)S(1)}, s32[]{:S(2)}) async-start(s8[7864320]{0:T(1024)(128)(4,1)} %bitcast.175), calls=%async_computation.3 | async-start | bytes 8388608
  261.6 8.1 %slice-start.1 = ((s8[7864320]{0:T(1024)(128)(4,1)}), s8[3670016]{0:T(1024)(128)(4,1)S(1)}, s32[]{:S(2)}) async-start(s8[7864320]{0:T(1024)(128)(4,1)} %bitcast.175), calls=%async_computation.4 | async-start | bytes 7340032
  269.7 2.5 copy-start.2
Sparse Core Ops, SparseCore 0:
  108.8 102.9 all-gather.1
  272.2 60.8 reduce-scatter.1
where the time goes:
time: 342 us
  blocking collectives  175 us (51%)
  waiting for transfers between devices  92.4 us (27%)
  local copies, waits for them, and re-layouts  28.3 us (8%)
  matrix products  19.2 us (6%)
  between operations  14.7 us (4%)
  other arithmetic  11.1 us (3%)
    all_gather x2, blocking collectives, joined_2(): gathered = jax.tree.map(lambda a: lax.all_gather(a, axis), part)  63.8 us
    reduce_scatter x1, waiting for transfers between devices, per_device(): lax.psum_scatter(jnp.einsum('tuh,uhd->td', activated, down_weight, prefer...  60.1 us
    all_gather x1, waiting for transfers between devices, joined_2(): gathered = jax.tree.map(lambda a: lax.all_gather(a, axis), part)  32.2 us
    all_gather x1, blocking collectives, per_device(): lax.all_gather(own_q, 'tp', axis=0, tiled=True)  31.7 us
    all_gather x1, blocking collectives, per_device(): normed_all = lax.all_gather(normed_own, 'tp', axis=0, tiled=True)  31.1 us
    all_gather x1, blocking collectives, per_device(): lax.all_gather(own_kv, 'tp', axis=0, tiled=True)  30.7 us
    dynamic_slice x14, local copies, waits for them, and re-layouts, take(): lax.dynamic_index_in_dim(a, source, 0, False)  10.1 us
    dot_general x1, matrix products, per_device(): jnp.einsum('td,udh->tuh', normed_all, gate_up, preferred_element_type=jnp...  7.84 us
  transfers between devices with their start and end apart: 2, of which 2 were waited for; matrix products, arithmetic and copies ran while one was open for 1% of the time, Pallas kernels for 0%

commit v1 on v0

--- a/solution.py
+++ b/solution.py
@@ -1,8 +1,11 @@
+import functools
 import math
 
 import jax
 import jax.numpy as jnp
 from jax import lax
+from jax.experimental import pallas as pl
+from jax.experimental.pallas import tpu as pltpu
 from jax.sharding import PartitionSpec as P
 
 HEADS = 24
@@ -11,6 +14,7 @@
 FF_E = 512
 UNIT = 128
 DRAFT = 64
+WIDE = 128
 
 
 neg_big = -1e30
@@ -92,7 +96,7 @@
     return jnp.dot(routing, pick, precision=lax.Precision.HIGHEST)
 
 
-def per_device(
+def per_device_plain(
     queries,
     new_kv,
     residual,
@@ -242,6 +246,344 @@
     return (attn_own, layer_out, accepted)
 
 
+def pack_kernel(
+    row_slot, placement_ref, pages_ref, pulled_ref, keys_ref, values_ref, sent_ref, res_ref
+):
+    slot_count = placement_ref.shape[0]
+    group_size = HEADS // KV_HEADS
+    page_len = keys_ref.shape[1]
+    kv_width = keys_ref.shape[2]
+    q_width = HEADS * HEAD
+    tok_dev = pulled_ref.shape[1]
+    slot = row_slot(lax.axis_index("tp"))
+    source = placement_ref[slot] // slot_count
+    rows = pulled_ref[source]
+    res_ref[...] = rows[:, q_width + 2 * kv_width :]
+    head_rows = group_size * HEAD
+    tail = jnp.zeros((tok_dev, 2 * WIDE - head_rows), rows.dtype)
+    cache_rows = slot_count * page_len
+    for head in range(KV_HEADS):
+        low = head * HEAD
+        for s in range(slot_count):
+            page = pages_ref[s, 0, 0]
+            sent_ref[head, s * page_len : (s + 1) * page_len, :] = jnp.concatenate(
+                [keys_ref[page, :, low : low + HEAD], values_ref[page, :, low : low + HEAD]], axis=1
+            )
+        q_low = head * head_rows
+        pair = jnp.concatenate([rows[:, q_low : q_low + head_rows], tail], axis=1)
+        sent_ref[head, cache_rows : cache_rows + tok_dev, :] = pair[:, :WIDE]
+        sent_ref[head, cache_rows + tok_dev : cache_rows + 2 * tok_dev, :] = pair[:, WIDE:]
+        k_low = q_width + low
+        sent_ref[head, cache_rows + 2 * tok_dev :, :] = jnp.concatenate(
+            [rows[:, k_low : k_low + HEAD], rows[:, k_low + kv_width : k_low + kv_width + HEAD]],
+            axis=1,
+        )
+
+
+def ancestor_rows(parents_ref):
+    slot_count = parents_ref.shape[0]
+    total = slot_count * DRAFT
+    row = jnp.concatenate(
+        [parents_ref[s : s + 1, :] + s * DRAFT for s in range(slot_count)], axis=1
+    )
+    from_ids = lax.broadcasted_iota(jnp.int32, (total, total), 0)
+    to_ids = lax.broadcasted_iota(jnp.int32, (total, total), 1)
+    linked = (from_ids == jnp.broadcast_to(row, (total, total))) & (lax.rem(to_ids, DRAFT) > 0)
+    reached = jnp.where(linked | (from_ids == to_ids), 1.0, 0.0)
+    for _ in range((DRAFT - 1).bit_length()):
+        half = reached.astype(jnp.bfloat16)
+        reached = jnp.minimum(jnp.dot(half, half, preferred_element_type=jnp.float32), 1.0)
+    return reached.T
+
+
+def attend_kernel(
+    lengths_ref, leaf_ref, parents_ref, got_ref, res_ref, sent_ref, reach_ref
+):
+    slot_count = lengths_ref.shape[0]
+    sources = got_ref.shape[0]
+    tok_dev = res_ref.shape[0]
+    page_len = (got_ref.shape[1] - 3 * tok_dev) // slot_count
+    cache_rows = slot_count * page_len
+    per_slot = DRAFT // tok_dev
+    group_size = HEADS // KV_HEADS
+    f32, bf16 = jnp.float32, jnp.bfloat16
+    reach_ref[...] = ancestor_rows(parents_ref)
+    lane_low = lax.broadcasted_iota(jnp.int32, (DRAFT, WIDE), 1) < HEAD
+    positions = lax.broadcasted_iota(jnp.int32, (1, sources * page_len), 1)
+    outs, picked = [], []
+    for s in range(slot_count):
+        first = s * per_slot
+        part = lambda k: jnp.concatenate(
+            [
+                got_ref[first + i, cache_rows + k * tok_dev : cache_rows + (k + 1) * tok_dev, :]
+                for i in range(per_slot)
+            ],
+            axis=0,
+        )
+        q_pair = part(0).astype(f32) * (1.0 / math.sqrt(HEAD))
+        q_last = part(1).astype(f32) * (1.0 / math.sqrt(HEAD))
+        tree_kv = part(2)
+        q_rows = jnp.concatenate(
+            [
+                jnp.where(lane_low, q_pair, 0.0),
+                jnp.where(lane_low, pltpu.roll(q_pair, HEAD, 1), 0.0),
+                jnp.where(lane_low, q_last, 0.0),
+            ],
+            axis=0,
+        ).astype(bf16)
+        cache_kv = got_ref[:, s * page_len : (s + 1) * page_len, :].reshape(
+            sources * page_len, WIDE
+        )
+        dims = (((1,), (1,)), ((), ()))
+        scores = lax.dot_general(q_rows, cache_kv, dims, preferred_element_type=f32)
+        is_valid = positions < lengths_ref[s]
+        scores = jnp.where(is_valid, scores, neg_big)
+        reach = reach_ref[s * DRAFT : (s + 1) * DRAFT, s * DRAFT : (s + 1) * DRAFT]
+        allowed = jnp.concatenate([reach] * group_size, axis=0) > 0.5
+        tree_scores = lax.dot_general(q_rows, tree_kv, dims, preferred_element_type=f32)
+        tree_scores = jnp.where(allowed, tree_scores, neg_big)
+        top = jnp.maximum(
+            jnp.max(scores, axis=1, keepdims=True), jnp.max(tree_scores, axis=1, keepdims=True)
+        )
+        weights = jnp.where(is_valid, jnp.exp(scores - top), 0.0).astype(bf16)
+        tree_weights = jnp.where(allowed, jnp.exp(tree_scores - top), 0.0).astype(bf16)
+        total = jnp.sum(weights.astype(f32), axis=1, keepdims=True) + jnp.sum(
+            tree_weights.astype(f32), axis=1, keepdims=True
+        )
+        mixed = jnp.dot(weights, cache_kv, preferred_element_type=f32) + jnp.dot(
+            tree_weights, tree_kv, preferred_element_type=f32
+        )
+        outs.append(mixed / total)
+        path = reach_ref[pl.ds(s * DRAFT + leaf_ref[s], 1), s * DRAFT : (s + 1) * DRAFT]
+        path = jnp.broadcast_to(path, (DRAFT, DRAFT))
+        node_from = lax.broadcasted_iota(jnp.int32, (DRAFT, DRAFT), 0)
+        node_to = lax.broadcasted_iota(jnp.int32, (DRAFT, DRAFT), 1)
+        upto = jnp.where(node_from <= node_to, 1.0, 0.0).astype(bf16)
+        rank = jnp.dot(path.astype(bf16), upto, preferred_element_type=f32)
+        chosen = (path > 0.5) & (rank == (node_from + 1).astype(f32))
+        picked.append(
+            jnp.dot(
+                jnp.where(chosen, 1.0, 0.0).astype(bf16), tree_kv, preferred_element_type=f32
+            ).astype(bf16)
+        )
+    pair_rows, last_rows = [], []
+    for s in range(slot_count):
+        out = outs[s]
+        head_out = [out[r * DRAFT : (r + 1) * DRAFT] for r in range(group_size)]
+        pair_rows.append(
+            jnp.where(lane_low, pltpu.roll(head_out[0], HEAD, 1), head_out[1]).astype(bf16)
+        )
+        last_rows.append(head_out[2])
+    last = jnp.where(lane_low, pltpu.roll(last_rows[0], HEAD, 1), last_rows[1]).astype(bf16)
+    res_tiles = [res_ref[:, c * WIDE : (c + 1) * WIDE] for c in range(res_ref.shape[1] // WIDE)]
+    shared = jnp.concatenate(pair_rows + [last] + res_tiles, axis=0)
+    shared_rows = shared.shape[0]
+    for target in range(sources):
+        sent_ref[target, :shared_rows, :] = shared
+        row = (target % per_slot) * tok_dev
+        sent_ref[target, shared_rows:, :] = picked[target // per_slot][row : row + tok_dev]
+
+
+def expert_kernel(
+    got_ref, ids_ref, gain_ref, out_weight_ref, router_ref, gate_up_ref, down_ref,
+    moe_ref, hidden_ref, attn_ref, accepted_ref, x_ref, hid_ref, normed_ref, share_ref,
+):
+    f32, bf16 = jnp.float32, jnp.bfloat16
+    sources = got_ref.shape[0]
+    tok_dev = hidden_ref.shape[0]
+    group_rows = sources * tok_dev
+    half = group_rows // 2
+    width = out_weight_ref.shape[0]
+    model = out_weight_ref.shape[1]
+    rank = lax.axis_index("tp")
+    lane_low = lax.broadcasted_iota(jnp.int32, (half, WIDE), 1) < HEAD
+    head_rows = width // sources
+    res_start = group_rows + half
+    res_rows = (model // WIDE) * tok_dev
+    for p in range(sources // 2):
+        even, odd = got_ref.at[2 * p], got_ref.at[2 * p + 1]
+        last_even = even[group_rows:res_start, :].astype(f32)
+        last_odd = odd[group_rows:res_start, :].astype(f32)
+        pair_odd = odd[:group_rows, :].astype(f32)
+        odd_swapped = pltpu.roll(pair_odd, HEAD, 1)
+        base = 2 * p * head_rows
+        x_ref[:, base : base + WIDE] = even[:group_rows, :]
+        x_ref[:half, base + WIDE : base + 2 * WIDE] = jnp.where(
+            lane_low, last_even, odd_swapped[:half]
+        ).astype(bf16)
+        x_ref[half:, base + WIDE : base + 2 * WIDE] = jnp.where(
+            lane_low, pltpu.roll(last_even, HEAD, 1), odd_swapped[half:]
+        ).astype(bf16)
+        x_ref[:half, base + 2 * WIDE : base + 3 * WIDE] = jnp.where(
+            lane_low, odd_swapped[:half], pltpu.roll(last_odd, HEAD, 1)
+        ).astype(bf16)
+        x_ref[half:, base + 2 * WIDE : base + 3 * WIDE] = jnp.where(
+            lane_low, odd_swapped[half:], last_odd
+        ).astype(bf16)
+        kv_even = even[res_start + res_rows :, :].astype(f32)
+        kv_odd = odd[res_start + res_rows :, :].astype(f32)
+        low = lane_low[:tok_dev]
+        kv_width = accepted_ref.shape[1] // 2
+        accepted_ref[:, p * WIDE : (p + 1) * WIDE] = jnp.where(
+            low, kv_even, pltpu.roll(kv_odd, HEAD, 1)
+        ).astype(bf16)
+        accepted_ref[:, kv_width + p * WIDE : kv_width + (p + 1) * WIDE] = jnp.where(
+            low, pltpu.roll(kv_even, HEAD, 1), kv_odd
+        ).astype(bf16)
+    own = pl.multiple_of(rank * tok_dev, tok_dev)
+    attn_ref[...] = x_ref[pl.ds(own, tok_dev), :]
+    projected = jnp.dot(x_ref[...], out_weight_ref[...], preferred_element_type=f32)
+    residual = jnp.concatenate(
+        [
+            jnp.concatenate(
+                [
+                    got_ref[j, res_start + c * tok_dev : res_start + (c + 1) * tok_dev, :]
+                    for c in range(model // WIDE)
+                ],
+                axis=1,
+            )
+            for j in range(sources)
+        ],
+        axis=0,
+    )
+    hidden = residual.astype(f32) + projected
+    hid_ref[...] = hidden
+    scale = lax.rsqrt(jnp.mean(hidden * hidden, axis=1, keepdims=True) + norm_eps)
+    normed_ref[...] = (hidden * scale * gain_ref[...]).astype(bf16)
+    hidden_ref[...] = hid_ref[pl.ds(own, tok_dev), :]
+    logits = jnp.dot(normed_ref[...], router_ref[...], preferred_element_type=f32)
+    experts = router_ref.shape[1]
+    expert_range = lax.broadcasted_iota(jnp.int32, (group_rows, experts), 1)
+    count = jnp.zeros((group_rows, experts), f32)
+    for k in range(ids_ref.shape[1]):
+        count = count + jnp.where(ids_ref[:, k : k + 1] == expert_range, 1.0, 0.0)
+    expo = jnp.where(count > 0.0, jnp.exp(logits), 0.0) * count
+    routing = expo / jnp.sum(expo, axis=1, keepdims=True)
+    units = gate_up_ref.shape[0]
+    unit_width = gate_up_ref.shape[2] // 2
+    span = FF_E // unit_width
+    for u in range(units):
+        expert = (rank * units + u) // span
+        share_ref[u] = jnp.broadcast_to(
+            jnp.sum(jnp.where(expert_range == expert, routing, 0.0), axis=1, keepdims=True),
+            (group_rows, unit_width),
+        )
+
+    def one_unit(u):
+        both = jnp.dot(normed_ref[...], gate_up_ref[u], preferred_element_type=f32)
+        gate, up = both[:, :unit_width], both[:, unit_width:]
+        return (gate / (1.0 + jnp.exp(-gate)) * up * share_ref[u]).astype(bf16)
+
+    step = 2
+
+    def body(i, total):
+        act = jnp.concatenate([one_unit(i * step + k) for k in range(step)], axis=1)
+        down = down_ref[pl.ds(i * step, step)].reshape(step * unit_width, model)
+        hid_ref[...] += jnp.dot(act, down, preferred_element_type=f32)
+        return total
+
+    hid_ref[...] = jnp.zeros_like(hid_ref)
+    lax.fori_loop(0, units // step, body, 0)
+    moe_ref[...] = hid_ref[...].astype(bf16)
+
+
+def in_vmem(*arrays):
+    return tuple(pltpu.with_memory_space_constraint(a, pltpu.VMEM) for a in arrays)
+
+
+def spaces(text):
+    kinds = {"s": pltpu.SMEM, "v": pltpu.VMEM}
+    return [pl.BlockSpec(memory_space=kinds[c]) for c in text]
+
+
+def params():
+    return pltpu.CompilerParams(vmem_limit_bytes=20 << 20)
+
+
+def per_device_packed(
+    queries,
+    new_kv,
+    residual,
+    placement,
+    lengths,
+    page_table,
+    cache_keys,
+    cache_values,
+    parents,
+    accept_leaf,
+    out_weight,
+    norm_gain,
+    router_weight,
+    expert_ids,
+    gate_up,
+    down_weight,
+):
+    f32, bf16 = jnp.float32, jnp.bfloat16
+    tok_dev, model = residual.shape
+    tp_count = lax.axis_size("tp")
+    slot_count = placement.shape[0]
+    page_len, kv_width = cache_keys.shape[1:]
+    group_rows = tok_dev * tp_count
+    sent = lambda rows: jax.ShapeDtypeStruct((tp_count, rows, WIDE), bf16)
+    row_slot = lambda rank: rank * tok_dev // DRAFT
+    pulled = lax.all_gather(
+        jnp.concatenate([queries, new_kv, residual], axis=1), "req", axis=0
+    )
+    pack_rows = slot_count * page_len + 3 * tok_dev
+    packed, own_res = pl.pallas_call(
+        functools.partial(pack_kernel, row_slot),
+        out_shape=(sent(pack_rows), jax.ShapeDtypeStruct(residual.shape, bf16)),
+        in_specs=spaces("ssvvv"),
+        out_specs=tuple(spaces("vv")),
+        compiler_params=params(),
+        name="pack",
+    )(placement, page_table, pulled, cache_keys, cache_values)
+    packed = lax.all_to_all(packed, "tp", 0, 0, tiled=True)
+    out_rows = group_rows + group_rows // 2 + (model // WIDE) * tok_dev + tok_dev
+    outs = pl.pallas_call(
+        attend_kernel,
+        out_shape=sent(out_rows),
+        in_specs=spaces("ssvvv"),
+        out_specs=spaces("v")[0],
+        scratch_shapes=[pltpu.VMEM((slot_count * DRAFT, slot_count * DRAFT), f32)],
+        compiler_params=params(),
+        name="attend",
+    )(lengths, accept_leaf, parents, packed, own_res)
+    outs = lax.all_to_all(outs, "tp", 0, 0, tiled=True)
+    weights = in_vmem(out_weight, router_weight, gate_up, down_weight)
+    moe, hidden, attn_own, accepted = pl.pallas_call(
+        expert_kernel,
+        out_shape=(
+            jax.ShapeDtypeStruct((group_rows, model), bf16),
+            jax.ShapeDtypeStruct((tok_dev, model), f32),
+            jax.ShapeDtypeStruct(queries.shape, bf16),
+            jax.ShapeDtypeStruct(new_kv.shape, bf16),
+        ),
+        in_specs=spaces("vvvvvvv"),
+        out_specs=tuple(spaces("vvvv")),
+        scratch_shapes=[
+            pltpu.VMEM((group_rows, HEADS * HEAD), bf16),
+            pltpu.VMEM((group_rows, model), f32),
+            pltpu.VMEM((group_rows, model), bf16),
+            pltpu.VMEM((gate_up.shape[0], group_rows, gate_up.shape[2] // 2), f32),
+        ],
+        compiler_params=params(),
+        name="experts",
+    )(outs, expert_ids, norm_gain[None, :], *weights)
+    parts = lax.all_to_all(moe, "tp", 0, 0, tiled=True).reshape(tp_count, tok_dev, model)
+    layer_out = (hidden + jnp.sum(parts.astype(f32), axis=0)).astype(bf16)
+    return attn_own, layer_out, accepted
+
+
+def per_device(queries, new_kv, residual, placement, *rest):
+    tok_dev = queries.shape[0]
+    one_head_each = lax.axis_size("tp") == KV_HEADS
+    whole_tiles = tok_dev % 16 == 0 and tok_dev * KV_HEADS == 2 * DRAFT
+    if one_head_each and whole_tiles and rest[1].shape[1] == 1:
+        return per_device_packed(queries, new_kv, residual, placement, *rest)
+    return per_device_plain(queries, new_kv, residual, placement, *rest)
+
+
 def solution(mesh):
     in_specs = (
         P(("req", "tp"), None),

time: 342 us -> 103 us (0.30)
  blocking collectives: 175 us -> 47.3 us
  waiting for transfers between devices: 92.4 us -> 17.8 us
  matrix products: 19.2 us -> 0 us
  between operations: 14.7 us -> 0.68 us
  Pallas kernels: 0 us -> 12.3 us
  other arithmetic: 11.1 us -> 1.54 us
  local copies, waits for them, and re-layouts: 28.3 us -> 18.9 us
  starting transfers between devices: 0.08 us -> 3.55 us
    all_gather x8 -> x1, blocking collectives: 175 us -> 8.65 us  [per_device_packed(): lax.all_gather(jnp.concatenate([queries, new_kv, residual], axis=1), 'req...]
    reduce_scatter x1 -> x0, waiting for transfers between devices: 60.1 us -> none  [per_device(): lax.psum_scatter(jnp.einsum('tuh,uhd->td', activated, down_weight, prefer...]
    all_to_all x0 -> x2, blocking collectives: none -> 38.7 us  [the longest x1 23.2 us: per_device_packed(): packed = lax.all_to_all(packed, 'tp', 0, 0, tiled=True)]
    all_gather x1 -> x0, waiting for transfers between devices: 32.2 us -> none  [joined_2(): gathered = jax.tree.map(lambda a: lax.all_gather(a, axis), part)]
    dot_general x18 -> x0, matrix products: 19.2 us -> none  [the longest x1 7.84 us: per_device(): jnp.einsum('td,udh->tuh', normed_all, gate_up, preferred_element_type=jnp...]
    all_to_all x0 -> x1, waiting for transfers between devices: none -> 17.8 us  [per_device_packed(): outs = lax.all_to_all(outs, 'tp', 0, 0, tiled=True)]
    unnamed x30 -> x21, local copies, waits for them, and re-layouts: 0.81 us -> 18.2 us
    pallas_call x0 -> x3, Pallas kernels: none -> 12.3 us  [the longest x1 7.86 us: per_device_packed(): pl.pallas_call(expert_kernel, out_shape=(jax.ShapeDtypeStruct((group_rows...]
  transfers between devices with their start and end apart: 2 -> 1, of which waited for: 2 -> 1; matrix products, arithmetic and copies ran while one was open for 1% -> 3% of each run, Pallas kernels for 0% -> 0%
where the time goes in v1:
time: 103 us; the launch traced here: 102 us
  blocking collectives  47.3 us (46%)
  local copies, waits for them, and re-layouts  18.9 us (18%)
  waiting for transfers between devices  17.8 us (17%)
  Pallas kernels  12.3 us (12%)
  starting transfers between devices  3.55 us (3%)
  other arithmetic  1.54 us (1%)
    all_to_all x1, blocking collectives, per_device_packed(): packed = lax.all_to_all(packed, 'tp', 0, 0, tiled=True)  23.2 us
    unnamed x21, local copies, waits for them, and re-layouts  18.2 us
    all_to_all x1, waiting for transfers between devices, per_device_packed(): outs = lax.all_to_all(outs, 'tp', 0, 0, tiled=True)  17.8 us
    all_to_all x1, blocking collectives, per_device_packed(): lax.all_to_all(moe, 'tp', 0, 0, tiled=True)  15.5 us
    all_gather x1, blocking collectives, per_device_packed(): lax.all_gather(jnp.concatenate([queries, new_kv, residual], axis=1), 'req...  8.65 us
    pallas_call x1, Pallas kernels, per_device_packed(): pl.pallas_call(expert_kernel, out_shape=(jax.ShapeDtypeStruct((group_rows...  7.86 us
    pallas_call x1, Pallas kernels, per_device_packed(): pl.pallas_call(attend_kernel, out_shape=sent(out_rows), in_specs=spaces('...  3.63 us
    all_to_all x1, starting transfers between devices, per_device_packed(): outs = lax.all_to_all(outs, 'tp', 0, 0, tiled=True)  3.55 us
  transfers between devices with their start and end apart: 1, of which 1 were waited for; matrix products, arithmetic and copies ran while one was open for 3% of the time, Pallas kernels for 0%

profile of v1, /device:TPU:0, one launch (start us, length us, event | category | flops | bytes accessed | tf_op | source)
XLA Modules:
  0.0 102.1 jit_solution(13313541778661818813)
XLA Ops:
  0.6 0.7 copy.19.pages_ref
  1.4 0.9 pad_maximum_fusion
  2.2 8.6 %all-gather = bf16[64,4096]{1,0:T(8,128)(2,1)S(1)} all-gather(bf16[16,4096]{1,0:T(8,128)(2,1)S(1)} %pad_maximum_fusion), channel_id=2, replica_groups=mesh['req'=4,'tp'=8] {'req'}, dimensions={0}, use_global_device_ids=true | all-gather | bytes 655360 | tf_op jit(solution)/shard_map/all_gather | solution.py:529
  10.9 0.9 copy-done.3
  11.8 0.9 copy-done.4
  12.8 0.7 copy-done.6
  13.4 0.8 pack.1
  14.2 23.2 %all_to_all.19.got_ref = bf16[8,304,128]{2,1,0:T(8,128)(2,1)S(1)} all-to-all(bf16[8,304,128]{2,1,0:T(8,128)(2,1)S(1)} %get-tuple-element.9), channel_id=1, replica_groups=mesh['req'=4,'tp'=8] {'tp'}, dimensions={0} | all-to-all | bytes 1245184 | tf_op jit(solution)/shard_map/all_to_all | solution.py:541
  37.4 0.7 copy-done.5
  38.1 0.7 copy-done.7
  38.8 0.7 copy-done.8
  39.4 3.6 %attend.1 = bf16[8,400,128]{2,1,0:T(8,128)(2,1)} custom-call(s32[2]{0:T(128)S(1)} %copy-done.7, s32[2]{0:T(128)S(1)} %copy-done.8, s32[2,64]{1,0:T(2,128)S(1)} %copy-done.5, bf16[8,304,128]{2,1,0:T(8,128)(2,1)S(1)} %all_to_all.19.got_ref, bf16[16,1536]{1,0:T(8,128)(2,1)S(1)} %get-tuple-element.10.res_ref), custom_call_target="tpu_custom_call" | custom-call | tf_op jit(solution)/shard_map/attend/pallas_call | solution.py:543
  43.0 3.5 %all-to-all-start.1 = ((bf16[8,400,128]{2,1,0:T(8,128)(2,1)}), bf16[8,400,128]{2,1,0:T(8,128)(2,1)S(1)}, u32[]{:S(2)}, u32[]{:S(2)}) async-start(bf16[8,400,128]{2,1,0:T(8,128)(2,1)} %attend.1), calls=%async_computation.1 | async-start | bytes 1638400 | tf_op jit(solution)/shard_map/all_to_all | solution.py:552
  46.6 0.7 broadcast_in_dim.3.gain_ref
  47.3 0.8 copy.20.ids_ref
  48.1 1.1 %copy.21.router_ref = bf16[1536,40]{1,0:T(8,128)(2,1)S(1)} copy(bf16[1536,40]{0,1:T(8,128)(2,1)} %param.28) | data formatting | bytes 245760 | tf_op args[12]
  49.2 17.8 %all-to-all-done.1.got_ref = bf16[8,400,128]{2,1,0:T(8,128)(2,1)S(1)} async-done(((bf16[8,400,128]{2,1,0:T(8,128)(2,1)}), bf16[8,400,128]{2,1,0:T(8,128)(2,1)S(1)}, u32[]{:S(2)}, u32[]{:S(2)}) %all-to-all-start.1) | async-done | bytes 819232 | tf_op jit(solution)/shard_map/all_to_all | solution.py:552
  67.0 5.5 %copy-done = bf16[20,1536,256]{2,1,0:T(8,128)(2,1)S(1)} copy-done((bf16[20,1536,256]{2,1,0:T(8,128)(2,1)S(1)}, bf16[20,1536,256]{2,1,0:T(8,128)(2,1)}, u32[]{:S(2)}) %copy-start) | copy-done | bytes 15728664
  72.5 3.2 %copy-done.1 = bf16[20,128,1536]{2,1,0:T(8,128)(2,1)S(1)} copy-done((bf16[20,128,1536]{2,1,0:T(8,128)(2,1)S(1)}, bf16[20,128,1536]{2,1,0:T(8,128)(2,1)}, u32[]{:S(2)}) %copy-start.1) | copy-done | bytes 7864344
  75.7 2.3 %copy-done.2 = bf16[1536,1536]{1,0:T(8,128)(2,1)S(1)} copy-done((bf16[1536,1536]{1,0:T(8,128)(2,1)S(1)}, bf16[1536,1536]{1,0:T(8,128)(2,1)}, u32[]{:S(2)}) %copy-start.2) | copy-done | bytes 4718616
  78.1 7.9 %experts.1 = (bf16[128,1536]{1,0:T(8,128)(2,1)S(1)}, f32[16,1536]{1,0:T(8,128)S(1)}, bf16[16,1536]{1,0:T(8,128)(2,1)}, bf16[16,1024]{1,0:T(8,128)(2,1)}) custom-call(bf16[8,400,128]{2,1,0:T(8,128)(2,1)S(1)} %all-to-all-done.1.got_ref, s32[128,8]{1,0:T(8,128)S(1)} %copy.20.ids_ref, f32[1,1536]{1,0:T(1,128)S(1)} %broadcast_in_dim.3.gain_ref, ...), custom_call_target="tpu_custom_call" | custom-call | tf_op jit(solution)/shard_map/experts/pallas_call | solution.py:554
  85.9 15.5 %all_to_all.20 = bf16[8,16,1536]{2,1,0:T(8,128)(2,1)S(1)} all-to-all(bf16[8,16,1536]{2,1,0:T(8,128)(2,1)S(1)} %bitcast.3), channel_id=1, replica_groups=mesh['req'=4,'tp'=8] {'tp'}, dimensions={0} | all-to-all | bytes 786432 | tf_op jit(solution)/shard_map/all_to_all | solution.py:573
  101.4 0.1 convert_reduce_fusion
  101.5 0.6 add_convert_fusion
  (9 shorter events, 0.0 us)
Async XLA Ops:
  10.9 0.9 copy-start.3
  11.8 0.9 copy-start.4
  12.8 0.7 copy-start.6
  37.4 0.7 copy-start.5
  38.1 0.7 copy-start.7
  38.8 0.7 copy-start.8
  43.0 24.0 %all-to-all-start.1 = ((bf16[8,400,128]{2,1,0:T(8,128)(2,1)}), bf16[8,400,128]{2,1,0:T(8,128)(2,1)S(1)}, u32[]{:S(2)}, u32[]{:S(2)}) async-start(bf16[8,400,128]{2,1,0:T(8,128)(2,1)} %attend.1), calls=%async_computation.1 | async-start | bytes 1638400 | tf_op jit(solution)/shard_map/all_to_all | solution.py:552
  67.0 5.5 %copy-start = (bf16[20,1536,256]{2,1,0:T(8,128)(2,1)S(1)}, bf16[20,1536,256]{2,1,0:T(8,128)(2,1)}, u32[]{:S(2)}) copy-start(bf16[20,1536,256]{2,1,0:T(8,128)(2,1)} %gate_up_ref.1) | copy-start | bytes 47185924
  72.5 3.2 %copy-start.1 = (bf16[20,128,1536]{2,1,0:T(8,128)(2,1)S(1)}, bf16[20,128,1536]{2,1,0:T(8,128)(2,1)}, u32[]{:S(2)}) copy-start(bf16[20,128,1536]{2,1,0:T(8,128)(2,1)} %down_ref.1) | copy-start | bytes 23592964
  75.7 2.3 %copy-start.2 = (bf16[1536,1536]{1,0:T(8,128)(2,1)S(1)}, bf16[1536,1536]{1,0:T(8,128)(2,1)}, u32[]{:S(2)}) copy-start(bf16[1536,1536]{1,0:T(8,128)(2,1)} %out_weight_ref.1) | copy-start | bytes 14155780

commit v2 on v1

--- a/solution.py
+++ b/solution.py
@@ -15,6 +15,8 @@
 UNIT = 128
 DRAFT = 64
 WIDE = 128
+STEP = 2
+AHEAD = 4
 
 
 neg_big = -1e30
@@ -246,35 +248,54 @@
     return (attn_own, layer_out, accepted)
 
 
+def start_all(copies):
+    for copy in copies:
+        copy.start()
+    for copy in copies:
+        copy.wait()
+
+
 def pack_kernel(
-    row_slot, placement_ref, pages_ref, pulled_ref, keys_ref, values_ref, sent_ref, res_ref
+    slot_of, placement_hbm, pages_hbm, keys_hbm, values_hbm, pulled_ref, sent_ref, res_ref,
+    placement_ref, pages_ref, keys_ref, values_ref, sems,
 ):
     slot_count = placement_ref.shape[0]
-    group_size = HEADS // KV_HEADS
-    page_len = keys_ref.shape[1]
-    kv_width = keys_ref.shape[2]
+    page_len, kv_width = keys_ref.shape[1:]
+    start_all(
+        [
+            pltpu.make_async_copy(source, target, sems.at[k])
+            for k, (source, target) in enumerate(
+                [
+                    (placement_hbm, placement_ref),
+                    (pages_hbm, pages_ref),
+                    (keys_hbm, keys_ref),
+                    (values_hbm, values_ref),
+                ]
+            )
+        ]
+    )
     q_width = HEADS * HEAD
     tok_dev = pulled_ref.shape[1]
-    slot = row_slot(lax.axis_index("tp"))
-    source = placement_ref[slot] // slot_count
+    slot = slot_of(lax.axis_index("tp"))
+    source = lax.div(placement_ref[slot], slot_count)
     rows = pulled_ref[source]
     res_ref[...] = rows[:, q_width + 2 * kv_width :]
-    head_rows = group_size * HEAD
+    head_rows = (HEADS // KV_HEADS) * HEAD
     tail = jnp.zeros((tok_dev, 2 * WIDE - head_rows), rows.dtype)
-    cache_rows = slot_count * page_len
+    base = slot_count * page_len
     for head in range(KV_HEADS):
         low = head * HEAD
         for s in range(slot_count):
-            page = pages_ref[s, 0, 0]
+            page = pages_ref[s]
             sent_ref[head, s * page_len : (s + 1) * page_len, :] = jnp.concatenate(
                 [keys_ref[page, :, low : low + HEAD], values_ref[page, :, low : low + HEAD]], axis=1
             )
         q_low = head * head_rows
         pair = jnp.concatenate([rows[:, q_low : q_low + head_rows], tail], axis=1)
-        sent_ref[head, cache_rows : cache_rows + tok_dev, :] = pair[:, :WIDE]
-        sent_ref[head, cache_rows + tok_dev : cache_rows + 2 * tok_dev, :] = pair[:, WIDE:]
+        sent_ref[head, base : base + tok_dev, :] = pair[:, :WIDE]
+        sent_ref[head, base + tok_dev : base + 2 * tok_dev, :] = pair[:, WIDE:]
         k_low = q_width + low
-        sent_ref[head, cache_rows + 2 * tok_dev :, :] = jnp.concatenate(
+        sent_ref[head, base + 2 * tok_dev :, :] = jnp.concatenate(
             [rows[:, k_low : k_low + HEAD], rows[:, k_low + kv_width : k_low + kv_width + HEAD]],
             axis=1,
         )
@@ -297,32 +318,46 @@
 
 
 def attend_kernel(
-    lengths_ref, leaf_ref, parents_ref, got_ref, res_ref, sent_ref, reach_ref
+    lengths_hbm, leaf_hbm, parents_hbm, weight_hbm, got_ref, res_ref, sent_ref, picked_ref,
+    weight_ref,
+    lengths_ref, leaf_ref, parents_ref, reach_ref, sems,
 ):
+    start_all(
+        [
+            pltpu.make_async_copy(lengths_hbm, lengths_ref, sems.at[0]),
+            pltpu.make_async_copy(leaf_hbm, leaf_ref, sems.at[1]),
+            pltpu.make_async_copy(parents_hbm, parents_ref, sems.at[2]),
+        ]
+    )
+    weight_copy = pltpu.make_async_copy(weight_hbm, weight_ref, sems.at[3])
+    weight_copy.start()
+    reach_ref[...] = ancestor_rows(parents_ref)
     slot_count = lengths_ref.shape[0]
     sources = got_ref.shape[0]
     tok_dev = res_ref.shape[0]
-    page_len = (got_ref.shape[1] - 3 * tok_dev) // slot_count
-    cache_rows = slot_count * page_len
+    base = got_ref.shape[1] - 3 * tok_dev
+    page_len = base // slot_count
     per_slot = DRAFT // tok_dev
     group_size = HEADS // KV_HEADS
     f32, bf16 = jnp.float32, jnp.bfloat16
-    reach_ref[...] = ancestor_rows(parents_ref)
     lane_low = lax.broadcasted_iota(jnp.int32, (DRAFT, WIDE), 1) < HEAD
     positions = lax.broadcasted_iota(jnp.int32, (1, sources * page_len), 1)
+    dims = (((1,), (1,)), ((), ()))
+    scale = 1.0 / math.sqrt(HEAD)
+    node_from = lax.broadcasted_iota(jnp.int32, (DRAFT, DRAFT), 0)
+    node_to = lax.broadcasted_iota(jnp.int32, (DRAFT, DRAFT), 1)
+    upto = jnp.where(node_from <= node_to, 1.0, 0.0).astype(bf16)
     outs, picked = [], []
     for s in range(slot_count):
         first = s * per_slot
-        part = lambda k: jnp.concatenate(
-            [
-                got_ref[first + i, cache_rows + k * tok_dev : cache_rows + (k + 1) * tok_dev, :]
-                for i in range(per_slot)
-            ],
-            axis=0,
-        )
-        q_pair = part(0).astype(f32) * (1.0 / math.sqrt(HEAD))
-        q_last = part(1).astype(f32) * (1.0 / math.sqrt(HEAD))
-        tree_kv = part(2)
+
+        def part(k):
+            low = base + k * tok_dev
+            return jnp.concatenate(
+                [got_ref[first + i, low : low + tok_dev, :] for i in range(per_slot)], axis=0
+            )
+
+        q_pair, q_last, tree_kv = part(0).astype(f32) * scale, part(1).astype(f32) * scale, part(2)
         q_rows = jnp.concatenate(
             [
                 jnp.where(lane_low, q_pair, 0.0),
@@ -334,7 +369,6 @@
         cache_kv = got_ref[:, s * page_len : (s + 1) * page_len, :].reshape(
             sources * page_len, WIDE
         )
-        dims = (((1,), (1,)), ((), ()))
         scores = lax.dot_general(q_rows, cache_kv, dims, preferred_element_type=f32)
         is_valid = positions < lengths_ref[s]
         scores = jnp.where(is_valid, scores, neg_big)
@@ -356,19 +390,12 @@
         outs.append(mixed / total)
         path = reach_ref[pl.ds(s * DRAFT + leaf_ref[s], 1), s * DRAFT : (s + 1) * DRAFT]
         path = jnp.broadcast_to(path, (DRAFT, DRAFT))
-        node_from = lax.broadcasted_iota(jnp.int32, (DRAFT, DRAFT), 0)
-        node_to = lax.broadcasted_iota(jnp.int32, (DRAFT, DRAFT), 1)
-        upto = jnp.where(node_from <= node_to, 1.0, 0.0).astype(bf16)
         rank = jnp.dot(path.astype(bf16), upto, preferred_element_type=f32)
         chosen = (path > 0.5) & (rank == (node_from + 1).astype(f32))
-        picked.append(
-            jnp.dot(
-                jnp.where(chosen, 1.0, 0.0).astype(bf16), tree_kv, preferred_element_type=f32
-            ).astype(bf16)
-        )
+        chosen = jnp.where(chosen, 1.0, 0.0).astype(bf16)
+        picked.append(jnp.dot(chosen, tree_kv, preferred_element_type=f32).astype(bf16))
     pair_rows, last_rows = [], []
-    for s in range(slot_count):
-        out = outs[s]
+    for out in outs:
         head_out = [out[r * DRAFT : (r + 1) * DRAFT] for r in range(group_size)]
         pair_rows.append(
             jnp.where(lane_low, pltpu.roll(head_out[0], HEAD, 1), head_out[1]).astype(bf16)
@@ -376,90 +403,111 @@
         last_rows.append(head_out[2])
     last = jnp.where(lane_low, pltpu.roll(last_rows[0], HEAD, 1), last_rows[1]).astype(bf16)
     res_tiles = [res_ref[:, c * WIDE : (c + 1) * WIDE] for c in range(res_ref.shape[1] // WIDE)]
-    shared = jnp.concatenate(pair_rows + [last] + res_tiles, axis=0)
-    shared_rows = shared.shape[0]
+    sent_ref[...] = jnp.concatenate(pair_rows + [last] + res_tiles, axis=0)
     for target in range(sources):
-        sent_ref[target, :shared_rows, :] = shared
         row = (target % per_slot) * tok_dev
-        sent_ref[target, shared_rows:, :] = picked[target // per_slot][row : row + tok_dev]
+        picked_ref[target] = picked[target // per_slot][row : row + tok_dev]
+    weight_copy.wait()
 
 
 def expert_kernel(
-    got_ref, ids_ref, gain_ref, out_weight_ref, router_ref, gate_up_ref, down_ref,
-    moe_ref, hidden_ref, attn_ref, accepted_ref, x_ref, hid_ref, normed_ref, share_ref,
+    router_hbm, ids_hbm, gain_hbm, gate_up_hbm, down_hbm, out_weight_ref, picked_ref, *refs
 ):
+    blocks, refs = refs[:KV_HEADS], refs[KV_HEADS:]
+    moe_ref, hidden_ref, attn_ref, x_ref, hid_ref, normed_ref, share_ref = refs[:7]
+    router_ref, ids_ref, gain_ref, gate_up_ref, down_ref, sems, unit_sems, down_sems = refs[7:]
     f32, bf16 = jnp.float32, jnp.bfloat16
-    sources = got_ref.shape[0]
+    units = gate_up_ref.shape[0]
+    small = [
+        pltpu.make_async_copy(router_hbm, router_ref, sems.at[0]),
+        pltpu.make_async_copy(ids_hbm, ids_ref, sems.at[1]),
+        pltpu.make_async_copy(gain_hbm, gain_ref, sems.at[2]),
+    ]
+    for copy in small:
+        copy.start()
+
+    def unit_copy(u):
+        return pltpu.make_async_copy(gate_up_hbm.at[u], gate_up_ref.at[u], unit_sems.at[u])
+
+    def down_copy(i):
+        at = pl.ds(i * STEP, STEP)
+        return pltpu.make_async_copy(down_hbm.at[at], down_ref.at[at], down_sems.at[i])
+
+    def start_step(i):
+        for k in range(STEP):
+            unit_copy(i * STEP + k).start()
+        down_copy(i).start()
+
+    steps = units // STEP
+    for i in range(min(AHEAD, steps)):
+        start_step(i)
     tok_dev = hidden_ref.shape[0]
+    sources = len(blocks)
     group_rows = sources * tok_dev
     half = group_rows // 2
-    width = out_weight_ref.shape[0]
-    model = out_weight_ref.shape[1]
+    width, model = out_weight_ref.shape
     rank = lax.axis_index("tp")
     lane_low = lax.broadcasted_iota(jnp.int32, (half, WIDE), 1) < HEAD
     head_rows = width // sources
     res_start = group_rows + half
-    res_rows = (model // WIDE) * tok_dev
-    for p in range(sources // 2):
-        even, odd = got_ref.at[2 * p], got_ref.at[2 * p + 1]
-        last_even = even[group_rows:res_start, :].astype(f32)
-        last_odd = odd[group_rows:res_start, :].astype(f32)
-        pair_odd = odd[:group_rows, :].astype(f32)
-        odd_swapped = pltpu.roll(pair_odd, HEAD, 1)
-        base = 2 * p * head_rows
-        x_ref[:, base : base + WIDE] = even[:group_rows, :]
-        x_ref[:half, base + WIDE : base + 2 * WIDE] = jnp.where(
-            lane_low, last_even, odd_swapped[:half]
+    is_even = lax.rem(rank, 2) == 0
+    for k in range(sources // 2):
+        pair = lax.bitwise_xor(lax.div(rank, 2), k)
+        mine, other = blocks[2 * k][...], blocks[2 * k + 1][...]
+        even, odd = jnp.where(is_even, mine, other), jnp.where(is_even, other, mine)
+        last_even = even[group_rows:res_start].astype(f32)
+        last_odd = odd[group_rows:res_start].astype(f32)
+        odd_swapped = pltpu.roll(odd[:group_rows].astype(f32), HEAD, 1)
+        middle = jnp.concatenate(
+            [
+                jnp.where(lane_low, last_even, odd_swapped[:half]),
+                jnp.where(lane_low, pltpu.roll(last_even, HEAD, 1), odd_swapped[half:]),
+            ],
+            axis=0,
         ).astype(bf16)
-        x_ref[half:, base + WIDE : base + 2 * WIDE] = jnp.where(
-            lane_low, pltpu.roll(last_even, HEAD, 1), odd_swapped[half:]
+        end = jnp.concatenate(
+            [
+                jnp.where(lane_low, odd_swapped[:half], pltpu.roll(last_odd, HEAD, 1)),
+                jnp.where(lane_low, odd_swapped[half:], last_odd),
+            ],
+            axis=0,
         ).astype(bf16)
-        x_ref[:half, base + 2 * WIDE : base + 3 * WIDE] = jnp.where(
-            lane_low, odd_swapped[:half], pltpu.roll(last_odd, HEAD, 1)
-        ).astype(bf16)
-        x_ref[half:, base + 2 * WIDE : base + 3 * WIDE] = jnp.where(
-            lane_low, odd_swapped[half:], last_odd
-        ).astype(bf16)
-        kv_even = even[res_start + res_rows :, :].astype(f32)
-        kv_odd = odd[res_start + res_rows :, :].astype(f32)
-        low = lane_low[:tok_dev]
-        kv_width = accepted_ref.shape[1] // 2
-        accepted_ref[:, p * WIDE : (p + 1) * WIDE] = jnp.where(
-            low, kv_even, pltpu.roll(kv_odd, HEAD, 1)
-        ).astype(bf16)
-        accepted_ref[:, kv_width + p * WIDE : kv_width + (p + 1) * WIDE] = jnp.where(
-            low, pltpu.roll(kv_even, HEAD, 1), kv_odd
-        ).astype(bf16)
+        base = pl.multiple_of(pair * 2 * head_rows, WIDE)
+        x_ref[:, pl.ds(base, 2 * head_rows)] = jnp.concatenate(
+            [even[:group_rows], middle, end], axis=1
+        )
+        for q, block in enumerate((even, odd)):
+            row = pl.multiple_of((2 * pair + q) * tok_dev, tok_dev)
+            hid_ref[pl.ds(row, tok_dev), :] = jnp.concatenate(
+                [
+                    block[res_start + c * tok_dev : res_start + (c + 1) * tok_dev]
+                    for c in range(model // WIDE)
+                ],
+                axis=1,
+            ).astype(f32)
     own = pl.multiple_of(rank * tok_dev, tok_dev)
     attn_ref[...] = x_ref[pl.ds(own, tok_dev), :]
     projected = jnp.dot(x_ref[...], out_weight_ref[...], preferred_element_type=f32)
-    residual = jnp.concatenate(
-        [
-            jnp.concatenate(
-                [
-                    got_ref[j, res_start + c * tok_dev : res_start + (c + 1) * tok_dev, :]
-                    for c in range(model // WIDE)
-                ],
-                axis=1,
-            )
-            for j in range(sources)
-        ],
-        axis=0,
-    )
-    hidden = residual.astype(f32) + projected
+    hidden = hid_ref[...] + projected
     hid_ref[...] = hidden
+    for copy in small:
+        copy.wait()
+    gain = jnp.concatenate([gain_ref[c : c + 1, :] for c in range(model // WIDE)], axis=1)
     scale = lax.rsqrt(jnp.mean(hidden * hidden, axis=1, keepdims=True) + norm_eps)
-    normed_ref[...] = (hidden * scale * gain_ref[...]).astype(bf16)
+    normed_ref[...] = (hidden * scale * gain).astype(bf16)
     hidden_ref[...] = hid_ref[pl.ds(own, tok_dev), :]
-    logits = jnp.dot(normed_ref[...], router_ref[...], preferred_element_type=f32)
-    experts = router_ref.shape[1]
+    logits = lax.dot_general(
+        normed_ref[...], router_ref[...], (((1,), (1,)), ((), ())), preferred_element_type=f32
+    )
+    experts = router_ref.shape[0]
+    ids = ids_ref[...].astype(f32).T
     expert_range = lax.broadcasted_iota(jnp.int32, (group_rows, experts), 1)
+    expert_names = expert_range.astype(f32)
     count = jnp.zeros((group_rows, experts), f32)
-    for k in range(ids_ref.shape[1]):
-        count = count + jnp.where(ids_ref[:, k : k + 1] == expert_range, 1.0, 0.0)
+    for k in range(ids_ref.shape[0]):
+        count = count + jnp.where(ids[:, k : k + 1] == expert_names, 1.0, 0.0)
     expo = jnp.where(count > 0.0, jnp.exp(logits), 0.0) * count
     routing = expo / jnp.sum(expo, axis=1, keepdims=True)
-    units = gate_up_ref.shape[0]
     unit_width = gate_up_ref.shape[2] // 2
     span = FF_E // unit_width
     for u in range(units):
@@ -474,30 +522,65 @@
         gate, up = both[:, :unit_width], both[:, unit_width:]
         return (gate / (1.0 + jnp.exp(-gate)) * up * share_ref[u]).astype(bf16)
 
-    step = 2
-
-    def body(i, total):
-        act = jnp.concatenate([one_unit(i * step + k) for k in range(step)], axis=1)
-        down = down_ref[pl.ds(i * step, step)].reshape(step * unit_width, model)
+    def body(i, carry):
+        @pl.when(i + AHEAD < steps)
+        def _():
+            start_step(i + AHEAD)
+
+        for k in range(STEP):
+            unit_copy(i * STEP + k).wait()
+        act = jnp.concatenate([one_unit(i * STEP + k) for k in range(STEP)], axis=1)
+        down_copy(i).wait()
+        down = down_ref[pl.ds(i * STEP, STEP)].reshape(STEP * unit_width, model)
         hid_ref[...] += jnp.dot(act, down, preferred_element_type=f32)
-        return total
+        return carry
 
     hid_ref[...] = jnp.zeros_like(hid_ref)
-    lax.fori_loop(0, units // step, body, 0)
-    moe_ref[...] = hid_ref[...].astype(bf16)
-
-
-def in_vmem(*arrays):
-    return tuple(pltpu.with_memory_space_constraint(a, pltpu.VMEM) for a in arrays)
+    lax.fori_loop(0, steps, body, 0)
+    for j in range(sources):
+        moe_ref[j, :, :model] = hid_ref[j * tok_dev : (j + 1) * tok_dev, :].astype(bf16)
+    moe_ref[:, :, model:] = picked_ref[...]
+
+
+def finish_kernel(parts_ref, hidden_ref, layer_ref, accepted_ref):
+    f32, bf16 = jnp.float32, jnp.bfloat16
+    model = hidden_ref.shape[1]
+    kv_width = accepted_ref.shape[1] // 2
+    total = hidden_ref[...]
+    for j in range(parts_ref.shape[0]):
+        total = total + parts_ref[j, :, :model].astype(f32)
+    layer_ref[...] = total.astype(bf16)
+    low = lax.broadcasted_iota(jnp.int32, (hidden_ref.shape[0], WIDE), 1) < HEAD
+    for p in range(parts_ref.shape[0] // 2):
+        even = parts_ref[2 * p, :, model:].astype(f32)
+        odd = parts_ref[2 * p + 1, :, model:].astype(f32)
+        at = p * WIDE
+        accepted_ref[:, at : at + WIDE] = jnp.where(low, even, pltpu.roll(odd, HEAD, 1)).astype(bf16)
+        at = kv_width + p * WIDE
+        accepted_ref[:, at : at + WIDE] = jnp.where(low, pltpu.roll(even, HEAD, 1), odd).astype(bf16)
+
+
+def in_hbm(*arrays):
+    return tuple(pltpu.with_memory_space_constraint(a, pltpu.HBM) for a in arrays)
 
 
 def spaces(text):
-    kinds = {"s": pltpu.SMEM, "v": pltpu.VMEM}
+    kinds = {"a": pl.ANY, "v": pltpu.VMEM}
     return [pl.BlockSpec(memory_space=kinds[c]) for c in text]
 
 
-def params():
-    return pltpu.CompilerParams(vmem_limit_bytes=20 << 20)
+def params(mebibytes=12):
+    return pltpu.CompilerParams(vmem_limit_bytes=mebibytes << 20)
+
+
+def swap(rows, mask):
+    count = lax.axis_size("tp")
+    return lax.ppermute(rows, "tp", [(i, i ^ mask) for i in range(count)])
+
+
+def gather_blocks(block):
+    pairs = [block] + [swap(block, 2 * k) for k in range(1, lax.axis_size("tp") // 2)]
+    return [a for rows in pairs for a in (rows, swap(rows, 1))]
 
 
 def per_device_packed(
@@ -525,53 +608,99 @@
     page_len, kv_width = cache_keys.shape[1:]
     group_rows = tok_dev * tp_count
     sent = lambda rows: jax.ShapeDtypeStruct((tp_count, rows, WIDE), bf16)
-    row_slot = lambda rank: rank * tok_dev // DRAFT
+    dma = pltpu.SemaphoreType.DMA
+    slots_smem = pltpu.SMEM((slot_count,), jnp.int32)
     pulled = lax.all_gather(
         jnp.concatenate([queries, new_kv, residual], axis=1), "req", axis=0
     )
-    pack_rows = slot_count * page_len + 3 * tok_dev
     packed, own_res = pl.pallas_call(
-        functools.partial(pack_kernel, row_slot),
-        out_shape=(sent(pack_rows), jax.ShapeDtypeStruct(residual.shape, bf16)),
-        in_specs=spaces("ssvvv"),
+        functools.partial(pack_kernel, lambda rank: lax.div(rank * tok_dev, DRAFT)),
+        out_shape=(
+            sent(slot_count * page_len + 3 * tok_dev),
+            jax.ShapeDtypeStruct(residual.shape, bf16),
+        ),
+        in_specs=spaces("aaaav"),
         out_specs=tuple(spaces("vv")),
+        scratch_shapes=[
+            slots_smem,
+            slots_smem,
+            pltpu.VMEM(cache_keys.shape, bf16),
+            pltpu.VMEM(cache_values.shape, bf16),
+            dma((4,)),
+        ],
         compiler_params=params(),
         name="pack",
-    )(placement, page_table, pulled, cache_keys, cache_values)
+    )(*in_hbm(placement, page_table.reshape(slot_count), cache_keys, cache_values), pulled)
     packed = lax.all_to_all(packed, "tp", 0, 0, tiled=True)
-    out_rows = group_rows + group_rows // 2 + (model // WIDE) * tok_dev + tok_dev
-    outs = pl.pallas_call(
+    block, picked, out_weight = pl.pallas_call(
         attend_kernel,
-        out_shape=sent(out_rows),
-        in_specs=spaces("ssvvv"),
-        out_specs=spaces("v")[0],
-        scratch_shapes=[pltpu.VMEM((slot_count * DRAFT, slot_count * DRAFT), f32)],
+        out_shape=(
+            jax.ShapeDtypeStruct(
+                (group_rows + group_rows // 2 + (model // WIDE) * tok_dev, WIDE), bf16
+            ),
+            sent(tok_dev),
+            pltpu.VMEM(out_weight.shape, bf16),
+        ),
+        in_specs=spaces("aaaavv"),
+        out_specs=tuple(spaces("vvv")),
+        scratch_shapes=[
+            slots_smem,
+            slots_smem,
+            pltpu.VMEM((slot_count, DRAFT), jnp.int32),
+            pltpu.VMEM((slot_count * DRAFT, slot_count * DRAFT), f32),
+            dma((4,)),
+        ],
         compiler_params=params(),
         name="attend",
-    )(lengths, accept_leaf, parents, packed, own_res)
-    outs = lax.all_to_all(outs, "tp", 0, 0, tiled=True)
-    weights = in_vmem(out_weight, router_weight, gate_up, down_weight)
-    moe, hidden, attn_own, accepted = pl.pallas_call(
+    )(*in_hbm(lengths, accept_leaf, parents, out_weight), packed, own_res)
+    blocks = gather_blocks(block)
+    streamed = (
+        router_weight.T,
+        expert_ids.T,
+        norm_gain.reshape(model // WIDE, WIDE),
+        gate_up,
+        down_weight,
+    )
+    units = gate_up.shape[0]
+    moe, hidden, attn_own = pl.pallas_call(
         expert_kernel,
         out_shape=(
-            jax.ShapeDtypeStruct((group_rows, model), bf16),
+            jax.ShapeDtypeStruct((tp_count, tok_dev, model + WIDE), bf16),
             jax.ShapeDtypeStruct((tok_dev, model), f32),
             jax.ShapeDtypeStruct(queries.shape, bf16),
-            jax.ShapeDtypeStruct(new_kv.shape, bf16),
         ),
-        in_specs=spaces("vvvvvvv"),
-        out_specs=tuple(spaces("vvvv")),
+        in_specs=spaces("aaaaav" + "v" * (1 + tp_count)),
+        out_specs=tuple(spaces("vvv")),
         scratch_shapes=[
             pltpu.VMEM((group_rows, HEADS * HEAD), bf16),
             pltpu.VMEM((group_rows, model), f32),
             pltpu.VMEM((group_rows, model), bf16),
-            pltpu.VMEM((gate_up.shape[0], group_rows, gate_up.shape[2] // 2), f32),
+            pltpu.VMEM((units, group_rows, gate_up.shape[2] // 2), f32),
+            *[pltpu.VMEM(a.shape, a.dtype) for a in streamed],
+            dma((3,)),
+            dma((units,)),
+            dma((units // STEP,)),
         ],
+        compiler_params=params(36),
+        name="experts",
+    )(
+        *in_hbm(*streamed),
+        out_weight,
+        picked,
+        *blocks,
+    )
+    parts = lax.all_to_all(moe, "tp", 0, 0, tiled=True)
+    layer_out, accepted = pl.pallas_call(
+        finish_kernel,
+        out_shape=(
+            jax.ShapeDtypeStruct(residual.shape, bf16),
+            jax.ShapeDtypeStruct(new_kv.shape, bf16),
+        ),
+        in_specs=spaces("vv"),
+        out_specs=tuple(spaces("vv")),
         compiler_params=params(),
-        name="experts",
-    )(outs, expert_ids, norm_gain[None, :], *weights)
-    parts = lax.all_to_all(moe, "tp", 0, 0, tiled=True).reshape(tp_count, tok_dev, model)
-    layer_out = (hidden + jnp.sum(parts.astype(f32), axis=0)).astype(bf16)
+        name="finish",
+    )(parts, hidden)
     return attn_own, layer_out, accepted
 
 

time: 103 us -> 83.9 us (0.81)
  local copies, waits for them, and re-layouts: 18.9 us -> 0 us
  waiting for transfers between devices: 17.8 us -> 7.95 us
  Pallas kernels: 12.3 us -> 17.6 us
  starting transfers between devices: 3.55 us -> 8.7 us
    unnamed x21 -> x0, local copies, waits for them, and re-layouts: 18.2 us -> none
    all_to_all x1 -> x0, waiting for transfers between devices: 17.8 us -> none  [per_device_packed(): outs = lax.all_to_all(outs, 'tp', 0, 0, tiled=True)]
    ppermute x0 -> x7, starting transfers between devices: none -> 8.7 us  [swap(): return lax.ppermute(rows, 'tp', [(i, i ^ mask) for i in range(count)])]
    ppermute x0 -> x7, waiting for transfers between devices: none -> 7.95 us  [swap(): return lax.ppermute(rows, 'tp', [(i, i ^ mask) for i in range(count)])]
    pallas_call x3 -> x4, Pallas kernels: 12.3 us -> 17.6 us  [the longest x1 12.6 us: per_device_packed(): pl.pallas_call(expert_kernel, out_shape=(jax.ShapeDtypeStruct((tp_count,...]
    all_to_all x1 -> x0, starting transfers between devices: 3.55 us -> none  [per_device_packed(): outs = lax.all_to_all(outs, 'tp', 0, 0, tiled=True)]
  transfers between devices with their start and end apart: 1 -> 7, of which waited for: 1 -> 4; matrix products, arithmetic and copies ran while one was open for 3% -> 0% of each run, Pallas kernels for 0% -> 0%
where the time goes in v2:
time: 83.9 us; the launch traced here: 83.6 us
  blocking collectives  47.8 us (57%)
  Pallas kernels  17.6 us (21%)
  starting transfers between devices  8.7 us (10%)
  waiting for transfers between devices  7.95 us (9%)
  other arithmetic  0.85 us (1%)
    all_to_all x1, blocking collectives, per_device_packed(): packed = lax.all_to_all(packed, 'tp', 0, 0, tiled=True)  23.2 us
    all_to_all x1, blocking collectives, per_device_packed(): parts = lax.all_to_all(moe, 'tp', 0, 0, tiled=True)  15.9 us
    pallas_call x1, Pallas kernels, per_device_packed(): pl.pallas_call(expert_kernel, out_shape=(jax.ShapeDtypeStruct((tp_count,...  12.6 us
    ppermute x7, starting transfers between devices, swap(): return lax.ppermute(rows, 'tp', [(i, i ^ mask) for i in range(count)])  8.7 us
    all_gather x1, blocking collectives, per_device_packed(): lax.all_gather(jnp.concatenate([queries, new_kv, residual], axis=1), 'req...  8.65 us
    ppermute x7, waiting for transfers between devices, swap(): return lax.ppermute(rows, 'tp', [(i, i ^ mask) for i in range(count)])  7.95 us
    pallas_call x1, Pallas kernels, per_device_packed(): pl.pallas_call(attend_kernel, out_shape=(jax.ShapeDtypeStruct((group_rows...  3.06 us
  transfers between devices with their start and end apart: 7, of which 4 were waited for; matrix products, arithmetic and copies ran while one was open for 0% of the time, Pallas kernels for 0%

profile of v2, /device:TPU:0, one launch (start us, length us, event | category | flops | bytes accessed | tf_op | source)
XLA Modules:
  0.0 83.6 jit_solution(4032920486463441100)
XLA Ops:
  0.6 0.9 %pad_maximum_fusion = bf16[16,4096]{1,0:T(8,128)(2,1)S(1)} fusion(bf16[16,1536]{1,0:T(8,128)(2,1)} %param.18, bf16[16,1024]{1,0:T(8,128)(2,1)} %param.17, bf16[16,1536]{1,0:T(8,128)(2,1)} %param.16), kind=kLoop, calls=%fused_computation | loop fusion | flops 393216 | bytes 262144 | tf_op jit(solution)/shard_map/concatenate | solution.py:614
  1.5 8.6 %all-gather = bf16[64,4096]{1,0:T(8,128)(2,1)S(1)} all-gather(bf16[16,4096]{1,0:T(8,128)(2,1)S(1)} %pad_maximum_fusion), channel_id=2, replica_groups=mesh['req'=4,'tp'=8] {'req'}, dimensions={0}, use_global_device_ids=true | all-gather | bytes 655360 | tf_op jit(solution)/shard_map/all_gather | solution.py:613
  10.1 1.3 %pack.1 = (bf16[8,304,128]{2,1,0:T(8,128)(2,1)S(1)}, bf16[16,1536]{1,0:T(8,128)(2,1)S(1)}) custom-call(s32[2]{0:T(128)} %placement_hbm.1, s32[2]{0:T(128)} %bitcast.9, bf16[2,128,512]{2,1,0:T(8,128)(2,1)} %keys_hbm.1, bf16[2,128,512]{2,1,0:T(8,128)(2,1)} %values_hbm.1, bf16[4,16,4096]{2,1,0:T(8,128)(2,1)S(1)} %bitcast.5), custom_call_target="tpu_custom_call" | custom-call | tf_op jit(solution)/shard_map/pack/pallas_call | solution.py:616
  11.4 23.2 %all_to_all.10.got_ref = bf16[8,304,128]{2,1,0:T(8,128)(2,1)S(1)} all-to-all(bf16[8,304,128]{2,1,0:T(8,128)(2,1)S(1)} %get-tuple-element.13), channel_id=1, replica_groups=mesh['req'=4,'tp'=8] {'tp'}, dimensions={0} | all-to-all | bytes 1245184 | tf_op jit(solution)/shard_map/all_to_all | solution.py:634
  34.6 3.1 %attend.1 = (bf16[384,128]{1,0:T(8,128)(2,1)S(1)}, bf16[8,16,128]{2,1,0:T(8,128)(2,1)S(1)}, bf16[1536,1536]{1,0:T(8,128)(2,1)S(1)}) custom-call(s32[2]{0:T(128)} %lengths_hbm.1, s32[2]{0:T(128)} %leaf_hbm.1, s32[2,64]{1,0:T(2,128)} %parents_hbm.1, bf16[1536,1536]{1,0:T(8,128)(2,1)} %weight_hbm.1, bf16[8,304,128]{2,1,0:T(8,128)(2,1)S(1)} %all_to_all.10.got_ref, ...), custom_call_target="tpu_custom_call" | custom-call | tf_op jit(solution)/shard_map/attend/pallas_call | solution.py:635
  37.7 1.3 %collective-permute-start.5 = (bf16[384,128]{1,0:T(8,128)(2,1)S(1)}, bf16[384,128]{1,0:T(8,128)(2,1)S(1)}, u32[]{:S(2)}, u32[]{:S(2)}) collective-permute-start(bf16[384,128]{1,0:T(8,128)(2,1)S(1)} %get-tuple-element.17.refs_0_), channel_id=1, source_target_pairs={{0,6},{1,7},{2,4},{3,5},{4,2},{5,3},{6,0},{7,1},{8,14},{9,15},{10,... | collective-permute-start | bytes 294920 | tf_op jit(solution)/shard_map/ppermute | solution.py:578
  39.0 1.0 %collective-permute-start.3 = (bf16[384,128]{1,0:T(8,128)(2,1)S(1)}, bf16[384,128]{1,0:T(8,128)(2,1)S(1)}, u32[]{:S(2)}, u32[]{:S(2)}) collective-permute-start(bf16[384,128]{1,0:T(8,128)(2,1)S(1)} %get-tuple-element.17.refs_0_), channel_id=1, source_target_pairs={{0,4},{1,5},{2,6},{3,7},{4,0},{5,1},{6,2},{7,3},{8,12},{9,13},{10,... | collective-permute-start | bytes 294920 | tf_op jit(solution)/shard_map/ppermute | solution.py:578
  40.1 2.1 %collective-permute-start.1 = (bf16[384,128]{1,0:T(8,128)(2,1)S(1)}, bf16[384,128]{1,0:T(8,128)(2,1)S(1)}, u32[]{:S(2)}, u32[]{:S(2)}) collective-permute-start(bf16[384,128]{1,0:T(8,128)(2,1)S(1)} %get-tuple-element.17.refs_0_), channel_id=1, source_target_pairs={{0,2},{1,3},{2,0},{3,1},{4,6},{5,7},{6,4},{7,5},{8,10},{9,11},{10,... | collective-permute-start | bytes 294920 | tf_op jit(solution)/shard_map/ppermute | solution.py:578
  42.2 1.0 %collective-permute-start = (bf16[384,128]{1,0:T(8,128)(2,1)S(1)}, bf16[384,128]{1,0:T(8,128)(2,1)S(1)}, u32[]{:S(2)}, u32[]{:S(2)}) collective-permute-start(bf16[384,128]{1,0:T(8,128)(2,1)S(1)} %get-tuple-element.17.refs_0_), channel_id=1, source_target_pairs={{0,1},{1,0},{2,3},{3,2},{4,5},{5,4},{6,7},{7,6},{8,9},{9,8},{10,11... | collective-permute-start | bytes 294920 | tf_op jit(solution)/shard_map/ppermute | solution.py:578
  43.1 1.9 %collective-permute-done.5.refs_6_ = bf16[384,128]{1,0:T(8,128)(2,1)S(1)} collective-permute-done((bf16[384,128]{1,0:T(8,128)(2,1)S(1)}, bf16[384,128]{1,0:T(8,128)(2,1)S(1)}, u32[]{:S(2)}, u32[]{:S(2)}) %collective-permute-start.5) | collective-permute-done | bytes 98336 | tf_op jit(solution)/shard_map/ppermute | solution.py:578
  45.0 1.3 %collective-permute-start.6 = (bf16[384,128]{1,0:T(8,128)(2,1)S(1)}, bf16[384,128]{1,0:T(8,128)(2,1)S(1)}, u32[]{:S(2)}, u32[]{:S(2)}) collective-permute-start(bf16[384,128]{1,0:T(8,128)(2,1)S(1)} %collective-permute-done.5.refs_6_), channel_id=1, source_target_pairs={{0,1},{1,0},{2,3},{3,2},{4,5},{5,4},{6,7},{7,6},{8,9},{9,8},{10,11... | collective-permute-start | bytes 294920 | tf_op jit(solution)/shard_map/ppermute | solution.py:578
  46.3 1.9 %collective-permute-done.3.refs_4_ = bf16[384,128]{1,0:T(8,128)(2,1)S(1)} collective-permute-done((bf16[384,128]{1,0:T(8,128)(2,1)S(1)}, bf16[384,128]{1,0:T(8,128)(2,1)S(1)}, u32[]{:S(2)}, u32[]{:S(2)}) %collective-permute-start.3) | collective-permute-done | bytes 98336 | tf_op jit(solution)/shard_map/ppermute | solution.py:578
  48.2 1.3 %collective-permute-start.4 = (bf16[384,128]{1,0:T(8,128)(2,1)S(1)}, bf16[384,128]{1,0:T(8,128)(2,1)S(1)}, u32[]{:S(2)}, u32[]{:S(2)}) collective-permute-start(bf16[384,128]{1,0:T(8,128)(2,1)S(1)} %collective-permute-done.3.refs_4_), channel_id=1, source_target_pairs={{0,1},{1,0},{2,3},{3,2},{4,5},{5,4},{6,7},{7,6},{8,9},{9,8},{10,11... | collective-permute-start | bytes 294920 | tf_op jit(solution)/shard_map/ppermute | solution.py:578
  49.4 0.0 collective-permute-done.1.refs_2_
  49.4 0.8 collective-permute-start.2
  50.2 0.0 collective-permute-done.refs_1_
  50.2 0.0 collective-permute-done.6.refs_7_
  50.2 3.1 %collective-permute-done.4.refs_5_ = bf16[384,128]{1,0:T(8,128)(2,1)S(1)} collective-permute-done((bf16[384,128]{1,0:T(8,128)(2,1)S(1)}, bf16[384,128]{1,0:T(8,128)(2,1)S(1)}, u32[]{:S(2)}, u32[]{:S(2)}) %collective-permute-start.4) | collective-permute-done | bytes 98336 | tf_op jit(solution)/shard_map/ppermute | solution.py:578
  53.3 1.1 %collective-permute-done.2.refs_3_ = bf16[384,128]{1,0:T(8,128)(2,1)S(1)} collective-permute-done((bf16[384,128]{1,0:T(8,128)(2,1)S(1)}, bf16[384,128]{1,0:T(8,128)(2,1)S(1)}, u32[]{:S(2)}, u32[]{:S(2)}) %collective-permute-start.2) | collective-permute-done | bytes 98336 | tf_op jit(solution)/shard_map/ppermute | solution.py:578
  54.4 12.6 %experts.1 = (bf16[8,16,1664]{2,1,0:T(8,128)(2,1)S(1)}, f32[16,1536]{1,0:T(8,128)S(1)}, bf16[16,1536]{1,0:T(8,128)(2,1)}) custom-call(bf16[40,1536]{1,0:T(8,128)(2,1)} %bitcast.6, s32[8,128]{1,0:T(8,128)} %bitcast.8, f32[12,128]{1,0:T(8,128)} %bitcast.7, bf16[20,1536,256]{2,1,0:T(8,128)(2,1)} %gate_up_hbm.1, bf16[20,128,1536]{2,1,0:T(8,128)(2,1)} %down_hbm.1, ...), custom_call_target="tpu_custom_call" | custom-call | tf_op jit(solution)/shard_map/experts/pallas_call | solution.py:665
  67.0 15.9 %all_to_all.11.parts_ref = bf16[8,16,1664]{2,1,0:T(8,128)(2,1)S(1)} all-to-all(bf16[8,16,1664]{2,1,0:T(8,128)(2,1)S(1)} %get-tuple-element.19), channel_id=1, replica_groups=mesh['req'=4,'tp'=8] {'tp'}, dimensions={0} | all-to-all | bytes 851968 | tf_op jit(solution)/shard_map/all_to_all | solution.py:692
  82.9 0.7 finish.1
Async XLA Ops:
  37.7 7.3 %collective-permute-start.5 = (bf16[384,128]{1,0:T(8,128)(2,1)S(1)}, bf16[384,128]{1,0:T(8,128)(2,1)S(1)}, u32[]{:S(2)}, u32[]{:S(2)}) collective-permute-start(bf16[384,128]{1,0:T(8,128)(2,1)S(1)} %get-tuple-element.17.refs_0_), channel_id=1, source_target_pairs={{0,6},{1,7},{2,4},{3,5},{4,2},{5,3},{6,0},{7,1},{8,14},{9,15},{10,... | collective-permute-start | bytes 294920 | tf_op jit(solution)/shard_map/ppermute | solution.py:578
  39.0 9.1 %collective-permute-start.3 = (bf16[384,128]{1,0:T(8,128)(2,1)S(1)}, bf16[384,128]{1,0:T(8,128)(2,1)S(1)}, u32[]{:S(2)}, u32[]{:S(2)}) collective-permute-start(bf16[384,128]{1,0:T(8,128)(2,1)S(1)} %get-tuple-element.17.refs_0_), channel_id=1, source_target_pairs={{0,4},{1,5},{2,6},{3,7},{4,0},{5,1},{6,2},{7,3},{8,12},{9,13},{10,... | collective-permute-start | bytes 294920 | tf_op jit(solution)/shard_map/ppermute | solution.py:578
  40.1 9.3 %collective-permute-start.1 = (bf16[384,128]{1,0:T(8,128)(2,1)S(1)}, bf16[384,128]{1,0:T(8,128)(2,1)S(1)}, u32[]{:S(2)}, u32[]{:S(2)}) collective-permute-start(bf16[384,128]{1,0:T(8,128)(2,1)S(1)} %get-tuple-element.17.refs_0_), channel_id=1, source_target_pairs={{0,2},{1,3},{2,0},{3,1},{4,6},{5,7},{6,4},{7,5},{8,10},{9,11},{10,... | collective-permute-start | bytes 294920 | tf_op jit(solution)/shard_map/ppermute | solution.py:578
  42.2 8.0 %collective-permute-start = (bf16[384,128]{1,0:T(8,128)(2,1)S(1)}, bf16[384,128]{1,0:T(8,128)(2,1)S(1)}, u32[]{:S(2)}, u32[]{:S(2)}) collective-permute-start(bf16[384,128]{1,0:T(8,128)(2,1)S(1)} %get-tuple-element.17.refs_0_), channel_id=1, source_target_pairs={{0,1},{1,0},{2,3},{3,2},{4,5},{5,4},{6,7},{7,6},{8,9},{9,8},{10,11... | collective-permute-start | bytes 294920 | tf_op jit(solution)/shard_map/ppermute | solution.py:578
  45.0 5.2 %collective-permute-start.6 = (bf16[384,128]{1,0:T(8,128)(2,1)S(1)}, bf16[384,128]{1,0:T(8,128)(2,1)S(1)}, u32[]{:S(2)}, u32[]{:S(2)}) collective-permute-start(bf16[384,128]{1,0:T(8,128)(2,1)S(1)} %collective-permute-done.5.refs_6_), channel_id=1, source_target_pairs={{0,1},{1,0},{2,3},{3,2},{4,5},{5,4},{6,7},{7,6},{8,9},{9,8},{10,11... | collective-permute-start | bytes 294920 | tf_op jit(solution)/shard_map/ppermute | solution.py:578
  48.2 5.2 %collective-permute-start.4 = (bf16[384,128]{1,0:T(8,128)(2,1)S(1)}, bf16[384,128]{1,0:T(8,128)(2,1)S(1)}, u32[]{:S(2)}, u32[]{:S(2)}) collective-permute-start(bf16[384,128]{1,0:T(8,128)(2,1)S(1)} %collective-permute-done.3.refs_4_), channel_id=1, source_target_pairs={{0,1},{1,0},{2,3},{3,2},{4,5},{5,4},{6,7},{7,6},{8,9},{9,8},{10,11... | collective-permute-start | bytes 294920 | tf_op jit(solution)/shard_map/ppermute | solution.py:578
  49.4 5.0 %collective-permute-start.2 = (bf16[384,128]{1,0:T(8,128)(2,1)S(1)}, bf16[384,128]{1,0:T(8,128)(2,1)S(1)}, u32[]{:S(2)}, u32[]{:S(2)}) collective-permute-start(bf16[384,128]{1,0:T(8,128)(2,1)S(1)} %collective-permute-done.1.refs_2_), channel_id=1, source_target_pairs={{0,1},{1,0},{2,3},{3,2},{4,5},{5,4},{6,7},{7,6},{8,9},{9,8},{10,11... | collective-permute-start | bytes 294920 | tf_op jit(solution)/shard_map/ppermute | solution.py:578

commit v3 on v2

--- a/solution.py
+++ b/solution.py
@@ -16,7 +16,6 @@
 DRAFT = 64
 WIDE = 128
 STEP = 2
-AHEAD = 4
 
 
 neg_big = -1e30
@@ -255,47 +254,78 @@
         copy.wait()
 
 
-def pack_kernel(
-    slot_of, placement_hbm, pages_hbm, keys_hbm, values_hbm, pulled_ref, sent_ref, res_ref,
-    placement_ref, pages_ref, keys_ref, values_ref, sems,
-):
-    slot_count = placement_ref.shape[0]
-    page_len, kv_width = keys_ref.shape[1:]
+def split_kernel(pairs, *refs):
+    (
+        pages_hbm, placement_hbm, lengths_hbm, leaf_hbm, keys_hbm, values_hbm, queries_hbm,
+        new_kv_hbm, residual_hbm, parents_hbm, router_hbm, ids_hbm, gain_hbm,
+    ) = refs[:13]
+    parts, refs = refs[13 : 13 + pairs], refs[13 + pairs :]
+    joined_ref, table_ref, parents_ref, router_ref, ids_ref, gain_ref = refs[:6]
+    pages_ref, placement_ref, lengths_ref, leaf_ref, keys_ref, values_ref, split_ref, sems = refs[6:]
+    slot_count = pages_ref.shape[0]
+    page_len = keys_ref.shape[1]
+    tok_dev = joined_ref.shape[0]
+    moves = [
+        (pages_hbm, pages_ref),
+        (keys_hbm, keys_ref),
+        (values_hbm, values_ref),
+        (placement_hbm, placement_ref),
+        (lengths_hbm, lengths_ref),
+        (leaf_hbm, leaf_ref),
+        (parents_hbm, parents_ref),
+        (router_hbm, router_ref),
+        (ids_hbm, ids_ref),
+        (gain_hbm, gain_ref),
+    ]
+    column = 0
+    for source in (queries_hbm, new_kv_hbm, residual_hbm):
+        moves.append((source, joined_ref.at[:, column : column + source.shape[1]]))
+        column += source.shape[1]
     start_all(
-        [
-            pltpu.make_async_copy(source, target, sems.at[k])
-            for k, (source, target) in enumerate(
-                [
-                    (placement_hbm, placement_ref),
-                    (pages_hbm, pages_ref),
-                    (keys_hbm, keys_ref),
-                    (values_hbm, values_ref),
-                ]
-            )
-        ]
-    )
-    q_width = HEADS * HEAD
-    tok_dev = pulled_ref.shape[1]
-    slot = slot_of(lax.axis_index("tp"))
-    source = lax.div(placement_ref[slot], slot_count)
-    rows = pulled_ref[source]
-    res_ref[...] = rows[:, q_width + 2 * kv_width :]
-    head_rows = (HEADS // KV_HEADS) * HEAD
-    tail = jnp.zeros((tok_dev, 2 * WIDE - head_rows), rows.dtype)
-    base = slot_count * page_len
+        [pltpu.make_async_copy(a, b, sems.at[k]) for k, (a, b) in enumerate(moves)]
+    )
+    slot = lax.div(lax.axis_index("tp") * tok_dev, DRAFT)
+    numbers = [lax.div(placement_ref[slot], slot_count)]
+    numbers += [lengths_ref[s] for s in range(slot_count)]
+    numbers += [leaf_ref[s] for s in range(slot_count)]
+    for row, number in enumerate(numbers):
+        table_ref[row : row + 1, :] = jnp.full((1, WIDE), number, jnp.int32).astype(jnp.float32)
     for head in range(KV_HEADS):
         low = head * HEAD
         for s in range(slot_count):
             page = pages_ref[s]
-            sent_ref[head, s * page_len : (s + 1) * page_len, :] = jnp.concatenate(
+            split_ref[head // 2, head % 2, s * page_len : (s + 1) * page_len, :] = jnp.concatenate(
                 [keys_ref[page, :, low : low + HEAD], values_ref[page, :, low : low + HEAD]], axis=1
             )
+    pair = lax.div(lax.axis_index("tp"), 2)
+    for k, part in enumerate(parts):
+        part[...] = split_ref[lax.bitwise_xor(pair, k)]
+
+
+def number(table_ref, row):
+    return jnp.max(table_ref[row : row + 1, :]).astype(jnp.int32)
+
+
+def route_kernel(kv_width, after_ref, table_ref, pulled_ref, *refs):
+    del after_ref
+    parts, (sent_ref, res_ref, turned_ref) = refs[:-3], refs[-3:]
+    rank = lax.axis_index("tp")
+    other = 1 - lax.rem(rank, 2)
+    for k, part in enumerate(parts):
+        turned_ref[k] = part[other]
+    q_width = HEADS * HEAD
+    tok_dev = pulled_ref.shape[1]
+    rows = pulled_ref[number(table_ref, 0)]
+    res_ref[...] = rows[:, q_width + 2 * kv_width :]
+    head_rows = (HEADS // KV_HEADS) * HEAD
+    tail = jnp.zeros((tok_dev, 2 * WIDE - head_rows), rows.dtype)
+    for head in range(KV_HEADS):
         q_low = head * head_rows
         pair = jnp.concatenate([rows[:, q_low : q_low + head_rows], tail], axis=1)
-        sent_ref[head, base : base + tok_dev, :] = pair[:, :WIDE]
-        sent_ref[head, base + tok_dev : base + 2 * tok_dev, :] = pair[:, WIDE:]
-        k_low = q_width + low
-        sent_ref[head, base + 2 * tok_dev :, :] = jnp.concatenate(
+        sent_ref[head, :tok_dev, :] = pair[:, :WIDE]
+        sent_ref[head, tok_dev : 2 * tok_dev, :] = pair[:, WIDE:]
+        k_low = q_width + head * HEAD
+        sent_ref[head, 2 * tok_dev :, :] = jnp.concatenate(
             [rows[:, k_low : k_low + HEAD], rows[:, k_low + kv_width : k_low + kv_width + HEAD]],
             axis=1,
         )
@@ -317,42 +347,54 @@
     return reached.T
 
 
-def attend_kernel(
-    lengths_hbm, leaf_hbm, parents_hbm, weight_hbm, got_ref, res_ref, sent_ref, picked_ref,
-    weight_ref,
-    lengths_ref, leaf_ref, parents_ref, reach_ref, sems,
+def tree_kernel(
+    after_ref, down_hbm, table_ref, parents_ref, down_ref, reach_ref, chosen_ref, sem
 ):
-    start_all(
-        [
-            pltpu.make_async_copy(lengths_hbm, lengths_ref, sems.at[0]),
-            pltpu.make_async_copy(leaf_hbm, leaf_ref, sems.at[1]),
-            pltpu.make_async_copy(parents_hbm, parents_ref, sems.at[2]),
-        ]
-    )
-    weight_copy = pltpu.make_async_copy(weight_hbm, weight_ref, sems.at[3])
-    weight_copy.start()
+    del after_ref
+    copy = pltpu.make_async_copy(down_hbm, down_ref, sem)
+    copy.start()
+    slot_count = parents_ref.shape[0]
     reach_ref[...] = ancestor_rows(parents_ref)
-    slot_count = lengths_ref.shape[0]
+    node_from = lax.broadcasted_iota(jnp.int32, (DRAFT, DRAFT), 0)
+    node_to = lax.broadcasted_iota(jnp.int32, (DRAFT, DRAFT), 1)
+    upto = jnp.where(node_from <= node_to, 1.0, 0.0).astype(jnp.bfloat16)
+    for s in range(slot_count):
+        leaf = number(table_ref, 1 + slot_count + s)
+        path = reach_ref[pl.ds(s * DRAFT + leaf, 1), s * DRAFT : (s + 1) * DRAFT]
+        path = jnp.broadcast_to(path, (DRAFT, DRAFT))
+        rank = jnp.dot(path.astype(jnp.bfloat16), upto, preferred_element_type=jnp.float32)
+        chosen = (path > 0.5) & (rank == (node_from + 1).astype(jnp.float32))
+        chosen_ref[s] = jnp.where(chosen, 1.0, 0.0).astype(jnp.bfloat16)
+    copy.wait()
+
+
+def attend_kernel(table_ref, reach_ref, chosen_ref, got_ref, res_ref, turned_ref, *refs):
+    parts, (sent_ref, picked_ref) = refs[:-2], refs[-2:]
+    slot_count = chosen_ref.shape[0]
     sources = got_ref.shape[0]
     tok_dev = res_ref.shape[0]
-    base = got_ref.shape[1] - 3 * tok_dev
-    page_len = base // slot_count
+    page_len = turned_ref.shape[1] // slot_count
     per_slot = DRAFT // tok_dev
     group_size = HEADS // KV_HEADS
     f32, bf16 = jnp.float32, jnp.bfloat16
     lane_low = lax.broadcasted_iota(jnp.int32, (DRAFT, WIDE), 1) < HEAD
-    positions = lax.broadcasted_iota(jnp.int32, (1, sources * page_len), 1)
+    rank = lax.axis_index("tp")
+    side = lax.rem(rank, 2)
+    within = lax.broadcasted_iota(jnp.int32, (1, page_len), 1)
+    positions = []
+    for k in range(len(parts)):
+        pair = lax.bitwise_xor(lax.div(rank, 2), k)
+        for page in (2 * pair + side, 2 * pair + 1 - side):
+            positions.append(within + page * page_len)
+    positions = jnp.concatenate(positions, axis=1)
     dims = (((1,), (1,)), ((), ()))
     scale = 1.0 / math.sqrt(HEAD)
-    node_from = lax.broadcasted_iota(jnp.int32, (DRAFT, DRAFT), 0)
-    node_to = lax.broadcasted_iota(jnp.int32, (DRAFT, DRAFT), 1)
-    upto = jnp.where(node_from <= node_to, 1.0, 0.0).astype(bf16)
     outs, picked = [], []
     for s in range(slot_count):
         first = s * per_slot
 
         def part(k):
-            low = base + k * tok_dev
+            low = k * tok_dev
             return jnp.concatenate(
                 [got_ref[first + i, low : low + tok_dev, :] for i in range(per_slot)], axis=0
             )
@@ -366,11 +408,13 @@
             ],
             axis=0,
         ).astype(bf16)
-        cache_kv = got_ref[:, s * page_len : (s + 1) * page_len, :].reshape(
-            sources * page_len, WIDE
+        at = slice(s * page_len, (s + 1) * page_len)
+        cache_kv = jnp.concatenate(
+            [a for k, part in enumerate(parts) for a in (part[side, at, :], turned_ref[k, at, :])],
+            axis=0,
         )
         scores = lax.dot_general(q_rows, cache_kv, dims, preferred_element_type=f32)
-        is_valid = positions < lengths_ref[s]
+        is_valid = positions < number(table_ref, 1 + s)
         scores = jnp.where(is_valid, scores, neg_big)
         reach = reach_ref[s * DRAFT : (s + 1) * DRAFT, s * DRAFT : (s + 1) * DRAFT]
         allowed = jnp.concatenate([reach] * group_size, axis=0) > 0.5
@@ -388,12 +432,9 @@
             tree_weights, tree_kv, preferred_element_type=f32
         )
         outs.append(mixed / total)
-        path = reach_ref[pl.ds(s * DRAFT + leaf_ref[s], 1), s * DRAFT : (s + 1) * DRAFT]
-        path = jnp.broadcast_to(path, (DRAFT, DRAFT))
-        rank = jnp.dot(path.astype(bf16), upto, preferred_element_type=f32)
-        chosen = (path > 0.5) & (rank == (node_from + 1).astype(f32))
-        chosen = jnp.where(chosen, 1.0, 0.0).astype(bf16)
-        picked.append(jnp.dot(chosen, tree_kv, preferred_element_type=f32).astype(bf16))
+        picked.append(
+            jnp.dot(chosen_ref[s], tree_kv, preferred_element_type=f32).astype(bf16)
+        )
     pair_rows, last_rows = [], []
     for out in outs:
         head_out = [out[r * DRAFT : (r + 1) * DRAFT] for r in range(group_size)]
@@ -407,40 +448,28 @@
     for target in range(sources):
         row = (target % per_slot) * tok_dev
         picked_ref[target] = picked[target // per_slot][row : row + tok_dev]
-    weight_copy.wait()
+
+
+def fetch_kernel(spans, after_ref, *refs):
+    del after_ref
+    count = len(spans)
+    sems = refs[-1]
+    start_all(
+        [
+            pltpu.make_async_copy(refs[k].at[pl.ds(*spans[k])], refs[count + k], sems.at[k])
+            for k in range(count)
+        ]
+    )
 
 
 def expert_kernel(
-    router_hbm, ids_hbm, gain_hbm, gate_up_hbm, down_hbm, out_weight_ref, picked_ref, *refs
+    router_ref, ids_ref, gain_ref, out_weight_ref, down_ref, early_ref, late_ref, picked_ref, *refs
 ):
     blocks, refs = refs[:KV_HEADS], refs[KV_HEADS:]
-    moe_ref, hidden_ref, attn_ref, x_ref, hid_ref, normed_ref, share_ref = refs[:7]
-    router_ref, ids_ref, gain_ref, gate_up_ref, down_ref, sems, unit_sems, down_sems = refs[7:]
+    mine_ref, sent_ref, hidden_ref, attn_ref, x_ref, hid_ref, normed_ref, share_ref = refs
     f32, bf16 = jnp.float32, jnp.bfloat16
-    units = gate_up_ref.shape[0]
-    small = [
-        pltpu.make_async_copy(router_hbm, router_ref, sems.at[0]),
-        pltpu.make_async_copy(ids_hbm, ids_ref, sems.at[1]),
-        pltpu.make_async_copy(gain_hbm, gain_ref, sems.at[2]),
-    ]
-    for copy in small:
-        copy.start()
-
-    def unit_copy(u):
-        return pltpu.make_async_copy(gate_up_hbm.at[u], gate_up_ref.at[u], unit_sems.at[u])
-
-    def down_copy(i):
-        at = pl.ds(i * STEP, STEP)
-        return pltpu.make_async_copy(down_hbm.at[at], down_ref.at[at], down_sems.at[i])
-
-    def start_step(i):
-        for k in range(STEP):
-            unit_copy(i * STEP + k).start()
-        down_copy(i).start()
-
-    steps = units // STEP
-    for i in range(min(AHEAD, steps)):
-        start_step(i)
+    early = early_ref.shape[0]
+    units = early + late_ref.shape[0]
     tok_dev = hidden_ref.shape[0]
     sources = len(blocks)
     group_rows = sources * tok_dev
@@ -490,8 +519,6 @@
     projected = jnp.dot(x_ref[...], out_weight_ref[...], preferred_element_type=f32)
     hidden = hid_ref[...] + projected
     hid_ref[...] = hidden
-    for copy in small:
-        copy.wait()
     gain = jnp.concatenate([gain_ref[c : c + 1, :] for c in range(model // WIDE)], axis=1)
     scale = lax.rsqrt(jnp.mean(hidden * hidden, axis=1, keepdims=True) + norm_eps)
     normed_ref[...] = (hidden * scale * gain).astype(bf16)
@@ -508,56 +535,68 @@
         count = count + jnp.where(ids[:, k : k + 1] == expert_names, 1.0, 0.0)
     expo = jnp.where(count > 0.0, jnp.exp(logits), 0.0) * count
     routing = expo / jnp.sum(expo, axis=1, keepdims=True)
-    unit_width = gate_up_ref.shape[2] // 2
+    unit_width = early_ref.shape[2] // 2
     span = FF_E // unit_width
-    for u in range(units):
+    each = span if units % span == 0 else 1
+    for u in range(0, units, each):
         expert = (rank * units + u) // span
-        share_ref[u] = jnp.broadcast_to(
-            jnp.sum(jnp.where(expert_range == expert, routing, 0.0), axis=1, keepdims=True),
-            (group_rows, unit_width),
-        )
+        share = jnp.sum(jnp.where(expert_range == expert, routing, 0.0), axis=1, keepdims=True)
+        share_ref[u : u + each] = jnp.broadcast_to(share[None], (each, group_rows, unit_width))
 
     def one_unit(u):
-        both = jnp.dot(normed_ref[...], gate_up_ref[u], preferred_element_type=f32)
+        weight = early_ref[u] if u < early else late_ref[u - early]
+        both = jnp.dot(normed_ref[...], weight, preferred_element_type=f32)
         gate, up = both[:, :unit_width], both[:, unit_width:]
         return (gate / (1.0 + jnp.exp(-gate)) * up * share_ref[u]).astype(bf16)
 
-    def body(i, carry):
-        @pl.when(i + AHEAD < steps)
-        def _():
-            start_step(i + AHEAD)
-
-        for k in range(STEP):
-            unit_copy(i * STEP + k).wait()
+    for i in range(units // STEP):
         act = jnp.concatenate([one_unit(i * STEP + k) for k in range(STEP)], axis=1)
-        down_copy(i).wait()
-        down = down_ref[pl.ds(i * STEP, STEP)].reshape(STEP * unit_width, model)
-        hid_ref[...] += jnp.dot(act, down, preferred_element_type=f32)
-        return carry
-
-    hid_ref[...] = jnp.zeros_like(hid_ref)
-    lax.fori_loop(0, steps, body, 0)
-    for j in range(sources):
-        moe_ref[j, :, :model] = hid_ref[j * tok_dev : (j + 1) * tok_dev, :].astype(bf16)
-    moe_ref[:, :, model:] = picked_ref[...]
-
-
-def finish_kernel(parts_ref, hidden_ref, layer_ref, accepted_ref):
+        down = down_ref[i * STEP : (i + 1) * STEP].reshape(STEP * unit_width, model)
+        part = jnp.dot(act, down, preferred_element_type=f32)
+        hid_ref[...] = part if i == 0 else hid_ref[...] + part
+    side = lax.rem(rank, 2)
+    for k in range(sources // 2):
+        pair = lax.bitwise_xor(lax.div(rank, 2), k)
+        for target, ref in ((2 * pair + side, mine_ref), (2 * pair + 1 - side, sent_ref)):
+            row = pl.multiple_of(target * tok_dev, tok_dev)
+            ref[k, :, :model] = hid_ref[pl.ds(row, tok_dev), :].astype(ref.dtype)
+            ref[k, :, model:] = picked_ref[target].astype(ref.dtype)
+
+
+def fold_kernel(mine_ref, got_ref, hidden_ref, kept_ref, *sent_refs):
+    model = hidden_ref.shape[1]
+    is_even = lax.rem(lax.axis_index("tp"), 2) == 0
+    for k, ref in enumerate((kept_ref,) + sent_refs):
+        mine, got = mine_ref[k], got_ref[k].astype(jnp.float32)
+        total = mine[:, :model] + got[:, :model]
+        if k == 0:
+            total = total + hidden_ref[...]
+        ref[:, :model] = total.astype(ref.dtype)
+        low, high = mine[:, model:], got[:, model:]
+        even, odd = jnp.where(is_even, low, high), jnp.where(is_even, high, low)
+        ref[:, model:] = jnp.concatenate([even, odd], axis=1).astype(ref.dtype)
+
+
+def finish_kernel(attn_in_ref, *refs):
+    parts, (attn_ref, layer_ref, accepted_ref) = refs[:-3], refs[-3:]
+    attn_ref[...] = attn_in_ref[...]
     f32, bf16 = jnp.float32, jnp.bfloat16
-    model = hidden_ref.shape[1]
+    tok_dev, model = layer_ref.shape
     kv_width = accepted_ref.shape[1] // 2
-    total = hidden_ref[...]
-    for j in range(parts_ref.shape[0]):
-        total = total + parts_ref[j, :, :model].astype(f32)
+    total = parts[0][:, :model]
+    for part in parts[1:]:
+        total = total + part[:, :model].astype(f32)
     layer_ref[...] = total.astype(bf16)
-    low = lax.broadcasted_iota(jnp.int32, (hidden_ref.shape[0], WIDE), 1) < HEAD
-    for p in range(parts_ref.shape[0] // 2):
-        even = parts_ref[2 * p, :, model:].astype(f32)
-        odd = parts_ref[2 * p + 1, :, model:].astype(f32)
-        at = p * WIDE
-        accepted_ref[:, at : at + WIDE] = jnp.where(low, even, pltpu.roll(odd, HEAD, 1)).astype(bf16)
-        at = kv_width + p * WIDE
-        accepted_ref[:, at : at + WIDE] = jnp.where(low, pltpu.roll(even, HEAD, 1), odd).astype(bf16)
+    low = lax.broadcasted_iota(jnp.int32, (tok_dev, WIDE), 1) < HEAD
+    for k, part in enumerate(parts):
+        pair = lax.bitwise_xor(lax.div(lax.axis_index("tp"), 2), k)
+        even = part[:, model : model + WIDE].astype(f32)
+        odd = part[:, model + WIDE :].astype(f32)
+        at = pl.multiple_of(pair * WIDE, WIDE)
+        accepted_ref[:, pl.ds(at, WIDE)] = jnp.where(low, even, pltpu.roll(odd, HEAD, 1)).astype(bf16)
+        accepted_ref[:, pl.ds(kv_width + at, WIDE)] = jnp.where(
+            low, pltpu.roll(even, HEAD, 1), odd
+        ).astype(bf16)
 
 
 def in_hbm(*arrays):
@@ -573,14 +612,33 @@
     return pltpu.CompilerParams(vmem_limit_bytes=mebibytes << 20)
 
 
+def cost(mebibytes):
+    return pl.CostEstimate(flops=0, transcendentals=0, bytes_accessed=mebibytes << 20)
+
+
 def swap(rows, mask):
     count = lax.axis_size("tp")
     return lax.ppermute(rows, "tp", [(i, i ^ mask) for i in range(count)])
 
 
-def gather_blocks(block):
-    pairs = [block] + [swap(block, 2 * k) for k in range(1, lax.axis_size("tp") // 2)]
-    return [a for rows in pairs for a in (rows, swap(rows, 1))]
+def gather_blocks(block, early):
+    pairs = [swap(block, 2 * k) for k in range(1, lax.axis_size("tp") // 2)]
+    pairs, early = lax.optimization_barrier((pairs, early))
+    return [a for rows in [block] + pairs for a in (rows, swap(rows, 1))], early
+
+
+def fetch(name, after, *spans):
+    shapes = [(rows,) + array.shape[1:] for array, _, rows in spans]
+    return pl.pallas_call(
+        functools.partial(fetch_kernel, tuple((first, rows) for _, first, rows in spans)),
+        out_shape=tuple(pltpu.VMEM(shape, jnp.bfloat16) for shape in shapes),
+        in_specs=spaces("a" * (1 + len(spans))),
+        out_specs=tuple(spaces("v" * len(spans))),
+        scratch_shapes=[pltpu.SemaphoreType.DMA((len(spans),))],
+        compiler_params=params(),
+        cost_estimate=cost(sum(2 * math.prod(shape) for shape in shapes) >> 20),
+        name="fetch_" + name,
+    )(after, *in_hbm(*[array for array, _, _ in spans]))
 
 
 def per_device_packed(
@@ -610,104 +668,157 @@
     sent = lambda rows: jax.ShapeDtypeStruct((tp_count, rows, WIDE), bf16)
     dma = pltpu.SemaphoreType.DMA
     slots_smem = pltpu.SMEM((slot_count,), jnp.int32)
-    pulled = lax.all_gather(
-        jnp.concatenate([queries, new_kv, residual], axis=1), "req", axis=0
-    )
-    packed, own_res = pl.pallas_call(
-        functools.partial(pack_kernel, lambda rank: lax.div(rank * tok_dev, DRAFT)),
-        out_shape=(
-            sent(slot_count * page_len + 3 * tok_dev),
-            jax.ShapeDtypeStruct(residual.shape, bf16),
-        ),
-        in_specs=spaces("aaaav"),
-        out_specs=tuple(spaces("vv")),
+    pairs = tp_count // 2
+    part = jax.ShapeDtypeStruct((2, slot_count * page_len, WIDE), bf16)
+    loaded = (
+        page_table.reshape(slot_count),
+        placement,
+        lengths,
+        accept_leaf,
+        cache_keys,
+        cache_values,
+        queries,
+        new_kv,
+        residual,
+        parents,
+        router_weight.T,
+        expert_ids.T,
+        norm_gain.reshape(model // WIDE, WIDE),
+    )
+    *parts, joined, table, parents, router, ids, gain = pl.pallas_call(
+        functools.partial(split_kernel, pairs),
+        out_shape=(part,) * pairs
+        + (
+            jax.ShapeDtypeStruct((tok_dev, 2 * (model + kv_width)), bf16),
+            pltpu.VMEM((8, WIDE), f32),
+        )
+        + tuple(pltpu.VMEM(a.shape, a.dtype) for a in loaded[9:]),
+        in_specs=spaces("a" * len(loaded)),
+        out_specs=tuple(spaces("v" * (pairs + 6))),
         scratch_shapes=[
+            slots_smem,
+            slots_smem,
             slots_smem,
             slots_smem,
             pltpu.VMEM(cache_keys.shape, bf16),
             pltpu.VMEM(cache_values.shape, bf16),
-            dma((4,)),
+            pltpu.VMEM((pairs,) + part.shape, bf16),
+            dma((len(loaded),)),
         ],
         compiler_params=params(),
-        name="pack",
-    )(*in_hbm(placement, page_table.reshape(slot_count), cache_keys, cache_values), pulled)
+        cost_estimate=cost(4),
+        name="split",
+    )(*in_hbm(*loaded))
+    parts = [parts[0]] + [swap(parts[k], 2 * k) for k in range(1, pairs)]
+    pulled = lax.all_gather(joined, "req", axis=0)
+    nodes = slot_count * DRAFT
+    down_weight, reach, chosen = pl.pallas_call(
+        tree_kernel,
+        out_shape=(
+            pltpu.VMEM(down_weight.shape, bf16),
+            jax.ShapeDtypeStruct((nodes, nodes), f32),
+            jax.ShapeDtypeStruct((slot_count, DRAFT, DRAFT), bf16),
+        ),
+        in_specs=spaces("aavv"),
+        out_specs=tuple(spaces("vvv")),
+        scratch_shapes=[dma],
+        compiler_params=params(),
+        cost_estimate=cost(8),
+        name="tree",
+    )(pulled, *in_hbm(down_weight), table, parents)
+    packed, own_res, turned = pl.pallas_call(
+        functools.partial(route_kernel, kv_width),
+        out_shape=(
+            sent(3 * tok_dev),
+            jax.ShapeDtypeStruct(residual.shape, bf16),
+            jax.ShapeDtypeStruct((pairs,) + part.shape[1:], bf16),
+        ),
+        in_specs=spaces("avv" + "v" * pairs),
+        out_specs=tuple(spaces("vvv")),
+        compiler_params=params(),
+        cost_estimate=cost(4),
+        name="route",
+    )(down_weight, table, pulled, *parts)
+    turned = swap(turned, 1)
     packed = lax.all_to_all(packed, "tp", 0, 0, tiled=True)
-    block, picked, out_weight = pl.pallas_call(
+    block, picked = pl.pallas_call(
         attend_kernel,
         out_shape=(
             jax.ShapeDtypeStruct(
                 (group_rows + group_rows // 2 + (model // WIDE) * tok_dev, WIDE), bf16
             ),
             sent(tok_dev),
-            pltpu.VMEM(out_weight.shape, bf16),
         ),
-        in_specs=spaces("aaaavv"),
-        out_specs=tuple(spaces("vvv")),
-        scratch_shapes=[
-            slots_smem,
-            slots_smem,
-            pltpu.VMEM((slot_count, DRAFT), jnp.int32),
-            pltpu.VMEM((slot_count * DRAFT, slot_count * DRAFT), f32),
-            dma((4,)),
-        ],
+        in_specs=spaces("v" * (6 + pairs)),
+        out_specs=tuple(spaces("vv")),
         compiler_params=params(),
+        cost_estimate=cost(8),
         name="attend",
-    )(*in_hbm(lengths, accept_leaf, parents, out_weight), packed, own_res)
-    blocks = gather_blocks(block)
-    streamed = (
-        router_weight.T,
-        expert_ids.T,
-        norm_gain.reshape(model // WIDE, WIDE),
-        gate_up,
-        down_weight,
-    )
+    )(table, reach, chosen, packed, own_res, turned, *parts)
     units = gate_up.shape[0]
-    moe, hidden, attn_own = pl.pallas_call(
+    early = units // (2 * STEP) * STEP
+    ready = fetch("early", block, (gate_up, 0, early), (out_weight, 0, out_weight.shape[0]))
+    blocks, (early_units, out_weight) = gather_blocks(block, ready)
+    (late_units,) = fetch("late", block, (gate_up, early, units - early))
+    mine, sent_sums, hidden, attn_own = pl.pallas_call(
         expert_kernel,
         out_shape=(
-            jax.ShapeDtypeStruct((tp_count, tok_dev, model + WIDE), bf16),
+            jax.ShapeDtypeStruct((pairs, tok_dev, model + WIDE), f32),
+            jax.ShapeDtypeStruct((pairs, tok_dev, model + WIDE), bf16),
             jax.ShapeDtypeStruct((tok_dev, model), f32),
-            jax.ShapeDtypeStruct(queries.shape, bf16),
+            pltpu.VMEM(queries.shape, bf16),
         ),
-        in_specs=spaces("aaaaav" + "v" * (1 + tp_count)),
-        out_specs=tuple(spaces("vvv")),
+        in_specs=spaces("v" * (8 + tp_count)),
+        out_specs=tuple(spaces("vvvv")),
         scratch_shapes=[
             pltpu.VMEM((group_rows, HEADS * HEAD), bf16),
             pltpu.VMEM((group_rows, model), f32),
             pltpu.VMEM((group_rows, model), bf16),
             pltpu.VMEM((units, group_rows, gate_up.shape[2] // 2), f32),
-            *[pltpu.VMEM(a.shape, a.dtype) for a in streamed],
-            dma((3,)),
-            dma((units,)),
-            dma((units // STEP,)),
         ],
-        compiler_params=params(36),
+        compiler_params=params(),
         name="experts",
     )(
-        *in_hbm(*streamed),
+        router,
+        ids,
+        gain,
         out_weight,
+        down_weight,
+        early_units,
+        late_units,
         picked,
         *blocks,
     )
-    parts = lax.all_to_all(moe, "tp", 0, 0, tiled=True)
-    layer_out, accepted = pl.pallas_call(
+    sums = pl.pallas_call(
+        fold_kernel,
+        out_shape=tuple(
+            jax.ShapeDtypeStruct((tok_dev, model + 2 * WIDE), f32 if k == 0 else bf16)
+            for k in range(pairs)
+        ),
+        in_specs=spaces("vvv"),
+        out_specs=tuple(spaces("v" * pairs)),
+        compiler_params=params(),
+        name="fold",
+    )(mine, swap(sent_sums, 1), hidden)
+    sums = [sums[0]] + [swap(sums[k], 2 * k) for k in range(1, pairs)]
+    return pl.pallas_call(
         finish_kernel,
         out_shape=(
+            jax.ShapeDtypeStruct(queries.shape, bf16),
             jax.ShapeDtypeStruct(residual.shape, bf16),
             jax.ShapeDtypeStruct(new_kv.shape, bf16),
         ),
-        in_specs=spaces("vv"),
-        out_specs=tuple(spaces("vv")),
+        in_specs=spaces("v" * (1 + pairs)),
+        out_specs=tuple(spaces("vvv")),
         compiler_params=params(),
         name="finish",
-    )(parts, hidden)
-    return attn_own, layer_out, accepted
+    )(attn_own, *sums)
 
 
 def per_device(queries, new_kv, residual, placement, *rest):
     tok_dev = queries.shape[0]
     one_head_each = lax.axis_size("tp") == KV_HEADS
-    whole_tiles = tok_dev % 16 == 0 and tok_dev * KV_HEADS == 2 * DRAFT
+    whole_tiles = tok_dev % 16 == 0 and placement.shape[0] == 2 and tok_dev * KV_HEADS == 2 * DRAFT
     if one_head_each and whole_tiles and rest[1].shape[1] == 1:
         return per_device_packed(queries, new_kv, residual, placement, *rest)
     return per_device_plain(queries, new_kv, residual, placement, *rest)

time: 83.9 us -> 72.2 us (0.86)
  blocking collectives: 47.8 us -> 19.2 us
  starting transfers between devices: 8.7 us -> 20.5 us
  Pallas kernels: 17.6 us -> 20.7 us
  waiting for transfers between devices: 7.95 us -> 10.7 us
  other arithmetic: 0.85 us -> 0 us
    all_to_all x1 -> x0, blocking collectives: 15.9 us -> none  [per_device_packed(): parts = lax.all_to_all(moe, 'tp', 0, 0, tiled=True)]
    ppermute x7 -> x15, starting transfers between devices: 8.7 us -> 20.5 us  [swap(): return lax.ppermute(rows, 'tp', [(i, i ^ mask) for i in range(count)])]
    all_to_all x1, blocking collectives: 23.2 us -> 11.8 us  [per_device_packed(): packed = lax.all_to_all(packed, 'tp', 0, 0, tiled=True)]
    pallas_call x3 -> x8, Pallas kernels: 14.6 us -> 19.2 us  [the longest x2 7.83 us: fetch(): pl.pallas_call(functools.partial(fetch_kernel, tuple(((first, rows) for _...]
    ppermute x7 -> x15, waiting for transfers between devices: 7.95 us -> 10.7 us  [swap(): return lax.ppermute(rows, 'tp', [(i, i ^ mask) for i in range(count)])]
    pallas_call x1, Pallas kernels: 3.06 us -> 1.53 us  [per_device_packed(): pl.pallas_call(attend_kernel, out_shape=(jax.ShapeDtypeStruct((group_rows...]
    all_gather x1, blocking collectives: 8.65 us -> 7.4 us  [per_device_packed(): pulled = lax.all_gather(joined, 'req', axis=0)]
    concatenate x1 -> x0, other arithmetic: 0.85 us -> none  [per_device_packed(): jnp.concatenate([queries, new_kv, residual], axis=1)]
  transfers between devices with their start and end apart: 7 -> 15, of which waited for: 4 -> 5; matrix products, arithmetic and copies ran while one was open for 0% -> 0% of each run, Pallas kernels for 0% -> 15%
where the time goes in v3:
time: 72.2 us; the launch traced here: 71.9 us
  Pallas kernels  20.7 us (29%)
  starting transfers between devices  20.5 us (28%)
  blocking collectives  19.2 us (27%)
  waiting for transfers between devices  10.7 us (15%)
  between operations  0.77 us (1%)
    ppermute x15, starting transfers between devices, swap(): return lax.ppermute(rows, 'tp', [(i, i ^ mask) for i in range(count)])  20.5 us
    all_to_all x1, blocking collectives, per_device_packed(): packed = lax.all_to_all(packed, 'tp', 0, 0, tiled=True)  11.8 us
    ppermute x15, waiting for transfers between devices, swap(): return lax.ppermute(rows, 'tp', [(i, i ^ mask) for i in range(count)])  10.7 us
    pallas_call x2, Pallas kernels, fetch(): pl.pallas_call(functools.partial(fetch_kernel, tuple(((first, rows) for _...  7.83 us
    all_gather x1, blocking collectives, per_device_packed(): pulled = lax.all_gather(joined, 'req', axis=0)  7.4 us
    pallas_call x1, Pallas kernels, per_device_packed(): pl.pallas_call(expert_kernel, out_shape=(jax.ShapeDtypeStruct((pairs, tok...  5.67 us
    pallas_call x1, Pallas kernels, per_device_packed(): pl.pallas_call(tree_kernel, out_shape=(pltpu.VMEM(down_weight.shape, bf16...  3.24 us
    pallas_call x1, Pallas kernels, per_device_packed(): pl.pallas_call(attend_kernel, out_shape=(jax.ShapeDtypeStruct((group_rows...  1.53 us
  transfers between devices with their start and end apart: 15, of which 5 were waited for; matrix products, arithmetic and copies ran while one was open for 0% of the time, Pallas kernels for 15%

profile of v3, /device:TPU:0, one launch (start us, length us, event | category | flops | bytes accessed | tf_op | source)
XLA Modules:
  0.0 71.9 jit_solution(16184864740443373770)
XLA Ops:
  0.6 1.4 %split.1 = (bf16[2,256,128]{2,1,0:T(8,128)(2,1)S(1)}, bf16[2,256,128]{2,1,0:T(8,128)(2,1)S(1)}, bf16[2,256,128]{2,1,0:T(8,128)(2,1)S(1)}, bf16[2,256,128]{2,1,0:...) custom-call(s32[2]{0:T(128)} %bitcast.10, ...), custom_call_target="tpu_custom_call" | custom-call | bytes 4194304 | tf_op jit(solution)/shard_map/split/pallas_call | solution.py:688
  2.1 3.1 %collective-permute-start = (bf16[2,256,128]{2,1,0:T(8,128)(2,1)S(1)}, bf16[2,256,128]{2,1,0:T(8,128)(2,1)S(1)}, u32[]{:S(2)}, u32[]{:S(2)}) collective-permute-start(bf16[2,256,128]{2,1,0:T(8,128)(2,1)S(1)} %get-tuple-element.46), channel_id=1, source_target_pairs={{0,2},{1,3},{2,0},{3,1},{4,6},{5,7},{6,4},{7,5},{8,10},{9,11},{10,... | collective-permute-start | bytes 393224 | tf_op jit(solution)/shard_map/ppermute | solution.py:621
  5.2 2.6 %collective-permute-start.1 = (bf16[2,256,128]{2,1,0:T(8,128)(2,1)S(1)}, bf16[2,256,128]{2,1,0:T(8,128)(2,1)S(1)}, u32[]{:S(2)}, u32[]{:S(2)}) collective-permute-start(bf16[2,256,128]{2,1,0:T(8,128)(2,1)S(1)} %get-tuple-element.47), channel_id=1, source_target_pairs={{0,4},{1,5},{2,6},{3,7},{4,0},{5,1},{6,2},{7,3},{8,12},{9,13},{10,... | collective-permute-start | bytes 393224 | tf_op jit(solution)/shard_map/ppermute | solution.py:621
  7.8 7.4 %all-gather = bf16[64,4096]{1,0:T(8,128)(2,1)S(1)} all-gather(bf16[16,4096]{1,0:T(8,128)(2,1)S(1)} %get-tuple-element.40), channel_id=2, replica_groups=mesh['req'=4,'tp'=8] {'req'}, dimensions={0}, use_global_device_ids=true | all-gather | bytes 655360 | tf_op jit(solution)/shard_map/all_gather | solution.py:713
  15.2 3.2 %tree.1 = (bf16[20,128,1536]{2,1,0:T(8,128)(2,1)S(1)}, f32[128,128]{1,0:T(8,128)S(1)}, bf16[2,64,64]{2,1,0:T(8,128)(2,1)S(1)}) custom-call(bf16[4,16,4096]{2,1,0:T(8,128)(2,1)S(1)} %bitcast.5, bf16[20,128,1536]{2,1,0:T(8,128)(2,1)} %down_hbm.1, f32[8,128]{1,0:T(8,128)S(1)} %get-tuple-element.39.table_ref, s32[2,64]{1,0:T(2,128)S(1)} %get-tuple-element.41.parents_ref), custom_call_target="tpu_custom_call" | custom-call | bytes 8388608 | tf_op jit(solution)/shard_map/tree/pallas_call | solution.py:715
  18.7 1.6 %collective-permute-start.3 = (bf16[4,256,128]{2,1,0:T(8,128)(2,1)S(1)}, bf16[4,256,128]{2,1,0:T(8,128)(2,1)S(1)}, u32[]{:S(2)}, u32[]{:S(2)}) collective-permute-start(bf16[4,256,128]{2,1,0:T(8,128)(2,1)S(1)} %get-tuple-element.51), channel_id=1, source_target_pairs={{0,1},{1,0},{2,3},{3,2},{4,5},{5,4},{6,7},{7,6},{8,9},{9,8},{10,11... | collective-permute-start | bytes 786440 | tf_op jit(solution)/shard_map/ppermute | solution.py:621
  20.2 11.8 %all_to_all.5.got_ref = bf16[8,48,128]{2,1,0:T(8,128)(2,1)S(1)} all-to-all(bf16[8,48,128]{2,1,0:T(8,128)(2,1)S(1)} %get-tuple-element.49), channel_id=1, replica_groups=mesh['req'=4,'tp'=8] {'tp'}, dimensions={0} | all-to-all | bytes 196608 | tf_op jit(solution)/shard_map/all_to_all | solution.py:743
  32.0 1.5 %attend.1 = (bf16[384,128]{1,0:T(8,128)(2,1)S(1)}, bf16[8,16,128]{2,1,0:T(8,128)(2,1)S(1)}) custom-call(f32[8,128]{1,0:T(8,128)S(1)} %get-tuple-element.39.table_ref, f32[128,128]{1,0:T(8,128)S(1)} %get-tuple-element.42.reach_ref, bf16[2,64,64]{2,1,0:T(8,128)(2,1)S(1)} %get-tuple-element.43.chosen_ref, bf16[8,48,128]{2,1,0:T(8,128)(2,1)S(1)} %all_to_all.5.got_ref, ...), custom_call_target="tpu_custom_call" | custom-call | bytes 8388608 | tf_op jit(solution)/shard_map/attend/pallas_call | solution.py:744
  34.2 0.9 %collective-permute-start.5 = (bf16[384,128]{1,0:T(8,128)(2,1)S(1)}, bf16[384,128]{1,0:T(8,128)(2,1)S(1)}, u32[]{:S(2)}, u32[]{:S(2)}) collective-permute-start(bf16[384,128]{1,0:T(8,128)(2,1)S(1)} %get-tuple-element.52.after_ref.refs_0_), channel_id=1, source_target_pairs={{0,4},{1,5},{2,6},{3,7},{4,0},{5,1},{6,2},{7,3},{8,12},{9,13},{10,... | collective-permute-start | bytes 294920 | tf_op jit(solution)/shard_map/ppermute | solution.py:621
  35.1 2.9 %collective-permute-start.4 = (bf16[384,128]{1,0:T(8,128)(2,1)S(1)}, bf16[384,128]{1,0:T(8,128)(2,1)S(1)}, u32[]{:S(2)}, u32[]{:S(2)}) collective-permute-start(bf16[384,128]{1,0:T(8,128)(2,1)S(1)} %get-tuple-element.52.after_ref.refs_0_), channel_id=1, source_target_pairs={{0,2},{1,3},{2,0},{3,1},{4,6},{5,7},{6,4},{7,5},{8,10},{9,11},{10,... | collective-permute-start | bytes 294920 | tf_op jit(solution)/shard_map/ppermute | solution.py:621
  38.3 4.6 %fetch_early.1 = (bf16[10,1536,256]{2,1,0:T(8,128)(2,1)S(1)}, bf16[1536,1536]{1,0:T(8,128)(2,1)S(1)}) custom-call(bf16[384,128]{1,0:T(8,128)(2,1)S(1)} %get-tuple-element.52.after_ref.refs_0_, bf16[20,1536,256]{2,1,0:T(8,128)(2,1)} %refs_0_.3, bf16[1536,1536]{1,0:T(8,128)(2,1)} %refs_1_.3), custom_call_target="tpu_custom_call" | custom-call | bytes 12582912 | tf_op jit(solution)/shard_map/fetch_early/pallas_call | solution.py:632
  42.9 0.7 %collective-permute-done.5.refs_4_ = bf16[384,128]{1,0:T(8,128)(2,1)S(1)} collective-permute-done((bf16[384,128]{1,0:T(8,128)(2,1)S(1)}, bf16[384,128]{1,0:T(8,128)(2,1)S(1)}, u32[]{:S(2)}, u32[]{:S(2)}) %collective-permute-start.5) | collective-permute-done | bytes 98336 | tf_op jit(solution)/shard_map/ppermute | solution.py:621
  43.7 1.1 %collective-permute-start.8 = (bf16[384,128]{1,0:T(8,128)(2,1)S(1)}, bf16[384,128]{1,0:T(8,128)(2,1)S(1)}, u32[]{:S(2)}, u32[]{:S(2)}) collective-permute-start(bf16[384,128]{1,0:T(8,128)(2,1)S(1)} %collective-permute-done.4.refs_2_), channel_id=1, source_target_pairs={{0,1},{1,0},{2,3},{3,2},{4,5},{5,4},{6,7},{7,6},{8,9},{9,8},{10,11... | collective-permute-start | bytes 294920 | tf_op jit(solution)/shard_map/ppermute | solution.py:621
  44.7 1.0 %collective-permute-start.9 = (bf16[384,128]{1,0:T(8,128)(2,1)S(1)}, bf16[384,128]{1,0:T(8,128)(2,1)S(1)}, u32[]{:S(2)}, u32[]{:S(2)}) collective-permute-start(bf16[384,128]{1,0:T(8,128)(2,1)S(1)} %collective-permute-done.5.refs_4_), channel_id=1, source_target_pairs={{0,1},{1,0},{2,3},{3,2},{4,5},{5,4},{6,7},{7,6},{8,9},{9,8},{10,11... | collective-permute-start | bytes 294920 | tf_op jit(solution)/shard_map/ppermute | solution.py:621
  45.7 1.1 %collective-permute-start.10 = (bf16[384,128]{1,0:T(8,128)(2,1)S(1)}, bf16[384,128]{1,0:T(8,128)(2,1)S(1)}, u32[]{:S(2)}, u32[]{:S(2)}) collective-permute-start(bf16[384,128]{1,0:T(8,128)(2,1)S(1)} %collective-permute-done.6.refs_6_), channel_id=1, source_target_pairs={{0,1},{1,0},{2,3},{3,2},{4,5},{5,4},{6,7},{7,6},{8,9},{9,8},{10,11... | collective-permute-start | bytes 294920 | tf_op jit(solution)/shard_map/ppermute | solution.py:621
  46.8 3.2 %fetch_late.1.late_ref = bf16[10,1536,256]{2,1,0:T(8,128)(2,1)S(1)} custom-call(bf16[384,128]{1,0:T(8,128)(2,1)S(1)} %get-tuple-element.52.after_ref.refs_0_, bf16[20,1536,256]{2,1,0:T(8,128)(2,1)} %refs_0_.3), custom_call_target="tpu_custom_call" | custom-call | bytes 7340032 | tf_op jit(solution)/shard_map/fetch_late/pallas_call | solution.py:632
  50.0 1.0 %collective-permute-done.10.refs_7_ = bf16[384,128]{1,0:T(8,128)(2,1)S(1)} collective-permute-done((bf16[384,128]{1,0:T(8,128)(2,1)S(1)}, bf16[384,128]{1,0:T(8,128)(2,1)S(1)}, u32[]{:S(2)}, u32[]{:S(2)}) %collective-permute-start.10) | collective-permute-done | bytes 98336 | tf_op jit(solution)/shard_map/ppermute | solution.py:621
  51.1 5.7 %experts.1 = (f32[4,16,1664]{2,1,0:T(8,128)S(1)}, bf16[4,16,1664]{2,1,0:T(8,128)(2,1)S(1)}, f32[16,1536]{1,0:T(8,128)S(1)}, bf16[16,1536]{1,0:T(8,128)(2,1)S(1)}) custom-call(bf16[40,1536]{1,0:T(8,128)(2,1)S(1)} %get-tuple-element.36.router_ref, s32[8,128]{1,0:T(8,128)S(1)} %get-tuple-element.37.ids_ref, f32[12,128]{1,0:T(8,128)S(1)} %get-tuple-element.38.gain_ref, ...), custom_call_target="tpu_custom_call" | custom-call | tf_op jit(solution)/shard_map/experts/pallas_call | solution.py:763
  56.7 1.0 %collective-permute-start.11 = (bf16[4,16,1664]{2,1,0:T(8,128)(2,1)S(1)}, bf16[4,16,1664]{2,1,0:T(8,128)(2,1)S(1)}, u32[]{:S(2)}, u32[]{:S(2)}) collective-permute-start(bf16[4,16,1664]{2,1,0:T(8,128)(2,1)S(1)} %get-tuple-element.63), channel_id=1, source_target_pairs={{0,1},{1,0},{2,3},{3,2},{4,5},{5,4},{6,7},{7,6},{8,9},{9,8},{10,11... | collective-permute-start | bytes 638984 | tf_op jit(solution)/shard_map/ppermute | solution.py:621
  57.8 4.9 %collective-permute-done.11.got_ref = bf16[4,16,1664]{2,1,0:T(8,128)(2,1)S(1)} collective-permute-done((bf16[4,16,1664]{2,1,0:T(8,128)(2,1)S(1)}, bf16[4,16,1664]{2,1,0:T(8,128)(2,1)S(1)}, u32[]{:S(2)}, u32[]{:S(2)}) %collective-permute-start.11) | collective-permute-done | bytes 213024 | tf_op jit(solution)/shard_map/ppermute | solution.py:621
  62.8 2.5 %collective-permute-start.13 = (bf16[16,1792]{1,0:T(8,128)(2,1)S(1)}, bf16[16,1792]{1,0:T(8,128)(2,1)S(1)}, u32[]{:S(2)}, u32[]{:S(2)}) collective-permute-start(bf16[16,1792]{1,0:T(8,128)(2,1)S(1)} %get-tuple-element.67), channel_id=1, source_target_pairs={{0,4},{1,5},{2,6},{3,7},{4,0},{5,1},{6,2},{7,3},{8,12},{9,13},{10,... | collective-permute-start | bytes 172040 | tf_op jit(solution)/shard_map/ppermute | solution.py:621
  65.3 1.9 %collective-permute-start.14 = (bf16[16,1792]{1,0:T(8,128)(2,1)S(1)}, bf16[16,1792]{1,0:T(8,128)(2,1)S(1)}, u32[]{:S(2)}, u32[]{:S(2)}) collective-permute-start(bf16[16,1792]{1,0:T(8,128)(2,1)S(1)} %get-tuple-element.68), channel_id=1, source_target_pairs={{0,6},{1,7},{2,4},{3,5},{4,2},{5,3},{6,0},{7,1},{8,14},{9,15},{10,... | collective-permute-start | bytes 172040 | tf_op jit(solution)/shard_map/ppermute | solution.py:621
  67.2 1.0 %collective-permute-done.12.refs_1_ = bf16[16,1792]{1,0:T(8,128)(2,1)S(1)} collective-permute-done((bf16[16,1792]{1,0:T(8,128)(2,1)S(1)}, bf16[16,1792]{1,0:T(8,128)(2,1)S(1)}, u32[]{:S(2)}, u32[]{:S(2)}) %collective-permute-start.12) | collective-permute-done | bytes 57376 | tf_op jit(solution)/shard_map/ppermute | solution.py:621
  68.2 3.0 %collective-permute-done.14.refs_3_ = bf16[16,1792]{1,0:T(8,128)(2,1)S(1)} collective-permute-done((bf16[16,1792]{1,0:T(8,128)(2,1)S(1)}, bf16[16,1792]{1,0:T(8,128)(2,1)S(1)}, u32[]{:S(2)}, u32[]{:S(2)}) %collective-permute-start.14) | collective-permute-done | bytes 57376 | tf_op jit(solution)/shard_map/ppermute | solution.py:621
  (17 shorter events, 2.0 us)
Async XLA Ops:
  2.1 16.3 %collective-permute-start = (bf16[2,256,128]{2,1,0:T(8,128)(2,1)S(1)}, bf16[2,256,128]{2,1,0:T(8,128)(2,1)S(1)}, u32[]{:S(2)}, u32[]{:S(2)}) collective-permute-start(bf16[2,256,128]{2,1,0:T(8,128)(2,1)S(1)} %get-tuple-element.46), channel_id=1, source_target_pairs={{0,2},{1,3},{2,0},{3,1},{4,6},{5,7},{6,4},{7,5},{8,10},{9,11},{10,... | collective-permute-start | bytes 393224 | tf_op jit(solution)/shard_map/ppermute | solution.py:621
  5.2 13.3 %collective-permute-start.1 = (bf16[2,256,128]{2,1,0:T(8,128)(2,1)S(1)}, bf16[2,256,128]{2,1,0:T(8,128)(2,1)S(1)}, u32[]{:S(2)}, u32[]{:S(2)}) collective-permute-start(bf16[2,256,128]{2,1,0:T(8,128)(2,1)S(1)} %get-tuple-element.47), channel_id=1, source_target_pairs={{0,4},{1,5},{2,6},{3,7},{4,0},{5,1},{6,2},{7,3},{8,12},{9,13},{10,... | collective-permute-start | bytes 393224 | tf_op jit(solution)/shard_map/ppermute | solution.py:621
  7.8 10.7 %collective-permute-start.2 = (bf16[2,256,128]{2,1,0:T(8,128)(2,1)S(1)}, bf16[2,256,128]{2,1,0:T(8,128)(2,1)S(1)}, u32[]{:S(2)}, u32[]{:S(2)}) collective-permute-start(bf16[2,256,128]{2,1,0:T(8,128)(2,1)S(1)} %get-tuple-element.48), channel_id=1, source_target_pairs={{0,6},{1,7},{2,4},{3,5},{4,2},{5,3},{6,0},{7,1},{8,14},{9,15},{10,... | collective-permute-start | bytes 393224 | tf_op jit(solution)/shard_map/ppermute | solution.py:621
  18.7 13.3 %collective-permute-start.3 = (bf16[4,256,128]{2,1,0:T(8,128)(2,1)S(1)}, bf16[4,256,128]{2,1,0:T(8,128)(2,1)S(1)}, u32[]{:S(2)}, u32[]{:S(2)}) collective-permute-start(bf16[4,256,128]{2,1,0:T(8,128)(2,1)S(1)} %get-tuple-element.51), channel_id=1, source_target_pairs={{0,1},{1,0},{2,3},{3,2},{4,5},{5,4},{6,7},{7,6},{8,9},{9,8},{10,11... | collective-permute-start | bytes 786440 | tf_op jit(solution)/shard_map/ppermute | solution.py:621
  33.6 9.4 %collective-permute-start.6 = (bf16[384,128]{1,0:T(8,128)(2,1)S(1)}, bf16[384,128]{1,0:T(8,128)(2,1)S(1)}, u32[]{:S(2)}, u32[]{:S(2)}) collective-permute-start(bf16[384,128]{1,0:T(8,128)(2,1)S(1)} %get-tuple-element.52.after_ref.refs_0_), channel_id=1, source_target_pairs={{0,6},{1,7},{2,4},{3,5},{4,2},{5,3},{6,0},{7,1},{8,14},{9,15},{10,... | collective-permute-start | bytes 294920 | tf_op jit(solution)/shard_map/ppermute | solution.py:621
  34.2 9.5 %collective-permute-start.5 = (bf16[384,128]{1,0:T(8,128)(2,1)S(1)}, bf16[384,128]{1,0:T(8,128)(2,1)S(1)}, u32[]{:S(2)}, u32[]{:S(2)}) collective-permute-start(bf16[384,128]{1,0:T(8,128)(2,1)S(1)} %get-tuple-element.52.after_ref.refs_0_), channel_id=1, source_target_pairs={{0,4},{1,5},{2,6},{3,7},{4,0},{5,1},{6,2},{7,3},{8,12},{9,13},{10,... | collective-permute-start | bytes 294920 | tf_op jit(solution)/shard_map/ppermute | solution.py:621
  35.1 8.5 %collective-permute-start.4 = (bf16[384,128]{1,0:T(8,128)(2,1)S(1)}, bf16[384,128]{1,0:T(8,128)(2,1)S(1)}, u32[]{:S(2)}, u32[]{:S(2)}) collective-permute-start(bf16[384,128]{1,0:T(8,128)(2,1)S(1)} %get-tuple-element.52.after_ref.refs_0_), channel_id=1, source_target_pairs={{0,2},{1,3},{2,0},{3,1},{4,6},{5,7},{6,4},{7,5},{8,10},{9,11},{10,... | collective-permute-start | bytes 294920 | tf_op jit(solution)/shard_map/ppermute | solution.py:621
  38.0 12.0 %collective-permute-start.7 = (bf16[384,128]{1,0:T(8,128)(2,1)S(1)}, bf16[384,128]{1,0:T(8,128)(2,1)S(1)}, u32[]{:S(2)}, u32[]{:S(2)}) collective-permute-start(bf16[384,128]{1,0:T(8,128)(2,1)S(1)} %get-tuple-element.52.after_ref.refs_0_), channel_id=1, source_target_pairs={{0,1},{1,0},{2,3},{3,2},{4,5},{5,4},{6,7},{7,6},{8,9},{9,8},{10,11... | collective-permute-start | bytes 294920 | tf_op jit(solution)/shard_map/ppermute | solution.py:621
  43.7 6.4 %collective-permute-start.8 = (bf16[384,128]{1,0:T(8,128)(2,1)S(1)}, bf16[384,128]{1,0:T(8,128)(2,1)S(1)}, u32[]{:S(2)}, u32[]{:S(2)}) collective-permute-start(bf16[384,128]{1,0:T(8,128)(2,1)S(1)} %collective-permute-done.4.refs_2_), channel_id=1, source_target_pairs={{0,1},{1,0},{2,3},{3,2},{4,5},{5,4},{6,7},{7,6},{8,9},{9,8},{10,11... | collective-permute-start | bytes 294920 | tf_op jit(solution)/shard_map/ppermute | solution.py:621
  44.7 5.3 %collective-permute-start.9 = (bf16[384,128]{1,0:T(8,128)(2,1)S(1)}, bf16[384,128]{1,0:T(8,128)(2,1)S(1)}, u32[]{:S(2)}, u32[]{:S(2)}) collective-permute-start(bf16[384,128]{1,0:T(8,128)(2,1)S(1)} %collective-permute-done.5.refs_4_), channel_id=1, source_target_pairs={{0,1},{1,0},{2,3},{3,2},{4,5},{5,4},{6,7},{7,6},{8,9},{9,8},{10,11... | collective-permute-start | bytes 294920 | tf_op jit(solution)/shard_map/ppermute | solution.py:621
  45.7 5.4 %collective-permute-start.10 = (bf16[384,128]{1,0:T(8,128)(2,1)S(1)}, bf16[384,128]{1,0:T(8,128)(2,1)S(1)}, u32[]{:S(2)}, u32[]{:S(2)}) collective-permute-start(bf16[384,128]{1,0:T(8,128)(2,1)S(1)} %collective-permute-done.6.refs_6_), channel_id=1, source_target_pairs={{0,1},{1,0},{2,3},{3,2},{4,5},{5,4},{6,7},{7,6},{8,9},{9,8},{10,11... | collective-permute-start | bytes 294920 | tf_op jit(solution)/shard_map/ppermute | solution.py:621
  56.7 5.9 %collective-permute-start.11 = (bf16[4,16,1664]{2,1,0:T(8,128)(2,1)S(1)}, bf16[4,16,1664]{2,1,0:T(8,128)(2,1)S(1)}, u32[]{:S(2)}, u32[]{:S(2)}) collective-permute-start(bf16[4,16,1664]{2,1,0:T(8,128)(2,1)S(1)} %get-tuple-element.63), channel_id=1, source_target_pairs={{0,1},{1,0},{2,3},{3,2},{4,5},{5,4},{6,7},{7,6},{8,9},{9,8},{10,11... | collective-permute-start | bytes 638984 | tf_op jit(solution)/shard_map/ppermute | solution.py:621
  62.7 5.5 %collective-permute-start.12 = (bf16[16,1792]{1,0:T(8,128)(2,1)S(1)}, bf16[16,1792]{1,0:T(8,128)(2,1)S(1)}, u32[]{:S(2)}, u32[]{:S(2)}) collective-permute-start(bf16[16,1792]{1,0:T(8,128)(2,1)S(1)} %get-tuple-element.66), channel_id=1, source_target_pairs={{0,2},{1,3},{2,0},{3,1},{4,6},{5,7},{6,4},{7,5},{8,10},{9,11},{10,... | collective-permute-start | bytes 172040 | tf_op jit(solution)/shard_map/ppermute | solution.py:621
  62.8 5.4 %collective-permute-start.13 = (bf16[16,1792]{1,0:T(8,128)(2,1)S(1)}, bf16[16,1792]{1,0:T(8,128)(2,1)S(1)}, u32[]{:S(2)}, u32[]{:S(2)}) collective-permute-start(bf16[16,1792]{1,0:T(8,128)(2,1)S(1)} %get-tuple-element.67), channel_id=1, source_target_pairs={{0,4},{1,5},{2,6},{3,7},{4,0},{5,1},{6,2},{7,3},{8,12},{9,13},{10,... | collective-permute-start | bytes 172040 | tf_op jit(solution)/shard_map/ppermute | solution.py:621
  65.3 6.0 %collective-permute-start.14 = (bf16[16,1792]{1,0:T(8,128)(2,1)S(1)}, bf16[16,1792]{1,0:T(8,128)(2,1)S(1)}, u32[]{:S(2)}, u32[]{:S(2)}) collective-permute-start(bf16[16,1792]{1,0:T(8,128)(2,1)S(1)} %get-tuple-element.68), channel_id=1, source_target_pairs={{0,6},{1,7},{2,4},{3,5},{4,2},{5,3},{6,0},{7,1},{8,14},{9,15},{10,... | collective-permute-start | bytes 172040 | tf_op jit(solution)/shard_map/ppermute | solution.py:621

commit v4 on v3

--- a/solution.py
+++ b/solution.py
@@ -16,6 +16,7 @@
 DRAFT = 64
 WIDE = 128
 STEP = 2
+ORDER = (1, 3, 2)
 
 
 neg_big = -1e30
@@ -299,7 +300,7 @@
             )
     pair = lax.div(lax.axis_index("tp"), 2)
     for k, part in enumerate(parts):
-        part[...] = split_ref[lax.bitwise_xor(pair, k)]
+        part[...] = split_ref[lax.bitwise_xor(pair, pairs - 1 - k)]
 
 
 def number(table_ref, row):
@@ -368,7 +369,8 @@
     copy.wait()
 
 
-def attend_kernel(table_ref, reach_ref, chosen_ref, got_ref, res_ref, turned_ref, *refs):
+def attend_kernel(units_ref, table_ref, reach_ref, chosen_ref, got_ref, res_ref, turned_ref, *refs):
+    del units_ref
     parts, (sent_ref, picked_ref) = refs[:-2], refs[-2:]
     slot_count = chosen_ref.shape[0]
     sources = got_ref.shape[0]
@@ -463,18 +465,20 @@
 
 
 def expert_kernel(
-    router_ref, ids_ref, gain_ref, out_weight_ref, down_ref, early_ref, late_ref, picked_ref, *refs
+    router_ref, ids_ref, gain_ref, down_ref, picked_ref, *refs
 ):
     blocks, refs = refs[:KV_HEADS], refs[KV_HEADS:]
-    mine_ref, sent_ref, hidden_ref, attn_ref, x_ref, hid_ref, normed_ref, share_ref = refs
+    weight_refs, unit_refs, refs = refs[: KV_HEADS // 2 - 1], refs[KV_HEADS // 2 - 1 : -7], refs[-7:]
+    far_ref, hid_ref, hidden_ref, attn_ref, x_ref, normed_ref, share_ref = refs
     f32, bf16 = jnp.float32, jnp.bfloat16
-    early = early_ref.shape[0]
-    units = early + late_ref.shape[0]
+    unit_weights = [(ref, k) for ref in unit_refs for k in range(ref.shape[0])]
+    units = len(unit_weights)
     tok_dev = hidden_ref.shape[0]
     sources = len(blocks)
     group_rows = sources * tok_dev
     half = group_rows // 2
-    width, model = out_weight_ref.shape
+    model = hidden_ref.shape[1]
+    width = sum(ref.shape[0] for ref in weight_refs)
     rank = lax.axis_index("tp")
     lane_low = lax.broadcasted_iota(jnp.int32, (half, WIDE), 1) < HEAD
     head_rows = width // sources
@@ -516,8 +520,10 @@
             ).astype(f32)
     own = pl.multiple_of(rank * tok_dev, tok_dev)
     attn_ref[...] = x_ref[pl.ds(own, tok_dev), :]
-    projected = jnp.dot(x_ref[...], out_weight_ref[...], preferred_element_type=f32)
-    hidden = hid_ref[...] + projected
+    hidden, at = hid_ref[...], 0
+    for ref in weight_refs:
+        hidden += jnp.dot(x_ref[:, at : at + ref.shape[0]], ref[...], preferred_element_type=f32)
+        at += ref.shape[0]
     hid_ref[...] = hidden
     gain = jnp.concatenate([gain_ref[c : c + 1, :] for c in range(model // WIDE)], axis=1)
     scale = lax.rsqrt(jnp.mean(hidden * hidden, axis=1, keepdims=True) + norm_eps)
@@ -535,7 +541,7 @@
         count = count + jnp.where(ids[:, k : k + 1] == expert_names, 1.0, 0.0)
     expo = jnp.where(count > 0.0, jnp.exp(logits), 0.0) * count
     routing = expo / jnp.sum(expo, axis=1, keepdims=True)
-    unit_width = early_ref.shape[2] // 2
+    unit_width = unit_refs[0].shape[2] // 2
     span = FF_E // unit_width
     each = span if units % span == 0 else 1
     for u in range(0, units, each):
@@ -544,8 +550,8 @@
         share_ref[u : u + each] = jnp.broadcast_to(share[None], (each, group_rows, unit_width))
 
     def one_unit(u):
-        weight = early_ref[u] if u < early else late_ref[u - early]
-        both = jnp.dot(normed_ref[...], weight, preferred_element_type=f32)
+        ref, k = unit_weights[u]
+        both = jnp.dot(normed_ref[...], ref[k], preferred_element_type=f32)
         gate, up = both[:, :unit_width], both[:, unit_width:]
         return (gate / (1.0 + jnp.exp(-gate)) * up * share_ref[u]).astype(bf16)
 
@@ -554,20 +560,34 @@
         down = down_ref[i * STEP : (i + 1) * STEP].reshape(STEP * unit_width, model)
         part = jnp.dot(act, down, preferred_element_type=f32)
         hid_ref[...] = part if i == 0 else hid_ref[...] + part
+    for k in range(far_ref.shape[0]):
+        copy_sums(sources // 4 + k, True, hid_ref, picked_ref, far_ref.at[k])
+
+
+def copy_sums(k, crossing, hid_ref, picked_ref, ref):
+    tok_dev, model = ref.shape[0], hid_ref.shape[1]
+    rank = lax.axis_index("tp")
     side = lax.rem(rank, 2)
-    for k in range(sources // 2):
-        pair = lax.bitwise_xor(lax.div(rank, 2), k)
-        for target, ref in ((2 * pair + side, mine_ref), (2 * pair + 1 - side, sent_ref)):
-            row = pl.multiple_of(target * tok_dev, tok_dev)
-            ref[k, :, :model] = hid_ref[pl.ds(row, tok_dev), :].astype(ref.dtype)
-            ref[k, :, model:] = picked_ref[target].astype(ref.dtype)
-
-
-def fold_kernel(mine_ref, got_ref, hidden_ref, kept_ref, *sent_refs):
+    pair = lax.bitwise_xor(lax.div(rank, 2), k)
+    target = 2 * pair + (1 - side if crossing else side)
+    row = pl.multiple_of(target * tok_dev, tok_dev)
+    ref[:, :model] = hid_ref[pl.ds(row, tok_dev), :].astype(ref.dtype)
+    ref[:, model:] = picked_ref[target].astype(ref.dtype)
+
+
+def near_kernel(hid_ref, picked_ref, mine_ref, near_ref):
+    for k in range(mine_ref.shape[0]):
+        copy_sums(k, False, hid_ref, picked_ref, mine_ref.at[k])
+    for k in range(near_ref.shape[0]):
+        copy_sums(k, True, hid_ref, picked_ref, near_ref.at[k])
+
+
+def fold_kernel(first, after_ref, mine_ref, got_ref, hidden_ref, *sent_refs):
+    del after_ref
     model = hidden_ref.shape[1]
     is_even = lax.rem(lax.axis_index("tp"), 2) == 0
-    for k, ref in enumerate((kept_ref,) + sent_refs):
-        mine, got = mine_ref[k], got_ref[k].astype(jnp.float32)
+    for k, ref in enumerate(sent_refs, first):
+        mine, got = mine_ref[k], got_ref[k - first].astype(jnp.float32)
         total = mine[:, :model] + got[:, :model]
         if k == 0:
             total = total + hidden_ref[...]
@@ -619,12 +639,6 @@
 def swap(rows, mask):
     count = lax.axis_size("tp")
     return lax.ppermute(rows, "tp", [(i, i ^ mask) for i in range(count)])
-
-
-def gather_blocks(block, early):
-    pairs = [swap(block, 2 * k) for k in range(1, lax.axis_size("tp") // 2)]
-    pairs, early = lax.optimization_barrier((pairs, early))
-    return [a for rows in [block] + pairs for a in (rows, swap(rows, 1))], early
 
 
 def fetch(name, after, *spans):
@@ -709,6 +723,7 @@
         cost_estimate=cost(4),
         name="split",
     )(*in_hbm(*loaded))
+    parts = parts[::-1]
     parts = [parts[0]] + [swap(parts[k], 2 * k) for k in range(1, pairs)]
     pulled = lax.all_gather(joined, "req", axis=0)
     nodes = slot_count * DRAFT
@@ -741,6 +756,7 @@
     )(down_weight, table, pulled, *parts)
     turned = swap(turned, 1)
     packed = lax.all_to_all(packed, "tp", 0, 0, tiled=True)
+    gate_up = pltpu.with_memory_space_constraint(gate_up, pltpu.VMEM)
     block, picked = pl.pallas_call(
         attend_kernel,
         out_shape=(
@@ -749,30 +765,35 @@
             ),
             sent(tok_dev),
         ),
-        in_specs=spaces("v" * (6 + pairs)),
+        in_specs=spaces("v" * (7 + pairs)),
         out_specs=tuple(spaces("vv")),
         compiler_params=params(),
         cost_estimate=cost(8),
         name="attend",
-    )(table, reach, chosen, packed, own_res, turned, *parts)
+    )(gate_up, table, reach, chosen, packed, own_res, turned, *parts)
     units = gate_up.shape[0]
-    early = units // (2 * STEP) * STEP
-    ready = fetch("early", block, (gate_up, 0, early), (out_weight, 0, out_weight.shape[0]))
-    blocks, (early_units, out_weight) = gather_blocks(block, ready)
-    (late_units,) = fetch("late", block, (gate_up, early, units - early))
-    mine, sent_sums, hidden, attn_own = pl.pallas_call(
+    reached = [swap(block, 2 * k) for k in range(1, pairs)]
+    weights, after = [], block
+    rows = out_weight.shape[0] // (pairs - 1)
+    for step, k in enumerate(ORDER):
+        (weight,) = fetch("dense", after, (out_weight, step * rows, rows))
+        reached[k - 1], weight = lax.optimization_barrier((reached[k - 1], weight))
+        after = reached[k - 1]
+        weights.append(weight)
+    blocks = [a for rows in [block] + reached for a in (rows, swap(rows, 1))]
+    unit_weights = (gate_up,)
+    far, sums, hidden, attn_own = pl.pallas_call(
         expert_kernel,
         out_shape=(
-            jax.ShapeDtypeStruct((pairs, tok_dev, model + WIDE), f32),
-            jax.ShapeDtypeStruct((pairs, tok_dev, model + WIDE), bf16),
+            jax.ShapeDtypeStruct((pairs // 2, tok_dev, model + WIDE), bf16),
+            jax.ShapeDtypeStruct((group_rows, model), f32),
             jax.ShapeDtypeStruct((tok_dev, model), f32),
             pltpu.VMEM(queries.shape, bf16),
         ),
-        in_specs=spaces("v" * (8 + tp_count)),
+        in_specs=spaces("v" * (5 + len(weights) + len(unit_weights) + tp_count)),
         out_specs=tuple(spaces("vvvv")),
         scratch_shapes=[
             pltpu.VMEM((group_rows, HEADS * HEAD), bf16),
-            pltpu.VMEM((group_rows, model), f32),
             pltpu.VMEM((group_rows, model), bf16),
             pltpu.VMEM((units, group_rows, gate_up.shape[2] // 2), f32),
         ],
@@ -782,25 +803,43 @@
         router,
         ids,
         gain,
-        out_weight,
         down_weight,
-        early_units,
-        late_units,
         picked,
         *blocks,
-    )
-    sums = pl.pallas_call(
-        fold_kernel,
+        *weights,
+        *unit_weights,
+    )
+    far = swap(far, 1)
+    mine, near = pl.pallas_call(
+        near_kernel,
+        out_shape=(
+            jax.ShapeDtypeStruct((pairs, tok_dev, model + WIDE), f32),
+            jax.ShapeDtypeStruct((pairs // 2, tok_dev, model + WIDE), bf16),
+        ),
+        in_specs=spaces("vv"),
+        out_specs=tuple(spaces("vv")),
+        compiler_params=params(),
+        cost_estimate=cost(4),
+        name="near",
+    )(sums, picked)
+    near = swap(near, 1)
+    fold = lambda first, after, got: pl.pallas_call(
+        functools.partial(fold_kernel, first),
         out_shape=tuple(
             jax.ShapeDtypeStruct((tok_dev, model + 2 * WIDE), f32 if k == 0 else bf16)
-            for k in range(pairs)
+            for k in range(first, first + pairs // 2)
         ),
-        in_specs=spaces("vvv"),
-        out_specs=tuple(spaces("v" * pairs)),
+        in_specs=spaces("avvv"),
+        out_specs=tuple(spaces("v" * (pairs // 2))),
         compiler_params=params(),
+        cost_estimate=cost(1),
         name="fold",
-    )(mine, swap(sent_sums, 1), hidden)
-    sums = [sums[0]] + [swap(sums[k], 2 * k) for k in range(1, pairs)]
+    )(after, mine, got, hidden)
+    sums = fold(pairs // 2, hidden, far)
+    folded = sums[0]
+    sums = [swap(a, 2 * k) for k, a in enumerate(sums, pairs // 2)]
+    close = fold(0, folded, near)
+    sums = [close[0]] + [swap(close[k], 2 * k) for k in range(1, pairs // 2)] + sums
     return pl.pallas_call(
         finish_kernel,
         out_shape=(

time: 72.2 us -> 68.9 us (0.954)
  Pallas kernels: 20.7 us -> 17.2 us
    pallas_call x2 -> x3, Pallas kernels: 7.83 us -> 4.25 us  [fetch(): pl.pallas_call(functools.partial(fetch_kernel, tuple(((first, rows) for _...]
    ppermute x15 -> x16, waiting for transfers between devices: 10.7 us -> 10.5 us  [swap(): return lax.ppermute(rows, 'tp', [(i, i ^ mask) for i in range(count)])]
    ppermute x15 -> x16, starting transfers between devices: 20.5 us -> 20.6 us  [swap(): return lax.ppermute(rows, 'tp', [(i, i ^ mask) for i in range(count)])]
    pallas_call x2 -> x4, Pallas kernels: 5.73 us -> 5.72 us  [the longest x1 5.62 us: per_device_packed(): pl.pallas_call(expert_kernel, out_shape=(jax.ShapeDtypeStruct((pairs // 2...]
  transfers between devices with their start and end apart: 15 -> 16, of which waited for: 5 -> 7; matrix products, arithmetic and copies ran while one was open for 0% -> 0% of each run, Pallas kernels for 15% -> 11%
where the time goes in v4:
time: 68.9 us; the launch traced here: 68.6 us
  starting transfers between devices  20.6 us (30%)
  blocking collectives  19.5 us (28%)
  Pallas kernels  17.2 us (25%)
  waiting for transfers between devices  10.5 us (15%)
  between operations  0.76 us (1%)
    ppermute x16, starting transfers between devices, swap(): return lax.ppermute(rows, 'tp', [(i, i ^ mask) for i in range(count)])  20.6 us
    all_to_all x1, blocking collectives, per_device_packed(): packed = lax.all_to_all(packed, 'tp', 0, 0, tiled=True)  12.1 us
    ppermute x16, waiting for transfers between devices, swap(): return lax.ppermute(rows, 'tp', [(i, i ^ mask) for i in range(count)])  10.5 us
    all_gather x1, blocking collectives, per_device_packed(): pulled = lax.all_gather(joined, 'req', axis=0)  7.4 us
    pallas_call x1, Pallas kernels, per_device_packed(): pl.pallas_call(expert_kernel, out_shape=(jax.ShapeDtypeStruct((pairs // 2...  5.62 us
    pallas_call x3, Pallas kernels, fetch(): pl.pallas_call(functools.partial(fetch_kernel, tuple(((first, rows) for _...  4.25 us
    pallas_call x1, Pallas kernels, per_device_packed(): pl.pallas_call(tree_kernel, out_shape=(pltpu.VMEM(down_weight.shape, bf16...  3.39 us
    pallas_call x1, Pallas kernels, per_device_packed(): pl.pallas_call(attend_kernel, out_shape=(jax.ShapeDtypeStruct((group_rows...  1.52 us
  transfers between devices with their start and end apart: 16, of which 7 were waited for; matrix products, arithmetic and copies ran while one was open for 0% of the time, Pallas kernels for 11%

profile of v4, /device:TPU:0, one launch (start us, length us, event | category | flops | bytes accessed | tf_op | source)
XLA Modules:
  0.0 68.6 jit_solution(6399048016168411159)
XLA Ops:
  0.6 1.4 %split.1 = (bf16[2,256,128]{2,1,0:T(8,128)(2,1)S(1)}, bf16[2,256,128]{2,1,0:T(8,128)(2,1)S(1)}, bf16[2,256,128]{2,1,0:T(8,128)(2,1)S(1)}, bf16[2,256,128]{2,1,0:...) custom-call(s32[2]{0:T(128)} %bitcast.10, ...), custom_call_target="tpu_custom_call" | custom-call | bytes 4194304 | tf_op jit(solution)/shard_map/split/pallas_call | solution.py:702
  2.1 3.1 %collective-permute-start = (bf16[2,256,128]{2,1,0:T(8,128)(2,1)S(1)}, bf16[2,256,128]{2,1,0:T(8,128)(2,1)S(1)}, u32[]{:S(2)}, u32[]{:S(2)}) collective-permute-start(bf16[2,256,128]{2,1,0:T(8,128)(2,1)S(1)} %get-tuple-element.47), channel_id=1, source_target_pairs={{0,2},{1,3},{2,0},{3,1},{4,6},{5,7},{6,4},{7,5},{8,10},{9,11},{10,... | collective-permute-start | bytes 393224 | tf_op jit(solution)/shard_map/ppermute | solution.py:641
  5.2 2.6 %collective-permute-start.1 = (bf16[2,256,128]{2,1,0:T(8,128)(2,1)S(1)}, bf16[2,256,128]{2,1,0:T(8,128)(2,1)S(1)}, u32[]{:S(2)}, u32[]{:S(2)}) collective-permute-start(bf16[2,256,128]{2,1,0:T(8,128)(2,1)S(1)} %get-tuple-element.48), channel_id=1, source_target_pairs={{0,4},{1,5},{2,6},{3,7},{4,0},{5,1},{6,2},{7,3},{8,12},{9,13},{10,... | collective-permute-start | bytes 393224 | tf_op jit(solution)/shard_map/ppermute | solution.py:641
  7.8 7.4 %all-gather = bf16[64,4096]{1,0:T(8,128)(2,1)S(1)} all-gather(bf16[16,4096]{1,0:T(8,128)(2,1)S(1)} %get-tuple-element.40), channel_id=2, replica_groups=mesh['req'=4,'tp'=8] {'req'}, dimensions={0}, use_global_device_ids=true | all-gather | bytes 655360 | tf_op jit(solution)/shard_map/all_gather | solution.py:728
  15.2 3.4 %tree.1 = (bf16[20,128,1536]{2,1,0:T(8,128)(2,1)S(1)}, f32[128,128]{1,0:T(8,128)S(1)}, bf16[2,64,64]{2,1,0:T(8,128)(2,1)S(1)}) custom-call(bf16[4,16,4096]{2,1,0:T(8,128)(2,1)S(1)} %bitcast.5, bf16[20,128,1536]{2,1,0:T(8,128)(2,1)} %down_hbm.1, f32[8,128]{1,0:T(8,128)S(1)} %get-tuple-element.41.table_ref, s32[2,64]{1,0:T(2,128)S(1)} %get-tuple-element.42.parents_ref), custom_call_target="tpu_custom_call" | custom-call | bytes 8388608 | tf_op jit(solution)/shard_map/tree/pallas_call | solution.py:730
  18.8 1.6 %collective-permute-start.3 = (bf16[4,256,128]{2,1,0:T(8,128)(2,1)S(1)}, bf16[4,256,128]{2,1,0:T(8,128)(2,1)S(1)}, u32[]{:S(2)}, u32[]{:S(2)}) collective-permute-start(bf16[4,256,128]{2,1,0:T(8,128)(2,1)S(1)} %get-tuple-element.52), channel_id=1, source_target_pairs={{0,1},{1,0},{2,3},{3,2},{4,5},{5,4},{6,7},{7,6},{8,9},{9,8},{10,11... | collective-permute-start | bytes 786440 | tf_op jit(solution)/shard_map/ppermute | solution.py:641
  20.4 12.1 %all_to_all.5.got_ref = bf16[8,48,128]{2,1,0:T(8,128)(2,1)S(1)} all-to-all(bf16[8,48,128]{2,1,0:T(8,128)(2,1)S(1)} %get-tuple-element.50), channel_id=1, replica_groups=mesh['req'=4,'tp'=8] {'tp'}, dimensions={0} | all-to-all | bytes 196608 | tf_op jit(solution)/shard_map/all_to_all | solution.py:758
  32.4 1.5 %attend.1 = (bf16[384,128]{1,0:T(8,128)(2,1)S(1)}, bf16[8,16,128]{2,1,0:T(8,128)(2,1)S(1)}) custom-call(bf16[20,1536,256]{2,1,0:T(8,128)(2,1)S(1)} %copy-done, f32[8,128]{1,0:T(8,128)S(1)} %get-tuple-element.41.table_ref, f32[128,128]{1,0:T(8,128)S(1)} %get-tuple-element.44.reach_ref, bf16[2,64,64]{2,1,0:T(8,128)(2,1)S(1)} %get-tuple-element.45.chosen_ref, ...), custom_call_target="tpu_custom_call" | custom-call | bytes 8388608 | tf_op jit(solution)/shard_map/attend/pallas_call | solution.py:760
  34.1 1.9 %collective-permute-start.8 = (bf16[384,128]{1,0:T(8,128)(2,1)S(1)}, bf16[384,128]{1,0:T(8,128)(2,1)S(1)}, u32[]{:S(2)}, u32[]{:S(2)}) collective-permute-start(bf16[384,128]{1,0:T(8,128)(2,1)S(1)} %get-tuple-element.54.after_ref.refs_0_), channel_id=1, source_target_pairs={{0,6},{1,7},{2,4},{3,5},{4,2},{5,3},{6,0},{7,1},{8,14},{9,15},{10,... | collective-permute-start | bytes 294920 | tf_op jit(solution)/shard_map/ppermute | solution.py:641
  35.9 1.6 %collective-permute-start.7 = (bf16[384,128]{1,0:T(8,128)(2,1)S(1)}, bf16[384,128]{1,0:T(8,128)(2,1)S(1)}, u32[]{:S(2)}, u32[]{:S(2)}) collective-permute-start(bf16[384,128]{1,0:T(8,128)(2,1)S(1)} %get-tuple-element.54.after_ref.refs_0_), channel_id=1, source_target_pairs={{0,4},{1,5},{2,6},{3,7},{4,0},{5,1},{6,2},{7,3},{8,12},{9,13},{10,... | collective-permute-start | bytes 294920 | tf_op jit(solution)/shard_map/ppermute | solution.py:641
  37.8 1.4 %fetch_dense.3.refs_8_ = bf16[512,1536]{1,0:T(8,128)(2,1)S(1)} custom-call(bf16[384,128]{1,0:T(8,128)(2,1)S(1)} %get-tuple-element.54.after_ref.refs_0_, bf16[1536,1536]{1,0:T(8,128)(2,1)} %refs_0_.5), custom_call_target="tpu_custom_call" | custom-call | bytes 1048576 | tf_op jit(solution)/shard_map/fetch_dense/pallas_call | solution.py:646
  41.1 1.4 %fetch_dense.4.refs_9_ = bf16[512,1536]{1,0:T(8,128)(2,1)S(1)} custom-call(bf16[384,128]{1,0:T(8,128)(2,1)S(1)} %collective-permute-done.5.after_ref.refs_2_, bf16[1536,1536]{1,0:T(8,128)(2,1)} %refs_0_.5), custom_call_target="tpu_custom_call" | custom-call | bytes 1048576 | tf_op jit(solution)/shard_map/fetch_dense/pallas_call | solution.py:646
  42.5 1.4 %collective-permute-start.10 = (bf16[384,128]{1,0:T(8,128)(2,1)S(1)}, bf16[384,128]{1,0:T(8,128)(2,1)S(1)}, u32[]{:S(2)}, u32[]{:S(2)}) collective-permute-start(bf16[384,128]{1,0:T(8,128)(2,1)S(1)} %collective-permute-done.8.after_ref.refs_6_), channel_id=1, source_target_pairs={{0,1},{1,0},{2,3},{3,2},{4,5},{5,4},{6,7},{7,6},{8,9},{9,8},{10,11... | collective-permute-start | bytes 294920 | tf_op jit(solution)/shard_map/ppermute | solution.py:641
  43.9 1.4 %fetch_dense.5.refs_10_ = bf16[512,1536]{1,0:T(8,128)(2,1)S(1)} custom-call(bf16[384,128]{1,0:T(8,128)(2,1)S(1)} %collective-permute-done.8.after_ref.refs_6_, bf16[1536,1536]{1,0:T(8,128)(2,1)} %refs_0_.5), custom_call_target="tpu_custom_call" | custom-call | bytes 1048576 | tf_op jit(solution)/shard_map/fetch_dense/pallas_call | solution.py:646
  46.1 1.8 %collective-permute-done.10.refs_7_ = bf16[384,128]{1,0:T(8,128)(2,1)S(1)} collective-permute-done((bf16[384,128]{1,0:T(8,128)(2,1)S(1)}, bf16[384,128]{1,0:T(8,128)(2,1)S(1)}, u32[]{:S(2)}, u32[]{:S(2)}) %collective-permute-start.10) | collective-permute-done | bytes 98336 | tf_op jit(solution)/shard_map/ppermute | solution.py:641
  47.9 2.1 %collective-permute-done.9.refs_5_ = bf16[384,128]{1,0:T(8,128)(2,1)S(1)} collective-permute-done((bf16[384,128]{1,0:T(8,128)(2,1)S(1)}, bf16[384,128]{1,0:T(8,128)(2,1)S(1)}, u32[]{:S(2)}, u32[]{:S(2)}) %collective-permute-start.9) | collective-permute-done | bytes 98336 | tf_op jit(solution)/shard_map/ppermute | solution.py:641
  50.0 5.6 %experts.1 = (bf16[2,16,1664]{2,1,0:T(8,128)(2,1)S(1)}, f32[128,1536]{1,0:T(8,128)S(1)}, f32[16,1536]{1,0:T(8,128)S(1)}, bf16[16,1536]{1,0:T(8,128)(2,1)S(1)}) custom-call(bf16[40,1536]{1,0:T(8,128)(2,1)S(1)} %get-tuple-element.37.router_ref, s32[8,128]{1,0:T(8,128)S(1)} %get-tuple-element.38.ids_ref, f32[12,128]{1,0:T(8,128)S(1)} %get-tuple-element.39.gain_ref, ...), custom_call_target="tpu_custom_call" | custom-call | tf_op jit(solution)/shard_map/experts/pallas_call | solution.py:785
  56.4 1.4 %collective-permute-start.12 = (bf16[2,16,1664]{2,1,0:T(8,128)(2,1)S(1)}, bf16[2,16,1664]{2,1,0:T(8,128)(2,1)S(1)}, u32[]{:S(2)}, u32[]{:S(2)}) collective-permute-start(bf16[2,16,1664]{2,1,0:T(8,128)(2,1)S(1)} %get-tuple-element.67), channel_id=1, source_target_pairs={{0,1},{1,0},{2,3},{3,2},{4,5},{5,4},{6,7},{7,6},{8,9},{9,8},{10,11... | collective-permute-start | bytes 319496 | tf_op jit(solution)/shard_map/ppermute | solution.py:641
  57.8 2.6 %collective-permute-done.11.got_ref = bf16[2,16,1664]{2,1,0:T(8,128)(2,1)S(1)} collective-permute-done((bf16[2,16,1664]{2,1,0:T(8,128)(2,1)S(1)}, bf16[2,16,1664]{2,1,0:T(8,128)(2,1)S(1)}, u32[]{:S(2)}, u32[]{:S(2)}) %collective-permute-start.11) | collective-permute-done | bytes 106528 | tf_op jit(solution)/shard_map/ppermute | solution.py:641
  60.4 1.1 %collective-permute-start.15 = (bf16[16,1792]{1,0:T(8,128)(2,1)S(1)}, bf16[16,1792]{1,0:T(8,128)(2,1)S(1)}, u32[]{:S(2)}, u32[]{:S(2)}) collective-permute-start(bf16[16,1792]{1,0:T(8,128)(2,1)S(1)} %get-tuple-element.70), channel_id=1, source_target_pairs={{0,6},{1,7},{2,4},{3,5},{4,2},{5,3},{6,0},{7,1},{8,14},{9,15},{10,... | collective-permute-start | bytes 172040 | tf_op jit(solution)/shard_map/ppermute | solution.py:641
  61.6 1.5 %collective-permute-start.14 = (bf16[16,1792]{1,0:T(8,128)(2,1)S(1)}, bf16[16,1792]{1,0:T(8,128)(2,1)S(1)}, u32[]{:S(2)}, u32[]{:S(2)}) collective-permute-start(bf16[16,1792]{1,0:T(8,128)(2,1)S(1)} %get-tuple-element.66.after_ref), channel_id=1, source_target_pairs={{0,4},{1,5},{2,6},{3,7},{4,0},{5,1},{6,2},{7,3},{8,12},{9,13},{10,... | collective-permute-start | bytes 172040 | tf_op jit(solution)/shard_map/ppermute | solution.py:641
  63.1 1.8 %collective-permute-start.13 = (bf16[16,1792]{1,0:T(8,128)(2,1)S(1)}, bf16[16,1792]{1,0:T(8,128)(2,1)S(1)}, u32[]{:S(2)}, u32[]{:S(2)}) collective-permute-start(bf16[16,1792]{1,0:T(8,128)(2,1)S(1)} %get-tuple-element.69), channel_id=1, source_target_pairs={{0,2},{1,3},{2,0},{3,1},{4,6},{5,7},{6,4},{7,5},{8,10},{9,11},{10,... | collective-permute-start | bytes 172040 | tf_op jit(solution)/shard_map/ppermute | solution.py:641
  65.0 1.5 %collective-permute-done.15.refs_3_ = bf16[16,1792]{1,0:T(8,128)(2,1)S(1)} collective-permute-done((bf16[16,1792]{1,0:T(8,128)(2,1)S(1)}, bf16[16,1792]{1,0:T(8,128)(2,1)S(1)}, u32[]{:S(2)}, u32[]{:S(2)}) %collective-permute-start.15) | collective-permute-done | bytes 57376 | tf_op jit(solution)/shard_map/ppermute | solution.py:641
  66.5 1.3 %collective-permute-done.14.refs_2_ = bf16[16,1792]{1,0:T(8,128)(2,1)S(1)} collective-permute-done((bf16[16,1792]{1,0:T(8,128)(2,1)S(1)}, bf16[16,1792]{1,0:T(8,128)(2,1)S(1)}, u32[]{:S(2)}, u32[]{:S(2)}) %collective-permute-start.14) | collective-permute-done | bytes 57376 | tf_op jit(solution)/shard_map/ppermute | solution.py:641
  (24 shorter events, 4.9 us)
Async XLA Ops:
  2.1 16.5 %collective-permute-start = (bf16[2,256,128]{2,1,0:T(8,128)(2,1)S(1)}, bf16[2,256,128]{2,1,0:T(8,128)(2,1)S(1)}, u32[]{:S(2)}, u32[]{:S(2)}) collective-permute-start(bf16[2,256,128]{2,1,0:T(8,128)(2,1)S(1)} %get-tuple-element.47), channel_id=1, source_target_pairs={{0,2},{1,3},{2,0},{3,1},{4,6},{5,7},{6,4},{7,5},{8,10},{9,11},{10,... | collective-permute-start | bytes 393224 | tf_op jit(solution)/shard_map/ppermute | solution.py:641
  5.2 13.4 %collective-permute-start.1 = (bf16[2,256,128]{2,1,0:T(8,128)(2,1)S(1)}, bf16[2,256,128]{2,1,0:T(8,128)(2,1)S(1)}, u32[]{:S(2)}, u32[]{:S(2)}) collective-permute-start(bf16[2,256,128]{2,1,0:T(8,128)(2,1)S(1)} %get-tuple-element.48), channel_id=1, source_target_pairs={{0,4},{1,5},{2,6},{3,7},{4,0},{5,1},{6,2},{7,3},{8,12},{9,13},{10,... | collective-permute-start | bytes 393224 | tf_op jit(solution)/shard_map/ppermute | solution.py:641
  7.8 10.8 %collective-permute-start.2 = (bf16[2,256,128]{2,1,0:T(8,128)(2,1)S(1)}, bf16[2,256,128]{2,1,0:T(8,128)(2,1)S(1)}, u32[]{:S(2)}, u32[]{:S(2)}) collective-permute-start(bf16[2,256,128]{2,1,0:T(8,128)(2,1)S(1)} %get-tuple-element.49), channel_id=1, source_target_pairs={{0,6},{1,7},{2,4},{3,5},{4,2},{5,3},{6,0},{7,1},{8,14},{9,15},{10,... | collective-permute-start | bytes 393224 | tf_op jit(solution)/shard_map/ppermute | solution.py:641
  15.2 17.3 %copy-start = (bf16[20,1536,256]{2,1,0:T(8,128)(2,1)S(1)}, bf16[20,1536,256]{2,1,0:T(8,128)(2,1)}, u32[]{:S(2)}) copy-start(bf16[20,1536,256]{2,1,0:T(8,128)(2,1)} %refs_11_.1) | copy-start | bytes 47185924
  18.8 13.6 %collective-permute-start.3 = (bf16[4,256,128]{2,1,0:T(8,128)(2,1)S(1)}, bf16[4,256,128]{2,1,0:T(8,128)(2,1)S(1)}, u32[]{:S(2)}, u32[]{:S(2)}) collective-permute-start(bf16[4,256,128]{2,1,0:T(8,128)(2,1)S(1)} %get-tuple-element.52), channel_id=1, source_target_pairs={{0,1},{1,0},{2,3},{3,2},{4,5},{5,4},{6,7},{7,6},{8,9},{9,8},{10,11... | collective-permute-start | bytes 786440 | tf_op jit(solution)/shard_map/ppermute | solution.py:641
  34.0 6.4 %collective-permute-start.5 = (bf16[384,128]{1,0:T(8,128)(2,1)S(1)}, bf16[384,128]{1,0:T(8,128)(2,1)S(1)}, u32[]{:S(2)}, u32[]{:S(2)}) collective-permute-start(bf16[384,128]{1,0:T(8,128)(2,1)S(1)} %get-tuple-element.54.after_ref.refs_0_), channel_id=1, source_target_pairs={{0,2},{1,3},{2,0},{3,1},{4,6},{5,7},{6,4},{7,5},{8,10},{9,11},{10,... | collective-permute-start | bytes 294920 | tf_op jit(solution)/shard_map/ppermute | solution.py:641
  34.1 8.4 %collective-permute-start.8 = (bf16[384,128]{1,0:T(8,128)(2,1)S(1)}, bf16[384,128]{1,0:T(8,128)(2,1)S(1)}, u32[]{:S(2)}, u32[]{:S(2)}) collective-permute-start(bf16[384,128]{1,0:T(8,128)(2,1)S(1)} %get-tuple-element.54.after_ref.refs_0_), channel_id=1, source_target_pairs={{0,6},{1,7},{2,4},{3,5},{4,2},{5,3},{6,0},{7,1},{8,14},{9,15},{10,... | collective-permute-start | bytes 294920 | tf_op jit(solution)/shard_map/ppermute | solution.py:641
  35.9 9.4 %collective-permute-start.7 = (bf16[384,128]{1,0:T(8,128)(2,1)S(1)}, bf16[384,128]{1,0:T(8,128)(2,1)S(1)}, u32[]{:S(2)}, u32[]{:S(2)}) collective-permute-start(bf16[384,128]{1,0:T(8,128)(2,1)S(1)} %get-tuple-element.54.after_ref.refs_0_), channel_id=1, source_target_pairs={{0,4},{1,5},{2,6},{3,7},{4,0},{5,1},{6,2},{7,3},{8,12},{9,13},{10,... | collective-permute-start | bytes 294920 | tf_op jit(solution)/shard_map/ppermute | solution.py:641
  37.5 8.6 %collective-permute-start.4 = (bf16[384,128]{1,0:T(8,128)(2,1)S(1)}, bf16[384,128]{1,0:T(8,128)(2,1)S(1)}, u32[]{:S(2)}, u32[]{:S(2)}) collective-permute-start(bf16[384,128]{1,0:T(8,128)(2,1)S(1)} %get-tuple-element.54.after_ref.refs_0_), channel_id=1, source_target_pairs={{0,1},{1,0},{2,3},{3,2},{4,5},{5,4},{6,7},{7,6},{8,9},{9,8},{10,11... | collective-permute-start | bytes 294920 | tf_op jit(solution)/shard_map/ppermute | solution.py:641
  40.3 5.7 %collective-permute-start.6 = (bf16[384,128]{1,0:T(8,128)(2,1)S(1)}, bf16[384,128]{1,0:T(8,128)(2,1)S(1)}, u32[]{:S(2)}, u32[]{:S(2)}) collective-permute-start(bf16[384,128]{1,0:T(8,128)(2,1)S(1)} %collective-permute-done.5.after_ref.refs_2_), channel_id=1, source_target_pairs={{0,1},{1,0},{2,3},{3,2},{4,5},{5,4},{6,7},{7,6},{8,9},{9,8},{10,11... | collective-permute-start | bytes 294920 | tf_op jit(solution)/shard_map/ppermute | solution.py:641
  42.5 5.4 %collective-permute-start.10 = (bf16[384,128]{1,0:T(8,128)(2,1)S(1)}, bf16[384,128]{1,0:T(8,128)(2,1)S(1)}, u32[]{:S(2)}, u32[]{:S(2)}) collective-permute-start(bf16[384,128]{1,0:T(8,128)(2,1)S(1)} %collective-permute-done.8.after_ref.refs_6_), channel_id=1, source_target_pairs={{0,1},{1,0},{2,3},{3,2},{4,5},{5,4},{6,7},{7,6},{8,9},{9,8},{10,11... | collective-permute-start | bytes 294920 | tf_op jit(solution)/shard_map/ppermute | solution.py:641
  45.3 4.7 %collective-permute-start.9 = (bf16[384,128]{1,0:T(8,128)(2,1)S(1)}, bf16[384,128]{1,0:T(8,128)(2,1)S(1)}, u32[]{:S(2)}, u32[]{:S(2)}) collective-permute-start(bf16[384,128]{1,0:T(8,128)(2,1)S(1)} %collective-permute-done.7.refs_4_), channel_id=1, source_target_pairs={{0,1},{1,0},{2,3},{3,2},{4,5},{5,4},{6,7},{7,6},{8,9},{9,8},{10,11... | collective-permute-start | bytes 294920 | tf_op jit(solution)/shard_map/ppermute | solution.py:641
  55.6 4.8 %collective-permute-start.11 = (bf16[2,16,1664]{2,1,0:T(8,128)(2,1)S(1)}, bf16[2,16,1664]{2,1,0:T(8,128)(2,1)S(1)}, u32[]{:S(2)}, u32[]{:S(2)}) collective-permute-start(bf16[2,16,1664]{2,1,0:T(8,128)(2,1)S(1)} %get-tuple-element.65), channel_id=1, source_target_pairs={{0,1},{1,0},{2,3},{3,2},{4,5},{5,4},{6,7},{7,6},{8,9},{9,8},{10,11... | collective-permute-start | bytes 319496 | tf_op jit(solution)/shard_map/ppermute | solution.py:641
  56.4 6.7 %collective-permute-start.12 = (bf16[2,16,1664]{2,1,0:T(8,128)(2,1)S(1)}, bf16[2,16,1664]{2,1,0:T(8,128)(2,1)S(1)}, u32[]{:S(2)}, u32[]{:S(2)}) collective-permute-start(bf16[2,16,1664]{2,1,0:T(8,128)(2,1)S(1)} %get-tuple-element.67), channel_id=1, source_target_pairs={{0,1},{1,0},{2,3},{3,2},{4,5},{5,4},{6,7},{7,6},{8,9},{9,8},{10,11... | collective-permute-start | bytes 319496 | tf_op jit(solution)/shard_map/ppermute | solution.py:641
  60.4 6.1 %collective-permute-start.15 = (bf16[16,1792]{1,0:T(8,128)(2,1)S(1)}, bf16[16,1792]{1,0:T(8,128)(2,1)S(1)}, u32[]{:S(2)}, u32[]{:S(2)}) collective-permute-start(bf16[16,1792]{1,0:T(8,128)(2,1)S(1)} %get-tuple-element.70), channel_id=1, source_target_pairs={{0,6},{1,7},{2,4},{3,5},{4,2},{5,3},{6,0},{7,1},{8,14},{9,15},{10,... | collective-permute-start | bytes 172040 | tf_op jit(solution)/shard_map/ppermute | solution.py:641
  61.6 6.2 %collective-permute-start.14 = (bf16[16,1792]{1,0:T(8,128)(2,1)S(1)}, bf16[16,1792]{1,0:T(8,128)(2,1)S(1)}, u32[]{:S(2)}, u32[]{:S(2)}) collective-permute-start(bf16[16,1792]{1,0:T(8,128)(2,1)S(1)} %get-tuple-element.66.after_ref), channel_id=1, source_target_pairs={{0,4},{1,5},{2,6},{3,7},{4,0},{5,1},{6,2},{7,3},{8,12},{9,13},{10,... | collective-permute-start | bytes 172040 | tf_op jit(solution)/shard_map/ppermute | solution.py:641
  63.1 4.8 %collective-permute-start.13 = (bf16[16,1792]{1,0:T(8,128)(2,1)S(1)}, bf16[16,1792]{1,0:T(8,128)(2,1)S(1)}, u32[]{:S(2)}, u32[]{:S(2)}) collective-permute-start(bf16[16,1792]{1,0:T(8,128)(2,1)S(1)} %get-tuple-element.69), channel_id=1, source_target_pairs={{0,2},{1,3},{2,0},{3,1},{4,6},{5,7},{6,4},{7,5},{8,10},{9,11},{10,... | collective-permute-start | bytes 172040 | tf_op jit(solution)/shard_map/ppermute | solution.py:641

commit v5 on v4

--- a/solution.py
+++ b/solution.py
@@ -17,6 +17,7 @@
 WIDE = 128
 STEP = 2
 ORDER = (1, 3, 2)
+FETCHES = ((0, 1), (3,), (2,))
 
 
 neg_big = -1e30
@@ -309,15 +310,18 @@
 
 def route_kernel(kv_width, after_ref, table_ref, pulled_ref, *refs):
     del after_ref
-    parts, (sent_ref, res_ref, turned_ref) = refs[:-3], refs[-3:]
+    parts, (sent_ref, res_ref, turned_ref, kv_ref) = refs[:-4], refs[-4:]
     rank = lax.axis_index("tp")
     other = 1 - lax.rem(rank, 2)
+    size = parts[0].shape[1]
     for k, part in enumerate(parts):
-        turned_ref[k] = part[other]
+        turned_ref[k * size : (k + 1) * size, :] = part[other]
     q_width = HEADS * HEAD
     tok_dev = pulled_ref.shape[1]
     rows = pulled_ref[number(table_ref, 0)]
     res_ref[...] = rows[:, q_width + 2 * kv_width :]
+    tiles = [rows[:, q_width + c : q_width + c + WIDE] for c in range(0, 2 * kv_width, WIDE)]
+    kv_ref[...] = jnp.concatenate(tiles, axis=0)
     head_rows = (HEADS // KV_HEADS) * HEAD
     tail = jnp.zeros((tok_dev, 2 * WIDE - head_rows), rows.dtype)
     for head in range(KV_HEADS):
@@ -349,7 +353,8 @@
 
 
 def tree_kernel(
-    after_ref, down_hbm, table_ref, parents_ref, down_ref, reach_ref, chosen_ref, sem
+    after_ref, down_hbm, table_ref, parents_ref, ids_ref, down_ref, reach_ref, chosen_ref,
+    count_ref, sem,
 ):
     del after_ref
     copy = pltpu.make_async_copy(down_hbm, down_ref, sem)
@@ -366,16 +371,22 @@
         rank = jnp.dot(path.astype(jnp.bfloat16), upto, preferred_element_type=jnp.float32)
         chosen = (path > 0.5) & (rank == (node_from + 1).astype(jnp.float32))
         chosen_ref[s] = jnp.where(chosen, 1.0, 0.0).astype(jnp.bfloat16)
+    ids = ids_ref[...].astype(jnp.float32).T
+    names = lax.broadcasted_iota(jnp.int32, count_ref.shape, 1).astype(jnp.float32)
+    count = jnp.zeros(count_ref.shape, jnp.float32)
+    for k in range(ids.shape[1]):
+        count = count + jnp.where(ids[:, k : k + 1] == names, 1.0, 0.0)
+    count_ref[...] = count
     copy.wait()
 
 
-def attend_kernel(units_ref, table_ref, reach_ref, chosen_ref, got_ref, res_ref, turned_ref, *refs):
+def attend_kernel(units_ref, table_ref, reach_ref, got_ref, res_ref, turned_ref, kv_ref, *refs):
     del units_ref
-    parts, (sent_ref, picked_ref) = refs[:-2], refs[-2:]
-    slot_count = chosen_ref.shape[0]
+    parts, (sent_ref, near_ref) = refs[:-2], refs[-2:]
+    slot_count = reach_ref.shape[0] // DRAFT
     sources = got_ref.shape[0]
     tok_dev = res_ref.shape[0]
-    page_len = turned_ref.shape[1] // slot_count
+    page_len = parts[0].shape[1] // slot_count
     per_slot = DRAFT // tok_dev
     group_size = HEADS // KV_HEADS
     f32, bf16 = jnp.float32, jnp.bfloat16
@@ -391,7 +402,7 @@
     positions = jnp.concatenate(positions, axis=1)
     dims = (((1,), (1,)), ((), ()))
     scale = 1.0 / math.sqrt(HEAD)
-    outs, picked = [], []
+    outs = []
     for s in range(slot_count):
         first = s * per_slot
 
@@ -412,7 +423,7 @@
         ).astype(bf16)
         at = slice(s * page_len, (s + 1) * page_len)
         cache_kv = jnp.concatenate(
-            [a for k, part in enumerate(parts) for a in (part[side, at, :], turned_ref[k, at, :])],
+            [a for k, part in enumerate(parts) for a in (part[side, at, :], turned_ref[k * parts[0].shape[1] + at.start : k * parts[0].shape[1] + at.stop, :])],
             axis=0,
         )
         scores = lax.dot_general(q_rows, cache_kv, dims, preferred_element_type=f32)
@@ -434,9 +445,6 @@
             tree_weights, tree_kv, preferred_element_type=f32
         )
         outs.append(mixed / total)
-        picked.append(
-            jnp.dot(chosen_ref[s], tree_kv, preferred_element_type=f32).astype(bf16)
-        )
     pair_rows, last_rows = [], []
     for out in outs:
         head_out = [out[r * DRAFT : (r + 1) * DRAFT] for r in range(group_size)]
@@ -447,83 +455,148 @@
     last = jnp.where(lane_low, pltpu.roll(last_rows[0], HEAD, 1), last_rows[1]).astype(bf16)
     res_tiles = [res_ref[:, c * WIDE : (c + 1) * WIDE] for c in range(res_ref.shape[1] // WIDE)]
     sent_ref[...] = jnp.concatenate(pair_rows + [last] + res_tiles, axis=0)
-    for target in range(sources):
-        row = (target % per_slot) * tok_dev
-        picked_ref[target] = picked[target // per_slot][row : row + tok_dev]
-
-
-def fetch_kernel(spans, after_ref, *refs):
+    rows = sent_ref.shape[0]
+    near_ref[:rows, :] = sent_ref[...]
+    near_ref[rows:, :] = kv_ref[...]
+
+
+def accept_kernel(rows, chosen_ref, *refs):
+    accepted_ref = refs[-1]
+    tok_dev, width = accepted_ref.shape
+    rank = lax.axis_index("tp")
+    per_slot = DRAFT // tok_dev
+    place = lax.rem(rank, per_slot)
+    chosen = chosen_ref[lax.div(rank, per_slot), pl.ds(pl.multiple_of(place * tok_dev, tok_dev), tok_dev), :]
+    is_even, is_first = lax.rem(place, 2) == 0, place < 2
+    for c in range(width // WIDE):
+        low = rows + c * tok_dev
+        pairs = []
+        for mine, other in (refs[:2], refs[2:4]):
+            a, b = mine[low : low + tok_dev, :], other[low : low + tok_dev, :]
+            pairs.append(
+                jnp.concatenate([jnp.where(is_even, a, b), jnp.where(is_even, b, a)], axis=0)
+            )
+        near, far = pairs
+        nodes = jnp.concatenate(
+            [jnp.where(is_first, near, far), jnp.where(is_first, far, near)], axis=0
+        )
+        accepted_ref[:, c * WIDE : (c + 1) * WIDE] = jnp.dot(
+            chosen, nodes, preferred_element_type=jnp.float32
+        ).astype(jnp.bfloat16)
+
+
+def fetch_kernel(picks, after_ref, source_ref, target_ref, sems):
     del after_ref
-    count = len(spans)
-    sems = refs[-1]
-    start_all(
+    rows = target_ref.shape[0] // len(picks)
+    copies = []
+    for place, k in enumerate(picks):
+        pair = lax.bitwise_xor(lax.div(lax.axis_index("tp"), 2), k)
+        start = pl.multiple_of(pair * rows, WIDE)
+        copies.append(
+            pltpu.make_async_copy(
+                source_ref.at[pl.ds(start, rows)],
+                target_ref.at[place * rows : (place + 1) * rows],
+                sems.at[place],
+            )
+        )
+    start_all(copies)
+
+
+def join_heads(k, rows, group_rows, mine_ref, other_ref, residual_ref):
+    f32, bf16 = jnp.float32, jnp.bfloat16
+    half = group_rows // 2
+    tok_dev = group_rows // KV_HEADS
+    model = residual_ref.shape[1]
+    res_start = group_rows + half
+    rank = lax.axis_index("tp")
+    is_even = lax.rem(rank, 2) == 0
+    pair = lax.bitwise_xor(lax.div(rank, 2), k)
+    lane_low = lax.broadcasted_iota(jnp.int32, (half, WIDE), 1) < HEAD
+    mine, other = mine_ref[:rows, :], other_ref[:rows, :]
+    even, odd = jnp.where(is_even, mine, other), jnp.where(is_even, other, mine)
+    last_even = even[group_rows:res_start].astype(f32)
+    last_odd = odd[group_rows:res_start].astype(f32)
+    odd_swapped = pltpu.roll(odd[:group_rows].astype(f32), HEAD, 1)
+    middle = jnp.concatenate(
         [
-            pltpu.make_async_copy(refs[k].at[pl.ds(*spans[k])], refs[count + k], sems.at[k])
-            for k in range(count)
-        ]
+            jnp.where(lane_low, last_even, odd_swapped[:half]),
+            jnp.where(lane_low, pltpu.roll(last_even, HEAD, 1), odd_swapped[half:]),
+        ],
+        axis=0,
+    ).astype(bf16)
+    end = jnp.concatenate(
+        [
+            jnp.where(lane_low, odd_swapped[:half], pltpu.roll(last_odd, HEAD, 1)),
+            jnp.where(lane_low, odd_swapped[half:], last_odd),
+        ],
+        axis=0,
+    ).astype(bf16)
+    for q, block in enumerate((even, odd)):
+        row = pl.multiple_of((2 * pair + q) * tok_dev, tok_dev)
+        residual_ref[pl.ds(row, tok_dev), :] = jnp.concatenate(
+            [
+                block[res_start + c * tok_dev : res_start + (c + 1) * tok_dev]
+                for c in range(model // WIDE)
+            ],
+            axis=1,
+        ).astype(f32)
+    return jnp.concatenate([even[:group_rows], middle, end], axis=1)
+
+
+def keep_own(k, heads_ref, at, attn_ref):
+    tok_dev = attn_ref.shape[0]
+    width = attn_ref.shape[1] * 2 // KV_HEADS
+    rank = lax.axis_index("tp")
+    pair = lax.bitwise_xor(lax.div(rank, 2), k)
+    own = pl.multiple_of(rank * tok_dev, tok_dev)
+    attn_ref[:, pl.ds(pl.multiple_of(pair * width, WIDE), width)] = heads_ref[
+        pl.ds(own, tok_dev), at : at + width
+    ]
+
+
+def early_kernel(rows, after_ref, weight_ref, *refs):
+    del after_ref
+    blocks, (hid_ref, attn_ref, residual_ref, x_ref) = refs[:-4], refs[-4:]
+    group_rows = hid_ref.shape[0]
+    residual_ref[...] = jnp.zeros_like(residual_ref)
+    width = x_ref.shape[1] * 2 // len(blocks)
+    for k in range(len(blocks) // 2):
+        x_ref[:, k * width : (k + 1) * width] = join_heads(
+            k, rows, group_rows, blocks[2 * k], blocks[2 * k + 1], residual_ref
+        )
+    for k in range(len(blocks) // 2):
+        keep_own(k, x_ref, k * width, attn_ref)
+    hid_ref[...] = residual_ref[...] + jnp.dot(
+        x_ref[...], weight_ref[...], preferred_element_type=jnp.float32
     )
 
 
 def expert_kernel(
-    router_ref, ids_ref, gain_ref, down_ref, picked_ref, *refs
+    rows, count_ref, router_ref, gain_ref, down_ref, before_ref, part_ref, *refs
 ):
-    blocks, refs = refs[:KV_HEADS], refs[KV_HEADS:]
-    weight_refs, unit_refs, refs = refs[: KV_HEADS // 2 - 1], refs[KV_HEADS // 2 - 1 : -7], refs[-7:]
-    far_ref, hid_ref, hidden_ref, attn_ref, x_ref, normed_ref, share_ref = refs
+    refs, late = refs[:-8], refs[-8:]
+    far_ref, hid_ref, hidden_ref, attn_ref, x_ref, normed_ref, share_ref, residual_ref = late
     f32, bf16 = jnp.float32, jnp.bfloat16
+    pairs = KV_HEADS // 2
+    first = pairs // 2
+    blocks, refs = refs[: 2 * (pairs - first)], refs[2 * (pairs - first) :]
+    weight_refs, unit_refs = refs[: pairs - first], refs[pairs - first :]
     unit_weights = [(ref, k) for ref in unit_refs for k in range(ref.shape[0])]
     units = len(unit_weights)
-    tok_dev = hidden_ref.shape[0]
-    sources = len(blocks)
+    tok_dev, model = hidden_ref.shape
+    sources = KV_HEADS
     group_rows = sources * tok_dev
-    half = group_rows // 2
-    model = hidden_ref.shape[1]
-    width = sum(ref.shape[0] for ref in weight_refs)
     rank = lax.axis_index("tp")
-    lane_low = lax.broadcasted_iota(jnp.int32, (half, WIDE), 1) < HEAD
-    head_rows = width // sources
-    res_start = group_rows + half
-    is_even = lax.rem(rank, 2) == 0
-    for k in range(sources // 2):
-        pair = lax.bitwise_xor(lax.div(rank, 2), k)
-        mine, other = blocks[2 * k][...], blocks[2 * k + 1][...]
-        even, odd = jnp.where(is_even, mine, other), jnp.where(is_even, other, mine)
-        last_even = even[group_rows:res_start].astype(f32)
-        last_odd = odd[group_rows:res_start].astype(f32)
-        odd_swapped = pltpu.roll(odd[:group_rows].astype(f32), HEAD, 1)
-        middle = jnp.concatenate(
-            [
-                jnp.where(lane_low, last_even, odd_swapped[:half]),
-                jnp.where(lane_low, pltpu.roll(last_even, HEAD, 1), odd_swapped[half:]),
-            ],
-            axis=0,
-        ).astype(bf16)
-        end = jnp.concatenate(
-            [
-                jnp.where(lane_low, odd_swapped[:half], pltpu.roll(last_odd, HEAD, 1)),
-                jnp.where(lane_low, odd_swapped[half:], last_odd),
-            ],
-            axis=0,
-        ).astype(bf16)
-        base = pl.multiple_of(pair * 2 * head_rows, WIDE)
-        x_ref[:, pl.ds(base, 2 * head_rows)] = jnp.concatenate(
-            [even[:group_rows], middle, end], axis=1
-        )
-        for q, block in enumerate((even, odd)):
-            row = pl.multiple_of((2 * pair + q) * tok_dev, tok_dev)
-            hid_ref[pl.ds(row, tok_dev), :] = jnp.concatenate(
-                [
-                    block[res_start + c * tok_dev : res_start + (c + 1) * tok_dev]
-                    for c in range(model // WIDE)
-                ],
-                axis=1,
-            ).astype(f32)
     own = pl.multiple_of(rank * tok_dev, tok_dev)
-    attn_ref[...] = x_ref[pl.ds(own, tok_dev), :]
-    hidden, at = hid_ref[...], 0
-    for ref in weight_refs:
-        hidden += jnp.dot(x_ref[:, at : at + ref.shape[0]], ref[...], preferred_element_type=f32)
-        at += ref.shape[0]
+    attn_ref[...] = part_ref[...]
+    residual_ref[...] = jnp.zeros_like(residual_ref)
+    hidden, width = before_ref[...], x_ref.shape[1] // (pairs - first)
+    for q, k in enumerate(range(first, pairs)):
+        heads = join_heads(k, rows, group_rows, blocks[2 * q], blocks[2 * q + 1], residual_ref)
+        x_ref[:, q * width : (q + 1) * width] = heads
+        keep_own(k, x_ref, q * width, attn_ref)
+        hidden += jnp.dot(heads, weight_refs[q][...], preferred_element_type=f32)
+    hidden += residual_ref[...]
     hid_ref[...] = hidden
     gain = jnp.concatenate([gain_ref[c : c + 1, :] for c in range(model // WIDE)], axis=1)
     scale = lax.rsqrt(jnp.mean(hidden * hidden, axis=1, keepdims=True) + norm_eps)
@@ -533,12 +606,8 @@
         normed_ref[...], router_ref[...], (((1,), (1,)), ((), ())), preferred_element_type=f32
     )
     experts = router_ref.shape[0]
-    ids = ids_ref[...].astype(f32).T
     expert_range = lax.broadcasted_iota(jnp.int32, (group_rows, experts), 1)
-    expert_names = expert_range.astype(f32)
-    count = jnp.zeros((group_rows, experts), f32)
-    for k in range(ids_ref.shape[0]):
-        count = count + jnp.where(ids[:, k : k + 1] == expert_names, 1.0, 0.0)
+    count = count_ref[...]
     expo = jnp.where(count > 0.0, jnp.exp(logits), 0.0) * count
     routing = expo / jnp.sum(expo, axis=1, keepdims=True)
     unit_width = unit_refs[0].shape[2] // 2
@@ -561,62 +630,43 @@
         part = jnp.dot(act, down, preferred_element_type=f32)
         hid_ref[...] = part if i == 0 else hid_ref[...] + part
     for k in range(far_ref.shape[0]):
-        copy_sums(sources // 4 + k, True, hid_ref, picked_ref, far_ref.at[k])
-
-
-def copy_sums(k, crossing, hid_ref, picked_ref, ref):
-    tok_dev, model = ref.shape[0], hid_ref.shape[1]
+        copy_sums(sources // 4 + k, True, hid_ref, far_ref.at[k])
+
+
+def copy_sums(k, crossing, hid_ref, ref):
+    tok_dev = ref.shape[0]
     rank = lax.axis_index("tp")
     side = lax.rem(rank, 2)
     pair = lax.bitwise_xor(lax.div(rank, 2), k)
     target = 2 * pair + (1 - side if crossing else side)
     row = pl.multiple_of(target * tok_dev, tok_dev)
-    ref[:, :model] = hid_ref[pl.ds(row, tok_dev), :].astype(ref.dtype)
-    ref[:, model:] = picked_ref[target].astype(ref.dtype)
-
-
-def near_kernel(hid_ref, picked_ref, mine_ref, near_ref):
+    ref[...] = hid_ref[pl.ds(row, tok_dev), :].astype(ref.dtype)
+
+
+def near_kernel(hid_ref, mine_ref, near_ref):
     for k in range(mine_ref.shape[0]):
-        copy_sums(k, False, hid_ref, picked_ref, mine_ref.at[k])
+        copy_sums(k, False, hid_ref, mine_ref.at[k])
     for k in range(near_ref.shape[0]):
-        copy_sums(k, True, hid_ref, picked_ref, near_ref.at[k])
+        copy_sums(k, True, hid_ref, near_ref.at[k])
 
 
 def fold_kernel(first, after_ref, mine_ref, got_ref, hidden_ref, *sent_refs):
     del after_ref
-    model = hidden_ref.shape[1]
-    is_even = lax.rem(lax.axis_index("tp"), 2) == 0
     for k, ref in enumerate(sent_refs, first):
-        mine, got = mine_ref[k], got_ref[k - first].astype(jnp.float32)
-        total = mine[:, :model] + got[:, :model]
+        total = mine_ref[k] + got_ref[k - first].astype(jnp.float32)
         if k == 0:
             total = total + hidden_ref[...]
-        ref[:, :model] = total.astype(ref.dtype)
-        low, high = mine[:, model:], got[:, model:]
-        even, odd = jnp.where(is_even, low, high), jnp.where(is_even, high, low)
-        ref[:, model:] = jnp.concatenate([even, odd], axis=1).astype(ref.dtype)
-
-
-def finish_kernel(attn_in_ref, *refs):
+        ref[...] = total.astype(ref.dtype)
+
+
+def finish_kernel(attn_in_ref, accepted_in_ref, *refs):
     parts, (attn_ref, layer_ref, accepted_ref) = refs[:-3], refs[-3:]
     attn_ref[...] = attn_in_ref[...]
-    f32, bf16 = jnp.float32, jnp.bfloat16
-    tok_dev, model = layer_ref.shape
-    kv_width = accepted_ref.shape[1] // 2
-    total = parts[0][:, :model]
+    accepted_ref[...] = accepted_in_ref[...]
+    total = parts[0][...]
     for part in parts[1:]:
-        total = total + part[:, :model].astype(f32)
-    layer_ref[...] = total.astype(bf16)
-    low = lax.broadcasted_iota(jnp.int32, (tok_dev, WIDE), 1) < HEAD
-    for k, part in enumerate(parts):
-        pair = lax.bitwise_xor(lax.div(lax.axis_index("tp"), 2), k)
-        even = part[:, model : model + WIDE].astype(f32)
-        odd = part[:, model + WIDE :].astype(f32)
-        at = pl.multiple_of(pair * WIDE, WIDE)
-        accepted_ref[:, pl.ds(at, WIDE)] = jnp.where(low, even, pltpu.roll(odd, HEAD, 1)).astype(bf16)
-        accepted_ref[:, pl.ds(kv_width + at, WIDE)] = jnp.where(
-            low, pltpu.roll(even, HEAD, 1), odd
-        ).astype(bf16)
+        total = total + part[...].astype(jnp.float32)
+    layer_ref[...] = total.astype(jnp.bfloat16)
 
 
 def in_hbm(*arrays):
@@ -641,18 +691,18 @@
     return lax.ppermute(rows, "tp", [(i, i ^ mask) for i in range(count)])
 
 
-def fetch(name, after, *spans):
-    shapes = [(rows,) + array.shape[1:] for array, _, rows in spans]
+def fetch(after, array, rows, picks):
+    shape = (rows * len(picks),) + array.shape[1:]
     return pl.pallas_call(
-        functools.partial(fetch_kernel, tuple((first, rows) for _, first, rows in spans)),
-        out_shape=tuple(pltpu.VMEM(shape, jnp.bfloat16) for shape in shapes),
-        in_specs=spaces("a" * (1 + len(spans))),
-        out_specs=tuple(spaces("v" * len(spans))),
-        scratch_shapes=[pltpu.SemaphoreType.DMA((len(spans),))],
-        compiler_params=params(),
-        cost_estimate=cost(sum(2 * math.prod(shape) for shape in shapes) >> 20),
-        name="fetch_" + name,
-    )(after, *in_hbm(*[array for array, _, _ in spans]))
+        functools.partial(fetch_kernel, picks),
+        out_shape=pltpu.VMEM(shape, array.dtype),
+        in_specs=spaces("aa"),
+        out_specs=spaces("v")[0],
+        scratch_shapes=[pltpu.SemaphoreType.DMA((len(picks),))],
+        compiler_params=params(),
+        cost_estimate=cost(2 * math.prod(shape) >> 20),
+        name="fetch",
+    )(after, *in_hbm(array))
 
 
 def per_device_packed(
@@ -727,29 +777,32 @@
     parts = [parts[0]] + [swap(parts[k], 2 * k) for k in range(1, pairs)]
     pulled = lax.all_gather(joined, "req", axis=0)
     nodes = slot_count * DRAFT
-    down_weight, reach, chosen = pl.pallas_call(
+    down_weight, reach, chosen, count = pl.pallas_call(
         tree_kernel,
         out_shape=(
             pltpu.VMEM(down_weight.shape, bf16),
             jax.ShapeDtypeStruct((nodes, nodes), f32),
             jax.ShapeDtypeStruct((slot_count, DRAFT, DRAFT), bf16),
+            jax.ShapeDtypeStruct((group_rows, router_weight.shape[1]), f32),
         ),
-        in_specs=spaces("aavv"),
-        out_specs=tuple(spaces("vvv")),
+        in_specs=spaces("aavvv"),
+        out_specs=tuple(spaces("vvvv")),
         scratch_shapes=[dma],
         compiler_params=params(),
         cost_estimate=cost(8),
         name="tree",
-    )(pulled, *in_hbm(down_weight), table, parents)
-    packed, own_res, turned = pl.pallas_call(
+    )(pulled, *in_hbm(down_weight), table, parents, ids)
+    kv_rows = 2 * kv_width // WIDE * tok_dev
+    packed, own_res, turned, own_kv = pl.pallas_call(
         functools.partial(route_kernel, kv_width),
         out_shape=(
             sent(3 * tok_dev),
             jax.ShapeDtypeStruct(residual.shape, bf16),
-            jax.ShapeDtypeStruct((pairs,) + part.shape[1:], bf16),
+            jax.ShapeDtypeStruct((pairs * part.shape[1], WIDE), bf16),
+            jax.ShapeDtypeStruct((kv_rows, WIDE), bf16),
         ),
         in_specs=spaces("avv" + "v" * pairs),
-        out_specs=tuple(spaces("vvv")),
+        out_specs=tuple(spaces("vvvv")),
         compiler_params=params(),
         cost_estimate=cost(4),
         name="route",
@@ -757,76 +810,104 @@
     turned = swap(turned, 1)
     packed = lax.all_to_all(packed, "tp", 0, 0, tiled=True)
     gate_up = pltpu.with_memory_space_constraint(gate_up, pltpu.VMEM)
-    block, picked = pl.pallas_call(
+    block_rows = group_rows + group_rows // 2 + (model // WIDE) * tok_dev
+    block, near_block = pl.pallas_call(
         attend_kernel,
         out_shape=(
-            jax.ShapeDtypeStruct(
-                (group_rows + group_rows // 2 + (model // WIDE) * tok_dev, WIDE), bf16
-            ),
-            sent(tok_dev),
+            jax.ShapeDtypeStruct((block_rows, WIDE), bf16),
+            jax.ShapeDtypeStruct((block_rows + kv_rows, WIDE), bf16),
         ),
         in_specs=spaces("v" * (7 + pairs)),
         out_specs=tuple(spaces("vv")),
         compiler_params=params(),
         cost_estimate=cost(8),
         name="attend",
-    )(gate_up, table, reach, chosen, packed, own_res, turned, *parts)
+    )(gate_up, table, reach, packed, own_res, turned, own_kv, *parts)
     units = gate_up.shape[0]
-    reached = [swap(block, 2 * k) for k in range(1, pairs)]
+    reached = [swap(near_block, 2)] + [swap(block, 2 * k) for k in range(2, pairs)]
     weights, after = [], block
-    rows = out_weight.shape[0] // (pairs - 1)
-    for step, k in enumerate(ORDER):
-        (weight,) = fetch("dense", after, (out_weight, step * rows, rows))
+    rows = out_weight.shape[0] // pairs
+    for k, picks in zip(ORDER, FETCHES):
+        weight = fetch(after, out_weight, rows, picks)
         reached[k - 1], weight = lax.optimization_barrier((reached[k - 1], weight))
         after = reached[k - 1]
         weights.append(weight)
-    blocks = [a for rows in [block] + reached for a in (rows, swap(rows, 1))]
+    blocks = [block, swap(near_block, 1)]
+    blocks += [a for got in reached for a in (got, swap(got, 1))]
+    before, attn_part = pl.pallas_call(
+        functools.partial(early_kernel, block_rows),
+        out_shape=(
+            jax.ShapeDtypeStruct((group_rows, model), f32),
+            pltpu.VMEM(queries.shape, bf16),
+        ),
+        in_specs=spaces("av" + "v" * pairs),
+        out_specs=tuple(spaces("vv")),
+        scratch_shapes=[
+            pltpu.VMEM((group_rows, model), f32),
+            pltpu.VMEM((group_rows, HEADS * HEAD // 2), bf16),
+        ],
+        compiler_params=params(),
+        cost_estimate=cost(4),
+        name="early",
+    )(after, weights[0], *blocks[:pairs])
+    accepted = pl.pallas_call(
+        functools.partial(accept_kernel, block_rows),
+        out_shape=pltpu.VMEM(new_kv.shape, bf16),
+        in_specs=spaces("vvvvv"),
+        out_specs=spaces("v")[0],
+        compiler_params=params(),
+        cost_estimate=cost(1),
+        name="accept",
+    )(chosen, near_block, *blocks[1:4])
     unit_weights = (gate_up,)
     far, sums, hidden, attn_own = pl.pallas_call(
-        expert_kernel,
+        functools.partial(expert_kernel, block_rows),
         out_shape=(
-            jax.ShapeDtypeStruct((pairs // 2, tok_dev, model + WIDE), bf16),
+            jax.ShapeDtypeStruct((pairs // 2, tok_dev, model), bf16),
             jax.ShapeDtypeStruct((group_rows, model), f32),
             jax.ShapeDtypeStruct((tok_dev, model), f32),
             pltpu.VMEM(queries.shape, bf16),
         ),
-        in_specs=spaces("v" * (5 + len(weights) + len(unit_weights) + tp_count)),
+        in_specs=spaces("v" * (6 + pairs + pairs // 2 + len(unit_weights))),
         out_specs=tuple(spaces("vvvv")),
         scratch_shapes=[
-            pltpu.VMEM((group_rows, HEADS * HEAD), bf16),
+            pltpu.VMEM((group_rows, HEADS * HEAD // 2), bf16),
             pltpu.VMEM((group_rows, model), bf16),
             pltpu.VMEM((units, group_rows, gate_up.shape[2] // 2), f32),
+            pltpu.VMEM((group_rows, model), f32),
         ],
         compiler_params=params(),
         name="experts",
     )(
+        count,
         router,
-        ids,
         gain,
         down_weight,
-        picked,
-        *blocks,
-        *weights,
+        before,
+        attn_part,
+        *blocks[pairs:],
+        weights[2],
+        weights[1],
         *unit_weights,
     )
     far = swap(far, 1)
     mine, near = pl.pallas_call(
         near_kernel,
         out_shape=(
-            jax.ShapeDtypeStruct((pairs, tok_dev, model + WIDE), f32),
-            jax.ShapeDtypeStruct((pairs // 2, tok_dev, model + WIDE), bf16),
+            jax.ShapeDtypeStruct((pairs, tok_dev, model), f32),
+            jax.ShapeDtypeStruct((pairs // 2, tok_dev, model), bf16),
         ),
-        in_specs=spaces("vv"),
+        in_specs=spaces("v"),
         out_specs=tuple(spaces("vv")),
         compiler_params=params(),
         cost_estimate=cost(4),
         name="near",
-    )(sums, picked)
+    )(sums)
     near = swap(near, 1)
     fold = lambda first, after, got: pl.pallas_call(
         functools.partial(fold_kernel, first),
         out_shape=tuple(
-            jax.ShapeDtypeStruct((tok_dev, model + 2 * WIDE), f32 if k == 0 else bf16)
+            jax.ShapeDtypeStruct((tok_dev, model), f32 if k == 0 else bf16)
             for k in range(first, first + pairs // 2)
         ),
         in_specs=spaces("avvv"),
@@ -847,11 +928,11 @@
             jax.ShapeDtypeStruct(residual.shape, bf16),
             jax.ShapeDtypeStruct(new_kv.shape, bf16),
         ),
-        in_specs=spaces("v" * (1 + pairs)),
+        in_specs=spaces("v" * (2 + pairs)),
         out_specs=tuple(spaces("vvv")),
         compiler_params=params(),
         name="finish",
-    )(attn_own, *sums)
+    )(attn_own, accepted, *sums)
 
 
 def per_device(queries, new_kv, residual, placement, *rest):

time: 68.9 us -> 67.9 us (0.985)
  waiting for transfers between devices: 10.5 us -> 9.2 us
    ppermute x16, waiting for transfers between devices: 10.5 us -> 9.2 us  [swap(): return lax.ppermute(rows, 'tp', [(i, i ^ mask) for i in range(count)])]
    pallas_call x5 -> x7, Pallas kernels: 11.4 us -> 11.6 us  [the longest x1 5.02 us: per_device_packed(): pl.pallas_call(functools.partial(expert_kernel, block_rows), out_shape=(j...]
  transfers between devices with their start and end apart: 16 -> 16, of which waited for: 7 -> 6; matrix products, arithmetic and copies ran while one was open for 0% -> 0% of each run, Pallas kernels for 11% -> 12%
where the time goes in v5:
time: 67.9 us; the launch traced here: 67.7 us
  starting transfers between devices  20.9 us (31%)
  blocking collectives  19.5 us (29%)
  Pallas kernels  17.4 us (26%)
  waiting for transfers between devices  9.2 us (14%)
  between operations  0.77 us (1%)
    ppermute x16, starting transfers between devices, swap(): return lax.ppermute(rows, 'tp', [(i, i ^ mask) for i in range(count)])  20.9 us
    all_to_all x1, blocking collectives, per_device_packed(): packed = lax.all_to_all(packed, 'tp', 0, 0, tiled=True)  12.1 us
    ppermute x16, waiting for transfers between devices, swap(): return lax.ppermute(rows, 'tp', [(i, i ^ mask) for i in range(count)])  9.2 us
    all_gather x1, blocking collectives, per_device_packed(): pulled = lax.all_gather(joined, 'req', axis=0)  7.4 us
    pallas_call x1, Pallas kernels, per_device_packed(): pl.pallas_call(functools.partial(expert_kernel, block_rows), out_shape=(j...  5.02 us
    pallas_call x3, Pallas kernels, fetch(): pl.pallas_call(functools.partial(fetch_kernel, picks), out_shape=pltpu.VM...  4.2 us
    pallas_call x1, Pallas kernels, per_device_packed(): pl.pallas_call(tree_kernel, out_shape=(pltpu.VMEM(down_weight.shape, bf16...  3.39 us
    pallas_call x1, Pallas kernels, per_device_packed(): pl.pallas_call(attend_kernel, out_shape=(jax.ShapeDtypeStruct((block_rows...  1.62 us
  transfers between devices with their start and end apart: 16, of which 6 were waited for; matrix products, arithmetic and copies ran while one was open for 0% of the time, Pallas kernels for 12%

profile of v5, /device:TPU:0, one launch (start us, length us, event | category | flops | bytes accessed | tf_op | source)
XLA Modules:
  0.0 67.7 jit_solution(15686714222157268442)
XLA Ops:
  0.6 1.4 %split.1 = (bf16[2,256,128]{2,1,0:T(8,128)(2,1)S(1)}, bf16[2,256,128]{2,1,0:T(8,128)(2,1)S(1)}, bf16[2,256,128]{2,1,0:T(8,128)(2,1)S(1)}, bf16[2,256,128]{2,1,0:...) custom-call(s32[2]{0:T(128)} %bitcast.10, ...), custom_call_target="tpu_custom_call" | custom-call | bytes 4194304 | tf_op jit(solution)/shard_map/split/pallas_call | solution.py:752
  2.1 3.1 %collective-permute-start = (bf16[2,256,128]{2,1,0:T(8,128)(2,1)S(1)}, bf16[2,256,128]{2,1,0:T(8,128)(2,1)S(1)}, u32[]{:S(2)}, u32[]{:S(2)}) collective-permute-start(bf16[2,256,128]{2,1,0:T(8,128)(2,1)S(1)} %get-tuple-element.51), channel_id=1, source_target_pairs={{0,2},{1,3},{2,0},{3,1},{4,6},{5,7},{6,4},{7,5},{8,10},{9,11},{10,... | collective-permute-start | bytes 393224 | tf_op jit(solution)/shard_map/ppermute | solution.py:691
  5.2 2.6 %collective-permute-start.1 = (bf16[2,256,128]{2,1,0:T(8,128)(2,1)S(1)}, bf16[2,256,128]{2,1,0:T(8,128)(2,1)S(1)}, u32[]{:S(2)}, u32[]{:S(2)}) collective-permute-start(bf16[2,256,128]{2,1,0:T(8,128)(2,1)S(1)} %get-tuple-element.52), channel_id=1, source_target_pairs={{0,4},{1,5},{2,6},{3,7},{4,0},{5,1},{6,2},{7,3},{8,12},{9,13},{10,... | collective-permute-start | bytes 393224 | tf_op jit(solution)/shard_map/ppermute | solution.py:691
  7.8 7.4 %all-gather = bf16[64,4096]{1,0:T(8,128)(2,1)S(1)} all-gather(bf16[16,4096]{1,0:T(8,128)(2,1)S(1)} %get-tuple-element.41), channel_id=2, replica_groups=mesh['req'=4,'tp'=8] {'req'}, dimensions={0}, use_global_device_ids=true | all-gather | bytes 655360 | tf_op jit(solution)/shard_map/all_gather | solution.py:778
  15.2 3.4 %tree.1 = (bf16[20,128,1536]{2,1,0:T(8,128)(2,1)S(1)}, f32[128,128]{1,0:T(8,128)S(1)}, bf16[2,64,64]{2,1,0:T(8,128)(2,1)S(1)}, f32[128,40]{1,0:T(8,128)S(1)}) custom-call(bf16[4,16,4096]{2,1,0:T(8,128)(2,1)S(1)} %bitcast.5, bf16[20,128,1536]{2,1,0:T(8,128)(2,1)} %down_hbm.1, f32[8,128]{1,0:T(8,128)S(1)} %get-tuple-element.42.table_ref, ...), custom_call_target="tpu_custom_call" | custom-call | bytes 8388608 | tf_op jit(solution)/shard_map/tree/pallas_call | solution.py:780
  18.8 1.6 %collective-permute-start.3 = (bf16[1024,128]{1,0:T(8,128)(2,1)S(1)}, bf16[1024,128]{1,0:T(8,128)(2,1)S(1)}, u32[]{:S(2)}, u32[]{:S(2)}) collective-permute-start(bf16[1024,128]{1,0:T(8,128)(2,1)S(1)} %get-tuple-element.56), channel_id=1, source_target_pairs={{0,1},{1,0},{2,3},{3,2},{4,5},{5,4},{6,7},{7,6},{8,9},{9,8},{10,11... | collective-permute-start | bytes 786440 | tf_op jit(solution)/shard_map/ppermute | solution.py:691
  20.4 12.1 %all_to_all.5.got_ref = bf16[8,48,128]{2,1,0:T(8,128)(2,1)S(1)} all-to-all(bf16[8,48,128]{2,1,0:T(8,128)(2,1)S(1)} %get-tuple-element.54), channel_id=1, replica_groups=mesh['req'=4,'tp'=8] {'tp'}, dimensions={0} | all-to-all | bytes 196608 | tf_op jit(solution)/shard_map/all_to_all | solution.py:811
  32.4 1.6 %attend.1 = (bf16[384,128]{1,0:T(8,128)(2,1)S(1)}, bf16[512,128]{1,0:T(8,128)(2,1)S(1)}) custom-call(bf16[20,1536,256]{2,1,0:T(8,128)(2,1)S(1)} %copy-done, f32[8,128]{1,0:T(8,128)S(1)} %get-tuple-element.42.table_ref, f32[128,128]{1,0:T(8,128)S(1)} %get-tuple-element.49.reach_ref, bf16[8,48,128]{2,1,0:T(8,128)(2,1)S(1)} %all_to_all.5.got_ref, ...), custom_call_target="tpu_custom_call" | custom-call | bytes 8388608 | tf_op jit(solution)/shard_map/attend/pallas_call | solution.py:814
  34.2 1.9 %collective-permute-start.5 = (bf16[384,128]{1,0:T(8,128)(2,1)S(1)}, bf16[384,128]{1,0:T(8,128)(2,1)S(1)}, u32[]{:S(2)}, u32[]{:S(2)}) collective-permute-start(bf16[384,128]{1,0:T(8,128)(2,1)S(1)} %get-tuple-element.58.after_ref.refs_0_), channel_id=1, source_target_pairs={{0,6},{1,7},{2,4},{3,5},{4,2},{5,3},{6,0},{7,1},{8,14},{9,15},{10,... | collective-permute-start | bytes 294920 | tf_op jit(solution)/shard_map/ppermute | solution.py:691
  36.0 1.6 %collective-permute-start.4 = (bf16[384,128]{1,0:T(8,128)(2,1)S(1)}, bf16[384,128]{1,0:T(8,128)(2,1)S(1)}, u32[]{:S(2)}, u32[]{:S(2)}) collective-permute-start(bf16[384,128]{1,0:T(8,128)(2,1)S(1)} %get-tuple-element.58.after_ref.refs_0_), channel_id=1, source_target_pairs={{0,4},{1,5},{2,6},{3,7},{4,0},{5,1},{6,2},{7,3},{8,12},{9,13},{10,... | collective-permute-start | bytes 294920 | tf_op jit(solution)/shard_map/ppermute | solution.py:691
  37.9 1.6 %fetch.3.weight_ref = bf16[768,1536]{1,0:T(8,128)(2,1)S(1)} custom-call(bf16[384,128]{1,0:T(8,128)(2,1)S(1)} %get-tuple-element.58.after_ref.refs_0_, bf16[1536,1536]{1,0:T(8,128)(2,1)} %source_ref.5), custom_call_target="tpu_custom_call" | custom-call | bytes 2097152 | tf_op jit(solution)/shard_map/fetch/pallas_call | solution.py:696
  39.6 1.2 %collective-permute-done.6.after_ref.refs_2_ = bf16[512,128]{1,0:T(8,128)(2,1)S(1)} collective-permute-done((bf16[512,128]{1,0:T(8,128)(2,1)S(1)}, bf16[512,128]{1,0:T(8,128)(2,1)S(1)}, u32[]{:S(2)}, u32[]{:S(2)}) %collective-permute-start.6) | collective-permute-done | bytes 131104 | tf_op jit(solution)/shard_map/ppermute | solution.py:691
  41.7 1.3 %fetch.4.refs_5_ = bf16[384,1536]{1,0:T(8,128)(2,1)S(1)} custom-call(bf16[512,128]{1,0:T(8,128)(2,1)S(1)} %collective-permute-done.6.after_ref.refs_2_, bf16[1536,1536]{1,0:T(8,128)(2,1)} %source_ref.5), custom_call_target="tpu_custom_call" | custom-call | bytes 1048576 | tf_op jit(solution)/shard_map/fetch/pallas_call | solution.py:696
  43.0 1.1 %collective-permute-start.10 = (bf16[384,128]{1,0:T(8,128)(2,1)S(1)}, bf16[384,128]{1,0:T(8,128)(2,1)S(1)}, u32[]{:S(2)}, u32[]{:S(2)}) collective-permute-start(bf16[384,128]{1,0:T(8,128)(2,1)S(1)} %collective-permute-done.5.after_ref.refs_2_), channel_id=1, source_target_pairs={{0,1},{1,0},{2,3},{3,2},{4,5},{5,4},{6,7},{7,6},{8,9},{9,8},{10,11... | collective-permute-start | bytes 294920 | tf_op jit(solution)/shard_map/ppermute | solution.py:691
  44.2 1.3 %fetch.5.refs_4_ = bf16[384,1536]{1,0:T(8,128)(2,1)S(1)} custom-call(bf16[384,128]{1,0:T(8,128)(2,1)S(1)} %collective-permute-done.5.after_ref.refs_2_, bf16[1536,1536]{1,0:T(8,128)(2,1)} %source_ref.5), custom_call_target="tpu_custom_call" | custom-call | bytes 1048576 | tf_op jit(solution)/shard_map/fetch/pallas_call | solution.py:696
  47.9 2.2 %collective-permute-done.9.refs_1_ = bf16[384,128]{1,0:T(8,128)(2,1)S(1)} collective-permute-done((bf16[384,128]{1,0:T(8,128)(2,1)S(1)}, bf16[384,128]{1,0:T(8,128)(2,1)S(1)}, u32[]{:S(2)}, u32[]{:S(2)}) %collective-permute-start.9) | collective-permute-done | bytes 98336 | tf_op jit(solution)/shard_map/ppermute | solution.py:691
  50.1 5.0 %experts.1 = (bf16[2,16,1536]{2,1,0:T(8,128)(2,1)S(1)}, f32[128,1536]{1,0:T(8,128)S(1)}, f32[16,1536]{1,0:T(8,128)S(1)}, bf16[16,1536]{1,0:T(8,128)(2,1)S(1)}) custom-call(f32[128,40]{1,0:T(8,128)S(1)} %get-tuple-element.45.count_ref, bf16[40,1536]{1,0:T(8,128)(2,1)S(1)} %get-tuple-element.46.router_ref, f32[12,128]{1,0:T(8,128)S(1)} %get-tuple-element.47.gain_ref, ...), custom_call_target="tpu_custom_call" | custom-call | tf_op jit(solution)/shard_map/experts/pallas_call | solution.py:863
  56.2 1.1 %collective-permute-start.12 = (bf16[2,16,1536]{2,1,0:T(8,128)(2,1)S(1)}, bf16[2,16,1536]{2,1,0:T(8,128)(2,1)S(1)}, u32[]{:S(2)}, u32[]{:S(2)}) collective-permute-start(bf16[2,16,1536]{2,1,0:T(8,128)(2,1)S(1)} %get-tuple-element.75), channel_id=1, source_target_pairs={{0,1},{1,0},{2,3},{3,2},{4,5},{5,4},{6,7},{7,6},{8,9},{9,8},{10,11... | collective-permute-start | bytes 294920 | tf_op jit(solution)/shard_map/ppermute | solution.py:691
  57.4 2.5 %collective-permute-done.11.got_ref = bf16[2,16,1536]{2,1,0:T(8,128)(2,1)S(1)} collective-permute-done((bf16[2,16,1536]{2,1,0:T(8,128)(2,1)S(1)}, bf16[2,16,1536]{2,1,0:T(8,128)(2,1)S(1)}, u32[]{:S(2)}, u32[]{:S(2)}) %collective-permute-start.11) | collective-permute-done | bytes 98336 | tf_op jit(solution)/shard_map/ppermute | solution.py:691
  59.9 1.1 %collective-permute-start.15 = (bf16[16,1536]{1,0:T(8,128)(2,1)S(1)}, bf16[16,1536]{1,0:T(8,128)(2,1)S(1)}, u32[]{:S(2)}, u32[]{:S(2)}) collective-permute-start(bf16[16,1536]{1,0:T(8,128)(2,1)S(1)} %get-tuple-element.78), channel_id=1, source_target_pairs={{0,6},{1,7},{2,4},{3,5},{4,2},{5,3},{6,0},{7,1},{8,14},{9,15},{10,... | collective-permute-start | bytes 147464 | tf_op jit(solution)/shard_map/ppermute | solution.py:691
  61.0 1.4 %collective-permute-start.14 = (bf16[16,1536]{1,0:T(8,128)(2,1)S(1)}, bf16[16,1536]{1,0:T(8,128)(2,1)S(1)}, u32[]{:S(2)}, u32[]{:S(2)}) collective-permute-start(bf16[16,1536]{1,0:T(8,128)(2,1)S(1)} %get-tuple-element.74.after_ref), channel_id=1, source_target_pairs={{0,4},{1,5},{2,6},{3,7},{4,0},{5,1},{6,2},{7,3},{8,12},{9,13},{10,... | collective-permute-start | bytes 147464 | tf_op jit(solution)/shard_map/ppermute | solution.py:691
  62.4 2.1 %collective-permute-start.13 = (bf16[16,1536]{1,0:T(8,128)(2,1)S(1)}, bf16[16,1536]{1,0:T(8,128)(2,1)S(1)}, u32[]{:S(2)}, u32[]{:S(2)}) collective-permute-start(bf16[16,1536]{1,0:T(8,128)(2,1)S(1)} %get-tuple-element.77), channel_id=1, source_target_pairs={{0,2},{1,3},{2,0},{3,1},{4,6},{5,7},{6,4},{7,5},{8,10},{9,11},{10,... | collective-permute-start | bytes 147464 | tf_op jit(solution)/shard_map/ppermute | solution.py:691
  64.6 1.3 %collective-permute-done.15.refs_3_ = bf16[16,1536]{1,0:T(8,128)(2,1)S(1)} collective-permute-done((bf16[16,1536]{1,0:T(8,128)(2,1)S(1)}, bf16[16,1536]{1,0:T(8,128)(2,1)S(1)}, u32[]{:S(2)}, u32[]{:S(2)}) %collective-permute-start.15) | collective-permute-done | bytes 49184 | tf_op jit(solution)/shard_map/ppermute | solution.py:691
  65.9 1.1 %collective-permute-done.14.refs_2_ = bf16[16,1536]{1,0:T(8,128)(2,1)S(1)} collective-permute-done((bf16[16,1536]{1,0:T(8,128)(2,1)S(1)}, bf16[16,1536]{1,0:T(8,128)(2,1)S(1)}, u32[]{:S(2)}, u32[]{:S(2)}) %collective-permute-start.14) | collective-permute-done | bytes 49184 | tf_op jit(solution)/shard_map/ppermute | solution.py:691
  (26 shorter events, 6.0 us)
Async XLA Ops:
  2.1 16.5 %collective-permute-start = (bf16[2,256,128]{2,1,0:T(8,128)(2,1)S(1)}, bf16[2,256,128]{2,1,0:T(8,128)(2,1)S(1)}, u32[]{:S(2)}, u32[]{:S(2)}) collective-permute-start(bf16[2,256,128]{2,1,0:T(8,128)(2,1)S(1)} %get-tuple-element.51), channel_id=1, source_target_pairs={{0,2},{1,3},{2,0},{3,1},{4,6},{5,7},{6,4},{7,5},{8,10},{9,11},{10,... | collective-permute-start | bytes 393224 | tf_op jit(solution)/shard_map/ppermute | solution.py:691
  5.2 13.4 %collective-permute-start.1 = (bf16[2,256,128]{2,1,0:T(8,128)(2,1)S(1)}, bf16[2,256,128]{2,1,0:T(8,128)(2,1)S(1)}, u32[]{:S(2)}, u32[]{:S(2)}) collective-permute-start(bf16[2,256,128]{2,1,0:T(8,128)(2,1)S(1)} %get-tuple-element.52), channel_id=1, source_target_pairs={{0,4},{1,5},{2,6},{3,7},{4,0},{5,1},{6,2},{7,3},{8,12},{9,13},{10,... | collective-permute-start | bytes 393224 | tf_op jit(solution)/shard_map/ppermute | solution.py:691
  7.8 10.8 %collective-permute-start.2 = (bf16[2,256,128]{2,1,0:T(8,128)(2,1)S(1)}, bf16[2,256,128]{2,1,0:T(8,128)(2,1)S(1)}, u32[]{:S(2)}, u32[]{:S(2)}) collective-permute-start(bf16[2,256,128]{2,1,0:T(8,128)(2,1)S(1)} %get-tuple-element.53), channel_id=1, source_target_pairs={{0,6},{1,7},{2,4},{3,5},{4,2},{5,3},{6,0},{7,1},{8,14},{9,15},{10,... | collective-permute-start | bytes 393224 | tf_op jit(solution)/shard_map/ppermute | solution.py:691
  15.2 17.3 %copy-start = (bf16[20,1536,256]{2,1,0:T(8,128)(2,1)S(1)}, bf16[20,1536,256]{2,1,0:T(8,128)(2,1)}, u32[]{:S(2)}) copy-start(bf16[20,1536,256]{2,1,0:T(8,128)(2,1)} %refs_6_.3) | copy-start | bytes 47185924
  18.8 13.6 %collective-permute-start.3 = (bf16[1024,128]{1,0:T(8,128)(2,1)S(1)}, bf16[1024,128]{1,0:T(8,128)(2,1)S(1)}, u32[]{:S(2)}, u32[]{:S(2)}) collective-permute-start(bf16[1024,128]{1,0:T(8,128)(2,1)S(1)} %get-tuple-element.56), channel_id=1, source_target_pairs={{0,1},{1,0},{2,3},{3,2},{4,5},{5,4},{6,7},{7,6},{8,9},{9,8},{10,11... | collective-permute-start | bytes 786440 | tf_op jit(solution)/shard_map/ppermute | solution.py:691
  34.1 6.7 %collective-permute-start.6 = (bf16[512,128]{1,0:T(8,128)(2,1)S(1)}, bf16[512,128]{1,0:T(8,128)(2,1)S(1)}, u32[]{:S(2)}, u32[]{:S(2)}) collective-permute-start(bf16[512,128]{1,0:T(8,128)(2,1)S(1)} %get-tuple-element.59.refs_0_), channel_id=1, source_target_pairs={{0,2},{1,3},{2,0},{3,1},{4,6},{5,7},{6,4},{7,5},{8,10},{9,11},{10,... | collective-permute-start | bytes 393224 | tf_op jit(solution)/shard_map/ppermute | solution.py:691
  34.2 8.8 %collective-permute-start.5 = (bf16[384,128]{1,0:T(8,128)(2,1)S(1)}, bf16[384,128]{1,0:T(8,128)(2,1)S(1)}, u32[]{:S(2)}, u32[]{:S(2)}) collective-permute-start(bf16[384,128]{1,0:T(8,128)(2,1)S(1)} %get-tuple-element.58.after_ref.refs_0_), channel_id=1, source_target_pairs={{0,6},{1,7},{2,4},{3,5},{4,2},{5,3},{6,0},{7,1},{8,14},{9,15},{10,... | collective-permute-start | bytes 294920 | tf_op jit(solution)/shard_map/ppermute | solution.py:691
  36.0 9.4 %collective-permute-start.4 = (bf16[384,128]{1,0:T(8,128)(2,1)S(1)}, bf16[384,128]{1,0:T(8,128)(2,1)S(1)}, u32[]{:S(2)}, u32[]{:S(2)}) collective-permute-start(bf16[384,128]{1,0:T(8,128)(2,1)S(1)} %get-tuple-element.58.after_ref.refs_0_), channel_id=1, source_target_pairs={{0,4},{1,5},{2,6},{3,7},{4,0},{5,1},{6,2},{7,3},{8,12},{9,13},{10,... | collective-permute-start | bytes 294920 | tf_op jit(solution)/shard_map/ppermute | solution.py:691
  37.6 8.9 %collective-permute-start.7 = (bf16[512,128]{1,0:T(8,128)(2,1)S(1)}, bf16[512,128]{1,0:T(8,128)(2,1)S(1)}, u32[]{:S(2)}, u32[]{:S(2)}) collective-permute-start(bf16[512,128]{1,0:T(8,128)(2,1)S(1)} %get-tuple-element.59.refs_0_), channel_id=1, source_target_pairs={{0,1},{1,0},{2,3},{3,2},{4,5},{5,4},{6,7},{7,6},{8,9},{9,8},{10,11... | collective-permute-start | bytes 393224 | tf_op jit(solution)/shard_map/ppermute | solution.py:691
  40.8 5.7 %collective-permute-start.8 = (bf16[512,128]{1,0:T(8,128)(2,1)S(1)}, bf16[512,128]{1,0:T(8,128)(2,1)S(1)}, u32[]{:S(2)}, u32[]{:S(2)}) collective-permute-start(bf16[512,128]{1,0:T(8,128)(2,1)S(1)} %collective-permute-done.6.after_ref.refs_2_), channel_id=1, source_target_pairs={{0,1},{1,0},{2,3},{3,2},{4,5},{5,4},{6,7},{7,6},{8,9},{9,8},{10,11... | collective-permute-start | bytes 393224 | tf_op jit(solution)/shard_map/ppermute | solution.py:691
  43.0 4.9 %collective-permute-start.10 = (bf16[384,128]{1,0:T(8,128)(2,1)S(1)}, bf16[384,128]{1,0:T(8,128)(2,1)S(1)}, u32[]{:S(2)}, u32[]{:S(2)}) collective-permute-start(bf16[384,128]{1,0:T(8,128)(2,1)S(1)} %collective-permute-done.5.after_ref.refs_2_), channel_id=1, source_target_pairs={{0,1},{1,0},{2,3},{3,2},{4,5},{5,4},{6,7},{7,6},{8,9},{9,8},{10,11... | collective-permute-start | bytes 294920 | tf_op jit(solution)/shard_map/ppermute | solution.py:691
  45.5 4.7 %collective-permute-start.9 = (bf16[384,128]{1,0:T(8,128)(2,1)S(1)}, bf16[384,128]{1,0:T(8,128)(2,1)S(1)}, u32[]{:S(2)}, u32[]{:S(2)}) collective-permute-start(bf16[384,128]{1,0:T(8,128)(2,1)S(1)} %collective-permute-done.4.after_ref.refs_0_), channel_id=1, source_target_pairs={{0,1},{1,0},{2,3},{3,2},{4,5},{5,4},{6,7},{7,6},{8,9},{9,8},{10,11... | collective-permute-start | bytes 294920 | tf_op jit(solution)/shard_map/ppermute | solution.py:691
  55.2 4.7 %collective-permute-start.11 = (bf16[2,16,1536]{2,1,0:T(8,128)(2,1)S(1)}, bf16[2,16,1536]{2,1,0:T(8,128)(2,1)S(1)}, u32[]{:S(2)}, u32[]{:S(2)}) collective-permute-start(bf16[2,16,1536]{2,1,0:T(8,128)(2,1)S(1)} %get-tuple-element.73), channel_id=1, source_target_pairs={{0,1},{1,0},{2,3},{3,2},{4,5},{5,4},{6,7},{7,6},{8,9},{9,8},{10,11... | collective-permute-start | bytes 294920 | tf_op jit(solution)/shard_map/ppermute | solution.py:691
  56.2 6.1 %collective-permute-start.12 = (bf16[2,16,1536]{2,1,0:T(8,128)(2,1)S(1)}, bf16[2,16,1536]{2,1,0:T(8,128)(2,1)S(1)}, u32[]{:S(2)}, u32[]{:S(2)}) collective-permute-start(bf16[2,16,1536]{2,1,0:T(8,128)(2,1)S(1)} %get-tuple-element.75), channel_id=1, source_target_pairs={{0,1},{1,0},{2,3},{3,2},{4,5},{5,4},{6,7},{7,6},{8,9},{9,8},{10,11... | collective-permute-start | bytes 294920 | tf_op jit(solution)/shard_map/ppermute | solution.py:691
  59.9 6.0 %collective-permute-start.15 = (bf16[16,1536]{1,0:T(8,128)(2,1)S(1)}, bf16[16,1536]{1,0:T(8,128)(2,1)S(1)}, u32[]{:S(2)}, u32[]{:S(2)}) collective-permute-start(bf16[16,1536]{1,0:T(8,128)(2,1)S(1)} %get-tuple-element.78), channel_id=1, source_target_pairs={{0,6},{1,7},{2,4},{3,5},{4,2},{5,3},{6,0},{7,1},{8,14},{9,15},{10,... | collective-permute-start | bytes 147464 | tf_op jit(solution)/shard_map/ppermute | solution.py:691
  61.0 6.0 %collective-permute-start.14 = (bf16[16,1536]{1,0:T(8,128)(2,1)S(1)}, bf16[16,1536]{1,0:T(8,128)(2,1)S(1)}, u32[]{:S(2)}, u32[]{:S(2)}) collective-permute-start(bf16[16,1536]{1,0:T(8,128)(2,1)S(1)} %get-tuple-element.74.after_ref), channel_id=1, source_target_pairs={{0,4},{1,5},{2,6},{3,7},{4,0},{5,1},{6,2},{7,3},{8,12},{9,13},{10,... | collective-permute-start | bytes 147464 | tf_op jit(solution)/shard_map/ppermute | solution.py:691
  62.4 4.6 %collective-permute-start.13 = (bf16[16,1536]{1,0:T(8,128)(2,1)S(1)}, bf16[16,1536]{1,0:T(8,128)(2,1)S(1)}, u32[]{:S(2)}, u32[]{:S(2)}) collective-permute-start(bf16[16,1536]{1,0:T(8,128)(2,1)S(1)} %get-tuple-element.77), channel_id=1, source_target_pairs={{0,2},{1,3},{2,0},{3,1},{4,6},{5,7},{6,4},{7,5},{8,10},{9,11},{10,... | collective-permute-start | bytes 147464 | tf_op jit(solution)/shard_map/ppermute | solution.py:691

commit v6 on v5

--- a/solution.py
+++ b/solution.py
@@ -16,6 +16,7 @@
 DRAFT = 64
 WIDE = 128
 STEP = 2
+READY = 12
 ORDER = (1, 3, 2)
 FETCHES = ((0, 1), (3,), (2,))
 
@@ -310,7 +311,7 @@
 
 def route_kernel(kv_width, after_ref, table_ref, pulled_ref, *refs):
     del after_ref
-    parts, (sent_ref, res_ref, turned_ref, kv_ref) = refs[:-4], refs[-4:]
+    parts, (sent_ref, res_ref, turned_ref, kv_ref) = refs[:-4][::-1], refs[-4:]
     rank = lax.axis_index("tp")
     other = 1 - lax.rem(rank, 2)
     size = parts[0].shape[1]
@@ -357,7 +358,7 @@
     count_ref, sem,
 ):
     del after_ref
-    copy = pltpu.make_async_copy(down_hbm, down_ref, sem)
+    copy = pltpu.make_async_copy(down_hbm.at[: down_ref.shape[0]], down_ref, sem)
     copy.start()
     slot_count = parents_ref.shape[0]
     reach_ref[...] = ancestor_rows(parents_ref)
@@ -382,7 +383,7 @@
 
 def attend_kernel(units_ref, table_ref, reach_ref, got_ref, res_ref, turned_ref, kv_ref, *refs):
     del units_ref
-    parts, (sent_ref, near_ref) = refs[:-2], refs[-2:]
+    parts, (sent_ref, near_ref) = refs[:-2][::-1], refs[-2:]
     slot_count = reach_ref.shape[0] // DRAFT
     sources = got_ref.shape[0]
     tok_dev = res_ref.shape[0]
@@ -554,9 +555,13 @@
     ]
 
 
-def early_kernel(rows, after_ref, weight_ref, *refs):
+def early_kernel(rows, after_ref, down_hbm, weight_ref, *refs):
     del after_ref
-    blocks, (hid_ref, attn_ref, residual_ref, x_ref) = refs[:-4], refs[-4:]
+    blocks, refs = refs[:-6], refs[-6:]
+    hid_ref, attn_ref, down_ref, residual_ref, x_ref, sem = refs
+    start = down_hbm.shape[0] - down_ref.shape[0]
+    copy = pltpu.make_async_copy(down_hbm.at[start:], down_ref, sem)
+    copy.start()
     group_rows = hid_ref.shape[0]
     residual_ref[...] = jnp.zeros_like(residual_ref)
     width = x_ref.shape[1] * 2 // len(blocks)
@@ -569,10 +574,11 @@
     hid_ref[...] = residual_ref[...] + jnp.dot(
         x_ref[...], weight_ref[...], preferred_element_type=jnp.float32
     )
+    copy.wait()
 
 
 def expert_kernel(
-    rows, count_ref, router_ref, gain_ref, down_ref, before_ref, part_ref, *refs
+    rows, count_ref, router_ref, gain_ref, down_ref, rest_ref, before_ref, part_ref, *refs
 ):
     refs, late = refs[:-8], refs[-8:]
     far_ref, hid_ref, hidden_ref, attn_ref, x_ref, normed_ref, share_ref, residual_ref = late
@@ -591,7 +597,7 @@
     attn_ref[...] = part_ref[...]
     residual_ref[...] = jnp.zeros_like(residual_ref)
     hidden, width = before_ref[...], x_ref.shape[1] // (pairs - first)
-    for q, k in enumerate(range(first, pairs)):
+    for q, k in enumerate(reversed(range(first, pairs))):
         heads = join_heads(k, rows, group_rows, blocks[2 * q], blocks[2 * q + 1], residual_ref)
         x_ref[:, q * width : (q + 1) * width] = heads
         keep_own(k, x_ref, q * width, attn_ref)
@@ -624,9 +630,11 @@
         gate, up = both[:, :unit_width], both[:, unit_width:]
         return (gate / (1.0 + jnp.exp(-gate)) * up * share_ref[u]).astype(bf16)
 
+    ready = down_ref.shape[0] // STEP
     for i in range(units // STEP):
         act = jnp.concatenate([one_unit(i * STEP + k) for k in range(STEP)], axis=1)
-        down = down_ref[i * STEP : (i + 1) * STEP].reshape(STEP * unit_width, model)
+        ref, at = (down_ref, i) if i < ready else (rest_ref, i - ready)
+        down = ref[at * STEP : (at + 1) * STEP].reshape(STEP * unit_width, model)
         part = jnp.dot(act, down, preferred_element_type=f32)
         hid_ref[...] = part if i == 0 else hid_ref[...] + part
     for k in range(far_ref.shape[0]):
@@ -777,10 +785,12 @@
     parts = [parts[0]] + [swap(parts[k], 2 * k) for k in range(1, pairs)]
     pulled = lax.all_gather(joined, "req", axis=0)
     nodes = slot_count * DRAFT
-    down_weight, reach, chosen, count = pl.pallas_call(
+    units = gate_up.shape[0]
+    ready = READY * units // 20 // STEP * STEP
+    down_ready, reach, chosen, count = pl.pallas_call(
         tree_kernel,
         out_shape=(
-            pltpu.VMEM(down_weight.shape, bf16),
+            pltpu.VMEM((ready,) + down_weight.shape[1:], bf16),
             jax.ShapeDtypeStruct((nodes, nodes), f32),
             jax.ShapeDtypeStruct((slot_count, DRAFT, DRAFT), bf16),
             jax.ShapeDtypeStruct((group_rows, router_weight.shape[1]), f32),
@@ -806,7 +816,7 @@
         compiler_params=params(),
         cost_estimate=cost(4),
         name="route",
-    )(down_weight, table, pulled, *parts)
+    )(down_ready, table, pulled, *parts[::-1])
     turned = swap(turned, 1)
     packed = lax.all_to_all(packed, "tp", 0, 0, tiled=True)
     gate_up = pltpu.with_memory_space_constraint(gate_up, pltpu.VMEM)
@@ -822,8 +832,7 @@
         compiler_params=params(),
         cost_estimate=cost(8),
         name="attend",
-    )(gate_up, table, reach, packed, own_res, turned, own_kv, *parts)
-    units = gate_up.shape[0]
+    )(gate_up, table, reach, packed, own_res, turned, own_kv, *parts[::-1])
     reached = [swap(near_block, 2)] + [swap(block, 2 * k) for k in range(2, pairs)]
     weights, after = [], block
     rows = out_weight.shape[0] // pairs
@@ -834,22 +843,24 @@
         weights.append(weight)
     blocks = [block, swap(near_block, 1)]
     blocks += [a for got in reached for a in (got, swap(got, 1))]
-    before, attn_part = pl.pallas_call(
+    before, attn_part, down_rest = pl.pallas_call(
         functools.partial(early_kernel, block_rows),
         out_shape=(
             jax.ShapeDtypeStruct((group_rows, model), f32),
             pltpu.VMEM(queries.shape, bf16),
+            pltpu.VMEM((units - ready,) + down_weight.shape[1:], bf16),
         ),
-        in_specs=spaces("av" + "v" * pairs),
-        out_specs=tuple(spaces("vv")),
+        in_specs=spaces("aav" + "v" * pairs),
+        out_specs=tuple(spaces("vvv")),
         scratch_shapes=[
             pltpu.VMEM((group_rows, model), f32),
             pltpu.VMEM((group_rows, HEADS * HEAD // 2), bf16),
+            dma,
         ],
         compiler_params=params(),
         cost_estimate=cost(4),
         name="early",
-    )(after, weights[0], *blocks[:pairs])
+    )(after, *in_hbm(down_weight), weights[0], *blocks[:pairs])
     accepted = pl.pallas_call(
         functools.partial(accept_kernel, block_rows),
         out_shape=pltpu.VMEM(new_kv.shape, bf16),
@@ -868,7 +879,7 @@
             jax.ShapeDtypeStruct((tok_dev, model), f32),
             pltpu.VMEM(queries.shape, bf16),
         ),
-        in_specs=spaces("v" * (6 + pairs + pairs // 2 + len(unit_weights))),
+        in_specs=spaces("v" * (7 + pairs + pairs // 2 + len(unit_weights))),
         out_specs=tuple(spaces("vvvv")),
         scratch_shapes=[
             pltpu.VMEM((group_rows, HEADS * HEAD // 2), bf16),
@@ -882,12 +893,13 @@
         count,
         router,
         gain,
-        down_weight,
+        down_ready,
+        down_rest,
         before,
         attn_part,
-        *blocks[pairs:],
+        *[a for k in reversed(range(pairs // 2, pairs)) for a in blocks[2 * k : 2 * k + 2]],
+        weights[1],
         weights[2],
-        weights[1],
         *unit_weights,
     )
     far = swap(far, 1)
@@ -932,7 +944,7 @@
         out_specs=tuple(spaces("vvv")),
         compiler_params=params(),
         name="finish",
-    )(attn_own, accepted, *sums)
+    )(attn_own, accepted, sums[0], *sums[:0:-1])
 
 
 def per_device(queries, new_kv, residual, placement, *rest):

time: 67.9 us -> 67.2 us (0.990)
  blocking collectives: 19.5 us -> 18.4 us
  Pallas kernels: 17.4 us -> 18.1 us
    pallas_call x1, Pallas kernels: 0.59 us -> 2.19 us  [per_device_packed(): pl.pallas_call(functools.partial(early_kernel, block_rows), out_shape=(ja...]
    pallas_call x1, Pallas kernels: 3.39 us -> 2.35 us  [per_device_packed(): pl.pallas_call(tree_kernel, out_shape=(pltpu.VMEM((ready,) + down_weight....]
    all_to_all x1, blocking collectives: 12.1 us -> 11.1 us  [per_device_packed(): packed = lax.all_to_all(packed, 'tp', 0, 0, tiled=True)]
  transfers between devices with their start and end apart: 16 -> 16, of which waited for: 6 -> 8; matrix products, arithmetic and copies ran while one was open for 0% -> 0% of each run, Pallas kernels for 12% -> 13%
where the time goes in v6:
time: 67.2 us; the launch traced here: 66.9 us
  starting transfers between devices  20.8 us (31%)
  blocking collectives  18.4 us (27%)
  Pallas kernels  18.1 us (27%)
  waiting for transfers between devices  8.83 us (13%)
  between operations  0.76 us (1%)
    ppermute x16, starting transfers between devices, swap(): return lax.ppermute(rows, 'tp', [(i, i ^ mask) for i in range(count)])  20.8 us
    all_to_all x1, blocking collectives, per_device_packed(): packed = lax.all_to_all(packed, 'tp', 0, 0, tiled=True)  11.1 us
    ppermute x16, waiting for transfers between devices, swap(): return lax.ppermute(rows, 'tp', [(i, i ^ mask) for i in range(count)])  8.83 us
    all_gather x1, blocking collectives, per_device_packed(): pulled = lax.all_gather(joined, 'req', axis=0)  7.33 us
    pallas_call x1, Pallas kernels, per_device_packed(): pl.pallas_call(functools.partial(expert_kernel, block_rows), out_shape=(j...  5.02 us
    pallas_call x3, Pallas kernels, fetch(): pl.pallas_call(functools.partial(fetch_kernel, picks), out_shape=pltpu.VM...  4.21 us
    pallas_call x1, Pallas kernels, per_device_packed(): pl.pallas_call(tree_kernel, out_shape=(pltpu.VMEM((ready,) + down_weight....  2.35 us
    pallas_call x1, Pallas kernels, per_device_packed(): pl.pallas_call(functools.partial(early_kernel, block_rows), out_shape=(ja...  2.19 us
  transfers between devices with their start and end apart: 16, of which 8 were waited for; matrix products, arithmetic and copies ran while one was open for 0% of the time, Pallas kernels for 13%

profile of v6, /device:TPU:0, one launch (start us, length us, event | category | flops | bytes accessed | tf_op | source)
XLA Modules:
  0.0 66.9 jit_solution(9758370477258182427)
XLA Ops:
  0.6 1.6 %split.1 = (bf16[2,256,128]{2,1,0:T(8,128)(2,1)S(1)}, bf16[2,256,128]{2,1,0:T(8,128)(2,1)S(1)}, bf16[2,256,128]{2,1,0:T(8,128)(2,1)S(1)}, bf16[2,256,128]{2,1,0:...) custom-call(s32[2]{0:T(128)} %bitcast.10, ...), custom_call_target="tpu_custom_call" | custom-call | bytes 4194304 | tf_op jit(solution)/shard_map/split/pallas_call | solution.py:760
  2.3 5.1 %collective-permute-start = (bf16[2,256,128]{2,1,0:T(8,128)(2,1)S(1)}, bf16[2,256,128]{2,1,0:T(8,128)(2,1)S(1)}, u32[]{:S(2)}, u32[]{:S(2)}) collective-permute-start(bf16[2,256,128]{2,1,0:T(8,128)(2,1)S(1)} %get-tuple-element.51), channel_id=1, source_target_pairs={{0,6},{1,7},{2,4},{3,5},{4,2},{5,3},{6,0},{7,1},{8,14},{9,15},{10,... | collective-permute-start | bytes 393224 | tf_op jit(solution)/shard_map/ppermute | solution.py:699
  8.0 7.3 %all-gather = bf16[64,4096]{1,0:T(8,128)(2,1)S(1)} all-gather(bf16[16,4096]{1,0:T(8,128)(2,1)S(1)} %get-tuple-element.42), channel_id=2, replica_groups=mesh['req'=4,'tp'=8] {'req'}, dimensions={0}, use_global_device_ids=true | all-gather | bytes 655360 | tf_op jit(solution)/shard_map/all_gather | solution.py:786
  15.3 2.3 %tree.1 = (bf16[12,128,1536]{2,1,0:T(8,128)(2,1)S(1)}, f32[128,128]{1,0:T(8,128)S(1)}, bf16[2,64,64]{2,1,0:T(8,128)(2,1)S(1)}, f32[128,40]{1,0:T(8,128)S(1)}) custom-call(bf16[4,16,4096]{2,1,0:T(8,128)(2,1)S(1)} %bitcast.5, bf16[20,128,1536]{2,1,0:T(8,128)(2,1)} %down_hbm.3, f32[8,128]{1,0:T(8,128)S(1)} %get-tuple-element.43.table_ref, ...), custom_call_target="tpu_custom_call" | custom-call | bytes 8388608 | tf_op jit(solution)/shard_map/tree/pallas_call | solution.py:790
  18.7 1.6 %collective-permute-start.3 = (bf16[1024,128]{1,0:T(8,128)(2,1)S(1)}, bf16[1024,128]{1,0:T(8,128)(2,1)S(1)}, u32[]{:S(2)}, u32[]{:S(2)}) collective-permute-start(bf16[1024,128]{1,0:T(8,128)(2,1)S(1)} %get-tuple-element.57), channel_id=1, source_target_pairs={{0,1},{1,0},{2,3},{3,2},{4,5},{5,4},{6,7},{7,6},{8,9},{9,8},{10,11... | collective-permute-start | bytes 786440 | tf_op jit(solution)/shard_map/ppermute | solution.py:699
  20.2 11.1 %all_to_all.5.got_ref = bf16[8,48,128]{2,1,0:T(8,128)(2,1)S(1)} all-to-all(bf16[8,48,128]{2,1,0:T(8,128)(2,1)S(1)} %get-tuple-element.55), channel_id=1, replica_groups=mesh['req'=4,'tp'=8] {'tp'}, dimensions={0} | all-to-all | bytes 196608 | tf_op jit(solution)/shard_map/all_to_all | solution.py:821
  31.3 1.6 %attend.1 = (bf16[384,128]{1,0:T(8,128)(2,1)S(1)}, bf16[512,128]{1,0:T(8,128)(2,1)S(1)}) custom-call(bf16[20,1536,256]{2,1,0:T(8,128)(2,1)S(1)} %copy-done, f32[8,128]{1,0:T(8,128)S(1)} %get-tuple-element.43.table_ref, f32[128,128]{1,0:T(8,128)S(1)} %get-tuple-element.50.reach_ref, bf16[8,48,128]{2,1,0:T(8,128)(2,1)S(1)} %all_to_all.5.got_ref, ...), custom_call_target="tpu_custom_call" | custom-call | bytes 8388608 | tf_op jit(solution)/shard_map/attend/pallas_call | solution.py:824
  33.0 1.9 %collective-permute-start.5 = (bf16[384,128]{1,0:T(8,128)(2,1)S(1)}, bf16[384,128]{1,0:T(8,128)(2,1)S(1)}, u32[]{:S(2)}, u32[]{:S(2)}) collective-permute-start(bf16[384,128]{1,0:T(8,128)(2,1)S(1)} %get-tuple-element.59.after_ref.refs_0_), channel_id=1, source_target_pairs={{0,6},{1,7},{2,4},{3,5},{4,2},{5,3},{6,0},{7,1},{8,14},{9,15},{10,... | collective-permute-start | bytes 294920 | tf_op jit(solution)/shard_map/ppermute | solution.py:699
  34.9 1.6 %collective-permute-start.4 = (bf16[384,128]{1,0:T(8,128)(2,1)S(1)}, bf16[384,128]{1,0:T(8,128)(2,1)S(1)}, u32[]{:S(2)}, u32[]{:S(2)}) collective-permute-start(bf16[384,128]{1,0:T(8,128)(2,1)S(1)} %get-tuple-element.59.after_ref.refs_0_), channel_id=1, source_target_pairs={{0,4},{1,5},{2,6},{3,7},{4,0},{5,1},{6,2},{7,3},{8,12},{9,13},{10,... | collective-permute-start | bytes 294920 | tf_op jit(solution)/shard_map/ppermute | solution.py:699
  36.8 1.6 %fetch.3.weight_ref = bf16[768,1536]{1,0:T(8,128)(2,1)S(1)} custom-call(bf16[384,128]{1,0:T(8,128)(2,1)S(1)} %get-tuple-element.59.after_ref.refs_0_, bf16[1536,1536]{1,0:T(8,128)(2,1)} %source_ref.5), custom_call_target="tpu_custom_call" | custom-call | bytes 2097152 | tf_op jit(solution)/shard_map/fetch/pallas_call | solution.py:704
  38.4 1.2 %collective-permute-done.6.after_ref.refs_2_ = bf16[512,128]{1,0:T(8,128)(2,1)S(1)} collective-permute-done((bf16[512,128]{1,0:T(8,128)(2,1)S(1)}, bf16[512,128]{1,0:T(8,128)(2,1)S(1)}, u32[]{:S(2)}, u32[]{:S(2)}) %collective-permute-start.6) | collective-permute-done | bytes 131104 | tf_op jit(solution)/shard_map/ppermute | solution.py:699
  40.5 1.3 %fetch.4.refs_4_ = bf16[384,1536]{1,0:T(8,128)(2,1)S(1)} custom-call(bf16[512,128]{1,0:T(8,128)(2,1)S(1)} %collective-permute-done.6.after_ref.refs_2_, bf16[1536,1536]{1,0:T(8,128)(2,1)} %source_ref.5), custom_call_target="tpu_custom_call" | custom-call | bytes 1048576 | tf_op jit(solution)/shard_map/fetch/pallas_call | solution.py:704
  41.8 1.3 %fetch.5.refs_5_ = bf16[384,1536]{1,0:T(8,128)(2,1)S(1)} custom-call(bf16[384,128]{1,0:T(8,128)(2,1)S(1)} %collective-permute-done.5.after_ref.refs_0_, bf16[1536,1536]{1,0:T(8,128)(2,1)} %source_ref.5), custom_call_target="tpu_custom_call" | custom-call | bytes 1048576 | tf_op jit(solution)/shard_map/fetch/pallas_call | solution.py:704
  43.1 1.2 %collective-permute-start.9 = (bf16[384,128]{1,0:T(8,128)(2,1)S(1)}, bf16[384,128]{1,0:T(8,128)(2,1)S(1)}, u32[]{:S(2)}, u32[]{:S(2)}) collective-permute-start(bf16[384,128]{1,0:T(8,128)(2,1)S(1)} %collective-permute-done.5.after_ref.refs_0_), channel_id=1, source_target_pairs={{0,1},{1,0},{2,3},{3,2},{4,5},{5,4},{6,7},{7,6},{8,9},{9,8},{10,11... | collective-permute-start | bytes 294920 | tf_op jit(solution)/shard_map/ppermute | solution.py:699
  45.6 2.2 %early.1 = (f32[128,1536]{1,0:T(8,128)S(1)}, bf16[16,1536]{1,0:T(8,128)(2,1)S(1)}, bf16[8,128,1536]{2,1,0:T(8,128)(2,1)S(1)}) custom-call(bf16[384,128]{1,0:T(8,128)(2,1)S(1)} %collective-permute-done.4.after_ref.refs_2_, bf16[20,128,1536]{2,1,0:T(8,128)(2,1)} %down_hbm.3, bf16[768,1536]{1,0:T(8,128)(2,1)S(1)} %fetch.3.weight_ref, ...), custom_call_target="tpu_custom_call" | custom-call | bytes 4194304 | tf_op jit(solution)/shard_map/early/pallas_call | solution.py:846
  47.8 1.1 %collective-permute-done.10.refs_3_ = bf16[384,128]{1,0:T(8,128)(2,1)S(1)} collective-permute-done((bf16[384,128]{1,0:T(8,128)(2,1)S(1)}, bf16[384,128]{1,0:T(8,128)(2,1)S(1)}, u32[]{:S(2)}, u32[]{:S(2)}) %collective-permute-start.10) | collective-permute-done | bytes 98336 | tf_op jit(solution)/shard_map/ppermute | solution.py:699
  49.0 5.0 %experts.1 = (bf16[2,16,1536]{2,1,0:T(8,128)(2,1)S(1)}, f32[128,1536]{1,0:T(8,128)S(1)}, f32[16,1536]{1,0:T(8,128)S(1)}, bf16[16,1536]{1,0:T(8,128)(2,1)S(1)}) custom-call(f32[128,40]{1,0:T(8,128)S(1)} %get-tuple-element.46.count_ref, bf16[40,1536]{1,0:T(8,128)(2,1)S(1)} %get-tuple-element.47.router_ref, f32[12,128]{1,0:T(8,128)S(1)} %get-tuple-element.48.gain_ref, ...), custom_call_target="tpu_custom_call" | custom-call | tf_op jit(solution)/shard_map/experts/pallas_call | solution.py:874
  54.0 1.1 %collective-permute-start.11 = (bf16[2,16,1536]{2,1,0:T(8,128)(2,1)S(1)}, bf16[2,16,1536]{2,1,0:T(8,128)(2,1)S(1)}, u32[]{:S(2)}, u32[]{:S(2)}) collective-permute-start(bf16[2,16,1536]{2,1,0:T(8,128)(2,1)S(1)} %get-tuple-element.75), channel_id=1, source_target_pairs={{0,1},{1,0},{2,3},{3,2},{4,5},{5,4},{6,7},{7,6},{8,9},{9,8},{10,11... | collective-permute-start | bytes 294920 | tf_op jit(solution)/shard_map/ppermute | solution.py:699
  56.2 2.5 %collective-permute-done.11.got_ref = bf16[2,16,1536]{2,1,0:T(8,128)(2,1)S(1)} collective-permute-done((bf16[2,16,1536]{2,1,0:T(8,128)(2,1)S(1)}, bf16[2,16,1536]{2,1,0:T(8,128)(2,1)S(1)}, u32[]{:S(2)}, u32[]{:S(2)}) %collective-permute-start.11) | collective-permute-done | bytes 98336 | tf_op jit(solution)/shard_map/ppermute | solution.py:699
  58.7 1.1 %collective-permute-start.13 = (bf16[16,1536]{1,0:T(8,128)(2,1)S(1)}, bf16[16,1536]{1,0:T(8,128)(2,1)S(1)}, u32[]{:S(2)}, u32[]{:S(2)}) collective-permute-start(bf16[16,1536]{1,0:T(8,128)(2,1)S(1)} %get-tuple-element.79), channel_id=1, source_target_pairs={{0,6},{1,7},{2,4},{3,5},{4,2},{5,3},{6,0},{7,1},{8,14},{9,15},{10,... | collective-permute-start | bytes 147464 | tf_op jit(solution)/shard_map/ppermute | solution.py:699
  59.8 1.8 %collective-permute-start.14 = (bf16[16,1536]{1,0:T(8,128)(2,1)S(1)}, bf16[16,1536]{1,0:T(8,128)(2,1)S(1)}, u32[]{:S(2)}, u32[]{:S(2)}) collective-permute-start(bf16[16,1536]{1,0:T(8,128)(2,1)S(1)} %get-tuple-element.76.after_ref), channel_id=1, source_target_pairs={{0,4},{1,5},{2,6},{3,7},{4,0},{5,1},{6,2},{7,3},{8,12},{9,13},{10,... | collective-permute-start | bytes 147464 | tf_op jit(solution)/shard_map/ppermute | solution.py:699
  61.7 1.6 %collective-permute-start.15 = (bf16[16,1536]{1,0:T(8,128)(2,1)S(1)}, bf16[16,1536]{1,0:T(8,128)(2,1)S(1)}, u32[]{:S(2)}, u32[]{:S(2)}) collective-permute-start(bf16[16,1536]{1,0:T(8,128)(2,1)S(1)} %get-tuple-element.80), channel_id=1, source_target_pairs={{0,2},{1,3},{2,0},{3,1},{4,6},{5,7},{6,4},{7,5},{8,10},{9,11},{10,... | collective-permute-start | bytes 147464 | tf_op jit(solution)/shard_map/ppermute | solution.py:699
  63.4 1.3 %collective-permute-done.13.refs_1_ = bf16[16,1536]{1,0:T(8,128)(2,1)S(1)} collective-permute-done((bf16[16,1536]{1,0:T(8,128)(2,1)S(1)}, bf16[16,1536]{1,0:T(8,128)(2,1)S(1)}, u32[]{:S(2)}, u32[]{:S(2)}) %collective-permute-start.13) | collective-permute-done | bytes 49184 | tf_op jit(solution)/shard_map/ppermute | solution.py:699
  64.7 1.1 %collective-permute-done.14.refs_2_ = bf16[16,1536]{1,0:T(8,128)(2,1)S(1)} collective-permute-done((bf16[16,1536]{1,0:T(8,128)(2,1)S(1)}, bf16[16,1536]{1,0:T(8,128)(2,1)S(1)}, u32[]{:S(2)}, u32[]{:S(2)}) %collective-permute-start.14) | collective-permute-done | bytes 49184 | tf_op jit(solution)/shard_map/ppermute | solution.py:699
  (26 shorter events, 6.6 us)
Async XLA Ops:
  0.6 30.7 %copy-start = (bf16[20,1536,256]{2,1,0:T(8,128)(2,1)S(1)}, bf16[20,1536,256]{2,1,0:T(8,128)(2,1)}, u32[]{:S(2)}) copy-start(bf16[20,1536,256]{2,1,0:T(8,128)(2,1)} %refs_6_.3) | copy-start | bytes 47185924
  2.3 15.4 %collective-permute-start = (bf16[2,256,128]{2,1,0:T(8,128)(2,1)S(1)}, bf16[2,256,128]{2,1,0:T(8,128)(2,1)S(1)}, u32[]{:S(2)}, u32[]{:S(2)}) collective-permute-start(bf16[2,256,128]{2,1,0:T(8,128)(2,1)S(1)} %get-tuple-element.51), channel_id=1, source_target_pairs={{0,6},{1,7},{2,4},{3,5},{4,2},{5,3},{6,0},{7,1},{8,14},{9,15},{10,... | collective-permute-start | bytes 393224 | tf_op jit(solution)/shard_map/ppermute | solution.py:699
  7.4 11.1 %collective-permute-start.1 = (bf16[2,256,128]{2,1,0:T(8,128)(2,1)S(1)}, bf16[2,256,128]{2,1,0:T(8,128)(2,1)S(1)}, u32[]{:S(2)}, u32[]{:S(2)}) collective-permute-start(bf16[2,256,128]{2,1,0:T(8,128)(2,1)S(1)} %get-tuple-element.52), channel_id=1, source_target_pairs={{0,4},{1,5},{2,6},{3,7},{4,0},{5,1},{6,2},{7,3},{8,12},{9,13},{10,... | collective-permute-start | bytes 393224 | tf_op jit(solution)/shard_map/ppermute | solution.py:699
  7.4 11.1 %collective-permute-start.2 = (bf16[2,256,128]{2,1,0:T(8,128)(2,1)S(1)}, bf16[2,256,128]{2,1,0:T(8,128)(2,1)S(1)}, u32[]{:S(2)}, u32[]{:S(2)}) collective-permute-start(bf16[2,256,128]{2,1,0:T(8,128)(2,1)S(1)} %get-tuple-element.53), channel_id=1, source_target_pairs={{0,2},{1,3},{2,0},{3,1},{4,6},{5,7},{6,4},{7,5},{8,10},{9,11},{10,... | collective-permute-start | bytes 393224 | tf_op jit(solution)/shard_map/ppermute | solution.py:699
  18.7 12.6 %collective-permute-start.3 = (bf16[1024,128]{1,0:T(8,128)(2,1)S(1)}, bf16[1024,128]{1,0:T(8,128)(2,1)S(1)}, u32[]{:S(2)}, u32[]{:S(2)}) collective-permute-start(bf16[1024,128]{1,0:T(8,128)(2,1)S(1)} %get-tuple-element.57), channel_id=1, source_target_pairs={{0,1},{1,0},{2,3},{3,2},{4,5},{5,4},{6,7},{7,6},{8,9},{9,8},{10,11... | collective-permute-start | bytes 786440 | tf_op jit(solution)/shard_map/ppermute | solution.py:699
  32.9 6.7 %collective-permute-start.6 = (bf16[512,128]{1,0:T(8,128)(2,1)S(1)}, bf16[512,128]{1,0:T(8,128)(2,1)S(1)}, u32[]{:S(2)}, u32[]{:S(2)}) collective-permute-start(bf16[512,128]{1,0:T(8,128)(2,1)S(1)} %get-tuple-element.60.refs_0_), channel_id=1, source_target_pairs={{0,2},{1,3},{2,0},{3,1},{4,6},{5,7},{6,4},{7,5},{8,10},{9,11},{10,... | collective-permute-start | bytes 393224 | tf_op jit(solution)/shard_map/ppermute | solution.py:699
  33.0 8.8 %collective-permute-start.5 = (bf16[384,128]{1,0:T(8,128)(2,1)S(1)}, bf16[384,128]{1,0:T(8,128)(2,1)S(1)}, u32[]{:S(2)}, u32[]{:S(2)}) collective-permute-start(bf16[384,128]{1,0:T(8,128)(2,1)S(1)} %get-tuple-element.59.after_ref.refs_0_), channel_id=1, source_target_pairs={{0,6},{1,7},{2,4},{3,5},{4,2},{5,3},{6,0},{7,1},{8,14},{9,15},{10,... | collective-permute-start | bytes 294920 | tf_op jit(solution)/shard_map/ppermute | solution.py:699
  34.9 9.5 %collective-permute-start.4 = (bf16[384,128]{1,0:T(8,128)(2,1)S(1)}, bf16[384,128]{1,0:T(8,128)(2,1)S(1)}, u32[]{:S(2)}, u32[]{:S(2)}) collective-permute-start(bf16[384,128]{1,0:T(8,128)(2,1)S(1)} %get-tuple-element.59.after_ref.refs_0_), channel_id=1, source_target_pairs={{0,4},{1,5},{2,6},{3,7},{4,0},{5,1},{6,2},{7,3},{8,12},{9,13},{10,... | collective-permute-start | bytes 294920 | tf_op jit(solution)/shard_map/ppermute | solution.py:699
  36.5 8.8 %collective-permute-start.7 = (bf16[512,128]{1,0:T(8,128)(2,1)S(1)}, bf16[512,128]{1,0:T(8,128)(2,1)S(1)}, u32[]{:S(2)}, u32[]{:S(2)}) collective-permute-start(bf16[512,128]{1,0:T(8,128)(2,1)S(1)} %get-tuple-element.60.refs_0_), channel_id=1, source_target_pairs={{0,1},{1,0},{2,3},{3,2},{4,5},{5,4},{6,7},{7,6},{8,9},{9,8},{10,11... | collective-permute-start | bytes 393224 | tf_op jit(solution)/shard_map/ppermute | solution.py:699
  39.7 6.0 %collective-permute-start.8 = (bf16[512,128]{1,0:T(8,128)(2,1)S(1)}, bf16[512,128]{1,0:T(8,128)(2,1)S(1)}, u32[]{:S(2)}, u32[]{:S(2)}) collective-permute-start(bf16[512,128]{1,0:T(8,128)(2,1)S(1)} %collective-permute-done.6.after_ref.refs_2_), channel_id=1, source_target_pairs={{0,1},{1,0},{2,3},{3,2},{4,5},{5,4},{6,7},{7,6},{8,9},{9,8},{10,11... | collective-permute-start | bytes 393224 | tf_op jit(solution)/shard_map/ppermute | solution.py:699
  43.1 4.7 %collective-permute-start.9 = (bf16[384,128]{1,0:T(8,128)(2,1)S(1)}, bf16[384,128]{1,0:T(8,128)(2,1)S(1)}, u32[]{:S(2)}, u32[]{:S(2)}) collective-permute-start(bf16[384,128]{1,0:T(8,128)(2,1)S(1)} %collective-permute-done.5.after_ref.refs_0_), channel_id=1, source_target_pairs={{0,1},{1,0},{2,3},{3,2},{4,5},{5,4},{6,7},{7,6},{8,9},{9,8},{10,11... | collective-permute-start | bytes 294920 | tf_op jit(solution)/shard_map/ppermute | solution.py:699
  44.3 4.6 %collective-permute-start.10 = (bf16[384,128]{1,0:T(8,128)(2,1)S(1)}, bf16[384,128]{1,0:T(8,128)(2,1)S(1)}, u32[]{:S(2)}, u32[]{:S(2)}) collective-permute-start(bf16[384,128]{1,0:T(8,128)(2,1)S(1)} %collective-permute-done.4.after_ref.refs_2_), channel_id=1, source_target_pairs={{0,1},{1,0},{2,3},{3,2},{4,5},{5,4},{6,7},{7,6},{8,9},{9,8},{10,11... | collective-permute-start | bytes 294920 | tf_op jit(solution)/shard_map/ppermute | solution.py:699
  54.0 4.7 %collective-permute-start.11 = (bf16[2,16,1536]{2,1,0:T(8,128)(2,1)S(1)}, bf16[2,16,1536]{2,1,0:T(8,128)(2,1)S(1)}, u32[]{:S(2)}, u32[]{:S(2)}) collective-permute-start(bf16[2,16,1536]{2,1,0:T(8,128)(2,1)S(1)} %get-tuple-element.75), channel_id=1, source_target_pairs={{0,1},{1,0},{2,3},{3,2},{4,5},{5,4},{6,7},{7,6},{8,9},{9,8},{10,11... | collective-permute-start | bytes 294920 | tf_op jit(solution)/shard_map/ppermute | solution.py:699
  55.2 6.5 %collective-permute-start.12 = (bf16[2,16,1536]{2,1,0:T(8,128)(2,1)S(1)}, bf16[2,16,1536]{2,1,0:T(8,128)(2,1)S(1)}, u32[]{:S(2)}, u32[]{:S(2)}) collective-permute-start(bf16[2,16,1536]{2,1,0:T(8,128)(2,1)S(1)} %get-tuple-element.77), channel_id=1, source_target_pairs={{0,1},{1,0},{2,3},{3,2},{4,5},{5,4},{6,7},{7,6},{8,9},{9,8},{10,11... | collective-permute-start | bytes 294920 | tf_op jit(solution)/shard_map/ppermute | solution.py:699
  58.7 6.0 %collective-permute-start.13 = (bf16[16,1536]{1,0:T(8,128)(2,1)S(1)}, bf16[16,1536]{1,0:T(8,128)(2,1)S(1)}, u32[]{:S(2)}, u32[]{:S(2)}) collective-permute-start(bf16[16,1536]{1,0:T(8,128)(2,1)S(1)} %get-tuple-element.79), channel_id=1, source_target_pairs={{0,6},{1,7},{2,4},{3,5},{4,2},{5,3},{6,0},{7,1},{8,14},{9,15},{10,... | collective-permute-start | bytes 147464 | tf_op jit(solution)/shard_map/ppermute | solution.py:699
  59.8 5.9 %collective-permute-start.14 = (bf16[16,1536]{1,0:T(8,128)(2,1)S(1)}, bf16[16,1536]{1,0:T(8,128)(2,1)S(1)}, u32[]{:S(2)}, u32[]{:S(2)}) collective-permute-start(bf16[16,1536]{1,0:T(8,128)(2,1)S(1)} %get-tuple-element.76.after_ref), channel_id=1, source_target_pairs={{0,4},{1,5},{2,6},{3,7},{4,0},{5,1},{6,2},{7,3},{8,12},{9,13},{10,... | collective-permute-start | bytes 147464 | tf_op jit(solution)/shard_map/ppermute | solution.py:699
  61.7 4.6 %collective-permute-start.15 = (bf16[16,1536]{1,0:T(8,128)(2,1)S(1)}, bf16[16,1536]{1,0:T(8,128)(2,1)S(1)}, u32[]{:S(2)}, u32[]{:S(2)}) collective-permute-start(bf16[16,1536]{1,0:T(8,128)(2,1)S(1)} %get-tuple-element.80), channel_id=1, source_target_pairs={{0,2},{1,3},{2,0},{3,1},{4,6},{5,7},{6,4},{7,5},{8,10},{9,11},{10,... | collective-permute-start | bytes 147464 | tf_op jit(solution)/shard_map/ppermute | solution.py:699

commit v7 on v6

--- a/solution.py
+++ b/solution.py
@@ -16,7 +16,7 @@
 DRAFT = 64
 WIDE = 128
 STEP = 2
-READY = 12
+CUTS = (6, 8, 10, 12)
 ORDER = (1, 3, 2)
 FETCHES = ((0, 1), (3,), (2,))
 
@@ -309,8 +309,8 @@
     return jnp.max(table_ref[row : row + 1, :]).astype(jnp.int32)
 
 
-def route_kernel(kv_width, after_ref, table_ref, pulled_ref, *refs):
-    del after_ref
+def route_kernel(kv_width, after_ref, weight_hbm, table_ref, pulled_ref, *refs):
+    del after_ref, weight_hbm
     parts, (sent_ref, res_ref, turned_ref, kv_ref) = refs[:-4][::-1], refs[-4:]
     rank = lax.axis_index("tp")
     other = 1 - lax.rem(rank, 2)
@@ -486,10 +486,11 @@
         ).astype(jnp.bfloat16)
 
 
-def fetch_kernel(picks, after_ref, source_ref, target_ref, sems):
+def fetch_kernel(picks, first, after_ref, source_ref, down_hbm, target_ref, down_ref, sems):
     del after_ref
     rows = target_ref.shape[0] // len(picks)
-    copies = []
+    span = pl.ds(first, down_ref.shape[0])
+    copies = [pltpu.make_async_copy(down_hbm.at[span], down_ref, sems.at[len(picks)])]
     for place, k in enumerate(picks):
         pair = lax.bitwise_xor(lax.div(lax.axis_index("tp"), 2), k)
         start = pl.multiple_of(pair * rows, WIDE)
@@ -578,13 +579,14 @@
 
 
 def expert_kernel(
-    rows, count_ref, router_ref, gain_ref, down_ref, rest_ref, before_ref, part_ref, *refs
+    rows, count_ref, router_ref, gain_ref, before_ref, part_ref, *refs
 ):
     refs, late = refs[:-8], refs[-8:]
     far_ref, hid_ref, hidden_ref, attn_ref, x_ref, normed_ref, share_ref, residual_ref = late
     f32, bf16 = jnp.float32, jnp.bfloat16
     pairs = KV_HEADS // 2
     first = pairs // 2
+    down_refs, refs = refs[: pairs + 1], refs[pairs + 1 :]
     blocks, refs = refs[: 2 * (pairs - first)], refs[2 * (pairs - first) :]
     weight_refs, unit_refs = refs[: pairs - first], refs[pairs - first :]
     unit_weights = [(ref, k) for ref in unit_refs for k in range(ref.shape[0])]
@@ -630,10 +632,10 @@
         gate, up = both[:, :unit_width], both[:, unit_width:]
         return (gate / (1.0 + jnp.exp(-gate)) * up * share_ref[u]).astype(bf16)
 
-    ready = down_ref.shape[0] // STEP
+    down_steps = [(ref, at) for ref in down_refs for at in range(ref.shape[0] // STEP)]
     for i in range(units // STEP):
         act = jnp.concatenate([one_unit(i * STEP + k) for k in range(STEP)], axis=1)
-        ref, at = (down_ref, i) if i < ready else (rest_ref, i - ready)
+        ref, at = down_steps[i]
         down = ref[at * STEP : (at + 1) * STEP].reshape(STEP * unit_width, model)
         part = jnp.dot(act, down, preferred_element_type=f32)
         hid_ref[...] = part if i == 0 else hid_ref[...] + part
@@ -699,18 +701,19 @@
     return lax.ppermute(rows, "tp", [(i, i ^ mask) for i in range(count)])
 
 
-def fetch(after, array, rows, picks):
+def fetch(after, array, rows, picks, down_weight, first, units):
     shape = (rows * len(picks),) + array.shape[1:]
+    down_shape = (units,) + down_weight.shape[1:]
     return pl.pallas_call(
-        functools.partial(fetch_kernel, picks),
-        out_shape=pltpu.VMEM(shape, array.dtype),
-        in_specs=spaces("aa"),
-        out_specs=spaces("v")[0],
-        scratch_shapes=[pltpu.SemaphoreType.DMA((len(picks),))],
-        compiler_params=params(),
-        cost_estimate=cost(2 * math.prod(shape) >> 20),
+        functools.partial(fetch_kernel, picks, first),
+        out_shape=(pltpu.VMEM(shape, array.dtype), pltpu.VMEM(down_shape, array.dtype)),
+        in_specs=spaces("aaa"),
+        out_specs=tuple(spaces("vv")),
+        scratch_shapes=[pltpu.SemaphoreType.DMA((len(picks) + 1,))],
+        compiler_params=params(),
+        cost_estimate=cost(2 * (math.prod(shape) + math.prod(down_shape)) >> 20),
         name="fetch",
-    )(after, *in_hbm(array))
+    )(after, *in_hbm(array, down_weight))
 
 
 def per_device_packed(
@@ -786,7 +789,8 @@
     pulled = lax.all_gather(joined, "req", axis=0)
     nodes = slot_count * DRAFT
     units = gate_up.shape[0]
-    ready = READY * units // 20 // STEP * STEP
+    cuts = [units * c // 20 // STEP * STEP for c in CUTS]
+    ready = cuts[0]
     down_ready, reach, chosen, count = pl.pallas_call(
         tree_kernel,
         out_shape=(
@@ -811,12 +815,12 @@
             jax.ShapeDtypeStruct((pairs * part.shape[1], WIDE), bf16),
             jax.ShapeDtypeStruct((kv_rows, WIDE), bf16),
         ),
-        in_specs=spaces("avv" + "v" * pairs),
+        in_specs=spaces("aavv" + "v" * pairs),
         out_specs=tuple(spaces("vvvv")),
         compiler_params=params(),
         cost_estimate=cost(4),
         name="route",
-    )(down_ready, table, pulled, *parts[::-1])
+    )(down_ready, *in_hbm(down_weight), table, pulled, *parts[::-1])
     turned = swap(turned, 1)
     packed = lax.all_to_all(packed, "tp", 0, 0, tiled=True)
     gate_up = pltpu.with_memory_space_constraint(gate_up, pltpu.VMEM)
@@ -834,11 +838,14 @@
         name="attend",
     )(gate_up, table, reach, packed, own_res, turned, own_kv, *parts[::-1])
     reached = [swap(near_block, 2)] + [swap(block, 2 * k) for k in range(2, pairs)]
-    weights, after = [], block
+    weights, downs, after = [], [down_ready], block
     rows = out_weight.shape[0] // pairs
     for k, picks in zip(ORDER, FETCHES):
-        weight = fetch(after, out_weight, rows, picks)
-        reached[k - 1], weight = lax.optimization_barrier((reached[k - 1], weight))
+        start, size = cuts[len(weights)], cuts[len(weights) + 1] - cuts[len(weights)]
+        weight, down = fetch(after, out_weight, rows, picks, down_weight, start, size)
+        fetched = (reached[k - 1], weight, down)
+        reached[k - 1], weight, down = lax.optimization_barrier(fetched)
+        downs.append(down)
         after = reached[k - 1]
         weights.append(weight)
     blocks = [block, swap(near_block, 1)]
@@ -848,7 +855,7 @@
         out_shape=(
             jax.ShapeDtypeStruct((group_rows, model), f32),
             pltpu.VMEM(queries.shape, bf16),
-            pltpu.VMEM((units - ready,) + down_weight.shape[1:], bf16),
+            pltpu.VMEM((units - cuts[-1],) + down_weight.shape[1:], bf16),
         ),
         in_specs=spaces("aav" + "v" * pairs),
         out_specs=tuple(spaces("vvv")),
@@ -879,7 +886,7 @@
             jax.ShapeDtypeStruct((tok_dev, model), f32),
             pltpu.VMEM(queries.shape, bf16),
         ),
-        in_specs=spaces("v" * (7 + pairs + pairs // 2 + len(unit_weights))),
+        in_specs=spaces("v" * (6 + len(downs) + pairs + pairs // 2 + len(unit_weights))),
         out_specs=tuple(spaces("vvvv")),
         scratch_shapes=[
             pltpu.VMEM((group_rows, HEADS * HEAD // 2), bf16),
@@ -893,10 +900,10 @@
         count,
         router,
         gain,
-        down_ready,
-        down_rest,
         before,
         attn_part,
+        *downs,
+        down_rest,
         *[a for k in reversed(range(pairs // 2, pairs)) for a in blocks[2 * k : 2 * k + 2]],
         weights[1],
         weights[2],

time: 67.2 us -> 66.8 us (level)
  waiting for transfers between devices: 8.83 us -> 8.09 us
    pallas_call x3, Pallas kernels: 4.21 us -> 4.95 us  [fetch(): pl.pallas_call(functools.partial(fetch_kernel, picks, first), out_shape=(...]
    ppermute x16, waiting for transfers between devices: 8.83 us -> 8.09 us  [swap(): return lax.ppermute(rows, 'tp', [(i, i ^ mask) for i in range(count)])]
  transfers between devices with their start and end apart: 16 -> 16, of which waited for: 8 -> 7; matrix products, arithmetic and copies ran while one was open for 0% -> 0% of each run, Pallas kernels for 13% -> 14%
where the time goes in v7:
time: 66.8 us; the launch traced here: 66.5 us
  starting transfers between devices  21.2 us (32%)
  blocking collectives  18.3 us (27%)
  Pallas kernels  18.2 us (27%)
  waiting for transfers between devices  8.09 us (12%)
  between operations  0.74 us (1%)
    ppermute x16, starting transfers between devices, swap(): return lax.ppermute(rows, 'tp', [(i, i ^ mask) for i in range(count)])  21.2 us
    all_to_all x1, blocking collectives, per_device_packed(): packed = lax.all_to_all(packed, 'tp', 0, 0, tiled=True)  10.9 us
    ppermute x16, waiting for transfers between devices, swap(): return lax.ppermute(rows, 'tp', [(i, i ^ mask) for i in range(count)])  8.09 us
    all_gather x1, blocking collectives, per_device_packed(): pulled = lax.all_gather(joined, 'req', axis=0)  7.33 us
    pallas_call x1, Pallas kernels, per_device_packed(): pl.pallas_call(functools.partial(expert_kernel, block_rows), out_shape=(j...  5.03 us
    pallas_call x3, Pallas kernels, fetch(): pl.pallas_call(functools.partial(fetch_kernel, picks, first), out_shape=(...  4.95 us
    pallas_call x1, Pallas kernels, per_device_packed(): pl.pallas_call(functools.partial(early_kernel, block_rows), out_shape=(ja...  2.19 us
    pallas_call x1, Pallas kernels, per_device_packed(): pl.pallas_call(tree_kernel, out_shape=(pltpu.VMEM((ready,) + down_weight....  1.82 us
  transfers between devices with their start and end apart: 16, of which 7 were waited for; matrix products, arithmetic and copies ran while one was open for 0% of the time, Pallas kernels for 14%

profile of v7, /device:TPU:0, one launch (start us, length us, event | category | flops | bytes accessed | tf_op | source)
XLA Modules:
  0.0 66.5 jit_solution(948295416739374076)
XLA Ops:
  0.6 1.4 %split.1 = (bf16[2,256,128]{2,1,0:T(8,128)(2,1)S(1)}, bf16[2,256,128]{2,1,0:T(8,128)(2,1)S(1)}, bf16[2,256,128]{2,1,0:T(8,128)(2,1)S(1)}, bf16[2,256,128]{2,1,0:...) custom-call(s32[2]{0:T(128)} %bitcast.10, ...), custom_call_target="tpu_custom_call" | custom-call | bytes 4194304 | tf_op jit(solution)/shard_map/split/pallas_call | solution.py:763
  2.1 5.1 %collective-permute-start = (bf16[2,256,128]{2,1,0:T(8,128)(2,1)S(1)}, bf16[2,256,128]{2,1,0:T(8,128)(2,1)S(1)}, u32[]{:S(2)}, u32[]{:S(2)}) collective-permute-start(bf16[2,256,128]{2,1,0:T(8,128)(2,1)S(1)} %get-tuple-element.60), channel_id=1, source_target_pairs={{0,6},{1,7},{2,4},{3,5},{4,2},{5,3},{6,0},{7,1},{8,14},{9,15},{10,... | collective-permute-start | bytes 393224 | tf_op jit(solution)/shard_map/ppermute | solution.py:701
  7.8 7.3 %all-gather = bf16[64,4096]{1,0:T(8,128)(2,1)S(1)} all-gather(bf16[16,4096]{1,0:T(8,128)(2,1)S(1)} %get-tuple-element.51), channel_id=2, replica_groups=mesh['req'=4,'tp'=8] {'req'}, dimensions={0}, use_global_device_ids=true | all-gather | bytes 655360 | tf_op jit(solution)/shard_map/all_gather | solution.py:789
  15.2 1.8 %tree.1 = (bf16[6,128,1536]{2,1,0:T(8,128)(2,1)S(1)}, f32[128,128]{1,0:T(8,128)S(1)}, bf16[2,64,64]{2,1,0:T(8,128)(2,1)S(1)}, f32[128,40]{1,0:T(8,128)S(1)}) custom-call(bf16[4,16,4096]{2,1,0:T(8,128)(2,1)S(1)} %bitcast.5, bf16[20,128,1536]{2,1,0:T(8,128)(2,1)} %down_hbm.9, f32[8,128]{1,0:T(8,128)S(1)} %get-tuple-element.52.table_ref, ...), custom_call_target="tpu_custom_call" | custom-call | bytes 8388608 | tf_op jit(solution)/shard_map/tree/pallas_call | solution.py:794
  17.0 1.3 %collective-permute-done.1.refs_1_ = bf16[2,256,128]{2,1,0:T(8,128)(2,1)S(1)} collective-permute-done((bf16[2,256,128]{2,1,0:T(8,128)(2,1)S(1)}, bf16[2,256,128]{2,1,0:T(8,128)(2,1)S(1)}, u32[]{:S(2)}, u32[]{:S(2)}) %collective-permute-start.1) | collective-permute-done | bytes 131104 | tf_op jit(solution)/shard_map/ppermute | solution.py:701
  18.5 1.6 %collective-permute-start.3 = (bf16[1024,128]{1,0:T(8,128)(2,1)S(1)}, bf16[1024,128]{1,0:T(8,128)(2,1)S(1)}, u32[]{:S(2)}, u32[]{:S(2)}) collective-permute-start(bf16[1024,128]{1,0:T(8,128)(2,1)S(1)} %get-tuple-element.66), channel_id=1, source_target_pairs={{0,1},{1,0},{2,3},{3,2},{4,5},{5,4},{6,7},{7,6},{8,9},{9,8},{10,11... | collective-permute-start | bytes 786440 | tf_op jit(solution)/shard_map/ppermute | solution.py:701
  20.1 10.9 %all_to_all.5.got_ref = bf16[8,48,128]{2,1,0:T(8,128)(2,1)S(1)} all-to-all(bf16[8,48,128]{2,1,0:T(8,128)(2,1)S(1)} %get-tuple-element.64), channel_id=1, replica_groups=mesh['req'=4,'tp'=8] {'tp'}, dimensions={0} | all-to-all | bytes 196608 | tf_op jit(solution)/shard_map/all_to_all | solution.py:825
  31.0 1.6 %attend.1 = (bf16[384,128]{1,0:T(8,128)(2,1)S(1)}, bf16[512,128]{1,0:T(8,128)(2,1)S(1)}) custom-call(bf16[20,1536,256]{2,1,0:T(8,128)(2,1)S(1)} %copy-done, f32[8,128]{1,0:T(8,128)S(1)} %get-tuple-element.52.table_ref, f32[128,128]{1,0:T(8,128)S(1)} %get-tuple-element.58.reach_ref, bf16[8,48,128]{2,1,0:T(8,128)(2,1)S(1)} %all_to_all.5.got_ref, ...), custom_call_target="tpu_custom_call" | custom-call | bytes 8388608 | tf_op jit(solution)/shard_map/attend/pallas_call | solution.py:828
  32.7 1.9 %collective-permute-start.5 = (bf16[384,128]{1,0:T(8,128)(2,1)S(1)}, bf16[384,128]{1,0:T(8,128)(2,1)S(1)}, u32[]{:S(2)}, u32[]{:S(2)}) collective-permute-start(bf16[384,128]{1,0:T(8,128)(2,1)S(1)} %get-tuple-element.68.after_ref.refs_0_), channel_id=1, source_target_pairs={{0,6},{1,7},{2,4},{3,5},{4,2},{5,3},{6,0},{7,1},{8,14},{9,15},{10,... | collective-permute-start | bytes 294920 | tf_op jit(solution)/shard_map/ppermute | solution.py:701
  34.6 1.6 %collective-permute-start.4 = (bf16[384,128]{1,0:T(8,128)(2,1)S(1)}, bf16[384,128]{1,0:T(8,128)(2,1)S(1)}, u32[]{:S(2)}, u32[]{:S(2)}) collective-permute-start(bf16[384,128]{1,0:T(8,128)(2,1)S(1)} %get-tuple-element.68.after_ref.refs_0_), channel_id=1, source_target_pairs={{0,4},{1,5},{2,6},{3,7},{4,0},{5,1},{6,2},{7,3},{8,12},{9,13},{10,... | collective-permute-start | bytes 294920 | tf_op jit(solution)/shard_map/ppermute | solution.py:701
  36.5 1.9 %fetch.3 = (bf16[768,1536]{1,0:T(8,128)(2,1)S(1)}, bf16[2,128,1536]{2,1,0:T(8,128)(2,1)S(1)}) custom-call(bf16[384,128]{1,0:T(8,128)(2,1)S(1)} %get-tuple-element.68.after_ref.refs_0_, bf16[1536,1536]{1,0:T(8,128)(2,1)} %source_ref.5, bf16[20,128,1536]{2,1,0:T(8,128)(2,1)} %down_hbm.9), custom_call_target="tpu_custom_call" | custom-call | bytes 3145728 | tf_op jit(solution)/shard_map/fetch/pallas_call | solution.py:707
  39.3 1.3 %collective-permute-start.8 = (bf16[512,128]{1,0:T(8,128)(2,1)S(1)}, bf16[512,128]{1,0:T(8,128)(2,1)S(1)}, u32[]{:S(2)}, u32[]{:S(2)}) collective-permute-start(bf16[512,128]{1,0:T(8,128)(2,1)S(1)} %collective-permute-done.6.after_ref.refs_2_), channel_id=1, source_target_pairs={{0,1},{1,0},{2,3},{3,2},{4,5},{5,4},{6,7},{7,6},{8,9},{9,8},{10,11... | collective-permute-start | bytes 393224 | tf_op jit(solution)/shard_map/ppermute | solution.py:701
  40.5 1.5 %fetch.4 = (bf16[384,1536]{1,0:T(8,128)(2,1)S(1)}, bf16[2,128,1536]{2,1,0:T(8,128)(2,1)S(1)}) custom-call(bf16[512,128]{1,0:T(8,128)(2,1)S(1)} %collective-permute-done.6.after_ref.refs_2_, bf16[1536,1536]{1,0:T(8,128)(2,1)} %source_ref.5, bf16[20,128,1536]{2,1,0:T(8,128)(2,1)} %down_hbm.9), custom_call_target="tpu_custom_call" | custom-call | bytes 1048576 | tf_op jit(solution)/shard_map/fetch/pallas_call | solution.py:707
  42.1 1.5 %fetch.5 = (bf16[384,1536]{1,0:T(8,128)(2,1)S(1)}, bf16[2,128,1536]{2,1,0:T(8,128)(2,1)S(1)}) custom-call(bf16[384,128]{1,0:T(8,128)(2,1)S(1)} %collective-permute-done.5.after_ref.refs_5_, bf16[1536,1536]{1,0:T(8,128)(2,1)} %source_ref.5, bf16[20,128,1536]{2,1,0:T(8,128)(2,1)} %down_hbm.9), custom_call_target="tpu_custom_call" | custom-call | bytes 1048576 | tf_op jit(solution)/shard_map/fetch/pallas_call | solution.py:707
  44.5 1.3 %collective-permute-start.10 = (bf16[384,128]{1,0:T(8,128)(2,1)S(1)}, bf16[384,128]{1,0:T(8,128)(2,1)S(1)}, u32[]{:S(2)}, u32[]{:S(2)}) collective-permute-start(bf16[384,128]{1,0:T(8,128)(2,1)S(1)} %collective-permute-done.4.after_ref.refs_7_), channel_id=1, source_target_pairs={{0,1},{1,0},{2,3},{3,2},{4,5},{5,4},{6,7},{7,6},{8,9},{9,8},{10,11... | collective-permute-start | bytes 294920 | tf_op jit(solution)/shard_map/ppermute | solution.py:701
  45.7 2.2 %early.1 = (f32[128,1536]{1,0:T(8,128)S(1)}, bf16[16,1536]{1,0:T(8,128)(2,1)S(1)}, bf16[8,128,1536]{2,1,0:T(8,128)(2,1)S(1)}) custom-call(bf16[384,128]{1,0:T(8,128)(2,1)S(1)} %collective-permute-done.4.after_ref.refs_7_, bf16[20,128,1536]{2,1,0:T(8,128)(2,1)} %down_hbm.9, bf16[768,1536]{1,0:T(8,128)(2,1)S(1)} %get-tuple-element.79.weight_ref, ...), custom_call_target="tpu_custom_call" | custom-call | bytes 4194304 | tf_op jit(solution)/shard_map/early/pallas_call | solution.py:853
  48.3 1.1 %collective-permute-done.10.refs_8_ = bf16[384,128]{1,0:T(8,128)(2,1)S(1)} collective-permute-done((bf16[384,128]{1,0:T(8,128)(2,1)S(1)}, bf16[384,128]{1,0:T(8,128)(2,1)S(1)}, u32[]{:S(2)}, u32[]{:S(2)}) %collective-permute-start.10) | collective-permute-done | bytes 98336 | tf_op jit(solution)/shard_map/ppermute | solution.py:701
  49.4 5.0 %experts.1 = (bf16[2,16,1536]{2,1,0:T(8,128)(2,1)S(1)}, f32[128,1536]{1,0:T(8,128)S(1)}, f32[16,1536]{1,0:T(8,128)S(1)}, bf16[16,1536]{1,0:T(8,128)(2,1)S(1)}) custom-call(f32[128,40]{1,0:T(8,128)S(1)} %get-tuple-element.55.count_ref, bf16[40,1536]{1,0:T(8,128)(2,1)S(1)} %get-tuple-element.56.router_ref, f32[12,128]{1,0:T(8,128)S(1)} %get-tuple-element.57.gain_ref, ...), custom_call_target="tpu_custom_call" | custom-call | tf_op jit(solution)/shard_map/experts/pallas_call | solution.py:881
  54.4 1.0 %collective-permute-start.11 = (bf16[2,16,1536]{2,1,0:T(8,128)(2,1)S(1)}, bf16[2,16,1536]{2,1,0:T(8,128)(2,1)S(1)}, u32[]{:S(2)}, u32[]{:S(2)}) collective-permute-start(bf16[2,16,1536]{2,1,0:T(8,128)(2,1)S(1)} %get-tuple-element.93), channel_id=1, source_target_pairs={{0,1},{1,0},{2,3},{3,2},{4,5},{5,4},{6,7},{7,6},{8,9},{9,8},{10,11... | collective-permute-start | bytes 294920 | tf_op jit(solution)/shard_map/ppermute | solution.py:701
  55.5 1.1 %collective-permute-start.12 = (bf16[2,16,1536]{2,1,0:T(8,128)(2,1)S(1)}, bf16[2,16,1536]{2,1,0:T(8,128)(2,1)S(1)}, u32[]{:S(2)}, u32[]{:S(2)}) collective-permute-start(bf16[2,16,1536]{2,1,0:T(8,128)(2,1)S(1)} %get-tuple-element.95), channel_id=1, source_target_pairs={{0,1},{1,0},{2,3},{3,2},{4,5},{5,4},{6,7},{7,6},{8,9},{9,8},{10,11... | collective-permute-start | bytes 294920 | tf_op jit(solution)/shard_map/ppermute | solution.py:701
  56.6 2.5 %collective-permute-done.11.got_ref = bf16[2,16,1536]{2,1,0:T(8,128)(2,1)S(1)} collective-permute-done((bf16[2,16,1536]{2,1,0:T(8,128)(2,1)S(1)}, bf16[2,16,1536]{2,1,0:T(8,128)(2,1)S(1)}, u32[]{:S(2)}, u32[]{:S(2)}) %collective-permute-start.11) | collective-permute-done | bytes 98336 | tf_op jit(solution)/shard_map/ppermute | solution.py:701
  59.7 1.9 %collective-permute-start.14 = (bf16[16,1536]{1,0:T(8,128)(2,1)S(1)}, bf16[16,1536]{1,0:T(8,128)(2,1)S(1)}, u32[]{:S(2)}, u32[]{:S(2)}) collective-permute-start(bf16[16,1536]{1,0:T(8,128)(2,1)S(1)} %get-tuple-element.94.after_ref), channel_id=1, source_target_pairs={{0,4},{1,5},{2,6},{3,7},{4,0},{5,1},{6,2},{7,3},{8,12},{9,13},{10,... | collective-permute-start | bytes 147464 | tf_op jit(solution)/shard_map/ppermute | solution.py:701
  61.6 2.1 %collective-permute-start.15 = (bf16[16,1536]{1,0:T(8,128)(2,1)S(1)}, bf16[16,1536]{1,0:T(8,128)(2,1)S(1)}, u32[]{:S(2)}, u32[]{:S(2)}) collective-permute-start(bf16[16,1536]{1,0:T(8,128)(2,1)S(1)} %get-tuple-element.98), channel_id=1, source_target_pairs={{0,2},{1,3},{2,0},{3,1},{4,6},{5,7},{6,4},{7,5},{8,10},{9,11},{10,... | collective-permute-start | bytes 147464 | tf_op jit(solution)/shard_map/ppermute | solution.py:701
  63.8 1.3 %collective-permute-done.13.refs_1_ = bf16[16,1536]{1,0:T(8,128)(2,1)S(1)} collective-permute-done((bf16[16,1536]{1,0:T(8,128)(2,1)S(1)}, bf16[16,1536]{1,0:T(8,128)(2,1)S(1)}, u32[]{:S(2)}, u32[]{:S(2)}) %collective-permute-start.13) | collective-permute-done | bytes 49184 | tf_op jit(solution)/shard_map/ppermute | solution.py:701
  (26 shorter events, 5.5 us)
Async XLA Ops:
  2.1 14.9 %collective-permute-start = (bf16[2,256,128]{2,1,0:T(8,128)(2,1)S(1)}, bf16[2,256,128]{2,1,0:T(8,128)(2,1)S(1)}, u32[]{:S(2)}, u32[]{:S(2)}) collective-permute-start(bf16[2,256,128]{2,1,0:T(8,128)(2,1)S(1)} %get-tuple-element.60), channel_id=1, source_target_pairs={{0,6},{1,7},{2,4},{3,5},{4,2},{5,3},{6,0},{7,1},{8,14},{9,15},{10,... | collective-permute-start | bytes 393224 | tf_op jit(solution)/shard_map/ppermute | solution.py:701
  7.2 11.1 %collective-permute-start.1 = (bf16[2,256,128]{2,1,0:T(8,128)(2,1)S(1)}, bf16[2,256,128]{2,1,0:T(8,128)(2,1)S(1)}, u32[]{:S(2)}, u32[]{:S(2)}) collective-permute-start(bf16[2,256,128]{2,1,0:T(8,128)(2,1)S(1)} %get-tuple-element.61), channel_id=1, source_target_pairs={{0,4},{1,5},{2,6},{3,7},{4,0},{5,1},{6,2},{7,3},{8,12},{9,13},{10,... | collective-permute-start | bytes 393224 | tf_op jit(solution)/shard_map/ppermute | solution.py:701
  7.2 11.1 %collective-permute-start.2 = (bf16[2,256,128]{2,1,0:T(8,128)(2,1)S(1)}, bf16[2,256,128]{2,1,0:T(8,128)(2,1)S(1)}, u32[]{:S(2)}, u32[]{:S(2)}) collective-permute-start(bf16[2,256,128]{2,1,0:T(8,128)(2,1)S(1)} %get-tuple-element.62), channel_id=1, source_target_pairs={{0,2},{1,3},{2,0},{3,1},{4,6},{5,7},{6,4},{7,5},{8,10},{9,11},{10,... | collective-permute-start | bytes 393224 | tf_op jit(solution)/shard_map/ppermute | solution.py:701
  15.2 15.8 %copy-start = (bf16[20,1536,256]{2,1,0:T(8,128)(2,1)S(1)}, bf16[20,1536,256]{2,1,0:T(8,128)(2,1)}, u32[]{:S(2)}) copy-start(bf16[20,1536,256]{2,1,0:T(8,128)(2,1)} %refs_11_.1) | copy-start | bytes 47185924
  18.5 12.5 %collective-permute-start.3 = (bf16[1024,128]{1,0:T(8,128)(2,1)S(1)}, bf16[1024,128]{1,0:T(8,128)(2,1)S(1)}, u32[]{:S(2)}, u32[]{:S(2)}) collective-permute-start(bf16[1024,128]{1,0:T(8,128)(2,1)S(1)} %get-tuple-element.66), channel_id=1, source_target_pairs={{0,1},{1,0},{2,3},{3,2},{4,5},{5,4},{6,7},{7,6},{8,9},{9,8},{10,11... | collective-permute-start | bytes 786440 | tf_op jit(solution)/shard_map/ppermute | solution.py:701
  32.6 6.7 %collective-permute-start.6 = (bf16[512,128]{1,0:T(8,128)(2,1)S(1)}, bf16[512,128]{1,0:T(8,128)(2,1)S(1)}, u32[]{:S(2)}, u32[]{:S(2)}) collective-permute-start(bf16[512,128]{1,0:T(8,128)(2,1)S(1)} %get-tuple-element.69.refs_0_), channel_id=1, source_target_pairs={{0,2},{1,3},{2,0},{3,1},{4,6},{5,7},{6,4},{7,5},{8,10},{9,11},{10,... | collective-permute-start | bytes 393224 | tf_op jit(solution)/shard_map/ppermute | solution.py:701
  32.7 9.4 %collective-permute-start.5 = (bf16[384,128]{1,0:T(8,128)(2,1)S(1)}, bf16[384,128]{1,0:T(8,128)(2,1)S(1)}, u32[]{:S(2)}, u32[]{:S(2)}) collective-permute-start(bf16[384,128]{1,0:T(8,128)(2,1)S(1)} %get-tuple-element.68.after_ref.refs_0_), channel_id=1, source_target_pairs={{0,6},{1,7},{2,4},{3,5},{4,2},{5,3},{6,0},{7,1},{8,14},{9,15},{10,... | collective-permute-start | bytes 294920 | tf_op jit(solution)/shard_map/ppermute | solution.py:701
  34.6 9.9 %collective-permute-start.4 = (bf16[384,128]{1,0:T(8,128)(2,1)S(1)}, bf16[384,128]{1,0:T(8,128)(2,1)S(1)}, u32[]{:S(2)}, u32[]{:S(2)}) collective-permute-start(bf16[384,128]{1,0:T(8,128)(2,1)S(1)} %get-tuple-element.68.after_ref.refs_0_), channel_id=1, source_target_pairs={{0,4},{1,5},{2,6},{3,7},{4,0},{5,1},{6,2},{7,3},{8,12},{9,13},{10,... | collective-permute-start | bytes 294920 | tf_op jit(solution)/shard_map/ppermute | solution.py:701
  36.2 9.6 %collective-permute-start.7 = (bf16[512,128]{1,0:T(8,128)(2,1)S(1)}, bf16[512,128]{1,0:T(8,128)(2,1)S(1)}, u32[]{:S(2)}, u32[]{:S(2)}) collective-permute-start(bf16[512,128]{1,0:T(8,128)(2,1)S(1)} %get-tuple-element.69.refs_0_), channel_id=1, source_target_pairs={{0,1},{1,0},{2,3},{3,2},{4,5},{5,4},{6,7},{7,6},{8,9},{9,8},{10,11... | collective-permute-start | bytes 393224 | tf_op jit(solution)/shard_map/ppermute | solution.py:701
  39.3 6.4 %collective-permute-start.8 = (bf16[512,128]{1,0:T(8,128)(2,1)S(1)}, bf16[512,128]{1,0:T(8,128)(2,1)S(1)}, u32[]{:S(2)}, u32[]{:S(2)}) collective-permute-start(bf16[512,128]{1,0:T(8,128)(2,1)S(1)} %collective-permute-done.6.after_ref.refs_2_), channel_id=1, source_target_pairs={{0,1},{1,0},{2,3},{3,2},{4,5},{5,4},{6,7},{7,6},{8,9},{9,8},{10,11... | collective-permute-start | bytes 393224 | tf_op jit(solution)/shard_map/ppermute | solution.py:701
  43.6 4.7 %collective-permute-start.9 = (bf16[384,128]{1,0:T(8,128)(2,1)S(1)}, bf16[384,128]{1,0:T(8,128)(2,1)S(1)}, u32[]{:S(2)}, u32[]{:S(2)}) collective-permute-start(bf16[384,128]{1,0:T(8,128)(2,1)S(1)} %collective-permute-done.5.after_ref.refs_5_), channel_id=1, source_target_pairs={{0,1},{1,0},{2,3},{3,2},{4,5},{5,4},{6,7},{7,6},{8,9},{9,8},{10,11... | collective-permute-start | bytes 294920 | tf_op jit(solution)/shard_map/ppermute | solution.py:701
  44.5 4.9 %collective-permute-start.10 = (bf16[384,128]{1,0:T(8,128)(2,1)S(1)}, bf16[384,128]{1,0:T(8,128)(2,1)S(1)}, u32[]{:S(2)}, u32[]{:S(2)}) collective-permute-start(bf16[384,128]{1,0:T(8,128)(2,1)S(1)} %collective-permute-done.4.after_ref.refs_7_), channel_id=1, source_target_pairs={{0,1},{1,0},{2,3},{3,2},{4,5},{5,4},{6,7},{7,6},{8,9},{9,8},{10,11... | collective-permute-start | bytes 294920 | tf_op jit(solution)/shard_map/ppermute | solution.py:701
  54.4 4.7 %collective-permute-start.11 = (bf16[2,16,1536]{2,1,0:T(8,128)(2,1)S(1)}, bf16[2,16,1536]{2,1,0:T(8,128)(2,1)S(1)}, u32[]{:S(2)}, u32[]{:S(2)}) collective-permute-start(bf16[2,16,1536]{2,1,0:T(8,128)(2,1)S(1)} %get-tuple-element.93), channel_id=1, source_target_pairs={{0,1},{1,0},{2,3},{3,2},{4,5},{5,4},{6,7},{7,6},{8,9},{9,8},{10,11... | collective-permute-start | bytes 294920 | tf_op jit(solution)/shard_map/ppermute | solution.py:701
  55.5 6.1 %collective-permute-start.12 = (bf16[2,16,1536]{2,1,0:T(8,128)(2,1)S(1)}, bf16[2,16,1536]{2,1,0:T(8,128)(2,1)S(1)}, u32[]{:S(2)}, u32[]{:S(2)}) collective-permute-start(bf16[2,16,1536]{2,1,0:T(8,128)(2,1)S(1)} %get-tuple-element.95), channel_id=1, source_target_pairs={{0,1},{1,0},{2,3},{3,2},{4,5},{5,4},{6,7},{7,6},{8,9},{9,8},{10,11... | collective-permute-start | bytes 294920 | tf_op jit(solution)/shard_map/ppermute | solution.py:701
  59.1 6.1 %collective-permute-start.13 = (bf16[16,1536]{1,0:T(8,128)(2,1)S(1)}, bf16[16,1536]{1,0:T(8,128)(2,1)S(1)}, u32[]{:S(2)}, u32[]{:S(2)}) collective-permute-start(bf16[16,1536]{1,0:T(8,128)(2,1)S(1)} %get-tuple-element.97), channel_id=1, source_target_pairs={{0,6},{1,7},{2,4},{3,5},{4,2},{5,3},{6,0},{7,1},{8,14},{9,15},{10,... | collective-permute-start | bytes 147464 | tf_op jit(solution)/shard_map/ppermute | solution.py:701
  59.7 6.1 %collective-permute-start.14 = (bf16[16,1536]{1,0:T(8,128)(2,1)S(1)}, bf16[16,1536]{1,0:T(8,128)(2,1)S(1)}, u32[]{:S(2)}, u32[]{:S(2)}) collective-permute-start(bf16[16,1536]{1,0:T(8,128)(2,1)S(1)} %get-tuple-element.94.after_ref), channel_id=1, source_target_pairs={{0,4},{1,5},{2,6},{3,7},{4,0},{5,1},{6,2},{7,3},{8,12},{9,13},{10,... | collective-permute-start | bytes 147464 | tf_op jit(solution)/shard_map/ppermute | solution.py:701
  61.6 4.2 %collective-permute-start.15 = (bf16[16,1536]{1,0:T(8,128)(2,1)S(1)}, bf16[16,1536]{1,0:T(8,128)(2,1)S(1)}, u32[]{:S(2)}, u32[]{:S(2)}) collective-permute-start(bf16[16,1536]{1,0:T(8,128)(2,1)S(1)} %get-tuple-element.98), channel_id=1, source_target_pairs={{0,2},{1,3},{2,0},{3,1},{4,6},{5,7},{6,4},{7,5},{8,10},{9,11},{10,... | collective-permute-start | bytes 147464 | tf_op jit(solution)/shard_map/ppermute | solution.py:701

commit v8 on v7

--- a/solution.py
+++ b/solution.py
@@ -260,11 +260,11 @@
 def split_kernel(pairs, *refs):
     (
         pages_hbm, placement_hbm, lengths_hbm, leaf_hbm, keys_hbm, values_hbm, queries_hbm,
-        new_kv_hbm, residual_hbm, parents_hbm, router_hbm, ids_hbm, gain_hbm,
-    ) = refs[:13]
-    parts, refs = refs[13 : 13 + pairs], refs[13 + pairs :]
-    joined_ref, table_ref, parents_ref, router_ref, ids_ref, gain_ref = refs[:6]
-    pages_ref, placement_ref, lengths_ref, leaf_ref, keys_ref, values_ref, split_ref, sems = refs[6:]
+        new_kv_hbm, residual_hbm, parents_hbm, ids_hbm, gain_hbm,
+    ) = refs[:12]
+    parts, refs = refs[12 : 12 + pairs], refs[12 + pairs :]
+    joined_ref, table_ref, parents_ref, ids_ref, gain_ref = refs[:5]
+    pages_ref, placement_ref, lengths_ref, leaf_ref, keys_ref, values_ref, split_ref, sems = refs[5:]
     slot_count = pages_ref.shape[0]
     page_len = keys_ref.shape[1]
     tok_dev = joined_ref.shape[0]
@@ -276,7 +276,6 @@
         (lengths_hbm, lengths_ref),
         (leaf_hbm, leaf_ref),
         (parents_hbm, parents_ref),
-        (router_hbm, router_ref),
         (ids_hbm, ids_ref),
         (gain_hbm, gain_ref),
     ]
@@ -756,11 +755,10 @@
         new_kv,
         residual,
         parents,
-        router_weight.T,
         expert_ids.T,
         norm_gain.reshape(model // WIDE, WIDE),
     )
-    *parts, joined, table, parents, router, ids, gain = pl.pallas_call(
+    *parts, joined, table, parents, ids, gain = pl.pallas_call(
         functools.partial(split_kernel, pairs),
         out_shape=(part,) * pairs
         + (
@@ -769,7 +767,7 @@
         )
         + tuple(pltpu.VMEM(a.shape, a.dtype) for a in loaded[9:]),
         in_specs=spaces("a" * len(loaded)),
-        out_specs=tuple(spaces("v" * (pairs + 6))),
+        out_specs=tuple(spaces("v" * (pairs + 5))),
         scratch_shapes=[
             slots_smem,
             slots_smem,
@@ -898,7 +896,7 @@
         name="experts",
     )(
         count,
-        router,
+        pltpu.with_memory_space_constraint(router_weight.T, pltpu.VMEM),
         gain,
         before,
         attn_part,

time: 66.8 us -> 66.8 us (level)
  no operation moved by 1% of the time
where the time goes in v8:
time: 66.8 us; the launch traced here: 66.5 us
  starting transfers between devices  21.1 us (32%)
  blocking collectives  18.3 us (27%)
  Pallas kernels  18.2 us (27%)
  waiting for transfers between devices  8.16 us (12%)
  between operations  0.74 us (1%)
    ppermute x16, starting transfers between devices, swap(): return lax.ppermute(rows, 'tp', [(i, i ^ mask) for i in range(count)])  21.1 us
    all_to_all x1, blocking collectives, per_device_packed(): packed = lax.all_to_all(packed, 'tp', 0, 0, tiled=True)  10.9 us
    ppermute x16, waiting for transfers between devices, swap(): return lax.ppermute(rows, 'tp', [(i, i ^ mask) for i in range(count)])  8.16 us
    all_gather x1, blocking collectives, per_device_packed(): pulled = lax.all_gather(joined, 'req', axis=0)  7.33 us
    pallas_call x1, Pallas kernels, per_device_packed(): pl.pallas_call(functools.partial(expert_kernel, block_rows), out_shape=(j...  5.05 us
    pallas_call x3, Pallas kernels, fetch(): pl.pallas_call(functools.partial(fetch_kernel, picks, first), out_shape=(...  4.95 us
    pallas_call x1, Pallas kernels, per_device_packed(): pl.pallas_call(functools.partial(early_kernel, block_rows), out_shape=(ja...  2.19 us
    pallas_call x1, Pallas kernels, per_device_packed(): pl.pallas_call(tree_kernel, out_shape=(pltpu.VMEM((ready,) + down_weight....  1.82 us
  transfers between devices with their start and end apart: 16, of which 7 were waited for; matrix products, arithmetic and copies ran while one was open for 0% of the time, Pallas kernels for 14%

profile of v8, /device:TPU:0, one launch (start us, length us, event | category | flops | bytes accessed | tf_op | source)
XLA Modules:
  0.0 66.5 jit_solution(12957580733326154683)
XLA Ops:
  0.6 1.4 %split.1 = (bf16[2,256,128]{2,1,0:T(8,128)(2,1)S(1)}, bf16[2,256,128]{2,1,0:T(8,128)(2,1)S(1)}, bf16[2,256,128]{2,1,0:T(8,128)(2,1)S(1)}, bf16[2,256,128]{2,1,0:...) custom-call(s32[2]{0:T(128)} %bitcast.10, ...), custom_call_target="tpu_custom_call" | custom-call | bytes 4194304 | tf_op jit(solution)/shard_map/split/pallas_call | solution.py:761
  2.1 5.1 %collective-permute-start = (bf16[2,256,128]{2,1,0:T(8,128)(2,1)S(1)}, bf16[2,256,128]{2,1,0:T(8,128)(2,1)S(1)}, u32[]{:S(2)}, u32[]{:S(2)}) collective-permute-start(bf16[2,256,128]{2,1,0:T(8,128)(2,1)S(1)} %get-tuple-element.58), channel_id=1, source_target_pairs={{0,6},{1,7},{2,4},{3,5},{4,2},{5,3},{6,0},{7,1},{8,14},{9,15},{10,... | collective-permute-start | bytes 393224 | tf_op jit(solution)/shard_map/ppermute | solution.py:700
  7.8 7.3 %all-gather = bf16[64,4096]{1,0:T(8,128)(2,1)S(1)} all-gather(bf16[16,4096]{1,0:T(8,128)(2,1)S(1)} %get-tuple-element.50), channel_id=2, replica_groups=mesh['req'=4,'tp'=8] {'req'}, dimensions={0}, use_global_device_ids=true | all-gather | bytes 655360 | tf_op jit(solution)/shard_map/all_gather | solution.py:787
  15.2 1.8 %tree.1 = (bf16[6,128,1536]{2,1,0:T(8,128)(2,1)S(1)}, f32[128,128]{1,0:T(8,128)S(1)}, bf16[2,64,64]{2,1,0:T(8,128)(2,1)S(1)}, f32[128,40]{1,0:T(8,128)S(1)}) custom-call(bf16[4,16,4096]{2,1,0:T(8,128)(2,1)S(1)} %bitcast.5, bf16[20,128,1536]{2,1,0:T(8,128)(2,1)} %down_hbm.9, f32[8,128]{1,0:T(8,128)S(1)} %get-tuple-element.51.table_ref, ...), custom_call_target="tpu_custom_call" | custom-call | bytes 8388608 | tf_op jit(solution)/shard_map/tree/pallas_call | solution.py:792
  17.0 1.3 %collective-permute-done.1.refs_1_ = bf16[2,256,128]{2,1,0:T(8,128)(2,1)S(1)} collective-permute-done((bf16[2,256,128]{2,1,0:T(8,128)(2,1)S(1)}, bf16[2,256,128]{2,1,0:T(8,128)(2,1)S(1)}, u32[]{:S(2)}, u32[]{:S(2)}) %collective-permute-start.1) | collective-permute-done | bytes 131104 | tf_op jit(solution)/shard_map/ppermute | solution.py:700
  18.5 1.6 %collective-permute-start.3 = (bf16[1024,128]{1,0:T(8,128)(2,1)S(1)}, bf16[1024,128]{1,0:T(8,128)(2,1)S(1)}, u32[]{:S(2)}, u32[]{:S(2)}) collective-permute-start(bf16[1024,128]{1,0:T(8,128)(2,1)S(1)} %get-tuple-element.64), channel_id=1, source_target_pairs={{0,1},{1,0},{2,3},{3,2},{4,5},{5,4},{6,7},{7,6},{8,9},{9,8},{10,11... | collective-permute-start | bytes 786440 | tf_op jit(solution)/shard_map/ppermute | solution.py:700
  20.0 10.9 %all_to_all.5.got_ref = bf16[8,48,128]{2,1,0:T(8,128)(2,1)S(1)} all-to-all(bf16[8,48,128]{2,1,0:T(8,128)(2,1)S(1)} %get-tuple-element.62), channel_id=1, replica_groups=mesh['req'=4,'tp'=8] {'tp'}, dimensions={0} | all-to-all | bytes 196608 | tf_op jit(solution)/shard_map/all_to_all | solution.py:823
  31.0 1.6 %attend.1 = (bf16[384,128]{1,0:T(8,128)(2,1)S(1)}, bf16[512,128]{1,0:T(8,128)(2,1)S(1)}) custom-call(bf16[20,1536,256]{2,1,0:T(8,128)(2,1)S(1)} %copy-done, f32[8,128]{1,0:T(8,128)S(1)} %get-tuple-element.51.table_ref, f32[128,128]{1,0:T(8,128)S(1)} %get-tuple-element.56.reach_ref, bf16[8,48,128]{2,1,0:T(8,128)(2,1)S(1)} %all_to_all.5.got_ref, ...), custom_call_target="tpu_custom_call" | custom-call | bytes 8388608 | tf_op jit(solution)/shard_map/attend/pallas_call | solution.py:826
  32.7 1.9 %collective-permute-start.5 = (bf16[384,128]{1,0:T(8,128)(2,1)S(1)}, bf16[384,128]{1,0:T(8,128)(2,1)S(1)}, u32[]{:S(2)}, u32[]{:S(2)}) collective-permute-start(bf16[384,128]{1,0:T(8,128)(2,1)S(1)} %get-tuple-element.66.after_ref.refs_0_), channel_id=1, source_target_pairs={{0,6},{1,7},{2,4},{3,5},{4,2},{5,3},{6,0},{7,1},{8,14},{9,15},{10,... | collective-permute-start | bytes 294920 | tf_op jit(solution)/shard_map/ppermute | solution.py:700
  34.5 1.6 %collective-permute-start.4 = (bf16[384,128]{1,0:T(8,128)(2,1)S(1)}, bf16[384,128]{1,0:T(8,128)(2,1)S(1)}, u32[]{:S(2)}, u32[]{:S(2)}) collective-permute-start(bf16[384,128]{1,0:T(8,128)(2,1)S(1)} %get-tuple-element.66.after_ref.refs_0_), channel_id=1, source_target_pairs={{0,4},{1,5},{2,6},{3,7},{4,0},{5,1},{6,2},{7,3},{8,12},{9,13},{10,... | collective-permute-start | bytes 294920 | tf_op jit(solution)/shard_map/ppermute | solution.py:700
  36.4 1.9 %fetch.3 = (bf16[768,1536]{1,0:T(8,128)(2,1)S(1)}, bf16[2,128,1536]{2,1,0:T(8,128)(2,1)S(1)}) custom-call(bf16[384,128]{1,0:T(8,128)(2,1)S(1)} %get-tuple-element.66.after_ref.refs_0_, bf16[1536,1536]{1,0:T(8,128)(2,1)} %source_ref.5, bf16[20,128,1536]{2,1,0:T(8,128)(2,1)} %down_hbm.9), custom_call_target="tpu_custom_call" | custom-call | bytes 3145728 | tf_op jit(solution)/shard_map/fetch/pallas_call | solution.py:706
  39.3 1.2 %collective-permute-start.8 = (bf16[512,128]{1,0:T(8,128)(2,1)S(1)}, bf16[512,128]{1,0:T(8,128)(2,1)S(1)}, u32[]{:S(2)}, u32[]{:S(2)}) collective-permute-start(bf16[512,128]{1,0:T(8,128)(2,1)S(1)} %collective-permute-done.6.after_ref.refs_2_), channel_id=1, source_target_pairs={{0,1},{1,0},{2,3},{3,2},{4,5},{5,4},{6,7},{7,6},{8,9},{9,8},{10,11... | collective-permute-start | bytes 393224 | tf_op jit(solution)/shard_map/ppermute | solution.py:700
  40.5 1.5 %fetch.4 = (bf16[384,1536]{1,0:T(8,128)(2,1)S(1)}, bf16[2,128,1536]{2,1,0:T(8,128)(2,1)S(1)}) custom-call(bf16[512,128]{1,0:T(8,128)(2,1)S(1)} %collective-permute-done.6.after_ref.refs_2_, bf16[1536,1536]{1,0:T(8,128)(2,1)} %source_ref.5, bf16[20,128,1536]{2,1,0:T(8,128)(2,1)} %down_hbm.9), custom_call_target="tpu_custom_call" | custom-call | bytes 1048576 | tf_op jit(solution)/shard_map/fetch/pallas_call | solution.py:706
  42.0 1.5 %fetch.5 = (bf16[384,1536]{1,0:T(8,128)(2,1)S(1)}, bf16[2,128,1536]{2,1,0:T(8,128)(2,1)S(1)}) custom-call(bf16[384,128]{1,0:T(8,128)(2,1)S(1)} %collective-permute-done.5.after_ref.refs_5_, bf16[1536,1536]{1,0:T(8,128)(2,1)} %source_ref.5, bf16[20,128,1536]{2,1,0:T(8,128)(2,1)} %down_hbm.9), custom_call_target="tpu_custom_call" | custom-call | bytes 1048576 | tf_op jit(solution)/shard_map/fetch/pallas_call | solution.py:706
  44.5 1.2 %collective-permute-start.10 = (bf16[384,128]{1,0:T(8,128)(2,1)S(1)}, bf16[384,128]{1,0:T(8,128)(2,1)S(1)}, u32[]{:S(2)}, u32[]{:S(2)}) collective-permute-start(bf16[384,128]{1,0:T(8,128)(2,1)S(1)} %collective-permute-done.4.after_ref.refs_7_), channel_id=1, source_target_pairs={{0,1},{1,0},{2,3},{3,2},{4,5},{5,4},{6,7},{7,6},{8,9},{9,8},{10,11... | collective-permute-start | bytes 294920 | tf_op jit(solution)/shard_map/ppermute | solution.py:700
  45.7 2.2 %early.1 = (f32[128,1536]{1,0:T(8,128)S(1)}, bf16[16,1536]{1,0:T(8,128)(2,1)S(1)}, bf16[8,128,1536]{2,1,0:T(8,128)(2,1)S(1)}) custom-call(bf16[384,128]{1,0:T(8,128)(2,1)S(1)} %collective-permute-done.4.after_ref.refs_7_, bf16[20,128,1536]{2,1,0:T(8,128)(2,1)} %down_hbm.9, bf16[768,1536]{1,0:T(8,128)(2,1)S(1)} %get-tuple-element.77.weight_ref, ...), custom_call_target="tpu_custom_call" | custom-call | bytes 4194304 | tf_op jit(solution)/shard_map/early/pallas_call | solution.py:851
  48.3 1.1 %collective-permute-done.10.refs_8_ = bf16[384,128]{1,0:T(8,128)(2,1)S(1)} collective-permute-done((bf16[384,128]{1,0:T(8,128)(2,1)S(1)}, bf16[384,128]{1,0:T(8,128)(2,1)S(1)}, u32[]{:S(2)}, u32[]{:S(2)}) %collective-permute-start.10) | collective-permute-done | bytes 98336 | tf_op jit(solution)/shard_map/ppermute | solution.py:700
  49.3 5.0 %experts.1 = (bf16[2,16,1536]{2,1,0:T(8,128)(2,1)S(1)}, f32[128,1536]{1,0:T(8,128)S(1)}, f32[16,1536]{1,0:T(8,128)S(1)}, bf16[16,1536]{1,0:T(8,128)(2,1)S(1)}) custom-call(f32[128,40]{1,0:T(8,128)S(1)} %get-tuple-element.54.count_ref, bf16[40,1536]{1,0:T(8,128)(2,1)S(1)} %bitcast.7, f32[12,128]{1,0:T(8,128)S(1)} %get-tuple-element.55.gain_ref, ...), custom_call_target="tpu_custom_call" | custom-call | tf_op jit(solution)/shard_map/experts/pallas_call | solution.py:879
  54.4 1.0 %collective-permute-start.11 = (bf16[2,16,1536]{2,1,0:T(8,128)(2,1)S(1)}, bf16[2,16,1536]{2,1,0:T(8,128)(2,1)S(1)}, u32[]{:S(2)}, u32[]{:S(2)}) collective-permute-start(bf16[2,16,1536]{2,1,0:T(8,128)(2,1)S(1)} %get-tuple-element.91), channel_id=1, source_target_pairs={{0,1},{1,0},{2,3},{3,2},{4,5},{5,4},{6,7},{7,6},{8,9},{9,8},{10,11... | collective-permute-start | bytes 294920 | tf_op jit(solution)/shard_map/ppermute | solution.py:700
  55.5 1.1 %collective-permute-start.12 = (bf16[2,16,1536]{2,1,0:T(8,128)(2,1)S(1)}, bf16[2,16,1536]{2,1,0:T(8,128)(2,1)S(1)}, u32[]{:S(2)}, u32[]{:S(2)}) collective-permute-start(bf16[2,16,1536]{2,1,0:T(8,128)(2,1)S(1)} %get-tuple-element.93), channel_id=1, source_target_pairs={{0,1},{1,0},{2,3},{3,2},{4,5},{5,4},{6,7},{7,6},{8,9},{9,8},{10,11... | collective-permute-start | bytes 294920 | tf_op jit(solution)/shard_map/ppermute | solution.py:700
  56.6 2.5 %collective-permute-done.11.got_ref = bf16[2,16,1536]{2,1,0:T(8,128)(2,1)S(1)} collective-permute-done((bf16[2,16,1536]{2,1,0:T(8,128)(2,1)S(1)}, bf16[2,16,1536]{2,1,0:T(8,128)(2,1)S(1)}, u32[]{:S(2)}, u32[]{:S(2)}) %collective-permute-start.11) | collective-permute-done | bytes 98336 | tf_op jit(solution)/shard_map/ppermute | solution.py:700
  59.7 1.9 %collective-permute-start.14 = (bf16[16,1536]{1,0:T(8,128)(2,1)S(1)}, bf16[16,1536]{1,0:T(8,128)(2,1)S(1)}, u32[]{:S(2)}, u32[]{:S(2)}) collective-permute-start(bf16[16,1536]{1,0:T(8,128)(2,1)S(1)} %get-tuple-element.92.after_ref), channel_id=1, source_target_pairs={{0,4},{1,5},{2,6},{3,7},{4,0},{5,1},{6,2},{7,3},{8,12},{9,13},{10,... | collective-permute-start | bytes 147464 | tf_op jit(solution)/shard_map/ppermute | solution.py:700
  61.6 2.1 %collective-permute-start.15 = (bf16[16,1536]{1,0:T(8,128)(2,1)S(1)}, bf16[16,1536]{1,0:T(8,128)(2,1)S(1)}, u32[]{:S(2)}, u32[]{:S(2)}) collective-permute-start(bf16[16,1536]{1,0:T(8,128)(2,1)S(1)} %get-tuple-element.96), channel_id=1, source_target_pairs={{0,2},{1,3},{2,0},{3,1},{4,6},{5,7},{6,4},{7,5},{8,10},{9,11},{10,... | collective-permute-start | bytes 147464 | tf_op jit(solution)/shard_map/ppermute | solution.py:700
  63.8 1.3 %collective-permute-done.13.refs_1_ = bf16[16,1536]{1,0:T(8,128)(2,1)S(1)} collective-permute-done((bf16[16,1536]{1,0:T(8,128)(2,1)S(1)}, bf16[16,1536]{1,0:T(8,128)(2,1)S(1)}, u32[]{:S(2)}, u32[]{:S(2)}) %collective-permute-start.13) | collective-permute-done | bytes 49184 | tf_op jit(solution)/shard_map/ppermute | solution.py:700
  (28 shorter events, 5.7 us)
Async XLA Ops:
  2.1 14.9 %collective-permute-start = (bf16[2,256,128]{2,1,0:T(8,128)(2,1)S(1)}, bf16[2,256,128]{2,1,0:T(8,128)(2,1)S(1)}, u32[]{:S(2)}, u32[]{:S(2)}) collective-permute-start(bf16[2,256,128]{2,1,0:T(8,128)(2,1)S(1)} %get-tuple-element.58), channel_id=1, source_target_pairs={{0,6},{1,7},{2,4},{3,5},{4,2},{5,3},{6,0},{7,1},{8,14},{9,15},{10,... | collective-permute-start | bytes 393224 | tf_op jit(solution)/shard_map/ppermute | solution.py:700
  7.2 11.1 %collective-permute-start.1 = (bf16[2,256,128]{2,1,0:T(8,128)(2,1)S(1)}, bf16[2,256,128]{2,1,0:T(8,128)(2,1)S(1)}, u32[]{:S(2)}, u32[]{:S(2)}) collective-permute-start(bf16[2,256,128]{2,1,0:T(8,128)(2,1)S(1)} %get-tuple-element.59), channel_id=1, source_target_pairs={{0,4},{1,5},{2,6},{3,7},{4,0},{5,1},{6,2},{7,3},{8,12},{9,13},{10,... | collective-permute-start | bytes 393224 | tf_op jit(solution)/shard_map/ppermute | solution.py:700
  7.2 11.1 %collective-permute-start.2 = (bf16[2,256,128]{2,1,0:T(8,128)(2,1)S(1)}, bf16[2,256,128]{2,1,0:T(8,128)(2,1)S(1)}, u32[]{:S(2)}, u32[]{:S(2)}) collective-permute-start(bf16[2,256,128]{2,1,0:T(8,128)(2,1)S(1)} %get-tuple-element.60), channel_id=1, source_target_pairs={{0,2},{1,3},{2,0},{3,1},{4,6},{5,7},{6,4},{7,5},{8,10},{9,11},{10,... | collective-permute-start | bytes 393224 | tf_op jit(solution)/shard_map/ppermute | solution.py:700
  15.1 15.8 %copy-start = (bf16[20,1536,256]{2,1,0:T(8,128)(2,1)S(1)}, bf16[20,1536,256]{2,1,0:T(8,128)(2,1)}, u32[]{:S(2)}) copy-start(bf16[20,1536,256]{2,1,0:T(8,128)(2,1)} %refs_11_.1) | copy-start | bytes 47185924
  18.5 12.5 %collective-permute-start.3 = (bf16[1024,128]{1,0:T(8,128)(2,1)S(1)}, bf16[1024,128]{1,0:T(8,128)(2,1)S(1)}, u32[]{:S(2)}, u32[]{:S(2)}) collective-permute-start(bf16[1024,128]{1,0:T(8,128)(2,1)S(1)} %get-tuple-element.64), channel_id=1, source_target_pairs={{0,1},{1,0},{2,3},{3,2},{4,5},{5,4},{6,7},{7,6},{8,9},{9,8},{10,11... | collective-permute-start | bytes 786440 | tf_op jit(solution)/shard_map/ppermute | solution.py:700
  32.6 6.7 %collective-permute-start.6 = (bf16[512,128]{1,0:T(8,128)(2,1)S(1)}, bf16[512,128]{1,0:T(8,128)(2,1)S(1)}, u32[]{:S(2)}, u32[]{:S(2)}) collective-permute-start(bf16[512,128]{1,0:T(8,128)(2,1)S(1)} %get-tuple-element.67.refs_0_), channel_id=1, source_target_pairs={{0,2},{1,3},{2,0},{3,1},{4,6},{5,7},{6,4},{7,5},{8,10},{9,11},{10,... | collective-permute-start | bytes 393224 | tf_op jit(solution)/shard_map/ppermute | solution.py:700
  32.7 9.3 %collective-permute-start.5 = (bf16[384,128]{1,0:T(8,128)(2,1)S(1)}, bf16[384,128]{1,0:T(8,128)(2,1)S(1)}, u32[]{:S(2)}, u32[]{:S(2)}) collective-permute-start(bf16[384,128]{1,0:T(8,128)(2,1)S(1)} %get-tuple-element.66.after_ref.refs_0_), channel_id=1, source_target_pairs={{0,6},{1,7},{2,4},{3,5},{4,2},{5,3},{6,0},{7,1},{8,14},{9,15},{10,... | collective-permute-start | bytes 294920 | tf_op jit(solution)/shard_map/ppermute | solution.py:700
  34.5 9.9 %collective-permute-start.4 = (bf16[384,128]{1,0:T(8,128)(2,1)S(1)}, bf16[384,128]{1,0:T(8,128)(2,1)S(1)}, u32[]{:S(2)}, u32[]{:S(2)}) collective-permute-start(bf16[384,128]{1,0:T(8,128)(2,1)S(1)} %get-tuple-element.66.after_ref.refs_0_), channel_id=1, source_target_pairs={{0,4},{1,5},{2,6},{3,7},{4,0},{5,1},{6,2},{7,3},{8,12},{9,13},{10,... | collective-permute-start | bytes 294920 | tf_op jit(solution)/shard_map/ppermute | solution.py:700
  36.1 9.5 %collective-permute-start.7 = (bf16[512,128]{1,0:T(8,128)(2,1)S(1)}, bf16[512,128]{1,0:T(8,128)(2,1)S(1)}, u32[]{:S(2)}, u32[]{:S(2)}) collective-permute-start(bf16[512,128]{1,0:T(8,128)(2,1)S(1)} %get-tuple-element.67.refs_0_), channel_id=1, source_target_pairs={{0,1},{1,0},{2,3},{3,2},{4,5},{5,4},{6,7},{7,6},{8,9},{9,8},{10,11... | collective-permute-start | bytes 393224 | tf_op jit(solution)/shard_map/ppermute | solution.py:700
  39.3 6.4 %collective-permute-start.8 = (bf16[512,128]{1,0:T(8,128)(2,1)S(1)}, bf16[512,128]{1,0:T(8,128)(2,1)S(1)}, u32[]{:S(2)}, u32[]{:S(2)}) collective-permute-start(bf16[512,128]{1,0:T(8,128)(2,1)S(1)} %collective-permute-done.6.after_ref.refs_2_), channel_id=1, source_target_pairs={{0,1},{1,0},{2,3},{3,2},{4,5},{5,4},{6,7},{7,6},{8,9},{9,8},{10,11... | collective-permute-start | bytes 393224 | tf_op jit(solution)/shard_map/ppermute | solution.py:700
  43.6 4.7 %collective-permute-start.9 = (bf16[384,128]{1,0:T(8,128)(2,1)S(1)}, bf16[384,128]{1,0:T(8,128)(2,1)S(1)}, u32[]{:S(2)}, u32[]{:S(2)}) collective-permute-start(bf16[384,128]{1,0:T(8,128)(2,1)S(1)} %collective-permute-done.5.after_ref.refs_5_), channel_id=1, source_target_pairs={{0,1},{1,0},{2,3},{3,2},{4,5},{5,4},{6,7},{7,6},{8,9},{9,8},{10,11... | collective-permute-start | bytes 294920 | tf_op jit(solution)/shard_map/ppermute | solution.py:700
  44.5 4.9 %copy-start.1 = (bf16[1536,40]{0,1:T(8,128)(2,1)S(1)}, bf16[1536,40]{0,1:T(8,128)(2,1)}, u32[]{:S(2)}) copy-start(bf16[1536,40]{0,1:T(8,128)(2,1)} %param.28) | copy-start | bytes 368644
  44.5 4.9 %collective-permute-start.10 = (bf16[384,128]{1,0:T(8,128)(2,1)S(1)}, bf16[384,128]{1,0:T(8,128)(2,1)S(1)}, u32[]{:S(2)}, u32[]{:S(2)}) collective-permute-start(bf16[384,128]{1,0:T(8,128)(2,1)S(1)} %collective-permute-done.4.after_ref.refs_7_), channel_id=1, source_target_pairs={{0,1},{1,0},{2,3},{3,2},{4,5},{5,4},{6,7},{7,6},{8,9},{9,8},{10,11... | collective-permute-start | bytes 294920 | tf_op jit(solution)/shard_map/ppermute | solution.py:700
  54.4 4.7 %collective-permute-start.11 = (bf16[2,16,1536]{2,1,0:T(8,128)(2,1)S(1)}, bf16[2,16,1536]{2,1,0:T(8,128)(2,1)S(1)}, u32[]{:S(2)}, u32[]{:S(2)}) collective-permute-start(bf16[2,16,1536]{2,1,0:T(8,128)(2,1)S(1)} %get-tuple-element.91), channel_id=1, source_target_pairs={{0,1},{1,0},{2,3},{3,2},{4,5},{5,4},{6,7},{7,6},{8,9},{9,8},{10,11... | collective-permute-start | bytes 294920 | tf_op jit(solution)/shard_map/ppermute | solution.py:700
  55.5 6.1 %collective-permute-start.12 = (bf16[2,16,1536]{2,1,0:T(8,128)(2,1)S(1)}, bf16[2,16,1536]{2,1,0:T(8,128)(2,1)S(1)}, u32[]{:S(2)}, u32[]{:S(2)}) collective-permute-start(bf16[2,16,1536]{2,1,0:T(8,128)(2,1)S(1)} %get-tuple-element.93), channel_id=1, source_target_pairs={{0,1},{1,0},{2,3},{3,2},{4,5},{5,4},{6,7},{7,6},{8,9},{9,8},{10,11... | collective-permute-start | bytes 294920 | tf_op jit(solution)/shard_map/ppermute | solution.py:700
  59.1 6.1 %collective-permute-start.13 = (bf16[16,1536]{1,0:T(8,128)(2,1)S(1)}, bf16[16,1536]{1,0:T(8,128)(2,1)S(1)}, u32[]{:S(2)}, u32[]{:S(2)}) collective-permute-start(bf16[16,1536]{1,0:T(8,128)(2,1)S(1)} %get-tuple-element.95), channel_id=1, source_target_pairs={{0,6},{1,7},{2,4},{3,5},{4,2},{5,3},{6,0},{7,1},{8,14},{9,15},{10,... | collective-permute-start | bytes 147464 | tf_op jit(solution)/shard_map/ppermute | solution.py:700
  59.7 6.1 %collective-permute-start.14 = (bf16[16,1536]{1,0:T(8,128)(2,1)S(1)}, bf16[16,1536]{1,0:T(8,128)(2,1)S(1)}, u32[]{:S(2)}, u32[]{:S(2)}) collective-permute-start(bf16[16,1536]{1,0:T(8,128)(2,1)S(1)} %get-tuple-element.92.after_ref), channel_id=1, source_target_pairs={{0,4},{1,5},{2,6},{3,7},{4,0},{5,1},{6,2},{7,3},{8,12},{9,13},{10,... | collective-permute-start | bytes 147464 | tf_op jit(solution)/shard_map/ppermute | solution.py:700
  61.6 4.2 %collective-permute-start.15 = (bf16[16,1536]{1,0:T(8,128)(2,1)S(1)}, bf16[16,1536]{1,0:T(8,128)(2,1)S(1)}, u32[]{:S(2)}, u32[]{:S(2)}) collective-permute-start(bf16[16,1536]{1,0:T(8,128)(2,1)S(1)} %get-tuple-element.96), channel_id=1, source_target_pairs={{0,2},{1,3},{2,0},{3,1},{4,6},{5,7},{6,4},{7,5},{8,10},{9,11},{10,... | collective-permute-start | bytes 147464 | tf_op jit(solution)/shard_map/ppermute | solution.py:700

commit v9 on v6

--- a/solution.py
+++ b/solution.py
@@ -16,7 +16,7 @@
 DRAFT = 64
 WIDE = 128
 STEP = 2
-READY = 12
+READY = 6
 ORDER = (1, 3, 2)
 FETCHES = ((0, 1), (3,), (2,))
 
@@ -260,11 +260,11 @@
 def split_kernel(pairs, *refs):
     (
         pages_hbm, placement_hbm, lengths_hbm, leaf_hbm, keys_hbm, values_hbm, queries_hbm,
-        new_kv_hbm, residual_hbm, parents_hbm, router_hbm, ids_hbm, gain_hbm,
-    ) = refs[:13]
-    parts, refs = refs[13 : 13 + pairs], refs[13 + pairs :]
-    joined_ref, table_ref, parents_ref, router_ref, ids_ref, gain_ref = refs[:6]
-    pages_ref, placement_ref, lengths_ref, leaf_ref, keys_ref, values_ref, split_ref, sems = refs[6:]
+        new_kv_hbm, residual_hbm, parents_hbm, ids_hbm, gain_hbm,
+    ) = refs[:12]
+    parts, refs = refs[12 : 12 + pairs], refs[12 + pairs :]
+    joined_ref, table_ref, parents_ref, ids_ref, gain_ref = refs[:5]
+    pages_ref, placement_ref, lengths_ref, leaf_ref, keys_ref, values_ref, split_ref, sems = refs[5:]
     slot_count = pages_ref.shape[0]
     page_len = keys_ref.shape[1]
     tok_dev = joined_ref.shape[0]
@@ -276,7 +276,6 @@
         (lengths_hbm, lengths_ref),
         (leaf_hbm, leaf_ref),
         (parents_hbm, parents_ref),
-        (router_hbm, router_ref),
         (ids_hbm, ids_ref),
         (gain_hbm, gain_ref),
     ]
@@ -309,8 +308,8 @@
     return jnp.max(table_ref[row : row + 1, :]).astype(jnp.int32)
 
 
-def route_kernel(kv_width, after_ref, table_ref, pulled_ref, *refs):
-    del after_ref
+def route_kernel(kv_width, after_ref, weight_hbm, table_ref, pulled_ref, *refs):
+    del after_ref, weight_hbm
     parts, (sent_ref, res_ref, turned_ref, kv_ref) = refs[:-4][::-1], refs[-4:]
     rank = lax.axis_index("tp")
     other = 1 - lax.rem(rank, 2)
@@ -578,13 +577,14 @@
 
 
 def expert_kernel(
-    rows, count_ref, router_ref, gain_ref, down_ref, rest_ref, before_ref, part_ref, *refs
+    rows, count_ref, router_ref, gain_ref, before_ref, part_ref, *refs
 ):
     refs, late = refs[:-8], refs[-8:]
     far_ref, hid_ref, hidden_ref, attn_ref, x_ref, normed_ref, share_ref, residual_ref = late
     f32, bf16 = jnp.float32, jnp.bfloat16
     pairs = KV_HEADS // 2
     first = pairs // 2
+    down_refs, refs = refs[:2], refs[2:]
     blocks, refs = refs[: 2 * (pairs - first)], refs[2 * (pairs - first) :]
     weight_refs, unit_refs = refs[: pairs - first], refs[pairs - first :]
     unit_weights = [(ref, k) for ref in unit_refs for k in range(ref.shape[0])]
@@ -630,10 +630,10 @@
         gate, up = both[:, :unit_width], both[:, unit_width:]
         return (gate / (1.0 + jnp.exp(-gate)) * up * share_ref[u]).astype(bf16)
 
-    ready = down_ref.shape[0] // STEP
+    down_steps = [(ref, at) for ref in down_refs for at in range(ref.shape[0] // STEP)]
     for i in range(units // STEP):
         act = jnp.concatenate([one_unit(i * STEP + k) for k in range(STEP)], axis=1)
-        ref, at = (down_ref, i) if i < ready else (rest_ref, i - ready)
+        ref, at = down_steps[i]
         down = ref[at * STEP : (at + 1) * STEP].reshape(STEP * unit_width, model)
         part = jnp.dot(act, down, preferred_element_type=f32)
         hid_ref[...] = part if i == 0 else hid_ref[...] + part
@@ -753,11 +753,10 @@
         new_kv,
         residual,
         parents,
-        router_weight.T,
         expert_ids.T,
         norm_gain.reshape(model // WIDE, WIDE),
     )
-    *parts, joined, table, parents, router, ids, gain = pl.pallas_call(
+    *parts, joined, table, parents, ids, gain = pl.pallas_call(
         functools.partial(split_kernel, pairs),
         out_shape=(part,) * pairs
         + (
@@ -766,7 +765,7 @@
         )
         + tuple(pltpu.VMEM(a.shape, a.dtype) for a in loaded[9:]),
         in_specs=spaces("a" * len(loaded)),
-        out_specs=tuple(spaces("v" * (pairs + 6))),
+        out_specs=tuple(spaces("v" * (pairs + 5))),
         scratch_shapes=[
             slots_smem,
             slots_smem,
@@ -811,12 +810,12 @@
             jax.ShapeDtypeStruct((pairs * part.shape[1], WIDE), bf16),
             jax.ShapeDtypeStruct((kv_rows, WIDE), bf16),
         ),
-        in_specs=spaces("avv" + "v" * pairs),
+        in_specs=spaces("aavv" + "v" * pairs),
         out_specs=tuple(spaces("vvvv")),
         compiler_params=params(),
         cost_estimate=cost(4),
         name="route",
-    )(down_ready, table, pulled, *parts[::-1])
+    )(down_ready, *in_hbm(down_weight), table, pulled, *parts[::-1])
     turned = swap(turned, 1)
     packed = lax.all_to_all(packed, "tp", 0, 0, tiled=True)
     gate_up = pltpu.with_memory_space_constraint(gate_up, pltpu.VMEM)
@@ -891,12 +890,12 @@
         name="experts",
     )(
         count,
-        router,
+        pltpu.with_memory_space_constraint(router_weight.T, pltpu.VMEM),
         gain,
+        before,
+        attn_part,
         down_ready,
         down_rest,
-        before,
-        attn_part,
         *[a for k in reversed(range(pairs // 2, pairs)) for a in blocks[2 * k : 2 * k + 2]],
         weights[1],
         weights[2],

time: 67.2 us -> 66.8 us (level)
  transfers between devices with their start and end apart: 16 -> 16, of which waited for: 8 -> 8; matrix products, arithmetic and copies ran while one was open for 0% -> 0% of each run, Pallas kernels for 13% -> 14%
where the time goes in v9:
time: 66.8 us; the launch traced here: 66.5 us
  starting transfers between devices  21.1 us (32%)
  blocking collectives  18.3 us (27%)
  Pallas kernels  18.1 us (27%)
  waiting for transfers between devices  8.25 us (12%)
  between operations  0.76 us (1%)
    ppermute x16, starting transfers between devices, swap(): return lax.ppermute(rows, 'tp', [(i, i ^ mask) for i in range(count)])  21.1 us
    all_to_all x1, blocking collectives, per_device_packed(): packed = lax.all_to_all(packed, 'tp', 0, 0, tiled=True)  10.9 us
    ppermute x16, waiting for transfers between devices, swap(): return lax.ppermute(rows, 'tp', [(i, i ^ mask) for i in range(count)])  8.25 us
    all_gather x1, blocking collectives, per_device_packed(): pulled = lax.all_gather(joined, 'req', axis=0)  7.33 us
    pallas_call x1, Pallas kernels, per_device_packed(): pl.pallas_call(functools.partial(expert_kernel, block_rows), out_shape=(j...  5.04 us
    pallas_call x3, Pallas kernels, fetch(): pl.pallas_call(functools.partial(fetch_kernel, picks), out_shape=pltpu.VM...  4.21 us
    pallas_call x1, Pallas kernels, per_device_packed(): pl.pallas_call(functools.partial(early_kernel, block_rows), out_shape=(ja...  2.86 us
    pallas_call x1, Pallas kernels, per_device_packed(): pl.pallas_call(tree_kernel, out_shape=(pltpu.VMEM((ready,) + down_weight....  1.82 us
  transfers between devices with their start and end apart: 16, of which 8 were waited for; matrix products, arithmetic and copies ran while one was open for 0% of the time, Pallas kernels for 14%

profile of v9, /device:TPU:0, one launch (start us, length us, event | category | flops | bytes accessed | tf_op | source)
XLA Modules:
  0.0 66.5 jit_solution(3923648006015244995)
XLA Ops:
  0.6 1.4 %split.1 = (bf16[2,256,128]{2,1,0:T(8,128)(2,1)S(1)}, bf16[2,256,128]{2,1,0:T(8,128)(2,1)S(1)}, bf16[2,256,128]{2,1,0:T(8,128)(2,1)S(1)}, bf16[2,256,128]{2,1,0:...) custom-call(s32[2]{0:T(128)} %bitcast.10, ...), custom_call_target="tpu_custom_call" | custom-call | bytes 4194304 | tf_op jit(solution)/shard_map/split/pallas_call | solution.py:759
  2.1 5.1 %collective-permute-start = (bf16[2,256,128]{2,1,0:T(8,128)(2,1)S(1)}, bf16[2,256,128]{2,1,0:T(8,128)(2,1)S(1)}, u32[]{:S(2)}, u32[]{:S(2)}) collective-permute-start(bf16[2,256,128]{2,1,0:T(8,128)(2,1)S(1)} %get-tuple-element.49), channel_id=1, source_target_pairs={{0,6},{1,7},{2,4},{3,5},{4,2},{5,3},{6,0},{7,1},{8,14},{9,15},{10,... | collective-permute-start | bytes 393224 | tf_op jit(solution)/shard_map/ppermute | solution.py:699
  7.8 7.3 %all-gather = bf16[64,4096]{1,0:T(8,128)(2,1)S(1)} all-gather(bf16[16,4096]{1,0:T(8,128)(2,1)S(1)} %get-tuple-element.41), channel_id=2, replica_groups=mesh['req'=4,'tp'=8] {'req'}, dimensions={0}, use_global_device_ids=true | all-gather | bytes 655360 | tf_op jit(solution)/shard_map/all_gather | solution.py:785
  15.2 1.8 %tree.1 = (bf16[6,128,1536]{2,1,0:T(8,128)(2,1)S(1)}, f32[128,128]{1,0:T(8,128)S(1)}, bf16[2,64,64]{2,1,0:T(8,128)(2,1)S(1)}, f32[128,40]{1,0:T(8,128)S(1)}) custom-call(bf16[4,16,4096]{2,1,0:T(8,128)(2,1)S(1)} %bitcast.5, bf16[20,128,1536]{2,1,0:T(8,128)(2,1)} %down_hbm.3, f32[8,128]{1,0:T(8,128)S(1)} %get-tuple-element.42.table_ref, ...), custom_call_target="tpu_custom_call" | custom-call | bytes 8388608 | tf_op jit(solution)/shard_map/tree/pallas_call | solution.py:789
  17.0 1.3 %collective-permute-done.1.refs_1_ = bf16[2,256,128]{2,1,0:T(8,128)(2,1)S(1)} collective-permute-done((bf16[2,256,128]{2,1,0:T(8,128)(2,1)S(1)}, bf16[2,256,128]{2,1,0:T(8,128)(2,1)S(1)}, u32[]{:S(2)}, u32[]{:S(2)}) %collective-permute-start.1) | collective-permute-done | bytes 131104 | tf_op jit(solution)/shard_map/ppermute | solution.py:699
  18.5 1.6 %collective-permute-start.3 = (bf16[1024,128]{1,0:T(8,128)(2,1)S(1)}, bf16[1024,128]{1,0:T(8,128)(2,1)S(1)}, u32[]{:S(2)}, u32[]{:S(2)}) collective-permute-start(bf16[1024,128]{1,0:T(8,128)(2,1)S(1)} %get-tuple-element.55), channel_id=1, source_target_pairs={{0,1},{1,0},{2,3},{3,2},{4,5},{5,4},{6,7},{7,6},{8,9},{9,8},{10,11... | collective-permute-start | bytes 786440 | tf_op jit(solution)/shard_map/ppermute | solution.py:699
  20.0 10.9 %all_to_all.5.got_ref = bf16[8,48,128]{2,1,0:T(8,128)(2,1)S(1)} all-to-all(bf16[8,48,128]{2,1,0:T(8,128)(2,1)S(1)} %get-tuple-element.53), channel_id=1, replica_groups=mesh['req'=4,'tp'=8] {'tp'}, dimensions={0} | all-to-all | bytes 196608 | tf_op jit(solution)/shard_map/all_to_all | solution.py:820
  31.0 1.6 %attend.1 = (bf16[384,128]{1,0:T(8,128)(2,1)S(1)}, bf16[512,128]{1,0:T(8,128)(2,1)S(1)}) custom-call(bf16[20,1536,256]{2,1,0:T(8,128)(2,1)S(1)} %copy-done, f32[8,128]{1,0:T(8,128)S(1)} %get-tuple-element.42.table_ref, f32[128,128]{1,0:T(8,128)S(1)} %get-tuple-element.47.reach_ref, bf16[8,48,128]{2,1,0:T(8,128)(2,1)S(1)} %all_to_all.5.got_ref, ...), custom_call_target="tpu_custom_call" | custom-call | bytes 8388608 | tf_op jit(solution)/shard_map/attend/pallas_call | solution.py:823
  32.7 1.9 %collective-permute-start.5 = (bf16[384,128]{1,0:T(8,128)(2,1)S(1)}, bf16[384,128]{1,0:T(8,128)(2,1)S(1)}, u32[]{:S(2)}, u32[]{:S(2)}) collective-permute-start(bf16[384,128]{1,0:T(8,128)(2,1)S(1)} %get-tuple-element.57.after_ref.refs_0_), channel_id=1, source_target_pairs={{0,6},{1,7},{2,4},{3,5},{4,2},{5,3},{6,0},{7,1},{8,14},{9,15},{10,... | collective-permute-start | bytes 294920 | tf_op jit(solution)/shard_map/ppermute | solution.py:699
  34.5 1.6 %collective-permute-start.4 = (bf16[384,128]{1,0:T(8,128)(2,1)S(1)}, bf16[384,128]{1,0:T(8,128)(2,1)S(1)}, u32[]{:S(2)}, u32[]{:S(2)}) collective-permute-start(bf16[384,128]{1,0:T(8,128)(2,1)S(1)} %get-tuple-element.57.after_ref.refs_0_), channel_id=1, source_target_pairs={{0,4},{1,5},{2,6},{3,7},{4,0},{5,1},{6,2},{7,3},{8,12},{9,13},{10,... | collective-permute-start | bytes 294920 | tf_op jit(solution)/shard_map/ppermute | solution.py:699
  36.4 1.6 %fetch.3.weight_ref = bf16[768,1536]{1,0:T(8,128)(2,1)S(1)} custom-call(bf16[384,128]{1,0:T(8,128)(2,1)S(1)} %get-tuple-element.57.after_ref.refs_0_, bf16[1536,1536]{1,0:T(8,128)(2,1)} %source_ref.5), custom_call_target="tpu_custom_call" | custom-call | bytes 2097152 | tf_op jit(solution)/shard_map/fetch/pallas_call | solution.py:704
  38.1 1.2 %collective-permute-done.6.after_ref.refs_2_ = bf16[512,128]{1,0:T(8,128)(2,1)S(1)} collective-permute-done((bf16[512,128]{1,0:T(8,128)(2,1)S(1)}, bf16[512,128]{1,0:T(8,128)(2,1)S(1)}, u32[]{:S(2)}, u32[]{:S(2)}) %collective-permute-start.6) | collective-permute-done | bytes 131104 | tf_op jit(solution)/shard_map/ppermute | solution.py:699
  39.3 1.2 %collective-permute-start.8 = (bf16[512,128]{1,0:T(8,128)(2,1)S(1)}, bf16[512,128]{1,0:T(8,128)(2,1)S(1)}, u32[]{:S(2)}, u32[]{:S(2)}) collective-permute-start(bf16[512,128]{1,0:T(8,128)(2,1)S(1)} %collective-permute-done.6.after_ref.refs_2_), channel_id=1, source_target_pairs={{0,1},{1,0},{2,3},{3,2},{4,5},{5,4},{6,7},{7,6},{8,9},{9,8},{10,11... | collective-permute-start | bytes 393224 | tf_op jit(solution)/shard_map/ppermute | solution.py:699
  40.5 1.3 %fetch.4.refs_6_ = bf16[384,1536]{1,0:T(8,128)(2,1)S(1)} custom-call(bf16[512,128]{1,0:T(8,128)(2,1)S(1)} %collective-permute-done.6.after_ref.refs_2_, bf16[1536,1536]{1,0:T(8,128)(2,1)} %source_ref.5), custom_call_target="tpu_custom_call" | custom-call | bytes 1048576 | tf_op jit(solution)/shard_map/fetch/pallas_call | solution.py:704
  41.8 1.3 %fetch.5.refs_7_ = bf16[384,1536]{1,0:T(8,128)(2,1)S(1)} custom-call(bf16[384,128]{1,0:T(8,128)(2,1)S(1)} %collective-permute-done.5.after_ref.refs_2_, bf16[1536,1536]{1,0:T(8,128)(2,1)} %source_ref.5), custom_call_target="tpu_custom_call" | custom-call | bytes 1048576 | tf_op jit(solution)/shard_map/fetch/pallas_call | solution.py:704
  44.0 1.2 %collective-permute-start.10 = (bf16[384,128]{1,0:T(8,128)(2,1)S(1)}, bf16[384,128]{1,0:T(8,128)(2,1)S(1)}, u32[]{:S(2)}, u32[]{:S(2)}) collective-permute-start(bf16[384,128]{1,0:T(8,128)(2,1)S(1)} %collective-permute-done.4.after_ref.refs_4_), channel_id=1, source_target_pairs={{0,1},{1,0},{2,3},{3,2},{4,5},{5,4},{6,7},{7,6},{8,9},{9,8},{10,11... | collective-permute-start | bytes 294920 | tf_op jit(solution)/shard_map/ppermute | solution.py:699
  45.3 2.9 %early.1 = (f32[128,1536]{1,0:T(8,128)S(1)}, bf16[16,1536]{1,0:T(8,128)(2,1)S(1)}, bf16[14,128,1536]{2,1,0:T(8,128)(2,1)S(1)}) custom-call(bf16[384,128]{1,0:T(8,128)(2,1)S(1)} %collective-permute-done.4.after_ref.refs_4_, bf16[20,128,1536]{2,1,0:T(8,128)(2,1)} %down_hbm.3, bf16[768,1536]{1,0:T(8,128)(2,1)S(1)} %fetch.3.weight_ref, ...), custom_call_target="tpu_custom_call" | custom-call | bytes 4194304 | tf_op jit(solution)/shard_map/early/pallas_call | solution.py:845
  48.8 5.0 %experts.1 = (bf16[2,16,1536]{2,1,0:T(8,128)(2,1)S(1)}, f32[128,1536]{1,0:T(8,128)S(1)}, f32[16,1536]{1,0:T(8,128)S(1)}, bf16[16,1536]{1,0:T(8,128)(2,1)S(1)}) custom-call(f32[128,40]{1,0:T(8,128)S(1)} %get-tuple-element.45.count_ref, bf16[40,1536]{1,0:T(8,128)(2,1)S(1)} %bitcast.7, f32[12,128]{1,0:T(8,128)S(1)} %get-tuple-element.46.gain_ref, ...), custom_call_target="tpu_custom_call" | custom-call | tf_op jit(solution)/shard_map/experts/pallas_call | solution.py:873
  53.9 1.0 %collective-permute-start.11 = (bf16[2,16,1536]{2,1,0:T(8,128)(2,1)S(1)}, bf16[2,16,1536]{2,1,0:T(8,128)(2,1)S(1)}, u32[]{:S(2)}, u32[]{:S(2)}) collective-permute-start(bf16[2,16,1536]{2,1,0:T(8,128)(2,1)S(1)} %get-tuple-element.73), channel_id=1, source_target_pairs={{0,1},{1,0},{2,3},{3,2},{4,5},{5,4},{6,7},{7,6},{8,9},{9,8},{10,11... | collective-permute-start | bytes 294920 | tf_op jit(solution)/shard_map/ppermute | solution.py:699
  55.0 1.1 %collective-permute-start.12 = (bf16[2,16,1536]{2,1,0:T(8,128)(2,1)S(1)}, bf16[2,16,1536]{2,1,0:T(8,128)(2,1)S(1)}, u32[]{:S(2)}, u32[]{:S(2)}) collective-permute-start(bf16[2,16,1536]{2,1,0:T(8,128)(2,1)S(1)} %get-tuple-element.75), channel_id=1, source_target_pairs={{0,1},{1,0},{2,3},{3,2},{4,5},{5,4},{6,7},{7,6},{8,9},{9,8},{10,11... | collective-permute-start | bytes 294920 | tf_op jit(solution)/shard_map/ppermute | solution.py:699
  56.1 2.5 %collective-permute-done.11.got_ref = bf16[2,16,1536]{2,1,0:T(8,128)(2,1)S(1)} collective-permute-done((bf16[2,16,1536]{2,1,0:T(8,128)(2,1)S(1)}, bf16[2,16,1536]{2,1,0:T(8,128)(2,1)S(1)}, u32[]{:S(2)}, u32[]{:S(2)}) %collective-permute-start.11) | collective-permute-done | bytes 98336 | tf_op jit(solution)/shard_map/ppermute | solution.py:699
  59.5 1.8 %collective-permute-start.14 = (bf16[16,1536]{1,0:T(8,128)(2,1)S(1)}, bf16[16,1536]{1,0:T(8,128)(2,1)S(1)}, u32[]{:S(2)}, u32[]{:S(2)}) collective-permute-start(bf16[16,1536]{1,0:T(8,128)(2,1)S(1)} %get-tuple-element.74.after_ref), channel_id=1, source_target_pairs={{0,4},{1,5},{2,6},{3,7},{4,0},{5,1},{6,2},{7,3},{8,12},{9,13},{10,... | collective-permute-start | bytes 147464 | tf_op jit(solution)/shard_map/ppermute | solution.py:699
  61.3 1.8 %collective-permute-start.15 = (bf16[16,1536]{1,0:T(8,128)(2,1)S(1)}, bf16[16,1536]{1,0:T(8,128)(2,1)S(1)}, u32[]{:S(2)}, u32[]{:S(2)}) collective-permute-start(bf16[16,1536]{1,0:T(8,128)(2,1)S(1)} %get-tuple-element.78), channel_id=1, source_target_pairs={{0,2},{1,3},{2,0},{3,1},{4,6},{5,7},{6,4},{7,5},{8,10},{9,11},{10,... | collective-permute-start | bytes 147464 | tf_op jit(solution)/shard_map/ppermute | solution.py:699
  63.3 1.3 %collective-permute-done.13.refs_1_ = bf16[16,1536]{1,0:T(8,128)(2,1)S(1)} collective-permute-done((bf16[16,1536]{1,0:T(8,128)(2,1)S(1)}, bf16[16,1536]{1,0:T(8,128)(2,1)S(1)}, u32[]{:S(2)}, u32[]{:S(2)}) %collective-permute-start.13) | collective-permute-done | bytes 49184 | tf_op jit(solution)/shard_map/ppermute | solution.py:699
  (28 shorter events, 5.9 us)
Async XLA Ops:
  2.1 14.9 %collective-permute-start = (bf16[2,256,128]{2,1,0:T(8,128)(2,1)S(1)}, bf16[2,256,128]{2,1,0:T(8,128)(2,1)S(1)}, u32[]{:S(2)}, u32[]{:S(2)}) collective-permute-start(bf16[2,256,128]{2,1,0:T(8,128)(2,1)S(1)} %get-tuple-element.49), channel_id=1, source_target_pairs={{0,6},{1,7},{2,4},{3,5},{4,2},{5,3},{6,0},{7,1},{8,14},{9,15},{10,... | collective-permute-start | bytes 393224 | tf_op jit(solution)/shard_map/ppermute | solution.py:699
  7.2 11.1 %collective-permute-start.1 = (bf16[2,256,128]{2,1,0:T(8,128)(2,1)S(1)}, bf16[2,256,128]{2,1,0:T(8,128)(2,1)S(1)}, u32[]{:S(2)}, u32[]{:S(2)}) collective-permute-start(bf16[2,256,128]{2,1,0:T(8,128)(2,1)S(1)} %get-tuple-element.50), channel_id=1, source_target_pairs={{0,4},{1,5},{2,6},{3,7},{4,0},{5,1},{6,2},{7,3},{8,12},{9,13},{10,... | collective-permute-start | bytes 393224 | tf_op jit(solution)/shard_map/ppermute | solution.py:699
  7.2 11.1 %collective-permute-start.2 = (bf16[2,256,128]{2,1,0:T(8,128)(2,1)S(1)}, bf16[2,256,128]{2,1,0:T(8,128)(2,1)S(1)}, u32[]{:S(2)}, u32[]{:S(2)}) collective-permute-start(bf16[2,256,128]{2,1,0:T(8,128)(2,1)S(1)} %get-tuple-element.51), channel_id=1, source_target_pairs={{0,2},{1,3},{2,0},{3,1},{4,6},{5,7},{6,4},{7,5},{8,10},{9,11},{10,... | collective-permute-start | bytes 393224 | tf_op jit(solution)/shard_map/ppermute | solution.py:699
  15.1 15.8 %copy-start = (bf16[20,1536,256]{2,1,0:T(8,128)(2,1)S(1)}, bf16[20,1536,256]{2,1,0:T(8,128)(2,1)}, u32[]{:S(2)}) copy-start(bf16[20,1536,256]{2,1,0:T(8,128)(2,1)} %refs_8_.3) | copy-start | bytes 47185924
  18.5 12.5 %collective-permute-start.3 = (bf16[1024,128]{1,0:T(8,128)(2,1)S(1)}, bf16[1024,128]{1,0:T(8,128)(2,1)S(1)}, u32[]{:S(2)}, u32[]{:S(2)}) collective-permute-start(bf16[1024,128]{1,0:T(8,128)(2,1)S(1)} %get-tuple-element.55), channel_id=1, source_target_pairs={{0,1},{1,0},{2,3},{3,2},{4,5},{5,4},{6,7},{7,6},{8,9},{9,8},{10,11... | collective-permute-start | bytes 786440 | tf_op jit(solution)/shard_map/ppermute | solution.py:699
  32.6 6.7 %collective-permute-start.6 = (bf16[512,128]{1,0:T(8,128)(2,1)S(1)}, bf16[512,128]{1,0:T(8,128)(2,1)S(1)}, u32[]{:S(2)}, u32[]{:S(2)}) collective-permute-start(bf16[512,128]{1,0:T(8,128)(2,1)S(1)} %get-tuple-element.58.refs_0_), channel_id=1, source_target_pairs={{0,2},{1,3},{2,0},{3,1},{4,6},{5,7},{6,4},{7,5},{8,10},{9,11},{10,... | collective-permute-start | bytes 393224 | tf_op jit(solution)/shard_map/ppermute | solution.py:699
  32.7 9.1 %collective-permute-start.5 = (bf16[384,128]{1,0:T(8,128)(2,1)S(1)}, bf16[384,128]{1,0:T(8,128)(2,1)S(1)}, u32[]{:S(2)}, u32[]{:S(2)}) collective-permute-start(bf16[384,128]{1,0:T(8,128)(2,1)S(1)} %get-tuple-element.57.after_ref.refs_0_), channel_id=1, source_target_pairs={{0,6},{1,7},{2,4},{3,5},{4,2},{5,3},{6,0},{7,1},{8,14},{9,15},{10,... | collective-permute-start | bytes 294920 | tf_op jit(solution)/shard_map/ppermute | solution.py:699
  34.5 9.4 %collective-permute-start.4 = (bf16[384,128]{1,0:T(8,128)(2,1)S(1)}, bf16[384,128]{1,0:T(8,128)(2,1)S(1)}, u32[]{:S(2)}, u32[]{:S(2)}) collective-permute-start(bf16[384,128]{1,0:T(8,128)(2,1)S(1)} %get-tuple-element.57.after_ref.refs_0_), channel_id=1, source_target_pairs={{0,4},{1,5},{2,6},{3,7},{4,0},{5,1},{6,2},{7,3},{8,12},{9,13},{10,... | collective-permute-start | bytes 294920 | tf_op jit(solution)/shard_map/ppermute | solution.py:699
  36.1 9.1 %collective-permute-start.7 = (bf16[512,128]{1,0:T(8,128)(2,1)S(1)}, bf16[512,128]{1,0:T(8,128)(2,1)S(1)}, u32[]{:S(2)}, u32[]{:S(2)}) collective-permute-start(bf16[512,128]{1,0:T(8,128)(2,1)S(1)} %get-tuple-element.58.refs_0_), channel_id=1, source_target_pairs={{0,1},{1,0},{2,3},{3,2},{4,5},{5,4},{6,7},{7,6},{8,9},{9,8},{10,11... | collective-permute-start | bytes 393224 | tf_op jit(solution)/shard_map/ppermute | solution.py:699
  39.3 6.0 %collective-permute-start.8 = (bf16[512,128]{1,0:T(8,128)(2,1)S(1)}, bf16[512,128]{1,0:T(8,128)(2,1)S(1)}, u32[]{:S(2)}, u32[]{:S(2)}) collective-permute-start(bf16[512,128]{1,0:T(8,128)(2,1)S(1)} %collective-permute-done.6.after_ref.refs_2_), channel_id=1, source_target_pairs={{0,1},{1,0},{2,3},{3,2},{4,5},{5,4},{6,7},{7,6},{8,9},{9,8},{10,11... | collective-permute-start | bytes 393224 | tf_op jit(solution)/shard_map/ppermute | solution.py:699
  43.1 5.8 %copy-start.1 = (bf16[1536,40]{0,1:T(8,128)(2,1)S(1)}, bf16[1536,40]{0,1:T(8,128)(2,1)}, u32[]{:S(2)}) copy-start(bf16[1536,40]{0,1:T(8,128)(2,1)} %param.28) | copy-start | bytes 368644
  43.1 5.1 %collective-permute-start.9 = (bf16[384,128]{1,0:T(8,128)(2,1)S(1)}, bf16[384,128]{1,0:T(8,128)(2,1)S(1)}, u32[]{:S(2)}, u32[]{:S(2)}) collective-permute-start(bf16[384,128]{1,0:T(8,128)(2,1)S(1)} %collective-permute-done.5.after_ref.refs_2_), channel_id=1, source_target_pairs={{0,1},{1,0},{2,3},{3,2},{4,5},{5,4},{6,7},{7,6},{8,9},{9,8},{10,11... | collective-permute-start | bytes 294920 | tf_op jit(solution)/shard_map/ppermute | solution.py:699
  44.0 4.9 %collective-permute-start.10 = (bf16[384,128]{1,0:T(8,128)(2,1)S(1)}, bf16[384,128]{1,0:T(8,128)(2,1)S(1)}, u32[]{:S(2)}, u32[]{:S(2)}) collective-permute-start(bf16[384,128]{1,0:T(8,128)(2,1)S(1)} %collective-permute-done.4.after_ref.refs_4_), channel_id=1, source_target_pairs={{0,1},{1,0},{2,3},{3,2},{4,5},{5,4},{6,7},{7,6},{8,9},{9,8},{10,11... | collective-permute-start | bytes 294920 | tf_op jit(solution)/shard_map/ppermute | solution.py:699
  53.9 4.7 %collective-permute-start.11 = (bf16[2,16,1536]{2,1,0:T(8,128)(2,1)S(1)}, bf16[2,16,1536]{2,1,0:T(8,128)(2,1)S(1)}, u32[]{:S(2)}, u32[]{:S(2)}) collective-permute-start(bf16[2,16,1536]{2,1,0:T(8,128)(2,1)S(1)} %get-tuple-element.73), channel_id=1, source_target_pairs={{0,1},{1,0},{2,3},{3,2},{4,5},{5,4},{6,7},{7,6},{8,9},{9,8},{10,11... | collective-permute-start | bytes 294920 | tf_op jit(solution)/shard_map/ppermute | solution.py:699
  55.0 6.3 %collective-permute-start.12 = (bf16[2,16,1536]{2,1,0:T(8,128)(2,1)S(1)}, bf16[2,16,1536]{2,1,0:T(8,128)(2,1)S(1)}, u32[]{:S(2)}, u32[]{:S(2)}) collective-permute-start(bf16[2,16,1536]{2,1,0:T(8,128)(2,1)S(1)} %get-tuple-element.75), channel_id=1, source_target_pairs={{0,1},{1,0},{2,3},{3,2},{4,5},{5,4},{6,7},{7,6},{8,9},{9,8},{10,11... | collective-permute-start | bytes 294920 | tf_op jit(solution)/shard_map/ppermute | solution.py:699
  58.6 6.1 %collective-permute-start.13 = (bf16[16,1536]{1,0:T(8,128)(2,1)S(1)}, bf16[16,1536]{1,0:T(8,128)(2,1)S(1)}, u32[]{:S(2)}, u32[]{:S(2)}) collective-permute-start(bf16[16,1536]{1,0:T(8,128)(2,1)S(1)} %get-tuple-element.77), channel_id=1, source_target_pairs={{0,6},{1,7},{2,4},{3,5},{4,2},{5,3},{6,0},{7,1},{8,14},{9,15},{10,... | collective-permute-start | bytes 147464 | tf_op jit(solution)/shard_map/ppermute | solution.py:699
  59.5 6.1 %collective-permute-start.14 = (bf16[16,1536]{1,0:T(8,128)(2,1)S(1)}, bf16[16,1536]{1,0:T(8,128)(2,1)S(1)}, u32[]{:S(2)}, u32[]{:S(2)}) collective-permute-start(bf16[16,1536]{1,0:T(8,128)(2,1)S(1)} %get-tuple-element.74.after_ref), channel_id=1, source_target_pairs={{0,4},{1,5},{2,6},{3,7},{4,0},{5,1},{6,2},{7,3},{8,12},{9,13},{10,... | collective-permute-start | bytes 147464 | tf_op jit(solution)/shard_map/ppermute | solution.py:699
  61.3 4.5 %collective-permute-start.15 = (bf16[16,1536]{1,0:T(8,128)(2,1)S(1)}, bf16[16,1536]{1,0:T(8,128)(2,1)S(1)}, u32[]{:S(2)}, u32[]{:S(2)}) collective-permute-start(bf16[16,1536]{1,0:T(8,128)(2,1)S(1)} %get-tuple-element.78), channel_id=1, source_target_pairs={{0,2},{1,3},{2,0},{3,1},{4,6},{5,7},{6,4},{7,5},{8,10},{9,11},{10,... | collective-permute-start | bytes 147464 | tf_op jit(solution)/shard_map/ppermute | solution.py:699

commit v10 on v8

--- a/solution.py
+++ b/solution.py
@@ -577,6 +577,16 @@
     copy.wait()
 
 
+def middle_kernel(k, rows, before_ref, part_ref, weight_ref, mine_ref, other_ref, *refs):
+    hid_ref, attn_ref, residual_ref, x_ref = refs
+    residual_ref[...] = jnp.zeros_like(residual_ref)
+    x_ref[...] = join_heads(k, rows, hid_ref.shape[0], mine_ref, other_ref, residual_ref)
+    attn_ref[...] = part_ref[...]
+    keep_own(k, x_ref, 0, attn_ref)
+    projected = jnp.dot(x_ref[...], weight_ref[...], preferred_element_type=jnp.float32)
+    hid_ref[...] = before_ref[...] + residual_ref[...] + projected
+
+
 def expert_kernel(
     rows, count_ref, router_ref, gain_ref, before_ref, part_ref, *refs
 ):
@@ -584,8 +594,8 @@
     far_ref, hid_ref, hidden_ref, attn_ref, x_ref, normed_ref, share_ref, residual_ref = late
     f32, bf16 = jnp.float32, jnp.bfloat16
     pairs = KV_HEADS // 2
-    first = pairs // 2
-    down_refs, refs = refs[: pairs + 1], refs[pairs + 1 :]
+    first, pairs = pairs // 2, pairs // 2 + 1
+    down_refs, refs = refs[: KV_HEADS // 2 + 1], refs[KV_HEADS // 2 + 1 :]
     blocks, refs = refs[: 2 * (pairs - first)], refs[2 * (pairs - first) :]
     weight_refs, unit_refs = refs[: pairs - first], refs[pairs - first :]
     unit_weights = [(ref, k) for ref in unit_refs for k in range(ref.shape[0])]
@@ -876,6 +886,22 @@
         name="accept",
     )(chosen, near_block, *blocks[1:4])
     unit_weights = (gate_up,)
+    before, attn_part = pl.pallas_call(
+        functools.partial(middle_kernel, pairs - 1, block_rows),
+        out_shape=(
+            jax.ShapeDtypeStruct((group_rows, model), f32),
+            pltpu.VMEM(queries.shape, bf16),
+        ),
+        in_specs=spaces("v" * 5),
+        out_specs=tuple(spaces("vv")),
+        scratch_shapes=[
+            pltpu.VMEM((group_rows, model), f32),
+            pltpu.VMEM((group_rows, HEADS * HEAD // pairs), bf16),
+        ],
+        compiler_params=params(),
+        cost_estimate=cost(1),
+        name="middle",
+    )(before, attn_part, weights[1], *blocks[-2:])
     far, sums, hidden, attn_own = pl.pallas_call(
         functools.partial(expert_kernel, block_rows),
         out_shape=(
@@ -884,10 +910,10 @@
             jax.ShapeDtypeStruct((tok_dev, model), f32),
             pltpu.VMEM(queries.shape, bf16),
         ),
-        in_specs=spaces("v" * (6 + len(downs) + pairs + pairs // 2 + len(unit_weights))),
+        in_specs=spaces("v" * (6 + len(downs) + 3 + len(unit_weights))),
         out_specs=tuple(spaces("vvvv")),
         scratch_shapes=[
-            pltpu.VMEM((group_rows, HEADS * HEAD // 2), bf16),
+            pltpu.VMEM((group_rows, HEADS * HEAD // pairs), bf16),
             pltpu.VMEM((group_rows, model), bf16),
             pltpu.VMEM((units, group_rows, gate_up.shape[2] // 2), f32),
             pltpu.VMEM((group_rows, model), f32),
@@ -902,8 +928,7 @@
         attn_part,
         *downs,
         down_rest,
-        *[a for k in reversed(range(pairs // 2, pairs)) for a in blocks[2 * k : 2 * k + 2]],
-        weights[1],
+        *blocks[pairs : pairs + 2],
         weights[2],
         *unit_weights,
     )

time: 66.8 us -> 66.6 us (level)
  transfers between devices with their start and end apart: 16 -> 16, of which waited for: 7 -> 7; matrix products, arithmetic and copies ran while one was open for 0% -> 0% of each run, Pallas kernels for 14% -> 15%
where the time goes in v10:
time: 66.6 us; the launch traced here: 66.3 us
  starting transfers between devices  21.1 us (32%)
  Pallas kernels  18.5 us (28%)
  blocking collectives  18.3 us (27%)
  waiting for transfers between devices  7.67 us (12%)
  between operations  0.75 us (1%)
    ppermute x16, starting transfers between devices, swap(): return lax.ppermute(rows, 'tp', [(i, i ^ mask) for i in range(count)])  21.1 us
    all_to_all x1, blocking collectives, per_device_packed(): packed = lax.all_to_all(packed, 'tp', 0, 0, tiled=True)  10.9 us
    ppermute x16, waiting for transfers between devices, swap(): return lax.ppermute(rows, 'tp', [(i, i ^ mask) for i in range(count)])  7.67 us
    all_gather x1, blocking collectives, per_device_packed(): pulled = lax.all_gather(joined, 'req', axis=0)  7.33 us
    pallas_call x3, Pallas kernels, fetch(): pl.pallas_call(functools.partial(fetch_kernel, picks, first), out_shape=(...  4.95 us
    pallas_call x1, Pallas kernels, per_device_packed(): pl.pallas_call(functools.partial(expert_kernel, block_rows), out_shape=(j...  4.84 us
    pallas_call x1, Pallas kernels, per_device_packed(): pl.pallas_call(functools.partial(early_kernel, block_rows), out_shape=(ja...  2.19 us
    pallas_call x1, Pallas kernels, per_device_packed(): pl.pallas_call(tree_kernel, out_shape=(pltpu.VMEM((ready,) + down_weight....  1.82 us
  transfers between devices with their start and end apart: 16, of which 7 were waited for; matrix products, arithmetic and copies ran while one was open for 0% of the time, Pallas kernels for 15%

profile of v10, /device:TPU:0, one launch (start us, length us, event | category | flops | bytes accessed | tf_op | source)
XLA Modules:
  0.0 66.3 jit_solution(9863518344356596464)
XLA Ops:
  0.6 1.4 %split.1 = (bf16[2,256,128]{2,1,0:T(8,128)(2,1)S(1)}, bf16[2,256,128]{2,1,0:T(8,128)(2,1)S(1)}, bf16[2,256,128]{2,1,0:T(8,128)(2,1)S(1)}, bf16[2,256,128]{2,1,0:...) custom-call(s32[2]{0:T(128)} %bitcast.10, ...), custom_call_target="tpu_custom_call" | custom-call | bytes 4194304 | tf_op jit(solution)/shard_map/split/pallas_call | solution.py:771
  2.1 5.1 %collective-permute-start = (bf16[2,256,128]{2,1,0:T(8,128)(2,1)S(1)}, bf16[2,256,128]{2,1,0:T(8,128)(2,1)S(1)}, u32[]{:S(2)}, u32[]{:S(2)}) collective-permute-start(bf16[2,256,128]{2,1,0:T(8,128)(2,1)S(1)} %get-tuple-element.60), channel_id=1, source_target_pairs={{0,6},{1,7},{2,4},{3,5},{4,2},{5,3},{6,0},{7,1},{8,14},{9,15},{10,... | collective-permute-start | bytes 393224 | tf_op jit(solution)/shard_map/ppermute | solution.py:710
  7.8 7.3 %all-gather = bf16[64,4096]{1,0:T(8,128)(2,1)S(1)} all-gather(bf16[16,4096]{1,0:T(8,128)(2,1)S(1)} %get-tuple-element.52), channel_id=2, replica_groups=mesh['req'=4,'tp'=8] {'req'}, dimensions={0}, use_global_device_ids=true | all-gather | bytes 655360 | tf_op jit(solution)/shard_map/all_gather | solution.py:797
  15.2 1.8 %tree.1 = (bf16[6,128,1536]{2,1,0:T(8,128)(2,1)S(1)}, f32[128,128]{1,0:T(8,128)S(1)}, bf16[2,64,64]{2,1,0:T(8,128)(2,1)S(1)}, f32[128,40]{1,0:T(8,128)S(1)}) custom-call(bf16[4,16,4096]{2,1,0:T(8,128)(2,1)S(1)} %bitcast.5, bf16[20,128,1536]{2,1,0:T(8,128)(2,1)} %down_hbm.9, f32[8,128]{1,0:T(8,128)S(1)} %get-tuple-element.53.table_ref, ...), custom_call_target="tpu_custom_call" | custom-call | bytes 8388608 | tf_op jit(solution)/shard_map/tree/pallas_call | solution.py:802
  17.0 1.3 %collective-permute-done.1.refs_1_ = bf16[2,256,128]{2,1,0:T(8,128)(2,1)S(1)} collective-permute-done((bf16[2,256,128]{2,1,0:T(8,128)(2,1)S(1)}, bf16[2,256,128]{2,1,0:T(8,128)(2,1)S(1)}, u32[]{:S(2)}, u32[]{:S(2)}) %collective-permute-start.1) | collective-permute-done | bytes 131104 | tf_op jit(solution)/shard_map/ppermute | solution.py:710
  18.5 1.6 %collective-permute-start.3 = (bf16[1024,128]{1,0:T(8,128)(2,1)S(1)}, bf16[1024,128]{1,0:T(8,128)(2,1)S(1)}, u32[]{:S(2)}, u32[]{:S(2)}) collective-permute-start(bf16[1024,128]{1,0:T(8,128)(2,1)S(1)} %get-tuple-element.66), channel_id=1, source_target_pairs={{0,1},{1,0},{2,3},{3,2},{4,5},{5,4},{6,7},{7,6},{8,9},{9,8},{10,11... | collective-permute-start | bytes 786440 | tf_op jit(solution)/shard_map/ppermute | solution.py:710
  20.0 10.9 %all_to_all.5.got_ref = bf16[8,48,128]{2,1,0:T(8,128)(2,1)S(1)} all-to-all(bf16[8,48,128]{2,1,0:T(8,128)(2,1)S(1)} %get-tuple-element.64), channel_id=1, replica_groups=mesh['req'=4,'tp'=8] {'tp'}, dimensions={0} | all-to-all | bytes 196608 | tf_op jit(solution)/shard_map/all_to_all | solution.py:833
  31.0 1.6 %attend.1 = (bf16[384,128]{1,0:T(8,128)(2,1)S(1)}, bf16[512,128]{1,0:T(8,128)(2,1)S(1)}) custom-call(bf16[20,1536,256]{2,1,0:T(8,128)(2,1)S(1)} %copy-done, f32[8,128]{1,0:T(8,128)S(1)} %get-tuple-element.53.table_ref, f32[128,128]{1,0:T(8,128)S(1)} %get-tuple-element.58.reach_ref, bf16[8,48,128]{2,1,0:T(8,128)(2,1)S(1)} %all_to_all.5.got_ref, ...), custom_call_target="tpu_custom_call" | custom-call | bytes 8388608 | tf_op jit(solution)/shard_map/attend/pallas_call | solution.py:836
  32.7 1.9 %collective-permute-start.5 = (bf16[384,128]{1,0:T(8,128)(2,1)S(1)}, bf16[384,128]{1,0:T(8,128)(2,1)S(1)}, u32[]{:S(2)}, u32[]{:S(2)}) collective-permute-start(bf16[384,128]{1,0:T(8,128)(2,1)S(1)} %get-tuple-element.68.after_ref.refs_0_), channel_id=1, source_target_pairs={{0,6},{1,7},{2,4},{3,5},{4,2},{5,3},{6,0},{7,1},{8,14},{9,15},{10,... | collective-permute-start | bytes 294920 | tf_op jit(solution)/shard_map/ppermute | solution.py:710
  34.5 1.6 %collective-permute-start.4 = (bf16[384,128]{1,0:T(8,128)(2,1)S(1)}, bf16[384,128]{1,0:T(8,128)(2,1)S(1)}, u32[]{:S(2)}, u32[]{:S(2)}) collective-permute-start(bf16[384,128]{1,0:T(8,128)(2,1)S(1)} %get-tuple-element.68.after_ref.refs_0_), channel_id=1, source_target_pairs={{0,4},{1,5},{2,6},{3,7},{4,0},{5,1},{6,2},{7,3},{8,12},{9,13},{10,... | collective-permute-start | bytes 294920 | tf_op jit(solution)/shard_map/ppermute | solution.py:710
  36.4 1.9 %fetch.3 = (bf16[768,1536]{1,0:T(8,128)(2,1)S(1)}, bf16[2,128,1536]{2,1,0:T(8,128)(2,1)S(1)}) custom-call(bf16[384,128]{1,0:T(8,128)(2,1)S(1)} %get-tuple-element.68.after_ref.refs_0_, bf16[1536,1536]{1,0:T(8,128)(2,1)} %source_ref.5, bf16[20,128,1536]{2,1,0:T(8,128)(2,1)} %down_hbm.9), custom_call_target="tpu_custom_call" | custom-call | bytes 3145728 | tf_op jit(solution)/shard_map/fetch/pallas_call | solution.py:716
  38.3 0.9 %collective-permute-done.6.after_ref.refs_2_ = bf16[512,128]{1,0:T(8,128)(2,1)S(1)} collective-permute-done((bf16[512,128]{1,0:T(8,128)(2,1)S(1)}, bf16[512,128]{1,0:T(8,128)(2,1)S(1)}, u32[]{:S(2)}, u32[]{:S(2)}) %collective-permute-start.6) | collective-permute-done | bytes 131104 | tf_op jit(solution)/shard_map/ppermute | solution.py:710
  39.3 1.2 %collective-permute-start.8 = (bf16[512,128]{1,0:T(8,128)(2,1)S(1)}, bf16[512,128]{1,0:T(8,128)(2,1)S(1)}, u32[]{:S(2)}, u32[]{:S(2)}) collective-permute-start(bf16[512,128]{1,0:T(8,128)(2,1)S(1)} %collective-permute-done.6.after_ref.refs_2_), channel_id=1, source_target_pairs={{0,1},{1,0},{2,3},{3,2},{4,5},{5,4},{6,7},{7,6},{8,9},{9,8},{10,11... | collective-permute-start | bytes 393224 | tf_op jit(solution)/shard_map/ppermute | solution.py:710
  40.5 1.5 %fetch.4 = (bf16[384,1536]{1,0:T(8,128)(2,1)S(1)}, bf16[2,128,1536]{2,1,0:T(8,128)(2,1)S(1)}) custom-call(bf16[512,128]{1,0:T(8,128)(2,1)S(1)} %collective-permute-done.6.after_ref.refs_2_, bf16[1536,1536]{1,0:T(8,128)(2,1)} %source_ref.5, bf16[20,128,1536]{2,1,0:T(8,128)(2,1)} %down_hbm.9), custom_call_target="tpu_custom_call" | custom-call | bytes 1048576 | tf_op jit(solution)/shard_map/fetch/pallas_call | solution.py:716
  42.0 1.5 %fetch.5 = (bf16[384,1536]{1,0:T(8,128)(2,1)S(1)}, bf16[2,128,1536]{2,1,0:T(8,128)(2,1)S(1)}) custom-call(bf16[384,128]{1,0:T(8,128)(2,1)S(1)} %collective-permute-done.5.after_ref.mine_ref, bf16[1536,1536]{1,0:T(8,128)(2,1)} %source_ref.5, bf16[20,128,1536]{2,1,0:T(8,128)(2,1)} %down_hbm.9), custom_call_target="tpu_custom_call" | custom-call | bytes 1048576 | tf_op jit(solution)/shard_map/fetch/pallas_call | solution.py:716
  44.5 1.2 %collective-permute-start.10 = (bf16[384,128]{1,0:T(8,128)(2,1)S(1)}, bf16[384,128]{1,0:T(8,128)(2,1)S(1)}, u32[]{:S(2)}, u32[]{:S(2)}) collective-permute-start(bf16[384,128]{1,0:T(8,128)(2,1)S(1)} %collective-permute-done.4.after_ref.refs_5_), channel_id=1, source_target_pairs={{0,1},{1,0},{2,3},{3,2},{4,5},{5,4},{6,7},{7,6},{8,9},{9,8},{10,11... | collective-permute-start | bytes 294920 | tf_op jit(solution)/shard_map/ppermute | solution.py:710
  45.7 2.2 %early.1 = (f32[128,1536]{1,0:T(8,128)S(1)}, bf16[16,1536]{1,0:T(8,128)(2,1)S(1)}, bf16[8,128,1536]{2,1,0:T(8,128)(2,1)S(1)}) custom-call(bf16[384,128]{1,0:T(8,128)(2,1)S(1)} %collective-permute-done.4.after_ref.refs_5_, bf16[20,128,1536]{2,1,0:T(8,128)(2,1)} %down_hbm.9, bf16[768,1536]{1,0:T(8,128)(2,1)S(1)} %get-tuple-element.79.weight_ref, ...), custom_call_target="tpu_custom_call" | custom-call | bytes 4194304 | tf_op jit(solution)/shard_map/early/pallas_call | solution.py:861
  49.3 4.8 %experts.1 = (bf16[2,16,1536]{2,1,0:T(8,128)(2,1)S(1)}, f32[128,1536]{1,0:T(8,128)S(1)}, f32[16,1536]{1,0:T(8,128)S(1)}, bf16[16,1536]{1,0:T(8,128)(2,1)S(1)}) custom-call(f32[128,40]{1,0:T(8,128)S(1)} %get-tuple-element.56.count_ref, bf16[40,1536]{1,0:T(8,128)(2,1)S(1)} %bitcast.7, f32[12,128]{1,0:T(8,128)S(1)} %get-tuple-element.57.gain_ref, ...), custom_call_target="tpu_custom_call" | custom-call | tf_op jit(solution)/shard_map/experts/pallas_call | solution.py:905
  54.2 1.0 %collective-permute-start.11 = (bf16[2,16,1536]{2,1,0:T(8,128)(2,1)S(1)}, bf16[2,16,1536]{2,1,0:T(8,128)(2,1)S(1)}, u32[]{:S(2)}, u32[]{:S(2)}) collective-permute-start(bf16[2,16,1536]{2,1,0:T(8,128)(2,1)S(1)} %get-tuple-element.95), channel_id=1, source_target_pairs={{0,1},{1,0},{2,3},{3,2},{4,5},{5,4},{6,7},{7,6},{8,9},{9,8},{10,11... | collective-permute-start | bytes 294920 | tf_op jit(solution)/shard_map/ppermute | solution.py:710
  55.3 1.1 %collective-permute-start.12 = (bf16[2,16,1536]{2,1,0:T(8,128)(2,1)S(1)}, bf16[2,16,1536]{2,1,0:T(8,128)(2,1)S(1)}, u32[]{:S(2)}, u32[]{:S(2)}) collective-permute-start(bf16[2,16,1536]{2,1,0:T(8,128)(2,1)S(1)} %get-tuple-element.97), channel_id=1, source_target_pairs={{0,1},{1,0},{2,3},{3,2},{4,5},{5,4},{6,7},{7,6},{8,9},{9,8},{10,11... | collective-permute-start | bytes 294920 | tf_op jit(solution)/shard_map/ppermute | solution.py:710
  56.4 2.5 %collective-permute-done.11.got_ref = bf16[2,16,1536]{2,1,0:T(8,128)(2,1)S(1)} collective-permute-done((bf16[2,16,1536]{2,1,0:T(8,128)(2,1)S(1)}, bf16[2,16,1536]{2,1,0:T(8,128)(2,1)S(1)}, u32[]{:S(2)}, u32[]{:S(2)}) %collective-permute-start.11) | collective-permute-done | bytes 98336 | tf_op jit(solution)/shard_map/ppermute | solution.py:710
  59.5 1.9 %collective-permute-start.14 = (bf16[16,1536]{1,0:T(8,128)(2,1)S(1)}, bf16[16,1536]{1,0:T(8,128)(2,1)S(1)}, u32[]{:S(2)}, u32[]{:S(2)}) collective-permute-start(bf16[16,1536]{1,0:T(8,128)(2,1)S(1)} %get-tuple-element.96.after_ref), channel_id=1, source_target_pairs={{0,4},{1,5},{2,6},{3,7},{4,0},{5,1},{6,2},{7,3},{8,12},{9,13},{10,... | collective-permute-start | bytes 147464 | tf_op jit(solution)/shard_map/ppermute | solution.py:710
  61.4 2.0 %collective-permute-start.15 = (bf16[16,1536]{1,0:T(8,128)(2,1)S(1)}, bf16[16,1536]{1,0:T(8,128)(2,1)S(1)}, u32[]{:S(2)}, u32[]{:S(2)}) collective-permute-start(bf16[16,1536]{1,0:T(8,128)(2,1)S(1)} %get-tuple-element.100), channel_id=1, source_target_pairs={{0,2},{1,3},{2,0},{3,1},{4,6},{5,7},{6,4},{7,5},{8,10},{9,11},{10,... | collective-permute-start | bytes 147464 | tf_op jit(solution)/shard_map/ppermute | solution.py:710
  63.6 1.3 %collective-permute-done.13.refs_1_ = bf16[16,1536]{1,0:T(8,128)(2,1)S(1)} collective-permute-done((bf16[16,1536]{1,0:T(8,128)(2,1)S(1)}, bf16[16,1536]{1,0:T(8,128)(2,1)S(1)}, u32[]{:S(2)}, u32[]{:S(2)}) %collective-permute-start.13) | collective-permute-done | bytes 49184 | tf_op jit(solution)/shard_map/ppermute | solution.py:710
  (29 shorter events, 5.8 us)
Async XLA Ops:
  2.1 14.9 %collective-permute-start = (bf16[2,256,128]{2,1,0:T(8,128)(2,1)S(1)}, bf16[2,256,128]{2,1,0:T(8,128)(2,1)S(1)}, u32[]{:S(2)}, u32[]{:S(2)}) collective-permute-start(bf16[2,256,128]{2,1,0:T(8,128)(2,1)S(1)} %get-tuple-element.60), channel_id=1, source_target_pairs={{0,6},{1,7},{2,4},{3,5},{4,2},{5,3},{6,0},{7,1},{8,14},{9,15},{10,... | collective-permute-start | bytes 393224 | tf_op jit(solution)/shard_map/ppermute | solution.py:710
  7.2 11.1 %collective-permute-start.1 = (bf16[2,256,128]{2,1,0:T(8,128)(2,1)S(1)}, bf16[2,256,128]{2,1,0:T(8,128)(2,1)S(1)}, u32[]{:S(2)}, u32[]{:S(2)}) collective-permute-start(bf16[2,256,128]{2,1,0:T(8,128)(2,1)S(1)} %get-tuple-element.61), channel_id=1, source_target_pairs={{0,4},{1,5},{2,6},{3,7},{4,0},{5,1},{6,2},{7,3},{8,12},{9,13},{10,... | collective-permute-start | bytes 393224 | tf_op jit(solution)/shard_map/ppermute | solution.py:710
  7.2 11.1 %collective-permute-start.2 = (bf16[2,256,128]{2,1,0:T(8,128)(2,1)S(1)}, bf16[2,256,128]{2,1,0:T(8,128)(2,1)S(1)}, u32[]{:S(2)}, u32[]{:S(2)}) collective-permute-start(bf16[2,256,128]{2,1,0:T(8,128)(2,1)S(1)} %get-tuple-element.62), channel_id=1, source_target_pairs={{0,2},{1,3},{2,0},{3,1},{4,6},{5,7},{6,4},{7,5},{8,10},{9,11},{10,... | collective-permute-start | bytes 393224 | tf_op jit(solution)/shard_map/ppermute | solution.py:710
  15.1 15.8 %copy-start = (bf16[20,1536,256]{2,1,0:T(8,128)(2,1)S(1)}, bf16[20,1536,256]{2,1,0:T(8,128)(2,1)}, u32[]{:S(2)}) copy-start(bf16[20,1536,256]{2,1,0:T(8,128)(2,1)} %refs_8_.3) | copy-start | bytes 47185924
  18.5 12.5 %collective-permute-start.3 = (bf16[1024,128]{1,0:T(8,128)(2,1)S(1)}, bf16[1024,128]{1,0:T(8,128)(2,1)S(1)}, u32[]{:S(2)}, u32[]{:S(2)}) collective-permute-start(bf16[1024,128]{1,0:T(8,128)(2,1)S(1)} %get-tuple-element.66), channel_id=1, source_target_pairs={{0,1},{1,0},{2,3},{3,2},{4,5},{5,4},{6,7},{7,6},{8,9},{9,8},{10,11... | collective-permute-start | bytes 786440 | tf_op jit(solution)/shard_map/ppermute | solution.py:710
  32.6 6.7 %collective-permute-start.6 = (bf16[512,128]{1,0:T(8,128)(2,1)S(1)}, bf16[512,128]{1,0:T(8,128)(2,1)S(1)}, u32[]{:S(2)}, u32[]{:S(2)}) collective-permute-start(bf16[512,128]{1,0:T(8,128)(2,1)S(1)} %get-tuple-element.69.refs_0_), channel_id=1, source_target_pairs={{0,2},{1,3},{2,0},{3,1},{4,6},{5,7},{6,4},{7,5},{8,10},{9,11},{10,... | collective-permute-start | bytes 393224 | tf_op jit(solution)/shard_map/ppermute | solution.py:710
  32.7 9.3 %collective-permute-start.5 = (bf16[384,128]{1,0:T(8,128)(2,1)S(1)}, bf16[384,128]{1,0:T(8,128)(2,1)S(1)}, u32[]{:S(2)}, u32[]{:S(2)}) collective-permute-start(bf16[384,128]{1,0:T(8,128)(2,1)S(1)} %get-tuple-element.68.after_ref.refs_0_), channel_id=1, source_target_pairs={{0,6},{1,7},{2,4},{3,5},{4,2},{5,3},{6,0},{7,1},{8,14},{9,15},{10,... | collective-permute-start | bytes 294920 | tf_op jit(solution)/shard_map/ppermute | solution.py:710
  34.5 9.9 %collective-permute-start.4 = (bf16[384,128]{1,0:T(8,128)(2,1)S(1)}, bf16[384,128]{1,0:T(8,128)(2,1)S(1)}, u32[]{:S(2)}, u32[]{:S(2)}) collective-permute-start(bf16[384,128]{1,0:T(8,128)(2,1)S(1)} %get-tuple-element.68.after_ref.refs_0_), channel_id=1, source_target_pairs={{0,4},{1,5},{2,6},{3,7},{4,0},{5,1},{6,2},{7,3},{8,12},{9,13},{10,... | collective-permute-start | bytes 294920 | tf_op jit(solution)/shard_map/ppermute | solution.py:710
  36.1 9.5 %collective-permute-start.7 = (bf16[512,128]{1,0:T(8,128)(2,1)S(1)}, bf16[512,128]{1,0:T(8,128)(2,1)S(1)}, u32[]{:S(2)}, u32[]{:S(2)}) collective-permute-start(bf16[512,128]{1,0:T(8,128)(2,1)S(1)} %get-tuple-element.69.refs_0_), channel_id=1, source_target_pairs={{0,1},{1,0},{2,3},{3,2},{4,5},{5,4},{6,7},{7,6},{8,9},{9,8},{10,11... | collective-permute-start | bytes 393224 | tf_op jit(solution)/shard_map/ppermute | solution.py:710
  39.3 6.4 %collective-permute-start.8 = (bf16[512,128]{1,0:T(8,128)(2,1)S(1)}, bf16[512,128]{1,0:T(8,128)(2,1)S(1)}, u32[]{:S(2)}, u32[]{:S(2)}) collective-permute-start(bf16[512,128]{1,0:T(8,128)(2,1)S(1)} %collective-permute-done.6.after_ref.refs_2_), channel_id=1, source_target_pairs={{0,1},{1,0},{2,3},{3,2},{4,5},{5,4},{6,7},{7,6},{8,9},{9,8},{10,11... | collective-permute-start | bytes 393224 | tf_op jit(solution)/shard_map/ppermute | solution.py:710
  43.6 4.7 %collective-permute-start.9 = (bf16[384,128]{1,0:T(8,128)(2,1)S(1)}, bf16[384,128]{1,0:T(8,128)(2,1)S(1)}, u32[]{:S(2)}, u32[]{:S(2)}) collective-permute-start(bf16[384,128]{1,0:T(8,128)(2,1)S(1)} %collective-permute-done.5.after_ref.mine_ref), channel_id=1, source_target_pairs={{0,1},{1,0},{2,3},{3,2},{4,5},{5,4},{6,7},{7,6},{8,9},{9,8},{10,11... | collective-permute-start | bytes 294920 | tf_op jit(solution)/shard_map/ppermute | solution.py:710
  44.5 4.9 %copy-start.1 = (bf16[1536,40]{0,1:T(8,128)(2,1)S(1)}, bf16[1536,40]{0,1:T(8,128)(2,1)}, u32[]{:S(2)}) copy-start(bf16[1536,40]{0,1:T(8,128)(2,1)} %param.28) | copy-start | bytes 368644
  44.5 4.9 %collective-permute-start.10 = (bf16[384,128]{1,0:T(8,128)(2,1)S(1)}, bf16[384,128]{1,0:T(8,128)(2,1)S(1)}, u32[]{:S(2)}, u32[]{:S(2)}) collective-permute-start(bf16[384,128]{1,0:T(8,128)(2,1)S(1)} %collective-permute-done.4.after_ref.refs_5_), channel_id=1, source_target_pairs={{0,1},{1,0},{2,3},{3,2},{4,5},{5,4},{6,7},{7,6},{8,9},{9,8},{10,11... | collective-permute-start | bytes 294920 | tf_op jit(solution)/shard_map/ppermute | solution.py:710
  54.2 4.7 %collective-permute-start.11 = (bf16[2,16,1536]{2,1,0:T(8,128)(2,1)S(1)}, bf16[2,16,1536]{2,1,0:T(8,128)(2,1)S(1)}, u32[]{:S(2)}, u32[]{:S(2)}) collective-permute-start(bf16[2,16,1536]{2,1,0:T(8,128)(2,1)S(1)} %get-tuple-element.95), channel_id=1, source_target_pairs={{0,1},{1,0},{2,3},{3,2},{4,5},{5,4},{6,7},{7,6},{8,9},{9,8},{10,11... | collective-permute-start | bytes 294920 | tf_op jit(solution)/shard_map/ppermute | solution.py:710
  55.3 6.1 %collective-permute-start.12 = (bf16[2,16,1536]{2,1,0:T(8,128)(2,1)S(1)}, bf16[2,16,1536]{2,1,0:T(8,128)(2,1)S(1)}, u32[]{:S(2)}, u32[]{:S(2)}) collective-permute-start(bf16[2,16,1536]{2,1,0:T(8,128)(2,1)S(1)} %get-tuple-element.97), channel_id=1, source_target_pairs={{0,1},{1,0},{2,3},{3,2},{4,5},{5,4},{6,7},{7,6},{8,9},{9,8},{10,11... | collective-permute-start | bytes 294920 | tf_op jit(solution)/shard_map/ppermute | solution.py:710
  58.9 6.1 %collective-permute-start.13 = (bf16[16,1536]{1,0:T(8,128)(2,1)S(1)}, bf16[16,1536]{1,0:T(8,128)(2,1)S(1)}, u32[]{:S(2)}, u32[]{:S(2)}) collective-permute-start(bf16[16,1536]{1,0:T(8,128)(2,1)S(1)} %get-tuple-element.99), channel_id=1, source_target_pairs={{0,6},{1,7},{2,4},{3,5},{4,2},{5,3},{6,0},{7,1},{8,14},{9,15},{10,... | collective-permute-start | bytes 147464 | tf_op jit(solution)/shard_map/ppermute | solution.py:710
  59.5 6.1 %collective-permute-start.14 = (bf16[16,1536]{1,0:T(8,128)(2,1)S(1)}, bf16[16,1536]{1,0:T(8,128)(2,1)S(1)}, u32[]{:S(2)}, u32[]{:S(2)}) collective-permute-start(bf16[16,1536]{1,0:T(8,128)(2,1)S(1)} %get-tuple-element.96.after_ref), channel_id=1, source_target_pairs={{0,4},{1,5},{2,6},{3,7},{4,0},{5,1},{6,2},{7,3},{8,12},{9,13},{10,... | collective-permute-start | bytes 147464 | tf_op jit(solution)/shard_map/ppermute | solution.py:710
  61.4 4.2 %collective-permute-start.15 = (bf16[16,1536]{1,0:T(8,128)(2,1)S(1)}, bf16[16,1536]{1,0:T(8,128)(2,1)S(1)}, u32[]{:S(2)}, u32[]{:S(2)}) collective-permute-start(bf16[16,1536]{1,0:T(8,128)(2,1)S(1)} %get-tuple-element.100), channel_id=1, source_target_pairs={{0,2},{1,3},{2,0},{3,1},{4,6},{5,7},{6,4},{7,5},{8,10},{9,11},{10,... | collective-permute-start | bytes 147464 | tf_op jit(solution)/shard_map/ppermute | solution.py:710
